TPU v7x, 32 devices: a whole 2x2x4 slice. The times are simulated.
32 devices in a mesh: inst: 16 (over z, x, core), tp: 2 (over y).
Axes of the slice: x: 2, y: 2, z: 4, core: 2. Of those that a mesh axis runs over, the one named last changes fastest.
Arguments:
- prompt_query: bfloat16 [10240, 8192], P('inst', 'tp'), may hold values from -40 to 40
- prompt_pairs: bfloat16 [10240, 2048], P('inst', 'tp'), may hold values from -40 to 40
- decode_query: bfloat16 [64, 8192], P('inst'), may hold values from -40 to 40
- arrival_query: bfloat16 [16, 8192], P('inst'), may hold values from -40 to 40
- cache_pool: bfloat16 [160, 64, 2048], P(('inst', 'tp')), may hold values from -40 to 40
- page_table: int32 [64, 16], P('inst', 'tp'), may hold values from 0 to 4
- lengths: int32 [64], P('inst'), may hold values from 1 to 1024, as said below
- assignment: int32 [8], replicated, may hold values from 0 to 7, each once
Outputs:
- prefill_out: bfloat16 [10240, 8192], P('inst', 'tp')
- handed: bfloat16 [10240, 2048], P(('inst', 'tp'))
- decode_out: bfloat16 [64, 8192], P('inst')
- arrival_out: bfloat16 [16, 8192], P('inst')
Inputs may be any that keep to these rules, and one draw needn't show every extreme that they name: `lengths`: some cached request of a decode instance has length 1024 in every draw. `assignment`: each decode instance receives the request of exactly one prefill instance.
All inputs are finite; a program needn't handle non-finite values.
Results may differ from a plain program's by a relative error of at most 0.0075.
Values may be sent and summed in bfloat16 or wider, within the bound.
No kernel may reach another device: no remote copies, remote signals or barrier semaphores. Data moves between devices by JAX's collectives and lax.ppermute only.
A program may use at most 128 MiB of HBM per device.

v0:
```python
import functools

import jax
import jax.numpy as jnp
from jax import lax
from jax.experimental import pallas as pl
from jax.experimental.pallas import tpu as pltpu
from jax.sharding import PartitionSpec as P

QHEADS = 64
KVHEADS = 8
HEADDIM = 128
GROUP = QHEADS // KVHEADS
SCALE = HEADDIM ** (-0.5)
LOG2E = 1.4426950408889634
NEG_FILL = -1e30
TILE = 128
VMEM = 48 * 1024 * 1024


def dot_t(a, b):
    return lax.dot_general(a, b, (((1,), (1,)), ((), ())), preferred_element_type=jnp.float32)


def dot(a, b):
    return lax.dot_general(a, b, (((1,), (0,)), ((), ())), preferred_element_type=jnp.float32)


def prompt_kernel(heads, flag_ref, q_ref, kv_ref, *rest):
    out_ref = rest[-1]
    length = q_ref.shape[0]

    @pl.when(flag_ref[0] == 0)
    def _():
        out_ref[...] = jnp.zeros_like(out_ref)

    @pl.when(flag_ref[0] != 0)
    def _():
        rows_all = lax.broadcasted_iota(jnp.int32, (TILE, TILE), 0)
        cols_all = lax.broadcasted_iota(jnp.int32, (TILE, TILE), 1)
        below = jnp.concatenate([rows_all >= cols_all] * heads, axis=0)
        ones = jnp.ones((length, HEADDIM), jnp.bfloat16)
        values = jnp.concatenate([kv_ref[:, HEADDIM:], ones], axis=1)
        for start in range(0, length, TILE):
            stop = start + TILE
            queries = jnp.concatenate(
                [q_ref[start:stop, h * HEADDIM : (h + 1) * HEADDIM] for h in range(heads)], axis=0
            )
            scores = dot_t(queries, kv_ref[:stop, :HEADDIM])
            last = jnp.where(below, scores[:, start:], NEG_FILL)
            scores = jnp.concatenate([scores[:, :start], last], axis=1) if start else last
            peak = jnp.max(scores, axis=1, keepdims=True)
            weights = jnp.exp2((scores - peak) * (SCALE * LOG2E)).astype(jnp.bfloat16)
            mixed = dot(weights, values[:stop])
            result = (mixed[:, :HEADDIM] / mixed[:, HEADDIM:]).astype(jnp.bfloat16)
            for h in range(heads):
                out_ref[start:stop, h * HEADDIM : (h + 1) * HEADDIM] = result[
                    h * TILE : (h + 1) * TILE
                ]


def prompt_attention(flag, queries, pairs, first, steps, heads, earlier):
    length, width = queries.shape
    per_kv = GROUP // heads

    def q_map(i, flag_ref):
        return (0, jnp.where(flag_ref[0] != 0, i + first, 0))

    def kv_map(i, flag_ref):
        return (0, jnp.where(flag_ref[0] != 0, (i + first) // per_kv, 0))

    in_specs = [
        pl.BlockSpec((length, heads * HEADDIM), q_map),
        pl.BlockSpec((length, 2 * HEADDIM), kv_map),
    ]
    operands = [flag, queries, pairs]
    aliases = {}
    if earlier is not None:
        in_specs.append(pl.BlockSpec(memory_space=pl.ANY))
        operands.append(earlier)
        aliases = {3: 0}
    return pl.pallas_call(
        functools.partial(prompt_kernel, heads),
        out_shape=jax.ShapeDtypeStruct((length, width), jnp.bfloat16),
        grid_spec=pltpu.PrefetchScalarGridSpec(
            num_scalar_prefetch=1,
            grid=(steps,),
            in_specs=in_specs,
            out_specs=pl.BlockSpec((length, heads * HEADDIM), lambda i, flag_ref: (0, i + first)),
        ),
        input_output_aliases=aliases,
        compiler_params=pltpu.CompilerParams(vmem_limit_bytes=VMEM),
        cost_estimate=pl.CostEstimate(
            flops=steps * heads * 4 * length * length * HEADDIM,
            bytes_accessed=steps * heads * length * HEADDIM * 4,
            transcendentals=steps * heads * length * length // 2,
        ),
        name="prompt_attention",
    )(*operands)


def cache_kernel(q_ref, kv_ref, count_ref, mixed_ref, stats_ref):
    count = count_ref[...]
    here = count > 0.0
    scores = dot_t(q_ref[0], kv_ref[:, :HEADDIM]) * SCALE
    scores = jnp.where(here, scores, NEG_FILL)
    peak = jnp.max(scores, axis=1, keepdims=True)
    weights = jnp.where(here, jnp.exp(scores - peak), 0.0)
    total = jnp.sum(weights * count, axis=1, keepdims=True)
    rounded = weights.astype(jnp.bfloat16).astype(jnp.float32) * count
    mixed_ref[0] = dot(rounded.astype(jnp.bfloat16), kv_ref[:, HEADDIM:])
    lane = lax.broadcasted_iota(jnp.int32, stats_ref.shape[1:], 1)
    stats_ref[0] = jnp.where(lane < HEADDIM // 2, peak, total)


def cache_attention(queries, pool, count):
    rows = queries.shape[1]
    tokens = pool.shape[0]
    shape = jax.ShapeDtypeStruct((KVHEADS, rows, HEADDIM), jnp.float32)
    block = pl.BlockSpec((1, rows, HEADDIM), lambda h: (h, 0, 0))
    return pl.pallas_call(
        cache_kernel,
        out_shape=(shape, shape),
        grid=(KVHEADS,),
        in_specs=[
            block,
            pl.BlockSpec((tokens, 2 * HEADDIM), lambda h: (0, h)),
            pl.BlockSpec((rows, tokens), lambda h: (0, 0)),
        ],
        out_specs=(block, block),
        compiler_params=pltpu.CompilerParams(vmem_limit_bytes=VMEM),
        name="cache_attention",
    )(queries, pool, count)


def fresh_kernel(q_ref, kv_ref, out_ref):
    scores = dot_t(q_ref[0], kv_ref[:, :HEADDIM]) * SCALE
    peak = jnp.max(scores, axis=1, keepdims=True)
    weights = jnp.exp(scores - peak)
    total = jnp.sum(weights, axis=1, keepdims=True)
    mixed = dot(weights.astype(jnp.bfloat16), kv_ref[:, HEADDIM:])
    out_ref[0] = (mixed / total).astype(jnp.bfloat16)


def fresh_attention(queries, pairs):
    length, width = pairs.shape
    block = pl.BlockSpec((1, GROUP, HEADDIM), lambda h: (h, 0, 0))
    return pl.pallas_call(
        fresh_kernel,
        out_shape=jax.ShapeDtypeStruct(queries.shape, jnp.bfloat16),
        grid=(queries.shape[0],),
        in_specs=[block, pl.BlockSpec((length, 2 * HEADDIM), lambda h: (0, h))],
        out_specs=block,
        compiler_params=pltpu.CompilerParams(vmem_limit_bytes=VMEM),
        name="fresh_attention",
    )(queries, pairs)


def relay_handoff(pairs, source, inst_count):
    half = inst_count // 2
    moved = lax.all_to_all(pairs, "tp", split_axis=0, concat_axis=1, tiled=True)
    lanes = 1024 if moved.size % (inst_count * 1024) == 0 else HEADDIM
    pieces = moved.reshape(inst_count, -1, lanes)
    spread = lax.all_to_all(pieces, "inst", split_axis=0, concat_axis=0, tiled=True)
    chosen = jnp.stack(
        [lax.dynamic_index_in_dim(spread, source[d], 0, False) for d in range(half)], axis=0
    )
    outgoing = jnp.concatenate([jnp.zeros_like(chosen), chosen], axis=0)
    delivered = lax.all_to_all(outgoing, "inst", split_axis=0, concat_axis=0, tiled=True)
    return delivered.reshape(moved.shape)


def shards(
    prompt_query,
    prompt_pairs,
    decode_query,
    arrival_query,
    cache_pool,
    page_table,
    lengths,
    assignment,
):
    inst_count = lax.axis_size("inst")
    tp_count = lax.axis_size("tp")
    half = inst_count // 2
    inst = lax.axis_index("inst")
    tp_index = lax.axis_index("tp")
    is_prefill = inst < half
    flag = is_prefill.astype(jnp.int32).reshape(1)
    groups = [list(range(half)), list(range(half, inst_count))]
    decode_ids = jnp.arange(half, dtype=jnp.int32)
    matches = assignment[None, :] == decode_ids[:, None]
    source = jnp.sum(jnp.where(matches, decode_ids[None, :], 0), axis=1).astype(jnp.int32)

    handed = relay_handoff(prompt_pairs, source, inst_count)

    sent = lax.ppermute(arrival_query, "inst", [(i + half, i) for i in range(half)])
    every = lax.all_gather(sent, "inst", axis=0, tiled=True, axis_index_groups=groups)
    target = lax.dynamic_index_in_dim(assignment, lax.rem(inst, half), 0, False)
    kv_here = prompt_pairs.shape[1] // (2 * HEADDIM)
    width = kv_here * GROUP * HEADDIM
    mine = lax.dynamic_slice(every, (target, tp_index * width), (1, width))
    fresh = fresh_attention(mine.reshape(kv_here, GROUP, HEADDIM), prompt_pairs)
    fresh = lax.ppermute(fresh.reshape(1, width), "inst", [(i, i + half) for i in range(half)])
    results = lax.all_gather(fresh, "inst", axis=0, tiled=True, axis_index_groups=groups)
    from_inst = lax.dynamic_index_in_dim(source, lax.rem(inst, half), 0, False)
    part = lax.dynamic_index_in_dim(results, from_inst, 0, True)
    arrival_out = lax.all_gather(part, "tp", axis=1, tiled=True)
    arrival_out = jnp.where(is_prefill, jnp.zeros_like(arrival_out), arrival_out)

    rows = decode_query.shape[0]
    pages, page_len = cache_pool.shape[0], cache_pool.shape[1]
    slots = page_table.shape[1]
    places = tp_index * slots * page_len + jnp.arange(slots * page_len, dtype=jnp.int32)
    valid = (places.reshape(1, slots, page_len) < lengths[:, None, None])[:, None]
    same = page_table[:, None, :] == jnp.arange(pages, dtype=jnp.int32)[None, :, None]
    count = jnp.sum(jnp.where(valid & same[..., None], 1.0, 0.0), axis=2)
    count = count.reshape(rows, 1, pages * page_len)
    count = jnp.broadcast_to(count, (rows, GROUP, pages * page_len)).reshape(rows * GROUP, -1)
    queries = decode_query.reshape(rows, KVHEADS, GROUP, HEADDIM).transpose(1, 0, 2, 3)
    mixed, stats = cache_attention(
        queries.reshape(KVHEADS, rows * GROUP, HEADDIM),
        cache_pool.reshape(pages * page_len, -1),
        count,
    )
    parts = lax.all_gather(jnp.concatenate([mixed, stats], axis=2), "tp")
    peaks = parts[:, :, :, HEADDIM : HEADDIM + 1]
    totals = parts[:, :, :, -1:]
    factors = jnp.exp(peaks - jnp.max(peaks, axis=0, keepdims=True))
    summed = jnp.sum(parts[:, :, :, :HEADDIM] * factors, axis=0)
    total = jnp.sum(totals * factors, axis=0)
    finished = (summed / total).astype(jnp.bfloat16)
    finished = finished.reshape(KVHEADS, rows, GROUP, HEADDIM).transpose(1, 0, 2, 3)
    finished = finished.reshape(rows, QHEADS * HEADDIM)
    decode_out = jnp.where(is_prefill, jnp.zeros_like(finished), finished)

    heads = GROUP // 2
    steps = prompt_query.shape[1] // (heads * HEADDIM)
    prefill_out = prompt_attention(flag, prompt_query, prompt_pairs, 0, steps, heads, None)
    return (prefill_out, handed, decode_out, arrival_out)


def solution(mesh):
    return jax.shard_map(
        shards,
        mesh=mesh,
        in_specs=(
            P("inst", "tp"),
            P("inst", "tp"),
            P("inst", None),
            P("inst", None),
            P(("inst", "tp"), None, None),
            P("inst", "tp"),
            P("inst"),
            P(),
        ),
        out_specs=(P("inst", "tp"), P(("inst", "tp"), None), P("inst", None), P("inst", None)),
        check_vma=False,
    )
```

profile of v0, /device:TPU:24, one launch (start us, length us, event | category | flops | bytes accessed | tf_op | source)
XLA Modules:
  0.0 157.3 jit_solution(11206844482196112572)
XLA Ops:
  0.6 0.0 copy-start.6
  0.6 0.0 copy-start.5
  0.7 3.8 %all-to-all-start = ((bf16[2,320,1024]{2,1,0:T(8,128)(2,1)}), bf16[2,320,1024]{2,1,0:T(8,128)(2,1)S(1)}, u32[]{:S(2)}, u32[]{:S(2)}) async-start(bf16[2,320,1024]{2,1,0:T(8,128)(2,1)} %bitcast.49), calls=%async_computation | async-start | bytes 2621440 | tf_op jit(solution)/shard_map/all_to_all | solution.py:161
  4.4 0.0 copy-done.6
  4.4 2.2 %collective-permute-start = (bf16[1,8192]{1,0:T(2,128)(2,1)S(1)}, bf16[1,8192]{1,0:T(2,128)(2,1)S(1)}, u32[]{:S(2)}, u32[]{:S(2)}) collective-permute-start(bf16[1,8192]{1,0:T(2,128)(2,1)S(1)} %copy-done.6), channel_id=1, source_target_pairs={{16,0},{18,2},{20,4},{22,6},{24,8},{26,10},{28,12},{30,14},{17,1},... | collective-permute-start | bytes 49160 | tf_op jit(solution)/shard_map/ppermute | solution.py:197
  6.7 0.0 copy-done.5
  6.7 0.1 broadcast_compare_fusion
  6.8 14.3 %all-to-all-done = bf16[2,320,1024]{2,1,0:T(8,128)(2,1)S(1)} async-done(((bf16[2,320,1024]{2,1,0:T(8,128)(2,1)}), bf16[2,320,1024]{2,1,0:T(8,128)(2,1)S(1)}, u32[]{:S(2)}, u32[]{:S(2)}) %all-to-all-start) | async-done | bytes 1310752 | tf_op jit(solution)/shard_map/all_to_all | solution.py:161
  21.1 1.3 copy.32
  22.4 1.4 reshape.76
  23.8 0.0 copy-start.4
  23.8 0.0 copy-start.3
  23.8 0.0 copy-start.1
  23.8 6.2 %all-to-all-start.1 = ((bf16[16,40,1024]{2,1,0:T(8,128)(2,1)}), bf16[16,40,1024]{2,1,0:T(8,128)(2,1)}, u32[]{:S(2)}, u32[]{:S(2)}) async-start(bf16[16,40,1024]{2,1,0:T(8,128)(2,1)} %reshape.76), calls=%async_computation.1 | async-start | bytes 2621440 | tf_op jit(solution)/shard_map/all_to_all | solution.py:164
  30.0 0.0 copy-done.4
  30.0 0.1 select_reduce_fusion
  30.1 0.1 broadcast_in_dim.51
  30.2 0.0 copy-done.3
  30.2 0.0 copy-done.1
  30.2 3.1 %cache_attention.1 = (f32[8,32,128]{2,1,0:T(8,128)S(1)}, f32[8,32,128]{2,1,0:T(8,128)S(1)}) custom-call(bf16[8,32,128]{2,1,0:T(8,128)(2,1)S(1)} %copy_bitcast_fusion.3.q_ref, bf16[320,2048]{1,0:T(8,128)(2,1)S(1)} %bitcast.50, f32[32,320]{1,0:T(8,128)S(1)} %broadcast_bitcast_fusion.count_ref), custom_call_target="tpu_custom_call" | custom-call | tf_op jit(solution)/shard_map/cache_attention/pallas_call | solution.py:121
  33.4 9.0 %all-gather = f32[16,32,256]{2,1,0:T(8,128)S(1)} all-gather(f32[8,32,256]{2,1,0:T(8,128)S(1)} %pad_maximum_fusion), channel_id=2, replica_groups=mesh['inst'=16,'tp'=2] {'tp'}, dimensions={0}, use_global_device_ids=true | all-gather | bytes 786432 | tf_op jit(solution)/shard_map/all_gather | solution.py:226
  42.4 0.0 copy-start.7
  42.4 1.3 copy.34
  43.7 0.0 copy-start
  43.8 0.0 copy-done.7
  43.8 0.1 select_reduce_fusion.1
  43.9 0.9 broadcast_dynamic-update-slice_fusion
  44.8 0.9 fusion
  45.7 0.0 copy-done
  45.7 0.0 copy-start.2
  45.7 4.9 %prompt_attention.1 = bf16[640,4096]{1,0:T(8,128)(2,1)} custom-call(s32[1]{0:T(128)} %bitcast.flag_ref, bf16[640,4096]{1,0:T(8,128)(2,1)} %q_ref.1, bf16[640,1024]{1,0:T(8,128)(2,1)S(1)} %copy-done), custom_call_target="tpu_custom_call" | custom-call | flops 6710886400 | bytes 10485760 | tf_op jit(solution)/shard_map/prompt_attention/pallas_call | solution.py:82
  50.6 0.7 fusion.4
  51.3 0.6 dynamic_slice.47
  63.1 0.0 copy-done.2
  63.1 0.2 copy.35
  63.3 0.1 div.11
  68.9 0.0 collective-permute-done
  68.9 12.2 %all-gather.1 = bf16[8,1,8192]{2,1,0:T(2,128)(2,1)S(1)} all-gather(bf16[1,1,8192]{2,1,0:T(2,128)(2,1)S(1)} %bitcast.58), channel_id=1, replica_groups={{0,2,4,6,8,10,12,14},{16,18,20,22,24,26,28,30},{1,3,5,7,9,11,13,15},{17..., dimensions={0}, use_global_device_ids=true | all-gather | bytes 147456 | tf_op jit(solution)/shard_map/all_gather | solution.py:198
  81.2 0.1 dynamic-slice_reduce_fusion
  81.2 1.8 %fresh_attention.1 = bf16[4,8,128]{2,1,0:T(8,128)(2,1)S(1)} custom-call(bf16[4,8,128]{2,1,0:T(8,128)(2,1)S(1)} %bitcast.51, bf16[640,1024]{1,0:T(8,128)(2,1)S(1)} %copy-done), custom_call_target="tpu_custom_call" | custom-call | tf_op jit(solution)/shard_map/fresh_attention/pallas_call | solution.py:148
  83.0 1.3 collective-permute-start.1
  84.3 0.0 all-to-all-done.1
  84.4 1.5 dynamic-slice_dynamic-update-slice_fusion.7
  85.9 1.5 dynamic-slice_dynamic-update-slice_fusion.6
  87.4 1.5 dynamic-slice_dynamic-update-slice_fusion.5
  88.9 1.5 dynamic-slice_dynamic-update-slice_fusion.4
  90.5 1.5 dynamic-slice_dynamic-update-slice_fusion.3
  92.0 1.5 dynamic-slice_dynamic-update-slice_fusion.2
  93.5 1.5 dynamic-slice_dynamic-update-slice_fusion.1
  95.1 1.5 dynamic-slice_dynamic-update-slice_fusion
  96.6 20.5 %all-to-all-start.2 = ((bf16[16,40,1024]{2,1,0:T(8,128)(2,1)}), bf16[16,40,1024]{2,1,0:T(8,128)(2,1)S(1)}, u32[]{:S(2)}, u32[]{:S(2)}) async-start(bf16[16,40,1024]{2,1,0:T(8,128)(2,1)} %dynamic-slice_dynamic-update-slice_fusion), calls=%async_computation.2 | async-start | bytes 2621440 | tf_op jit(solution)/shard_map/all_to_all | solution.py:169
  117.0 0.1 copy_bitcast_fusion.2
  118.5 0.7 copy.44
  119.8 0.0 collective-permute-done.1
  119.8 31.1 %all-gather.2 = bf16[8,1,4096]{2,1,0:T(2,128)(2,1)S(1)} all-gather(bf16[1,1,4096]{2,1,0:T(2,128)(2,1)S(1)} %bitcast.59), channel_id=1, replica_groups={{0,2,4,6,8,10,12,14},{16,18,20,22,24,26,28,30},{1,3,5,7,9,11,13,15},{17..., dimensions={0}, use_global_device_ids=true | all-gather | bytes 73728 | tf_op jit(solution)/shard_map/all_gather | solution.py:205
  151.0 4.4 %all_gather.19 = bf16[1,8192]{1,0:T(2,128)(2,1)S(1)} all-gather(bf16[1,4096]{1,0:T(2,128)(2,1)S(1)} %dynamic-slice_bitcast_fusion), channel_id=1, replica_groups=mesh['inst'=16,'tp'=2] {'tp'}, dimensions={1}, use_global_device_ids=true | all-gather | bytes 24576 | tf_op jit(solution)/shard_map/all_gather | solution.py:208
  155.4 0.7 broadcast_select_fusion
  156.0 0.0 all-to-all-done.2
  156.0 1.3 reshape.77
  (9 shorter events, 0.1 us)
Async XLA Ops:
  0.6 3.8 %copy-start.6 = (bf16[1,8192]{1,0:T(2,128)(2,1)S(1)}, bf16[1,8192]{1,0:T(2,128)(2,1)}, u32[]{:S(2)}) copy-start(bf16[1,8192]{1,0:T(2,128)(2,1)} %param.11) | copy-start | bytes 49156
  0.6 6.1 %copy-start.5 = (s32[4]{0:T(128)S(1)}, s32[4]{0:T(128)}, u32[]{:S(2)}) copy-start(s32[4]{0:T(128)} %param.14) | copy-start | bytes 52
  0.7 20.4 %all-to-all-start = ((bf16[2,320,1024]{2,1,0:T(8,128)(2,1)}), bf16[2,320,1024]{2,1,0:T(8,128)(2,1)S(1)}, u32[]{:S(2)}, u32[]{:S(2)}) async-start(bf16[2,320,1024]{2,1,0:T(8,128)(2,1)} %bitcast.49), calls=%async_computation | async-start | bytes 2621440 | tf_op jit(solution)/shard_map/all_to_all | solution.py:161
  4.4 64.5 %collective-permute-start = (bf16[1,8192]{1,0:T(2,128)(2,1)S(1)}, bf16[1,8192]{1,0:T(2,128)(2,1)S(1)}, u32[]{:S(2)}, u32[]{:S(2)}) collective-permute-start(bf16[1,8192]{1,0:T(2,128)(2,1)S(1)} %copy-done.6), channel_id=1, source_target_pairs={{16,0},{18,2},{20,4},{22,6},{24,8},{26,10},{28,12},{30,14},{17,1},... | collective-permute-start | bytes 49160 | tf_op jit(solution)/shard_map/ppermute | solution.py:197
  23.8 6.2 %copy-start.4 = (s32[4,8]{1,0:T(4,128)S(1)}, s32[4,8]{1,0:T(4,128)}, u32[]{:S(2)}) copy-start(s32[4,8]{1,0:T(4,128)} %param.13) | copy-start | bytes 388
  23.8 6.4 %copy-start.3 = (bf16[4,8192]{1,0:T(4,128)(2,1)S(1)}, bf16[4,8192]{1,0:T(4,128)(2,1)}, u32[]{:S(2)}) copy-start(bf16[4,8192]{1,0:T(4,128)(2,1)} %param.10) | copy-start | bytes 196612
  23.8 6.4 %copy-start.1 = (bf16[5,64,2048]{2,1,0:T(8,128)(2,1)S(1)}, bf16[5,64,2048]{2,1,0:T(8,128)(2,1)}, u32[]{:S(2)}) copy-start(bf16[5,64,2048]{2,1,0:T(8,128)(2,1)} %param.12) | copy-start | bytes 3932164
  23.8 60.5 %all-to-all-start.1 = ((bf16[16,40,1024]{2,1,0:T(8,128)(2,1)}), bf16[16,40,1024]{2,1,0:T(8,128)(2,1)}, u32[]{:S(2)}, u32[]{:S(2)}) async-start(bf16[16,40,1024]{2,1,0:T(8,128)(2,1)} %reshape.76), calls=%async_computation.1 | async-start | bytes 2621440 | tf_op jit(solution)/shard_map/all_to_all | solution.py:164
  42.4 1.3 copy-start.7
  43.7 2.0 %copy-start = (bf16[640,1024]{1,0:T(8,128)(2,1)S(1)}, bf16[640,1024]{1,0:T(8,128)(2,1)}, u32[]{:S(2)}) copy-start(bf16[640,1024]{1,0:T(8,128)(2,1)} %kv_ref.3) | copy-start | bytes 3932164
  45.7 17.3 %copy-start.2 = (f32[8,32,128]{1,0,2:T(8,128)S(1)}, f32[8,32,128]{1,0,2:T(8,128)}, u32[]{:S(2)}) copy-start(f32[8,32,128]{1,0,2:T(8,128)} %fusion) | copy-start | bytes 393220
  83.0 36.7 %collective-permute-start.1 = (bf16[1,4096]{1,0:T(2,128)(2,1)S(1)}, bf16[1,4096]{1,0:T(2,128)(2,1)S(1)}, u32[]{:S(2)}, u32[]{:S(2)}) collective-permute-start(bf16[1,4096]{1,0:T(2,128)(2,1)S(1)} %reshape.83), channel_id=1, source_target_pairs={{0,16},{2,18},{4,20},{6,22},{8,24},{10,26},{12,28},{14,30},{1,17},... | collective-permute-start | bytes 24584 | tf_op jit(solution)/shard_map/ppermute | solution.py:204
  96.6 59.4 %all-to-all-start.2 = ((bf16[16,40,1024]{2,1,0:T(8,128)(2,1)}), bf16[16,40,1024]{2,1,0:T(8,128)(2,1)S(1)}, u32[]{:S(2)}, u32[]{:S(2)}) async-start(bf16[16,40,1024]{2,1,0:T(8,128)(2,1)} %dynamic-slice_dynamic-update-slice_fusion), calls=%async_computation.2 | async-start | bytes 2621440 | tf_op jit(solution)/shard_map/all_to_all | solution.py:169
where the time goes:
time: 159 us; the launch traced here: 157 us
  blocking collectives  56.8 us (36%)
  starting transfers between devices  33.9 us (21%)
  local copies, waits for them, and re-layouts  20.9 us (13%)
  between operations  19.5 us (12%)
  waiting for transfers between devices  14.3 us (9%)
  Pallas kernels  9.83 us (6%)
  other arithmetic  2.02 us (1%)
    all_gather x1, blocking collectives, shards(): lax.all_gather(fresh, 'inst', axis=0, tiled=True, axis_index_groups=groups)  31.1 us
    all_to_all x1, starting transfers between devices, relay_handoff(): lax.all_to_all(outgoing, 'inst', split_axis=0, concat_axis=0, tiled=True)  20.5 us
    all_to_all x1, waiting for transfers between devices, relay_handoff(): moved = lax.all_to_all(pairs, 'tp', split_axis=0, concat_axis=1, tiled=True)  14.3 us
    unnamed x25, local copies, waits for them, and re-layouts  12.3 us
    all_gather x1, blocking collectives, shards(): lax.all_gather(sent, 'inst', axis=0, tiled=True, axis_index_groups=groups)  12.2 us
    all_gather x1, blocking collectives, shards(): parts = lax.all_gather(jnp.concatenate([mixed, stats], axis=2), 'tp')  9.04 us
    all_to_all x1, starting transfers between devices, relay_handoff(): lax.all_to_all(pieces, 'inst', split_axis=0, concat_axis=0, tiled=True)  6.18 us
    pallas_call x1, Pallas kernels, prompt_attention(): pl.pallas_call(functools.partial(prompt_kernel, heads), out_shape=jax.Sha...  4.9 us
  transfers between devices with their start and end apart: 5, of which 1 were waited for; matrix products, arithmetic and copies ran while one was open for 14% of the time, Pallas kernels for 6%

commit v1 on v0

v1 whole, which is shorter than its diff:
```python
import functools

import jax
import jax.numpy as jnp
from jax import lax
from jax.experimental import pallas as pl
from jax.experimental.pallas import tpu as pltpu
from jax.sharding import PartitionSpec as P

QHEADS = 64
KVHEADS = 8
HEADDIM = 128
GROUP = QHEADS // KVHEADS
SCALE = HEADDIM ** (-0.5)
LOG2E = 1.4426950408889634
NEG_FILL = -1e30
TILE = 128
VMEM = 24 * 1024 * 1024
SMALL = 1024 * 1024
LARGE = 57 * 1024 * 1024
COST = pl.CostEstimate(flops=1, bytes_accessed=1, transcendentals=0)


def dot_t(a, b):
    return lax.dot_general(a, b, (((1,), (1,)), ((), ())), preferred_element_type=jnp.float32)


def dot(a, b):
    return lax.dot_general(a, b, (((1,), (0,)), ((), ())), preferred_element_type=jnp.float32)


def prompt_kernel(heads, flag_ref, q_ref, kv_ref, *rest):
    out_ref = rest[-2]
    length = q_ref.shape[0]

    @pl.when(flag_ref[0] == 0)
    def _():
        out_ref[...] = jnp.zeros_like(out_ref)

    @pl.when(flag_ref[0] != 0)
    def _():
        rows_all = lax.broadcasted_iota(jnp.int32, (TILE, TILE), 0)
        cols_all = lax.broadcasted_iota(jnp.int32, (TILE, TILE), 1)
        below = jnp.concatenate([rows_all >= cols_all] * heads, axis=0)
        ones = jnp.ones((length, HEADDIM), jnp.bfloat16)
        values = jnp.concatenate([kv_ref[:, HEADDIM:], ones], axis=1)
        for start in range(0, length, TILE):
            stop = start + TILE
            queries = jnp.concatenate(
                [q_ref[start:stop, h * HEADDIM : (h + 1) * HEADDIM] for h in range(heads)], axis=0
            )
            scores = dot_t(queries, kv_ref[:stop, :HEADDIM])
            last = jnp.where(below, scores[:, start:], NEG_FILL)
            scores = jnp.concatenate([scores[:, :start], last], axis=1) if start else last
            peak = jnp.max(scores, axis=1, keepdims=True)
            weights = jnp.exp2((scores - peak) * (SCALE * LOG2E)).astype(jnp.bfloat16)
            mixed = dot(weights, values[:stop])
            result = (mixed[:, :HEADDIM] / mixed[:, HEADDIM:]).astype(jnp.bfloat16)
            for h in range(heads):
                out_ref[start:stop, h * HEADDIM : (h + 1) * HEADDIM] = result[
                    h * TILE : (h + 1) * TILE
                ]


MARK = jax.ShapeDtypeStruct((8, 128), jnp.float32)
IN_HBM = pl.BlockSpec(memory_space=pltpu.HBM)
ANYWHERE = pl.BlockSpec(memory_space=pl.ANY)


def prompt_attention(flag, queries, pairs, first, steps, heads, earlier, after):
    length, width = queries.shape
    per_kv = GROUP // heads

    def q_map(i, flag_ref):
        return (0, jnp.where(flag_ref[0] != 0, i + first, 0))

    def kv_map(i, flag_ref):
        return (0, jnp.where(flag_ref[0] != 0, (i + first) // per_kv, 0))

    in_specs = [
        pl.BlockSpec((length, heads * HEADDIM), q_map),
        pl.BlockSpec((length, 2 * HEADDIM), kv_map),
    ]
    operands = [flag, queries, pairs]
    aliases = {}
    if earlier is not None:
        in_specs.append(ANYWHERE)
        operands.append(earlier)
        aliases = {3: 0}
    return pl.pallas_call(
        functools.partial(prompt_kernel, heads),
        out_shape=(jax.ShapeDtypeStruct((length, width), jnp.bfloat16), MARK),
        grid_spec=pltpu.PrefetchScalarGridSpec(
            num_scalar_prefetch=1,
            grid=(steps,),
            in_specs=in_specs + [IN_HBM] * len(after),
            out_specs=(
                pl.BlockSpec((length, heads * HEADDIM), lambda i, flag_ref: (0, i + first)),
                IN_HBM,
            ),
        ),
        input_output_aliases=aliases,
        compiler_params=pltpu.CompilerParams(vmem_limit_bytes=LARGE),
        cost_estimate=COST,
        name="prompt_attention",
    )(*operands, *after)


def cache_kernel(flag_ref, q_ref, kv_ref, count_ref, *rest):
    out_ref = rest[-2]

    @pl.when(flag_ref[0] != 0)
    def _():
        out_ref[...] = jnp.zeros_like(out_ref)

    @pl.when(flag_ref[0] == 0)
    def _():
        rows, tokens = count_ref.shape
        count = jnp.broadcast_to(count_ref[...][:, None, :], (rows, GROUP, tokens))
        count = count.reshape(rows * GROUP, tokens)
        here = count > 0.0
        queries = q_ref[...].astype(jnp.float32).reshape(rows * GROUP, HEADDIM)
        scores = dot_t(queries.astype(jnp.bfloat16), kv_ref[:, :HEADDIM]) * SCALE
        scores = jnp.where(here, scores, NEG_FILL)
        peak = jnp.max(scores, axis=1, keepdims=True)
        weights = jnp.where(here, jnp.exp(scores - peak), 0.0)
        total = jnp.sum(weights * count, axis=1, keepdims=True)
        rounded = weights.astype(jnp.bfloat16).astype(jnp.float32) * count
        out_ref[0, :, :HEADDIM] = dot(rounded.astype(jnp.bfloat16), kv_ref[:, HEADDIM:])
        lane = lax.broadcasted_iota(jnp.int32, (rows * GROUP, HEADDIM), 1)
        out_ref[0, :, HEADDIM:] = jnp.where(lane < HEADDIM // 2, peak, total)


def cache_attention(flag, queries, pool, count, after):
    rows = queries.shape[0]
    tokens = pool.shape[0]
    return pl.pallas_call(
        cache_kernel,
        out_shape=(
            jax.ShapeDtypeStruct((KVHEADS, rows * GROUP, 2 * HEADDIM), jnp.float32),
            MARK,
        ),
        grid_spec=pltpu.PrefetchScalarGridSpec(
            num_scalar_prefetch=1,
            grid=(KVHEADS,),
            in_specs=[
                pl.BlockSpec((rows, GROUP, HEADDIM), lambda h, flag_ref: (0, h, 0)),
                pl.BlockSpec((tokens, 2 * HEADDIM), lambda h, flag_ref: (0, h * (1 - flag_ref[0]))),
                pl.BlockSpec((rows, tokens), lambda h, flag_ref: (0, 0)),
            ]
            + [IN_HBM] * len(after),
            out_specs=(
                pl.BlockSpec((1, rows * GROUP, 2 * HEADDIM), lambda h, flag_ref: (h, 0, 0)),
                IN_HBM,
            ),
        ),
        compiler_params=pltpu.CompilerParams(vmem_limit_bytes=VMEM),
        cost_estimate=COST,
        name="cache_attention",
    )(flag, queries, pool, count, *after)


def combine_kernel(count, flag_ref, *refs):
    part_refs, out_ref = refs[:count], refs[-2]

    @pl.when(flag_ref[0] != 0)
    def _():
        out_ref[...] = jnp.zeros_like(out_ref)

    @pl.when(flag_ref[0] == 0)
    def _():
        parts = [ref[n] for ref in part_refs for n in range(ref.shape[0])]
        peaks = [part[:, HEADDIM : HEADDIM + 1] for part in parts]
        peak = functools.reduce(jnp.maximum, peaks)
        factors = [jnp.exp(p - peak) for p in peaks]
        total = sum(part[:, -1:] * f for part, f in zip(parts, factors))
        mixed = sum(part[:, :HEADDIM] * f for part, f in zip(parts, factors))
        out_ref[...] = (mixed / total).reshape(out_ref.shape).astype(jnp.bfloat16)


def combine_parts(flag, parts, rows, after):
    return pl.pallas_call(
        functools.partial(combine_kernel, len(parts)),
        out_shape=(jax.ShapeDtypeStruct((rows, QHEADS, HEADDIM), jnp.bfloat16), MARK),
        grid_spec=pltpu.PrefetchScalarGridSpec(
            num_scalar_prefetch=1,
            grid=(KVHEADS,),
            in_specs=[
                pl.BlockSpec(
                    (part.shape[0], None, rows * GROUP, 2 * HEADDIM),
                    lambda h, flag_ref: (0, h, 0, 0),
                )
                for part in parts
            ]
            + [IN_HBM] * len(after),
            out_specs=(
                pl.BlockSpec((rows, GROUP, HEADDIM), lambda h, flag_ref: (0, h, 0)),
                IN_HBM,
            ),
        ),
        compiler_params=pltpu.CompilerParams(vmem_limit_bytes=VMEM),
        cost_estimate=COST,
        name="combine_parts",
    )(flag, *parts, *after)


def fresh_kernel(q_ref, kv_ref, *rest):
    out_ref = rest[-1]
    scores = dot_t(q_ref[0], kv_ref[:, :HEADDIM]) * SCALE
    peak = jnp.max(scores, axis=1, keepdims=True)
    weights = jnp.exp(scores - peak)
    total = jnp.sum(weights, axis=1, keepdims=True)
    mixed = dot(weights.astype(jnp.bfloat16), kv_ref[:, HEADDIM:])
    out_ref[...] = (mixed / total).astype(jnp.bfloat16)


def fresh_attention(queries, pairs, after=()):
    length, width = pairs.shape
    return pl.pallas_call(
        fresh_kernel,
        out_shape=jax.ShapeDtypeStruct((GROUP, width // 2), jnp.bfloat16),
        grid=(queries.shape[0],),
        in_specs=[
            pl.BlockSpec((1, GROUP, HEADDIM), lambda h: (h, 0, 0)),
            pl.BlockSpec((length, 2 * HEADDIM), lambda h: (0, h)),
        ]
        + [IN_HBM] * len(after),
        out_specs=pl.BlockSpec((GROUP, HEADDIM), lambda h: (0, h)),
        compiler_params=pltpu.CompilerParams(vmem_limit_bytes=VMEM),
        cost_estimate=COST,
        name="fresh_attention",
    )(queries, pairs, *after)


def relay_handoff(pairs, source, inst_count):
    half = inst_count // 2
    moved = lax.all_to_all(pairs, "tp", split_axis=0, concat_axis=1, tiled=True)
    lanes = 1024 if moved.size % (inst_count * 1024) == 0 else HEADDIM
    pieces = moved.reshape(inst_count, -1, lanes)
    spread = lax.all_to_all(pieces, "inst", split_axis=0, concat_axis=0, tiled=True)
    chosen = jnp.stack(
        [lax.dynamic_index_in_dim(spread, source[d], 0, False) for d in range(half)], axis=0
    )
    outgoing = jnp.concatenate([jnp.zeros_like(chosen), chosen], axis=0)
    delivered = lax.all_to_all(outgoing, "inst", split_axis=0, concat_axis=0, tiled=True)
    return delivered.reshape(moved.shape)


UNIT = 8
PAIRS = 4


def copy_kernel(plan, counts, prefetch_ref, *refs):
    inputs, marks, outputs = counts
    sources, targets, sems = refs[:inputs], refs[inputs + marks : inputs + marks + outputs], refs[-1]
    started = []
    for source, target in plan(prefetch_ref, sources, targets):
        started.append(pltpu.make_async_copy(source, target, sems.at[len(started)]))
    for copy in started:
        copy.start()
    for copy in started:
        copy.wait()


def copies(plan, number, prefetch, operands, shapes, name, after=()):
    return pl.pallas_call(
        functools.partial(copy_kernel, plan, (len(operands), len(after), len(shapes))),
        out_shape=tuple(jax.ShapeDtypeStruct(shape, jnp.bfloat16) for shape in shapes) + (MARK,),
        grid_spec=pltpu.PrefetchScalarGridSpec(
            num_scalar_prefetch=1,
            grid=(1,),
            in_specs=[ANYWHERE] * len(operands) + [IN_HBM] * len(after),
            out_specs=tuple([ANYWHERE] * len(shapes)) + (IN_HBM,),
            scratch_shapes=[pltpu.SemaphoreType.DMA((number,))],
        ),
        compiler_params=pltpu.CompilerParams(vmem_limit_bytes=SMALL),
        cost_estimate=COST,
        name=name,
    )(prefetch, *operands, *after)


def relay_slots_kernel(far, prefetch_ref, keep_ref, recv_ref, fresh_ref, out_ref, mark_ref, sems, fresh_sems):
    half = 2 * PAIRS
    waits = []
    for d in range(half):
        pair = lax.div(prefetch_ref[3 + d], 2)
        same = lax.rem(prefetch_ref[3 + d], 2) == prefetch_ref[1]
        shift = lax.rem(prefetch_ref[0] + PAIRS - pair, PAIRS)
        for tau in range(2):
            slot = tau * half + d
            target = out_ref.at[slot, pl.ds(0, far)]
            mine = pltpu.make_async_copy(keep_ref.at[shift, tau], target, sems.at[slot])
            other = pltpu.make_async_copy(recv_ref.at[shift, tau], target, sems.at[slot])
            pl.when(same)(mine.start)
            pl.when(jnp.logical_not(same))(other.start)
            extra = pltpu.make_async_copy(fresh_ref, out_ref.at[slot, far], fresh_sems.at[slot])
            extra.start()
            waits += [mine, extra]
    for copy in waits:
        copy.wait()


def rows_kernel(near, far, prefetch_ref, slots_ref, *refs):
    *parts, out_ref, zero_ref, sems = refs
    half = 2 * PAIRS
    width = slots_ref.shape[-1]
    near_all = near * half

    @pl.when(prefetch_ref[2] == 0)
    def _():
        waits = []
        for t in range(2):
            columns = pl.ds(t * width, width)
            for s, part in enumerate(parts):
                pair = lax.rem(prefetch_ref[0] + PAIRS - s, PAIRS)
                target = out_ref.at[pl.ds(pair * 2 * near, 2 * near), :, columns]
                waits.append(pltpu.make_async_copy(part.at[t], target, sems.at[len(waits)]))
            for i in range(half):
                source = slots_ref.at[t * half + i, pl.ds(0, far)]
                target = out_ref.at[pl.ds(near_all + i * far, far), :, columns]
                waits.append(pltpu.make_async_copy(source, target, sems.at[len(waits)]))
        for copy in waits:
            copy.start()
        for copy in waits:
            copy.wait()

    @pl.when(prefetch_ref[2] != 0)
    def _():
        zero_ref[...] = jnp.zeros_like(zero_ref)
        size = zero_ref.shape[0]
        waits = []
        for n in range(out_ref.shape[0] // size):
            target = out_ref.at[pl.ds(n * size, size)]
            waits.append(pltpu.make_async_copy(zero_ref, target, sems.at[n]))
        for copy in waits:
            copy.start()
        for copy in waits:
            copy.wait()


def two_way_handoff(pairs, source, flag, always, arrival_query, fresh_of, prompt_part, extra):
    half = 2 * PAIRS
    rows, width = pairs.shape
    units = rows // (2 * UNIT)
    far_all = -(-units * 3 // (5 * half)) * half
    near_all = units - far_all
    near, far = near_all // half, far_all // half
    inst = lax.axis_index("inst")
    pair, side = lax.div(lax.rem(inst, half), 2), lax.rem(inst, 2)
    prefetch = jnp.concatenate([jnp.stack([pair, side, flag[0]]), source])
    block = (UNIT, width)
    by_unit = pairs.reshape((rows // UNIT,) + block)
    groups = [[base + 2 * i + tau for tau in range(2) for i in range(half)] for base in (0, 2 * half)]

    def crossing(array, s):
        hops = [
            (2 * p + k, half + 2 * ((p + s) % PAIRS) + k) for p in range(PAIRS) for k in range(2)
        ]
        return lax.ppermute(array, "inst", hops)

    def beside(array, base):
        return lax.ppermute(array, "inst", [(base + i, base + (i ^ 1)) for i in range(half)])

    def spread_out(array):
        return lax.all_to_all(
            array, ("inst", "tp"), 0, 0, axis_index_groups=groups, tiled=True
        )

    def cut(pre, sources, targets):
        plan = []
        for s in range(PAIRS):
            start = near_all + lax.rem(pre[0] + s, PAIRS) * (2 * far)
            for tau in range(2):
                plan.append((sources[0].at[pl.ds(tau * units + start, 2 * far)], targets[s].at[tau]))
        return plan

    def near_slots(pre, sources, targets):
        plan = []
        for tau in range(2):
            for i in range(half):
                slot = tau * half + i
                rows_here = sources[0].at[pl.ds(tau * units + i * near, near)]
                plan.append((rows_here, targets[0].at[slot, pl.ds(0, near)]))
                plan.append((sources[1], targets[0].at[slot, near]))
        return plan

    def for_neighbour(pre, sources, targets):
        plan = []
        for s in range(PAIRS):
            receiver = lax.rem(pre[0] + s, PAIRS) * 2 + 1 - pre[1]
            for t in range(2):
                origin = t * half + pre[3 + receiver]
                plan.append((sources[0].at[origin, pl.ds(0, near)], targets[0].at[s, t]))
        return plan

    def for_receivers(pre, sources, targets):
        plan = []
        for s in range(PAIRS):
            receiver = lax.rem(pre[0] + s, PAIRS) * 2 + pre[1]
            for t in range(2):
                origin = t * half + pre[3 + receiver]
                mine = targets[s].at[t, pl.ds(pre[1] * near, near)]
                other = targets[s].at[t, pl.ds((1 - pre[1]) * near, near)]
                plan.append((sources[0].at[origin, pl.ds(0, near)], mine))
                plan.append((sources[1].at[s, t], other))
        return plan

    def split(pre, sources, targets):
        plan = []
        for s in range(PAIRS):
            for tau in range(2):
                mine = sources[s].at[tau, pl.ds(pre[1] * far, far)]
                other = sources[s].at[tau, pl.ds((1 - pre[1]) * far, far)]
                plan.append((mine, targets[0].at[s, tau]))
                plan.append((other, targets[1].at[s, tau]))
        return plan

    near_shape = (2, 2 * near) + block

    def first_stage(by_unit, asked):
        spread, mark = copies(
            near_slots,
            8 * PAIRS,
            prefetch,
            [by_unit, asked.reshape(block)],
            [(2 * half, near + 1) + block],
            "near_slots",
        )
        spread = spread_out(spread)
        part, mark = extra[0]([mark])
        prompt, mark = prompt_part(0, None, [mark])
        more, mark = extra[1](part, [mark])
        outgoing, mark = copies(
            for_neighbour,
            2 * PAIRS,
            prefetch,
            [spread],
            [(PAIRS, 2, near) + block],
            "for_neighbour",
            [mark],
        )
        incoming = beside(outgoing, 0)
        *near_parts, mark = copies(
            for_receivers, 4 * PAIRS, prefetch, [spread, incoming], [near_shape] * PAIRS, "for_receivers"
        )
        fresh = fresh_of(spread.reshape((2, half, near + 1) + block)[0, :, near], [mark])
        return *near_parts, prompt, fresh, more

    def second_stage(prompt, fresh, *far_here):
        keep, give, mark = copies(
            split, 4 * PAIRS, prefetch, list(far_here), [(PAIRS, 2, far) + block] * 2, "split_relays"
        )
        taken = beside(give, half)
        slots, mark = pl.pallas_call(
            functools.partial(relay_slots_kernel, far),
            out_shape=(jax.ShapeDtypeStruct((2 * half, far + 1) + block, jnp.bfloat16), MARK),
            grid_spec=pltpu.PrefetchScalarGridSpec(
                num_scalar_prefetch=1,
                grid=(1,),
                in_specs=[ANYWHERE] * 3,
                out_specs=(ANYWHERE, IN_HBM),
                scratch_shapes=[pltpu.SemaphoreType.DMA((2 * half,))] * 2,
            ),
            compiler_params=pltpu.CompilerParams(vmem_limit_bytes=SMALL),
            cost_estimate=COST,
            name="relay_slots",
        )(prefetch, keep, taken, jnp.pad(fresh, ((0, 0), (0, width // 2))))
        slots = spread_out(slots)
        prompt, mark = prompt_part(1, prompt, [mark])
        return prompt, slots

    def staged(stage, *operands):
        def never(*operands):
            outs = [jnp.zeros(out.shape, out.dtype) for out in jax.eval_shape(stage, *operands)]
            return tuple(outs) if stage is first_stage else (operands[0], *outs[1:])

        return lax.cond(always, lambda *operands: tuple(stage(*operands)), never, *operands)

    asked = lax.ppermute(arrival_query, "inst", [(i + half, i) for i in range(half)])
    *far_parts, _ = copies(
        cut, 2 * PAIRS, prefetch, [by_unit], [(2, 2 * far) + block] * PAIRS, "cut_far"
    )
    far_here = [crossing(part, s) for s, part in enumerate(far_parts)]
    *near_parts, prompt, fresh, more = staged(first_stage, by_unit, asked)
    near_here = [crossing(part, s) for s, part in enumerate(near_parts)]
    prompt, slots = staged(second_stage, prompt, fresh, *far_here)
    handed = pl.pallas_call(
        functools.partial(rows_kernel, near, far),
        out_shape=jax.ShapeDtypeStruct((units, UNIT, 2 * width), jnp.bfloat16),
        grid_spec=pltpu.PrefetchScalarGridSpec(
            num_scalar_prefetch=1,
            grid=(1,),
            in_specs=[ANYWHERE] * (PAIRS + 1),
            out_specs=ANYWHERE,
            scratch_shapes=[
                pltpu.VMEM((half, UNIT, 2 * width), jnp.bfloat16),
                pltpu.SemaphoreType.DMA((2 * (half + PAIRS),)),
            ],
        ),
        compiler_params=pltpu.CompilerParams(vmem_limit_bytes=SMALL),
        cost_estimate=COST,
        name="rows",
    )(prefetch, slots, *near_here)
    results = slots.reshape((2, half, far + 1) + block)[:, :, far]
    return handed.reshape(rows // 2, 2 * width), results, prompt, more


def shards(
    prompt_query,
    prompt_pairs,
    decode_query,
    arrival_query,
    cache_pool,
    page_table,
    lengths,
    assignment,
):
    inst_count = lax.axis_size("inst")
    tp_count = lax.axis_size("tp")
    half = inst_count // 2
    inst = lax.axis_index("inst")
    tp_index = lax.axis_index("tp")
    is_prefill = inst < half
    flag = is_prefill.astype(jnp.int32).reshape(1)
    groups = [list(range(half)), list(range(half, inst_count))]
    decode_ids = jnp.arange(half, dtype=jnp.int32)
    matches = assignment[None, :] == decode_ids[:, None]
    source = jnp.sum(jnp.where(matches, decode_ids[None, :], 0), axis=1).astype(jnp.int32)
    rows = decode_query.shape[0]
    pages, page_len = cache_pool.shape[0], cache_pool.shape[1]
    slots = page_table.shape[1]
    places = tp_index * slots * page_len + jnp.arange(slots * page_len, dtype=jnp.int32)
    valid = (places.reshape(1, slots, page_len) < lengths[:, None, None])[:, None]
    same = page_table[:, None, :] == jnp.arange(pages, dtype=jnp.int32)[None, :, None]
    count = jnp.sum(jnp.where(valid & same[..., None], 1.0, 0.0), axis=2)
    by_token = cache_pool.reshape(pages * page_len, -1)
    by_head = decode_query.reshape(rows, QHEADS, HEADDIM)
    count = count.reshape(rows, pages * page_len)

    def cached(after=()):
        part, mark = cache_attention(flag, by_head, by_token, count, after)
        part = part[None]
        if tp_count == 2:
            return (part, lax.ppermute(part, "tp", [(0, 1), (1, 0)])), mark
        return (lax.all_gather(part, "tp", axis=0, tiled=True),), mark

    def combined(parts, after=()):
        if tp_count == 2:
            here, there = parts
            parts = jnp.where(tp_index == 0, here, there), jnp.where(tp_index == 0, there, here)
        out, mark = combine_parts(flag, parts, rows, after)
        return out.reshape(rows, QHEADS * HEADDIM), mark

    heads = GROUP // 2
    steps = prompt_query.shape[1] // (heads * HEADDIM)
    kv_here = prompt_pairs.shape[1] // (2 * HEADDIM)
    width = kv_here * GROUP * HEADDIM
    from_inst = lax.dynamic_index_in_dim(source, lax.rem(inst, half), 0, False)
    target = lax.dynamic_index_in_dim(assignment, lax.rem(inst, half), 0, False)

    def fresh_of(queries, after=()):
        mine = lax.dynamic_index_in_dim(queries.reshape(half, -1), target, 0, True)
        mine = lax.dynamic_slice(mine, (0, tp_index * width), (1, width))
        fresh = fresh_attention(mine.reshape(kv_here, GROUP, HEADDIM), prompt_pairs, after)
        return lax.ppermute(fresh, "inst", [(i, i + half) for i in range(half)])

    def prompt_part(first, last, earlier, after=()):
        return prompt_attention(
            flag, prompt_query, prompt_pairs, first, last - first, heads, earlier, after
        )

    row_units = prompt_pairs.shape[0] // (2 * UNIT)
    if inst_count == 4 * PAIRS and tp_count == 2 and row_units == 5 * half and steps == 8:
        cuts = (0, 5, 8)
        handed, results, prefill_out, decode_out = two_way_handoff(
            prompt_pairs,
            source,
            flag,
            assignment[0] >= 0,
            arrival_query,
            fresh_of,
            lambda n, earlier, after: prompt_part(cuts[n], cuts[n + 1], earlier, after),
            (cached, combined),
        )
        part = lax.dynamic_index_in_dim(results, from_inst, 1, False)
        part = part[:, :, : kv_here * HEADDIM].reshape(tp_count, GROUP, kv_here, HEADDIM)
        arrival_out = part.transpose(0, 2, 1, 3).reshape(1, QHEADS * HEADDIM)
    else:
        handed = relay_handoff(prompt_pairs, source, inst_count)
        sent = lax.ppermute(arrival_query, "inst", [(i + half, i) for i in range(half)])
        every = lax.all_gather(sent, "inst", axis=0, tiled=True, axis_index_groups=groups)
        results = lax.all_gather(fresh_of(every), "inst", axis_index_groups=groups)
        part = lax.dynamic_index_in_dim(results, from_inst, 0, True)
        part = part[:, :, : kv_here * HEADDIM].reshape(1, GROUP, kv_here, HEADDIM)
        part = part.transpose(0, 2, 1, 3).reshape(1, width)
        arrival_out = lax.all_gather(part, "tp", axis=1, tiled=True)
        prefill_out, _ = prompt_part(0, steps, None)
        decode_out, _ = combined(cached()[0])
    arrival_out = jnp.where(is_prefill, jnp.zeros_like(arrival_out), arrival_out)
    return (prefill_out, handed, decode_out, arrival_out)


def solution(mesh):
    return jax.shard_map(
        shards,
        mesh=mesh,
        in_specs=(
            P("inst", "tp"),
            P("inst", "tp"),
            P("inst", None),
            P("inst", None),
            P(("inst", "tp"), None, None),
            P("inst", "tp"),
            P("inst"),
            P(),
        ),
        out_specs=(P("inst", "tp"), P(("inst", "tp"), None), P("inst", None), P("inst", None)),
        check_vma=False,
    )
```

time: 159 us -> 141 us (0.89)
  Pallas kernels: 9.83 us -> 66.9 us
  blocking collectives: 56.8 us -> 0 us
  between operations: 19.5 us -> 3.44 us
  local copies, waits for them, and re-layouts: 20.9 us -> 6.61 us
  waiting for transfers between devices: 14.3 us -> 24.1 us
  loops' own time: 0 us -> 2.18 us
    pallas_call x3 -> x12, Pallas kernels: 9.83 us -> 66.9 us  [the longest x1 25.7 us: two_way_handoff(): pl.pallas_call(functools.partial(rows_kernel, near, far), out_shape=jax.S...]
    all_gather x4 -> x0, blocking collectives: 56.8 us -> none  [the longest x1 31.1 us: shards(): lax.all_gather(fresh, 'inst', axis=0, tiled=True, axis_index_groups=groups)]
    all_to_all x3 -> x2, starting transfers between devices: 30.4 us -> 9.58 us  [spread_out(): lax.all_to_all(array, ('inst', 'tp'), 0, 0, axis_index_groups=groups, til...]
    ppermute x2 -> x13, starting transfers between devices: 3.53 us -> 24.1 us  [the longest x8 10.3 us: crossing(): return lax.ppermute(array, 'inst', hops)]
    unnamed x25 -> x2, local copies, waits for them, and re-layouts: 12.3 us -> 0.01 us
    ppermute x2 -> x13, waiting for transfers between devices: 0.01 us -> 10.2 us  [the longest x1 6.08 us: fresh_of(): return lax.ppermute(fresh, 'inst', [(i, i + half) for i in range(half)])]
    cond x0 -> x14, local copies, waits for them, and re-layouts: none -> 2.88 us
    reshape x5 -> x2, local copies, waits for them, and re-layouts: 2.68 us -> 0.09 us  [the longest x1 0.08 us: shards(): count = count.reshape(rows, pages * page_len)]
  transfers between devices with their start and end apart: 5 -> 15, of which waited for: 1 -> 4; matrix products, arithmetic and copies ran while one was open for 14% -> 5% of each run, Pallas kernels for 6% -> 28%
where the time goes in v1:
time: 141 us; the launch traced here: 140 us
  Pallas kernels  66.9 us (47%)
  starting transfers between devices  33.7 us (24%)
  waiting for transfers between devices  24.1 us (17%)
  local copies, waits for them, and re-layouts  6.61 us (5%)
  between operations  3.44 us (2%)
  other arithmetic  2.52 us (2%)
  loops' own time  2.18 us (2%)
    pallas_call x1, Pallas kernels, two_way_handoff(): pl.pallas_call(functools.partial(rows_kernel, near, far), out_shape=jax.S...  25.7 us
    pallas_call x5, Pallas kernels, copies(): pl.pallas_call(functools.partial(copy_kernel, plan, (len(operands), len(a...  23.9 us
    all_to_all x2, waiting for transfers between devices, spread_out(): lax.all_to_all(array, ('inst', 'tp'), 0, 0, axis_index_groups=groups, til...  13.9 us
    ppermute x8, starting transfers between devices, crossing(): return lax.ppermute(array, 'inst', hops)  10.3 us
    all_to_all x2, starting transfers between devices, spread_out(): lax.all_to_all(array, ('inst', 'tp'), 0, 0, axis_index_groups=groups, til...  9.58 us
    ppermute x1, starting transfers between devices, two_way_handoff(): lax.ppermute(arrival_query, 'inst', [(i + half, i) for i in range(half)])  8.41 us
    pallas_call x2, Pallas kernels, prompt_attention(): pl.pallas_call(functools.partial(prompt_kernel, heads), out_shape=(jax.Sh...  6.7 us
    ppermute x1, waiting for transfers between devices, fresh_of(): return lax.ppermute(fresh, 'inst', [(i, i + half) for i in range(half)])  6.08 us
  transfers between devices with their start and end apart: 15, of which 4 were waited for; matrix products, arithmetic and copies ran while one was open for 5% of the time, Pallas kernels for 28%

profile of v1, /device:TPU:24, one launch (start us, length us, event | category | flops | bytes accessed | tf_op | source)
XLA Modules:
  0.0 139.5 jit_solution(16871531190896608893)
XLA Ops:
  0.6 0.8 select_reduce_fusion.1
  1.4 0.1 pad_add_fusion.prefetch_ref
  1.5 1.8 %cut_far.1 = (bf16[2,6,8,1024]{3,2,1,0:T(8,128)(2,1)S(1)}, bf16[2,6,8,1024]{3,2,1,0:T(8,128)(2,1)S(1)}, bf16[2,6,8,1024]{3,2,1,0:T(8,128)(2,1)S(1)}, bf16[2,6,8,1024]{3,2,1,0:T(8,128)(2,1)S(1)}, f32[8,128]{1,0:T(8,128)}) custom-call(s32[11]{0:T(128)S(1)} %pad_add_fusion.prefetch_ref, bf16[80,8,1024]{2,1,0:T(8,128)(2,1)} %bitcast.45), custom_call_target="tpu_custom_call" | custom-call | flops 1 | bytes 1 | tf_op jit(solution)/shard_map/cut_far/pallas_call | solution.py:266
  3.3 1.3 collective-permute-start.5
  4.6 1.3 collective-permute-start.6
  5.9 1.3 collective-permute-start.7
  7.2 1.3 collective-permute-start.8
  8.5 8.4 %collective-permute-start.4 = (bf16[1,8192]{1,0:T(2,128)(2,1)}, bf16[1,8192]{1,0:T(2,128)(2,1)S(1)}, u32[]{:S(2)}, u32[]{:S(2)}) collective-permute-start(bf16[1,8192]{1,0:T(2,128)(2,1)} %param.15), channel_id=1, source_target_pairs={{16,0},{18,2},{20,4},{22,6},{24,8},{26,10},{28,12},{30,14},{17,1},... | collective-permute-start | bytes 49160 | tf_op jit(solution)/shard_map/ppermute | solution.py:479
  17.0 0.6 dynamic_slice.17
  20.1 0.0 collective-permute-done.4
  20.2 57.4 %conditional.2 = (bf16[2,4,8,1024]{3,2,1,0:T(8,128)(2,1)}, bf16[2,4,8,1024]{3,2,1,0:T(8,128)(2,1)}, bf16[2,4,8,1024]{3,2,1,0:T(8,128)(2,1)}, bf16[2,4,8,1024]{3,...) conditional(s32[]{:T(128)} %bitcast.6, () %tuple.47, ...), branch_computations={%region_1.2_spmd, %region_2.4_spmd} | conditional | flops 164274 | bytes 11711479 | solution.py:477
  20.2 0.0 copy-start.3
  20.2 0.1 reduce
  20.3 17.8 %near_slots.1 = (bf16[16,3,8,1024]{3,2,1,0:T(8,128)(2,1)}, f32[8,128]{1,0:T(8,128)S(1)}) custom-call(s32[11]{0:T(128)S(1)} %get-tuple-element.85.prefetch_ref, bf16[80,8,1024]{2,1,0:T(8,128)(2,1)} %bitcast.47, bf16[8,1024]{1,0:T(8,128)(2,1)S(1)} %reshape.64.refs_1_), custom_call_target="tpu_custom_call" | custom-call | flops 1 | bytes 1 | tf_op jit(solution)/shard_map/cond/branch_1_fun/near_slots/pallas_call | solution.py:266
  38.2 4.9 %all-to-all-start.1 = ((bf16[16,3,8,1024]{3,2,1,0:T(8,128)(2,1)}), bf16[16,3,8,1024]{3,2,1,0:T(8,128)(2,1)S(1)}, u32[]{:S(2)}, u32[]{:S(2)}) async-start(bf16[16,3,8,1024]{3,2,1,0:T(8,128)(2,1)} %get-tuple-element.88), calls=%async_computation.1 | async-start | bytes 1572864 | tf_op jit(solution)/shard_map/cond/branch_1_fun/all_to_all | solution.py:365
  43.1 0.7 compare_bitcast_fusion
  43.8 0.7 broadcast_compare_fusion
  44.5 0.1 select_reduce_fusion
  44.6 0.1 reshape.67.count_ref
  44.7 0.9 copy.25
  45.6 5.6 %cache_attention.1 = (f32[8,32,256]{2,1,0:T(8,128)S(1)}, f32[8,128]{1,0:T(8,128)S(1)}) custom-call(s32[1]{0:T(128)} %get-tuple-element.89.flag_ref, bf16[4,64,128]{2,1,0:T(8,128)(2,1)S(1)} %bitcast.41, bf16[320,2048]{1,0:T(8,128)(2,1)} %bitcast.48, f32[4,320]{1,0:T(4,128)S(1)} %reshape.67.count_ref, f32[8,128]{1,0:T(8,128)S(1)} %get-tuple-element.98.rest_0_), custom_call_target="tpu_custom_call" | custom-call | flops 1 | bytes 1 | tf_op jit(solution)/shard_map/cond/branch_1_fun/cache_attention/pallas_call | solution.py:137
  51.2 0.6 copy-done.2
  51.8 1.5 %collective-permute-start.1 = (f32[1,8,32,256]{3,2,1,0:T(8,128)S(1)}, f32[1,8,32,256]{3,2,1,0:T(8,128)S(1)}, u32[]{:S(2)}, u32[]{:S(2)}) collective-permute-start(f32[1,8,32,256]{3,2,1,0:T(8,128)S(1)} %bitcast.42), channel_id=1, source_target_pairs={{0,1},{1,0},{2,3},{3,2},{4,5},{5,4},{6,7},{7,6},{8,9},{9,8},{10,11... | collective-permute-start | bytes 786440 | tf_op jit(solution)/shard_map/cond/branch_1_fun/ppermute | solution.py:544
  53.2 3.7 %prompt_attention.2 = (bf16[640,4096]{1,0:T(8,128)(2,1)}, f32[8,128]{1,0:T(8,128)}) custom-call(s32[1]{0:T(128)} %get-tuple-element.89.flag_ref, bf16[640,4096]{1,0:T(8,128)(2,1)} %get-tuple-element.100.q_ref, bf16[640,1024]{1,0:T(8,128)(2,1)S(1)} %copy-done.3, f32[8,128]{1,0:T(8,128)} %copy-done.2), custom_call_target="tpu_custom_call" | custom-call | flops 1 | bytes 1 | tf_op jit(solution)/shard_map/cond/branch_1_fun/prompt_attention/pallas_call | solution.py:90
  57.0 3.2 %collective-permute-done.1 = f32[1,8,32,256]{3,2,1,0:T(8,128)S(1)} collective-permute-done((f32[1,8,32,256]{3,2,1,0:T(8,128)S(1)}, f32[1,8,32,256]{3,2,1,0:T(8,128)S(1)}, u32[]{:S(2)}, u32[]{:S(2)}) %collective-permute-start.1) | collective-permute-done | bytes 262176 | tf_op jit(solution)/shard_map/cond/branch_1_fun/ppermute | solution.py:544
  60.2 0.0 copy-start
  60.2 0.7 copy-done
  60.9 1.5 %combine_parts.1 = (bf16[4,64,128]{2,1,0:T(8,128)(2,1)S(1)}, f32[8,128]{1,0:T(8,128)S(1)}) custom-call(s32[1]{0:T(128)} %get-tuple-element.89.flag_ref, f32[1,8,32,256]{3,2,1,0:T(8,128)S(1)} %get-tuple-element.169.refs_0_, f32[1,8,32,256]{3,2,1,0:T(8,128)S(1)} %get-tuple-element.168.refs_1_, f32[8,128]{1,0:T(8,128)S(1)} %copy-done), custom_call_target="tpu_custom_call" | custom-call | flops 1 | bytes 1 | tf_op jit(solution)/shard_map/cond/branch_1_fun/combine_parts/pallas_call | solution.py:182
  62.3 0.0 all-to-all-done.1.refs_0_
  62.3 1.0 for_neighbour.1
  63.3 0.7 collective-permute-start.2
  64.0 0.6 dynamic_slice.13
  66.6 0.1 copy.20
  66.7 0.1 dynamic-slice_reduce_fusion
  66.8 0.0 collective-permute-done.2.refs_1_
  66.8 1.5 %for_receivers.1 = (bf16[2,4,8,1024]{3,2,1,0:T(8,128)(2,1)}, bf16[2,4,8,1024]{3,2,1,0:T(8,128)(2,1)}, bf16[2,4,8,1024]{3,2,1,0:T(8,128)(2,1)}, bf16[2,4,8,1024]{3,2,1,0:T(8,128)(2,1)}, f32[8,128]{1,0:T(8,128)S(1)}) custom-call(s32[11]{0:T(128)S(1)} %get-tuple-element.85.prefetch_ref, bf16[16,3,8,1024]{3,2,1,0:T(8,128)(2,1)S(1)} %all-to-all-done.1.refs_0_, ...), custom_call_target="tpu_custom_call" | custom-call | flops 1 | bytes 1 | tf_op jit(solution)/shard_map/cond/branch_1_fun/for_receivers/pallas_call | solution.py:266
  68.3 1.8 %fresh_attention.1 = bf16[8,512]{1,0:T(8,128)(2,1)S(1)} custom-call(bf16[4,8,128]{2,1,0:T(8,128)(2,1)S(1)} %bitcast.44, bf16[640,1024]{1,0:T(8,128)(2,1)S(1)} %copy-done.3, f32[8,128]{1,0:T(8,128)S(1)} %get-tuple-element.113.rest_0_), custom_call_target="tpu_custom_call" | custom-call | flops 1 | bytes 1 | tf_op jit(solution)/shard_map/cond/branch_1_fun/fresh_attention/pallas_call | solution.py:219
  70.1 1.3 collective-permute-start.3
  71.4 0.1 copy.24
  71.5 6.1 %collective-permute-done.3 = bf16[8,512]{1,0:T(8,128)(2,1)} collective-permute-done((bf16[8,512]{1,0:T(8,128)(2,1)S(1)}, bf16[8,512]{1,0:T(8,128)(2,1)}, u32[]{:S(2)}, u32[]{:S(2)}) %collective-permute-start.3) | collective-permute-done | bytes 8224 | tf_op jit(solution)/shard_map/cond/branch_1_fun/ppermute | solution.py:565
  77.6 1.3 collective-permute-start.9
  78.9 0.0 collective-permute-done.5
  78.9 1.3 collective-permute-start.10
  80.2 0.0 collective-permute-done.6
  80.2 1.3 collective-permute-start.11
  81.5 0.0 collective-permute-done.7
  81.5 1.3 collective-permute-start.12
  82.8 0.0 collective-permute-done.8
  82.8 29.3 %conditional.3 = (bf16[640,4096]{1,0:T(8,128)(2,1)}, bf16[16,4,8,1024]{3,2,1,0:T(8,128)(2,1)}) conditional(s32[]{:T(128)} %bitcast.6, bf16[640,4096]{1,0:T(8,128)(2,1)} %get-tuple-element.147, (s32[11]{0:T(128)S(1)}, bf16[2,6,8,1024]{3,2,1,0:T(8,128)(2,1)}, bf16[2,6,8,1024]{3,2,1,0:T(8,128)(2,1)}, bf16[2,6,8,1024]{3,2,1,0:T(8,128)(2,1)}, ...), branch_computations={%region_4.5_spmd, %region_5.6_spmd} | conditional | flops 3 | bytes 4759673 | solution.py:477
  82.8 1.8 %split_relays.1 = (bf16[4,2,3,8,1024]{4,3,2,1,0:T(8,128)(2,1)S(1)}, bf16[4,2,3,8,1024]{4,3,2,1,0:T(8,128)(2,1)S(1)}, f32[8,128]{1,0:T(8,128)}) custom-call(s32[11]{0:T(128)S(1)} %get-tuple-element.119.prefetch_ref, bf16[2,6,8,1024]{3,2,1,0:T(8,128)(2,1)} %get-tuple-element.120.refs_0_, bf16[2,6,8,1024]{3,2,1,0:T(8,128)(2,1)} %get-tuple-element.121.refs_1_, ...), custom_call_target="tpu_custom_call" | custom-call | flops 1 | bytes 1 | tf_op jit(solution)/shard_map/cond/branch_1_fun/split_relays/pallas_call | solution.py:266
  84.7 1.9 %collective-permute-start = (bf16[4,2,3,8,1024]{4,3,2,1,0:T(8,128)(2,1)S(1)}, bf16[4,2,3,8,1024]{4,3,2,1,0:T(8,128)(2,1)S(1)}, u32[]{:S(2)}, u32[]{:S(2)}) collective-permute-start(bf16[4,2,3,8,1024]{4,3,2,1,0:T(8,128)(2,1)S(1)} %get-tuple-element.125), channel_id=1, source_target_pairs={{16,18},{18,16},{20,22},{22,20},{24,26},{26,24},{28,30},{30,28},{1... | collective-permute-start | bytes 1179656 | tf_op jit(solution)/shard_map/cond/branch_1_fun/ppermute | solution.py:362
  86.6 0.7 pad.3.fresh_ref
  87.3 1.0 collective-permute-done.recv_ref
  88.3 1.8 %relay_slots.1 = (bf16[16,4,8,1024]{3,2,1,0:T(8,128)(2,1)}, f32[8,128]{1,0:T(8,128)S(1)}) custom-call(s32[11]{0:T(128)S(1)} %get-tuple-element.119.prefetch_ref, bf16[4,2,3,8,1024]{4,3,2,1,0:T(8,128)(2,1)S(1)} %get-tuple-element.124.keep_ref, bf16[4,2,3,8,1024]{4,3,2,1,0:T(8,128)(2,1)S(1)} %collective-permute-done.recv_ref, bf16[8,1024]{1,0:T(8,128)(2,1)S(1)} %pad.3.fresh_ref), custom_call_target="tpu_custom_call" | custom-call | flops 1 | bytes 1 | tf_op jit(solution)/shard_map/cond/branch_1_fun/relay_slots/pallas_call | solution.py:454
  90.1 0.0 copy-start.1
  90.1 0.6 copy-done.1
  90.7 4.6 %all-to-all-start = ((bf16[16,4,8,1024]{3,2,1,0:T(8,128)(2,1)}), bf16[16,4,8,1024]{3,2,1,0:T(8,128)(2,1)}, u32[]{:S(2)}, u32[]{:S(2)}) async-start(bf16[16,4,8,1024]{3,2,1,0:T(8,128)(2,1)} %get-tuple-element.129), calls=%async_computation | async-start | bytes 2097152 | tf_op jit(solution)/shard_map/cond/branch_1_fun/all_to_all | solution.py:365
  95.3 3.0 %prompt_attention.3 = (bf16[640,4096]{1,0:T(8,128)(2,1)}, f32[8,128]{1,0:T(8,128)}) custom-call(s32[1]{0:T(128)} %get-tuple-element.115.flag_ref, bf16[640,4096]{1,0:T(8,128)(2,1)} %get-tuple-element.116.q_ref, bf16[640,1024]{1,0:T(8,128)(2,1)} %get-tuple-element.117.kv_ref, ...), custom_call_target="tpu_custom_call", output_to_operand_aliasing={{0}: (3, {})} | custom-call | flops 1 | bytes 1 | tf_op jit(solution)/shard_map/cond/branch_1_fun/prompt_attention/pallas_call | solution.py:90
  98.3 13.9 %all-to-all-done = bf16[16,4,8,1024]{3,2,1,0:T(8,128)(2,1)} async-done(((bf16[16,4,8,1024]{3,2,1,0:T(8,128)(2,1)}), bf16[16,4,8,1024]{3,2,1,0:T(8,128)(2,1)}, u32[]{:S(2)}, u32[]{:S(2)}) %all-to-all-start) | async-done | bytes 1048608 | tf_op jit(solution)/shard_map/cond/branch_1_fun/all_to_all | solution.py:365
  112.2 1.0 slice.16
  113.2 0.6 select_n.73
  113.8 0.0 collective-permute-done.9.refs_0_
  113.8 0.0 collective-permute-done.12.refs_3_
  113.8 25.7 %rows.1 = bf16[40,8,2048]{2,1,0:T(8,128)(2,1)} custom-call(s32[11]{0:T(128)S(1)} %pad_add_fusion.prefetch_ref, bf16[16,4,8,1024]{3,2,1,0:T(8,128)(2,1)} %get-tuple-element.154.slots_ref, bf16[2,4,8,1024]{3,2,1,0:T(8,128)(2,1)S(1)} %collective-permute-done.9.refs_0_, bf16[2,4,8,1024]{3,2,1,0:T(8,128)(2,1)S(1)} %collective-permute-done.10.refs_1_, ...), custom_call_target="tpu_custom_call" | custom-call | flops 1 | bytes 1 | tf_op jit(solution)/shard_map/rows/pallas_call | solution.py:487
  (18 shorter events, 0.1 us)
Async XLA Ops:
  3.3 75.5 %collective-permute-start.5 = (bf16[2,6,8,1024]{3,2,1,0:T(8,128)(2,1)S(1)}, bf16[2,6,8,1024]{3,2,1,0:T(8,128)(2,1)}, u32[]{:S(2)}, u32[]{:S(2)}) collective-permute-start(bf16[2,6,8,1024]{3,2,1,0:T(8,128)(2,1)S(1)} %get-tuple-element.148), channel_id=1, source_target_pairs={{0,16},{2,18},{4,20},{6,22},{8,24},{10,26},{12,28},{14,30},{1,17},... | collective-permute-start | bytes 589832 | tf_op jit(solution)/shard_map/ppermute | solution.py:359
  4.6 75.5 %collective-permute-start.6 = (bf16[2,6,8,1024]{3,2,1,0:T(8,128)(2,1)S(1)}, bf16[2,6,8,1024]{3,2,1,0:T(8,128)(2,1)}, u32[]{:S(2)}, u32[]{:S(2)}) collective-permute-start(bf16[2,6,8,1024]{3,2,1,0:T(8,128)(2,1)S(1)} %get-tuple-element.149), channel_id=1, source_target_pairs={{0,20},{2,22},{4,24},{6,26},{8,28},{10,30},{12,16},{14,18},{1,21},... | collective-permute-start | bytes 589832 | tf_op jit(solution)/shard_map/ppermute | solution.py:359
  5.9 75.6 %collective-permute-start.7 = (bf16[2,6,8,1024]{3,2,1,0:T(8,128)(2,1)S(1)}, bf16[2,6,8,1024]{3,2,1,0:T(8,128)(2,1)}, u32[]{:S(2)}, u32[]{:S(2)}) collective-permute-start(bf16[2,6,8,1024]{3,2,1,0:T(8,128)(2,1)S(1)} %get-tuple-element.150), channel_id=1, source_target_pairs={{0,24},{2,26},{4,28},{6,30},{8,16},{10,18},{12,20},{14,22},{1,25},... | collective-permute-start | bytes 589832 | tf_op jit(solution)/shard_map/ppermute | solution.py:359
  7.2 75.6 %collective-permute-start.8 = (bf16[2,6,8,1024]{3,2,1,0:T(8,128)(2,1)S(1)}, bf16[2,6,8,1024]{3,2,1,0:T(8,128)(2,1)}, u32[]{:S(2)}, u32[]{:S(2)}) collective-permute-start(bf16[2,6,8,1024]{3,2,1,0:T(8,128)(2,1)S(1)} %get-tuple-element.151), channel_id=1, source_target_pairs={{0,28},{2,30},{4,16},{6,18},{8,20},{10,22},{12,24},{14,26},{1,29},... | collective-permute-start | bytes 589832 | tf_op jit(solution)/shard_map/ppermute | solution.py:359
  8.5 11.6 %collective-permute-start.4 = (bf16[1,8192]{1,0:T(2,128)(2,1)}, bf16[1,8192]{1,0:T(2,128)(2,1)S(1)}, u32[]{:S(2)}, u32[]{:S(2)}) collective-permute-start(bf16[1,8192]{1,0:T(2,128)(2,1)} %param.15), channel_id=1, source_target_pairs={{16,0},{18,2},{20,4},{22,6},{24,8},{26,10},{28,12},{30,14},{17,1},... | collective-permute-start | bytes 49160 | tf_op jit(solution)/shard_map/ppermute | solution.py:479
  20.2 33.0 %copy-start.3 = (bf16[640,1024]{1,0:T(8,128)(2,1)S(1)}, bf16[640,1024]{1,0:T(8,128)(2,1)}, u32[]{:S(2)}) copy-start(bf16[640,1024]{1,0:T(8,128)(2,1)} %get-tuple-element.101.kv_ref) | copy-start | bytes 3932164 | tf_op jit(solution)/shard_map/cond
  38.2 24.2 %all-to-all-start.1 = ((bf16[16,3,8,1024]{3,2,1,0:T(8,128)(2,1)}), bf16[16,3,8,1024]{3,2,1,0:T(8,128)(2,1)S(1)}, u32[]{:S(2)}, u32[]{:S(2)}) async-start(bf16[16,3,8,1024]{3,2,1,0:T(8,128)(2,1)} %get-tuple-element.88), calls=%async_computation.1 | async-start | bytes 1572864 | tf_op jit(solution)/shard_map/cond/branch_1_fun/all_to_all | solution.py:365
  44.7 19.3 %copy-start.5 = (s32[8]{0:T(128)S(1)}, s32[8]{0:T(128)}, u32[]{:S(2)}) copy-start(s32[8]{0:T(128)} %get-tuple-element.111) | copy-start | bytes 100 | tf_op jit(solution)/shard_map/cond
  51.2 0.6 copy-start.2
  51.8 8.4 %collective-permute-start.1 = (f32[1,8,32,256]{3,2,1,0:T(8,128)S(1)}, f32[1,8,32,256]{3,2,1,0:T(8,128)S(1)}, u32[]{:S(2)}, u32[]{:S(2)}) collective-permute-start(f32[1,8,32,256]{3,2,1,0:T(8,128)S(1)} %bitcast.42), channel_id=1, source_target_pairs={{0,1},{1,0},{2,3},{3,2},{4,5},{5,4},{6,7},{7,6},{8,9},{9,8},{10,11... | collective-permute-start | bytes 786440 | tf_op jit(solution)/shard_map/cond/branch_1_fun/ppermute | solution.py:544
  60.2 0.7 copy-start
  63.3 3.5 %collective-permute-start.2 = (bf16[4,2,2,8,1024]{4,3,2,1,0:T(8,128)(2,1)S(1)}, bf16[4,2,2,8,1024]{4,3,2,1,0:T(8,128)(2,1)S(1)}, u32[]{:S(2)}, u32[]{:S(2)}) collective-permute-start(bf16[4,2,2,8,1024]{4,3,2,1,0:T(8,128)(2,1)S(1)} %get-tuple-element.105), channel_id=1, source_target_pairs={{0,2},{2,0},{4,6},{6,4},{8,10},{10,8},{12,14},{14,12},{1,3},{3,1},... | collective-permute-start | bytes 786440 | tf_op jit(solution)/shard_map/cond/branch_1_fun/ppermute | solution.py:362
  70.1 7.4 %collective-permute-start.3 = (bf16[8,512]{1,0:T(8,128)(2,1)S(1)}, bf16[8,512]{1,0:T(8,128)(2,1)}, u32[]{:S(2)}, u32[]{:S(2)}) collective-permute-start(bf16[8,512]{1,0:T(8,128)(2,1)S(1)} %fresh_attention.1), channel_id=1, source_target_pairs={{0,16},{2,18},{4,20},{6,22},{8,24},{10,26},{12,28},{14,30},{1,17},... | collective-permute-start | bytes 24584 | tf_op jit(solution)/shard_map/cond/branch_1_fun/ppermute | solution.py:565
  77.6 5.2 %copy-start.4 = (bf16[4,8192]{1,0:T(4,128)(2,1)}, bf16[4,8192]{1,0:T(4,128)(2,1)S(1)}, u32[]{:S(2)}) copy-start(bf16[4,8192]{1,0:T(4,128)(2,1)S(1)} %get-tuple-element.145) | copy-start | bytes 196612
  77.6 36.2 %collective-permute-start.9 = (bf16[2,4,8,1024]{3,2,1,0:T(8,128)(2,1)}, bf16[2,4,8,1024]{3,2,1,0:T(8,128)(2,1)S(1)}, u32[]{:S(2)}, u32[]{:S(2)}) collective-permute-start(bf16[2,4,8,1024]{3,2,1,0:T(8,128)(2,1)} %get-tuple-element.155), channel_id=1, source_target_pairs={{0,16},{2,18},{4,20},{6,22},{8,24},{10,26},{12,28},{14,30},{1,17},... | collective-permute-start | bytes 393224 | tf_op jit(solution)/shard_map/ppermute | solution.py:359
  78.9 34.9 %collective-permute-start.10 = (bf16[2,4,8,1024]{3,2,1,0:T(8,128)(2,1)}, bf16[2,4,8,1024]{3,2,1,0:T(8,128)(2,1)S(1)}, u32[]{:S(2)}, u32[]{:S(2)}) collective-permute-start(bf16[2,4,8,1024]{3,2,1,0:T(8,128)(2,1)} %get-tuple-element.156), channel_id=1, source_target_pairs={{0,20},{2,22},{4,24},{6,26},{8,28},{10,30},{12,16},{14,18},{1,21},... | collective-permute-start | bytes 393224 | tf_op jit(solution)/shard_map/ppermute | solution.py:359
  80.2 33.6 %collective-permute-start.11 = (bf16[2,4,8,1024]{3,2,1,0:T(8,128)(2,1)}, bf16[2,4,8,1024]{3,2,1,0:T(8,128)(2,1)S(1)}, u32[]{:S(2)}, u32[]{:S(2)}) collective-permute-start(bf16[2,4,8,1024]{3,2,1,0:T(8,128)(2,1)} %get-tuple-element.157), channel_id=1, source_target_pairs={{0,24},{2,26},{4,28},{6,30},{8,16},{10,18},{12,20},{14,22},{1,25},... | collective-permute-start | bytes 393224 | tf_op jit(solution)/shard_map/ppermute | solution.py:359
  81.5 32.3 %collective-permute-start.12 = (bf16[2,4,8,1024]{3,2,1,0:T(8,128)(2,1)}, bf16[2,4,8,1024]{3,2,1,0:T(8,128)(2,1)S(1)}, u32[]{:S(2)}, u32[]{:S(2)}) collective-permute-start(bf16[2,4,8,1024]{3,2,1,0:T(8,128)(2,1)} %get-tuple-element.158), channel_id=1, source_target_pairs={{0,28},{2,30},{4,16},{6,18},{8,20},{10,22},{12,24},{14,26},{1,29},... | collective-permute-start | bytes 393224 | tf_op jit(solution)/shard_map/ppermute | solution.py:359
  84.7 3.6 %collective-permute-start = (bf16[4,2,3,8,1024]{4,3,2,1,0:T(8,128)(2,1)S(1)}, bf16[4,2,3,8,1024]{4,3,2,1,0:T(8,128)(2,1)S(1)}, u32[]{:S(2)}, u32[]{:S(2)}) collective-permute-start(bf16[4,2,3,8,1024]{4,3,2,1,0:T(8,128)(2,1)S(1)} %get-tuple-element.125), channel_id=1, source_target_pairs={{16,18},{18,16},{20,22},{22,20},{24,26},{26,24},{28,30},{30,28},{1... | collective-permute-start | bytes 1179656 | tf_op jit(solution)/shard_map/cond/branch_1_fun/ppermute | solution.py:362
  90.1 0.6 copy-start.1
  90.7 21.5 %all-to-all-start = ((bf16[16,4,8,1024]{3,2,1,0:T(8,128)(2,1)}), bf16[16,4,8,1024]{3,2,1,0:T(8,128)(2,1)}, u32[]{:S(2)}, u32[]{:S(2)}) async-start(bf16[16,4,8,1024]{3,2,1,0:T(8,128)(2,1)} %get-tuple-element.129), calls=%async_computation | async-start | bytes 2097152 | tf_op jit(solution)/shard_map/cond/branch_1_fun/all_to_all | solution.py:365

commit v2 on v1

--- a/solution.py
+++ b/solution.py
@@ -17,6 +17,7 @@
 TILE = 128
 VMEM = 24 * 1024 * 1024
 SMALL = 1024 * 1024
+MEDIUM = 8 * 1024 * 1024
 LARGE = 57 * 1024 * 1024
 COST = pl.CostEstimate(flops=1, bytes_accessed=1, transcendentals=0)
 
@@ -65,6 +66,7 @@
 MARK = jax.ShapeDtypeStruct((8, 128), jnp.float32)
 IN_HBM = pl.BlockSpec(memory_space=pltpu.HBM)
 ANYWHERE = pl.BlockSpec(memory_space=pl.ANY)
+IN_VMEM = pl.BlockSpec(memory_space=pltpu.VMEM)
 
 
 def prompt_attention(flag, queries, pairs, first, steps, heads, earlier, after):
@@ -106,18 +108,29 @@
     )(*operands, *after)
 
 
-def cache_kernel(flag_ref, q_ref, kv_ref, count_ref, *rest):
-    out_ref = rest[-2]
-
-    @pl.when(flag_ref[0] != 0)
+def cache_kernel(page_len, info_ref, table_ref, lengths_ref, q_ref, kv_ref, *rest):
+    out_ref, _, count_ref = rest[-3:]
+    rows, slots = table_ref.shape
+
+    @pl.when(info_ref[0] != 0)
     def _():
         out_ref[...] = jnp.zeros_like(out_ref)
 
-    @pl.when(flag_ref[0] == 0)
-    def _():
-        rows, tokens = count_ref.shape
-        count = jnp.broadcast_to(count_ref[...][:, None, :], (rows, GROUP, tokens))
-        count = count.reshape(rows * GROUP, tokens)
+    @pl.when(jnp.logical_and(info_ref[0] == 0, pl.program_id(0) == 0))
+    def _():
+        token = lax.broadcasted_iota(jnp.int32, (GROUP, count_ref.shape[1]), 1)
+        page, offset = token // page_len, token % page_len
+        for r in range(rows):
+            count = jnp.zeros(token.shape, jnp.float32)
+            for slot in range(slots):
+                left = lengths_ref[r] - (info_ref[1] * slots + slot) * page_len
+                valid = jnp.logical_and(page == table_ref[r, slot], offset < left)
+                count = count + jnp.where(valid, 1.0, 0.0)
+            count_ref[r * GROUP : (r + 1) * GROUP] = count
+
+    @pl.when(info_ref[0] == 0)
+    def _():
+        count = count_ref[...]
         here = count > 0.0
         queries = q_ref[...].astype(jnp.float32).reshape(rows * GROUP, HEADDIM)
         scores = dot_t(queries.astype(jnp.bfloat16), kv_ref[:, :HEADDIM]) * SCALE
@@ -131,33 +144,33 @@
         out_ref[0, :, HEADDIM:] = jnp.where(lane < HEADDIM // 2, peak, total)
 
 
-def cache_attention(flag, queries, pool, count, after):
+def cache_attention(info, table, lengths, queries, pool, page_len, after):
     rows = queries.shape[0]
     tokens = pool.shape[0]
     return pl.pallas_call(
-        cache_kernel,
+        functools.partial(cache_kernel, page_len),
         out_shape=(
             jax.ShapeDtypeStruct((KVHEADS, rows * GROUP, 2 * HEADDIM), jnp.float32),
             MARK,
         ),
         grid_spec=pltpu.PrefetchScalarGridSpec(
-            num_scalar_prefetch=1,
+            num_scalar_prefetch=3,
             grid=(KVHEADS,),
             in_specs=[
-                pl.BlockSpec((rows, GROUP, HEADDIM), lambda h, flag_ref: (0, h, 0)),
-                pl.BlockSpec((tokens, 2 * HEADDIM), lambda h, flag_ref: (0, h * (1 - flag_ref[0]))),
-                pl.BlockSpec((rows, tokens), lambda h, flag_ref: (0, 0)),
+                pl.BlockSpec((rows, GROUP, HEADDIM), lambda h, *_: (0, h, 0)),
+                pl.BlockSpec((tokens, 2 * HEADDIM), lambda h, info, *_: (0, h * (1 - info[0]))),
             ]
             + [IN_HBM] * len(after),
             out_specs=(
-                pl.BlockSpec((1, rows * GROUP, 2 * HEADDIM), lambda h, flag_ref: (h, 0, 0)),
+                pl.BlockSpec((1, rows * GROUP, 2 * HEADDIM), lambda h, *_: (h, 0, 0)),
                 IN_HBM,
             ),
+            scratch_shapes=[pltpu.VMEM((rows * GROUP, tokens), jnp.float32)],
         ),
         compiler_params=pltpu.CompilerParams(vmem_limit_bytes=VMEM),
         cost_estimate=COST,
         name="cache_attention",
-    )(flag, queries, pool, count, *after)
+    )(info, table, lengths, queries, pool, *after)
 
 
 def combine_kernel(count, flag_ref, *refs):
@@ -204,32 +217,75 @@
     )(flag, *parts, *after)
 
 
-def fresh_kernel(q_ref, kv_ref, *rest):
+def fresh_kernel(info_ref, q_ref, kv_ref, *rest):
     out_ref = rest[-1]
-    scores = dot_t(q_ref[0], kv_ref[:, :HEADDIM]) * SCALE
+    units = q_ref[...].astype(jnp.float32)
+    row = lax.broadcasted_iota(jnp.int32, units.shape, 0)
+    mine = jnp.where(row == info_ref[1] + pl.program_id(0), units, 0.0)
+    mine = jnp.sum(mine, axis=0, keepdims=True)
+    queries = jnp.concatenate(
+        [mine[:, g * HEADDIM : (g + 1) * HEADDIM] for g in range(GROUP)], axis=0
+    )
+    scores = dot_t(queries.astype(jnp.bfloat16), kv_ref[:, :HEADDIM]) * SCALE
     peak = jnp.max(scores, axis=1, keepdims=True)
     weights = jnp.exp(scores - peak)
     total = jnp.sum(weights, axis=1, keepdims=True)
     mixed = dot(weights.astype(jnp.bfloat16), kv_ref[:, HEADDIM:])
-    out_ref[...] = (mixed / total).astype(jnp.bfloat16)
-
-
-def fresh_attention(queries, pairs, after=()):
+    out_ref[:, :HEADDIM] = (mixed / total).astype(jnp.bfloat16)
+    out_ref[:, HEADDIM:] = jnp.zeros_like(mixed).astype(jnp.bfloat16)
+
+
+def fresh_attention(info, queries, pairs, after=()):
     length, width = pairs.shape
+    unit = (None, None) + queries.shape[2:]
     return pl.pallas_call(
         fresh_kernel,
-        out_shape=jax.ShapeDtypeStruct((GROUP, width // 2), jnp.bfloat16),
-        grid=(queries.shape[0],),
-        in_specs=[
-            pl.BlockSpec((1, GROUP, HEADDIM), lambda h: (h, 0, 0)),
-            pl.BlockSpec((length, 2 * HEADDIM), lambda h: (0, h)),
-        ]
-        + [IN_HBM] * len(after),
-        out_specs=pl.BlockSpec((GROUP, HEADDIM), lambda h: (0, h)),
+        out_shape=jax.ShapeDtypeStruct((GROUP, width), jnp.bfloat16),
+        grid_spec=pltpu.PrefetchScalarGridSpec(
+            num_scalar_prefetch=1,
+            grid=(width // (2 * HEADDIM),),
+            in_specs=[
+                pl.BlockSpec(unit, lambda h, info_ref: (info_ref[0], info_ref[2], 0, 0)),
+                pl.BlockSpec((length, 2 * HEADDIM), lambda h, info_ref: (0, h)),
+            ]
+            + [IN_HBM] * len(after),
+            out_specs=pl.BlockSpec((GROUP, 2 * HEADDIM), lambda h, info_ref: (0, h)),
+        ),
         compiler_params=pltpu.CompilerParams(vmem_limit_bytes=VMEM),
         cost_estimate=COST,
         name="fresh_attention",
-    )(queries, pairs, *after)
+    )(info, queries, pairs, *after)
+
+
+def results_kernel(info_ref, unit_ref, out_ref):
+    heads = out_ref.shape[0] // GROUP
+    for h in range(heads):
+        result = unit_ref[:, 2 * h * HEADDIM : (2 * h + 1) * HEADDIM].astype(jnp.float32)
+        result = jnp.where(info_ref[1] != 0, 0.0, result)
+        out_ref[h * GROUP : (h + 1) * GROUP] = result
+
+
+def arrival_results(info, slots):
+    devices, _, units, _, width = slots.shape
+    heads = width // (2 * HEADDIM)
+    return pl.pallas_call(
+        results_kernel,
+        out_shape=jax.ShapeDtypeStruct((QHEADS, HEADDIM), jnp.float32),
+        grid_spec=pltpu.PrefetchScalarGridSpec(
+            num_scalar_prefetch=1,
+            grid=(devices,),
+            in_specs=[
+                pl.BlockSpec(
+                    (None, None, None, GROUP, width),
+                    lambda t, info_ref: (t, info_ref[0], units - 1, 0, 0),
+                )
+            ],
+            out_specs=pl.BlockSpec((heads * GROUP, HEADDIM), lambda t, info_ref: (t, 0)),
+        ),
+        compiler_params=pltpu.CompilerParams(vmem_limit_bytes=SMALL),
+        cost_estimate=COST,
+        name="arrival_results",
+    )(info, slots)
 
 
 def relay_handoff(pairs, source, inst_count):
@@ -248,32 +304,37 @@
 
 UNIT = 8
 PAIRS = 4
-
-
-def copy_kernel(plan, counts, prefetch_ref, *refs):
+PREFILL, DECODE = 1, 0
+
+
+def copy_kernel(plan, side, counts, prefetch_ref, *refs):
     inputs, marks, outputs = counts
     sources, targets, sems = refs[:inputs], refs[inputs + marks : inputs + marks + outputs], refs[-1]
-    started = []
-    for source, target in plan(prefetch_ref, sources, targets):
-        started.append(pltpu.make_async_copy(source, target, sems.at[len(started)]))
-    for copy in started:
-        copy.start()
-    for copy in started:
-        copy.wait()
-
-
-def copies(plan, number, prefetch, operands, shapes, name, after=()):
+
+    @pl.when(prefetch_ref[2] == side)
+    def _():
+        started = []
+        for source, target in plan(prefetch_ref, sources, targets):
+            started.append(pltpu.make_async_copy(source, target, sems.at[len(started)]))
+        for copy in started:
+            copy.start()
+        for copy in started:
+            copy.wait()
+
+
+def copies(plan, number, prefetch, operands, shapes, name, after=(), inside=True, side=PREFILL):
+    place = IN_VMEM if inside else ANYWHERE
     return pl.pallas_call(
-        functools.partial(copy_kernel, plan, (len(operands), len(after), len(shapes))),
+        functools.partial(copy_kernel, plan, side, (len(operands), len(after), len(shapes))),
         out_shape=tuple(jax.ShapeDtypeStruct(shape, jnp.bfloat16) for shape in shapes) + (MARK,),
         grid_spec=pltpu.PrefetchScalarGridSpec(
             num_scalar_prefetch=1,
             grid=(1,),
-            in_specs=[ANYWHERE] * len(operands) + [IN_HBM] * len(after),
+            in_specs=[place] * len(operands) + [IN_HBM] * len(after),
             out_specs=tuple([ANYWHERE] * len(shapes)) + (IN_HBM,),
             scratch_shapes=[pltpu.SemaphoreType.DMA((number,))],
         ),
-        compiler_params=pltpu.CompilerParams(vmem_limit_bytes=SMALL),
+        compiler_params=pltpu.CompilerParams(vmem_limit_bytes=MEDIUM if inside else SMALL),
         cost_estimate=COST,
         name=name,
     )(prefetch, *operands, *after)
@@ -281,23 +342,26 @@
 
 def relay_slots_kernel(far, prefetch_ref, keep_ref, recv_ref, fresh_ref, out_ref, mark_ref, sems, fresh_sems):
     half = 2 * PAIRS
-    waits = []
-    for d in range(half):
-        pair = lax.div(prefetch_ref[3 + d], 2)
-        same = lax.rem(prefetch_ref[3 + d], 2) == prefetch_ref[1]
-        shift = lax.rem(prefetch_ref[0] + PAIRS - pair, PAIRS)
-        for tau in range(2):
-            slot = tau * half + d
-            target = out_ref.at[slot, pl.ds(0, far)]
-            mine = pltpu.make_async_copy(keep_ref.at[shift, tau], target, sems.at[slot])
-            other = pltpu.make_async_copy(recv_ref.at[shift, tau], target, sems.at[slot])
-            pl.when(same)(mine.start)
-            pl.when(jnp.logical_not(same))(other.start)
-            extra = pltpu.make_async_copy(fresh_ref, out_ref.at[slot, far], fresh_sems.at[slot])
-            extra.start()
-            waits += [mine, extra]
-    for copy in waits:
-        copy.wait()
+
+    @pl.when(prefetch_ref[2] == DECODE)
+    def _():
+        waits = []
+        for d in range(half):
+            pair = lax.div(prefetch_ref[3 + d], 2)
+            same = lax.rem(prefetch_ref[3 + d], 2) == prefetch_ref[1]
+            shift = lax.rem(prefetch_ref[0] + PAIRS - pair, PAIRS)
+            for tau in range(2):
+                slot = tau * half + d
+                target = out_ref.at[slot, pl.ds(0, far)]
+                mine = pltpu.make_async_copy(keep_ref.at[shift, tau], target, sems.at[slot])
+                other = pltpu.make_async_copy(recv_ref.at[shift, tau], target, sems.at[slot])
+                pl.when(same)(mine.start)
+                pl.when(jnp.logical_not(same))(other.start)
+                extra = pltpu.make_async_copy(fresh_ref, out_ref.at[slot, far], fresh_sems.at[slot])
+                extra.start()
+                waits += [mine, extra]
+        for copy in waits:
+            copy.wait()
 
 
 def rows_kernel(near, far, prefetch_ref, slots_ref, *refs):
@@ -338,7 +402,7 @@
             copy.wait()
 
 
-def two_way_handoff(pairs, source, flag, always, arrival_query, fresh_of, prompt_part, extra):
+def two_way_handoff(pairs, source, flag, always, arrival_query, fresh_of, results_of, prompt_part, extra):
     half = 2 * PAIRS
     rows, width = pairs.shape
     units = rows // (2 * UNIT)
@@ -356,7 +420,7 @@
         hops = [
             (2 * p + k, half + 2 * ((p + s) % PAIRS) + k) for p in range(PAIRS) for k in range(2)
         ]
-        return lax.ppermute(array, "inst", hops)
+        return lax.ppermute(array, "inst", hops + [(there, here) for here, there in hops])
 
     def beside(array, base):
         return lax.ppermute(array, "inst", [(base + i, base + (i ^ 1)) for i in range(half)])
@@ -443,12 +507,12 @@
         *near_parts, mark = copies(
             for_receivers, 4 * PAIRS, prefetch, [spread, incoming], [near_shape] * PAIRS, "for_receivers"
         )
-        fresh = fresh_of(spread.reshape((2, half, near + 1) + block)[0, :, near], [mark])
-        return *near_parts, prompt, fresh, more
-
-    def second_stage(prompt, fresh, *far_here):
+        return *near_parts, prompt, spread, more
+
+    def second_stage(prompt, spread, *far_here):
+        fresh = fresh_of(spread, near)
         keep, give, mark = copies(
-            split, 4 * PAIRS, prefetch, list(far_here), [(PAIRS, 2, far) + block] * 2, "split_relays"
+            split, 4 * PAIRS, prefetch, list(far_here), [(PAIRS, 2, far) + block] * 2, "split_relays", [fresh], side=DECODE
         )
         taken = beside(give, half)
         slots, mark = pl.pallas_call(
@@ -457,17 +521,17 @@
             grid_spec=pltpu.PrefetchScalarGridSpec(
                 num_scalar_prefetch=1,
                 grid=(1,),
-                in_specs=[ANYWHERE] * 3,
+                in_specs=[IN_VMEM] * 3,
                 out_specs=(ANYWHERE, IN_HBM),
                 scratch_shapes=[pltpu.SemaphoreType.DMA((2 * half,))] * 2,
             ),
-            compiler_params=pltpu.CompilerParams(vmem_limit_bytes=SMALL),
+            compiler_params=pltpu.CompilerParams(vmem_limit_bytes=MEDIUM),
             cost_estimate=COST,
             name="relay_slots",
-        )(prefetch, keep, taken, jnp.pad(fresh, ((0, 0), (0, width // 2))))
+        )(prefetch, keep, taken, fresh)
         slots = spread_out(slots)
         prompt, mark = prompt_part(1, prompt, [mark])
-        return prompt, slots
+        return prompt, slots, results_of(slots.reshape((2, half, far + 1) + block))
 
     def staged(stage, *operands):
         def never(*operands):
@@ -478,30 +542,29 @@
 
     asked = lax.ppermute(arrival_query, "inst", [(i + half, i) for i in range(half)])
     *far_parts, _ = copies(
-        cut, 2 * PAIRS, prefetch, [by_unit], [(2, 2 * far) + block] * PAIRS, "cut_far"
+        cut, 2 * PAIRS, prefetch, [by_unit], [(2, 2 * far) + block] * PAIRS, "cut_far", inside=False
     )
     far_here = [crossing(part, s) for s, part in enumerate(far_parts)]
-    *near_parts, prompt, fresh, more = staged(first_stage, by_unit, asked)
+    *near_parts, prompt, spread, more = staged(first_stage, by_unit, asked)
     near_here = [crossing(part, s) for s, part in enumerate(near_parts)]
-    prompt, slots = staged(second_stage, prompt, fresh, *far_here)
+    prompt, slots, results = staged(second_stage, prompt, spread, *far_here)
     handed = pl.pallas_call(
         functools.partial(rows_kernel, near, far),
         out_shape=jax.ShapeDtypeStruct((units, UNIT, 2 * width), jnp.bfloat16),
         grid_spec=pltpu.PrefetchScalarGridSpec(
             num_scalar_prefetch=1,
             grid=(1,),
-            in_specs=[ANYWHERE] * (PAIRS + 1),
+            in_specs=[IN_VMEM] * (PAIRS + 1),
             out_specs=ANYWHERE,
             scratch_shapes=[
                 pltpu.VMEM((half, UNIT, 2 * width), jnp.bfloat16),
                 pltpu.SemaphoreType.DMA((2 * (half + PAIRS),)),
             ],
         ),
-        compiler_params=pltpu.CompilerParams(vmem_limit_bytes=SMALL),
+        compiler_params=pltpu.CompilerParams(vmem_limit_bytes=MEDIUM),
         cost_estimate=COST,
         name="rows",
     )(prefetch, slots, *near_here)
-    results = slots.reshape((2, half, far + 1) + block)[:, :, far]
     return handed.reshape(rows // 2, 2 * width), results, prompt, more
 
 
@@ -528,17 +591,12 @@
     source = jnp.sum(jnp.where(matches, decode_ids[None, :], 0), axis=1).astype(jnp.int32)
     rows = decode_query.shape[0]
     pages, page_len = cache_pool.shape[0], cache_pool.shape[1]
-    slots = page_table.shape[1]
-    places = tp_index * slots * page_len + jnp.arange(slots * page_len, dtype=jnp.int32)
-    valid = (places.reshape(1, slots, page_len) < lengths[:, None, None])[:, None]
-    same = page_table[:, None, :] == jnp.arange(pages, dtype=jnp.int32)[None, :, None]
-    count = jnp.sum(jnp.where(valid & same[..., None], 1.0, 0.0), axis=2)
     by_token = cache_pool.reshape(pages * page_len, -1)
     by_head = decode_query.reshape(rows, QHEADS, HEADDIM)
-    count = count.reshape(rows, pages * page_len)
+    info = jnp.stack([flag[0], tp_index])
 
     def cached(after=()):
-        part, mark = cache_attention(flag, by_head, by_token, count, after)
+        part, mark = cache_attention(info, page_table, lengths, by_head, by_token, page_len, after)
         part = part[None]
         if tp_count == 2:
             return (part, lax.ppermute(part, "tp", [(0, 1), (1, 0)])), mark
@@ -558,11 +616,14 @@
     from_inst = lax.dynamic_index_in_dim(source, lax.rem(inst, half), 0, False)
     target = lax.dynamic_index_in_dim(assignment, lax.rem(inst, half), 0, False)
 
-    def fresh_of(queries, after=()):
-        mine = lax.dynamic_index_in_dim(queries.reshape(half, -1), target, 0, True)
-        mine = lax.dynamic_slice(mine, (0, tp_index * width), (1, width))
-        fresh = fresh_attention(mine.reshape(kv_here, GROUP, HEADDIM), prompt_pairs, after)
+    def fresh_of(queries, unit):
+        info = jnp.stack([target, tp_index * kv_here, jnp.int32(unit)])
+        fresh = fresh_attention(info, queries, prompt_pairs)
         return lax.ppermute(fresh, "inst", [(i, i + half) for i in range(half)])
+
+    def results_of(slots):
+        found = arrival_results(jnp.stack([from_inst, flag[0]]), slots)
+        return found.astype(jnp.bfloat16).reshape(1, QHEADS * HEADDIM)
 
     def prompt_part(first, last, earlier, after=()):
         return prompt_attention(
@@ -571,32 +632,27 @@
 
     row_units = prompt_pairs.shape[0] // (2 * UNIT)
     if inst_count == 4 * PAIRS and tp_count == 2 and row_units == 5 * half and steps == 8:
-        cuts = (0, 5, 8)
-        handed, results, prefill_out, decode_out = two_way_handoff(
+        cuts = (0, 3, 8)
+        handed, arrival_out, prefill_out, decode_out = two_way_handoff(
             prompt_pairs,
             source,
             flag,
             assignment[0] >= 0,
             arrival_query,
             fresh_of,
+            results_of,
             lambda n, earlier, after: prompt_part(cuts[n], cuts[n + 1], earlier, after),
             (cached, combined),
         )
-        part = lax.dynamic_index_in_dim(results, from_inst, 1, False)
-        part = part[:, :, : kv_here * HEADDIM].reshape(tp_count, GROUP, kv_here, HEADDIM)
-        arrival_out = part.transpose(0, 2, 1, 3).reshape(1, QHEADS * HEADDIM)
     else:
         handed = relay_handoff(prompt_pairs, source, inst_count)
         sent = lax.ppermute(arrival_query, "inst", [(i + half, i) for i in range(half)])
         every = lax.all_gather(sent, "inst", axis=0, tiled=True, axis_index_groups=groups)
-        results = lax.all_gather(fresh_of(every), "inst", axis_index_groups=groups)
-        part = lax.dynamic_index_in_dim(results, from_inst, 0, True)
-        part = part[:, :, : kv_here * HEADDIM].reshape(1, GROUP, kv_here, HEADDIM)
-        part = part.transpose(0, 2, 1, 3).reshape(1, width)
-        arrival_out = lax.all_gather(part, "tp", axis=1, tiled=True)
+        fresh = fresh_of(every.reshape(half, 1, KVHEADS, GROUP * HEADDIM), 0)
+        results = lax.all_gather(fresh, "inst", axis_index_groups=groups)
+        arrival_out = results_of(lax.all_gather(results, "tp")[:, :, None])
         prefill_out, _ = prompt_part(0, steps, None)
         decode_out, _ = combined(cached()[0])
-    arrival_out = jnp.where(is_prefill, jnp.zeros_like(arrival_out), arrival_out)
     return (prefill_out, handed, decode_out, arrival_out)
 
 

time: 141 us -> 130 us (0.922)
  the two profiles are of different devices: /device:TPU:24 before, /device:TPU:16 now
where the time goes in v2:
time: 130 us; the launch traced here: 129 us
  waiting for transfers between devices  45.1 us (35%)
  starting transfers between devices  43.5 us (33%)
  Pallas kernels  32.3 us (25%)
  local copies, waits for them, and re-layouts  4.02 us (3%)
  other arithmetic  2.43 us (2%)
  between operations  1.41 us (1%)
    ppermute x1, waiting for transfers between devices, two_way_handoff(): lax.ppermute(arrival_query, 'inst', [(i + half, i) for i in range(half)])  21.7 us
    all_to_all x2, starting transfers between devices, spread_out(): lax.all_to_all(array, ('inst', 'tp'), 0, 0, axis_index_groups=groups, til...  16.8 us
    ppermute x8, starting transfers between devices, crossing(): lax.ppermute(array, 'inst', hops + [(there, here) for here, there in hops])  16.8 us
    all_to_all x2, waiting for transfers between devices, spread_out(): lax.all_to_all(array, ('inst', 'tp'), 0, 0, axis_index_groups=groups, til...  11.3 us
    pallas_call x5, Pallas kernels, copies(): pl.pallas_call(functools.partial(copy_kernel, plan, side, (len(operands),...  8.09 us
    pallas_call x2, Pallas kernels, prompt_attention(): pl.pallas_call(functools.partial(prompt_kernel, heads), out_shape=(jax.Sh...  6.6 us
    pallas_call x1, Pallas kernels, cache_attention(): pl.pallas_call(functools.partial(cache_kernel, page_len), out_shape=(jax....  6.37 us
    ppermute x1, waiting for transfers between devices, fresh_of(): return lax.ppermute(fresh, 'inst', [(i, i + half) for i in range(half)])  5.53 us
  transfers between devices with their start and end apart: 15, of which 5 were waited for; matrix products, arithmetic and copies ran while one was open for 3% of the time, Pallas kernels for 22%

profile of v2, /device:TPU:16, one launch (start us, length us, event | category | flops | bytes accessed | tf_op | source)
XLA Modules:
  0.0 128.9 jit_solution(3956209448912186031)
XLA Ops:
  0.6 0.8 select_reduce_fusion
  1.4 0.1 pad_add_fusion.2.prefetch_ref
  1.5 0.6 cut_far.1
  2.2 0.1 collective-permute-start.5
  2.3 3.9 %collective-permute-start.6 = (bf16[2,6,8,1024]{3,2,1,0:T(8,128)(2,1)S(1)}, bf16[2,6,8,1024]{3,2,1,0:T(8,128)(2,1)S(1)}, u32[]{:S(2)}, u32[]{:S(2)}) collective-permute-start(bf16[2,6,8,1024]{3,2,1,0:T(8,128)(2,1)S(1)} %get-tuple-element.135), channel_id=1, source_target_pairs={{0,20},{2,22},{4,24},{6,26},{8,28},{10,30},{12,16},{14,18},{20,0},... | collective-permute-start | bytes 589832 | tf_op jit(solution)/shard_map/ppermute | solution.py:423
  6.2 1.5 %collective-permute-start.7 = (bf16[2,6,8,1024]{3,2,1,0:T(8,128)(2,1)S(1)}, bf16[2,6,8,1024]{3,2,1,0:T(8,128)(2,1)S(1)}, u32[]{:S(2)}, u32[]{:S(2)}) collective-permute-start(bf16[2,6,8,1024]{3,2,1,0:T(8,128)(2,1)S(1)} %get-tuple-element.136), channel_id=1, source_target_pairs={{0,24},{2,26},{4,28},{6,30},{8,16},{10,18},{12,20},{14,22},{24,0},... | collective-permute-start | bytes 589832 | tf_op jit(solution)/shard_map/ppermute | solution.py:423
  7.7 4.1 %collective-permute-start.4 = (bf16[1,8192]{1,0:T(2,128)(2,1)}, bf16[1,8192]{1,0:T(2,128)(2,1)S(1)}, u32[]{:S(2)}, u32[]{:S(2)}) collective-permute-start(bf16[1,8192]{1,0:T(2,128)(2,1)} %param.15), channel_id=1, source_target_pairs={{16,0},{18,2},{20,4},{22,6},{24,8},{26,10},{28,12},{30,14},{17,1},... | collective-permute-start | bytes 49160 | tf_op jit(solution)/shard_map/ppermute | solution.py:543
  11.8 0.1 collective-permute-start.8
  11.9 0.1 pad_add_fusion.3
  12.6 21.7 %collective-permute-done.4 = bf16[1,8192]{1,0:T(2,128)(2,1)S(1)} collective-permute-done((bf16[1,8192]{1,0:T(2,128)(2,1)}, bf16[1,8192]{1,0:T(2,128)(2,1)S(1)}, u32[]{:S(2)}, u32[]{:S(2)}) %collective-permute-start.4) | collective-permute-done | bytes 16416 | tf_op jit(solution)/shard_map/ppermute | solution.py:543
  34.3 31.7 %conditional.2 = (bf16[2,4,8,1024]{3,2,1,0:T(8,128)(2,1)}, bf16[2,4,8,1024]{3,2,1,0:T(8,128)(2,1)}, bf16[2,4,8,1024]{3,2,1,0:T(8,128)(2,1)}, bf16[2,4,8,1024]{3,...) conditional(s32[]{:T(128)} %bitcast.5, () %tuple.24, ...), branch_computations={%region_1.2_spmd, %region_2.3_spmd} | conditional | flops 131079 | bytes 11108622 | solution.py:541
  34.3 0.1 reduce
  34.4 2.1 %near_slots.1 = (bf16[16,3,8,1024]{3,2,1,0:T(8,128)(2,1)}, f32[8,128]{1,0:T(8,128)S(1)}) custom-call(s32[11]{0:T(128)S(1)} %get-tuple-element.68.prefetch_ref, bf16[80,8,1024]{2,1,0:T(8,128)(2,1)} %bitcast.34, bf16[8,1024]{1,0:T(8,128)(2,1)S(1)} %reshape.34.refs_1_), custom_call_target="tpu_custom_call" | custom-call | flops 1 | bytes 1 | tf_op jit(solution)/shard_map/cond/branch_1_fun/near_slots/pallas_call | solution.py:327
  36.6 5.4 %all-to-all-start.1 = ((bf16[16,3,8,1024]{3,2,1,0:T(8,128)(2,1)}), bf16[16,3,8,1024]{3,2,1,0:T(8,128)(2,1)}, u32[]{:S(2)}, u32[]{:S(2)}) async-start(bf16[16,3,8,1024]{3,2,1,0:T(8,128)(2,1)} %get-tuple-element.71), calls=%async_computation.1 | async-start | bytes 1572864 | tf_op jit(solution)/shard_map/cond/branch_1_fun/all_to_all | solution.py:429
  42.0 0.9 copy.25
  42.8 6.4 %cache_attention.1 = (f32[8,32,256]{2,1,0:T(8,128)S(1)}, f32[8,128]{1,0:T(8,128)S(1)}) custom-call(s32[2]{0:T(128)S(1)} %get-tuple-element.74.info_ref, s32[4,8]{1,0:T(4,128)} %get-tuple-element.152.table_ref, s32[4]{0:T(128)} %get-tuple-element.153.lengths_ref, bf16[4,64,128]{2,1,0:T(8,128)(2,1)S(1)} %bitcast.29, bf16[320,2048]{1,0:T(8,128)(2,1)} %bitcast.35, ...), custom_call_target="tpu_custom_call" | custom-call | flops 1 | bytes 1 | tf_op jit(solution)/shard_map/cond/branch_1_fun/cache_attention/pallas_call | solution.py:150
  49.2 0.6 copy-done.2
  49.8 1.9 %collective-permute-start.2 = (f32[1,8,32,256]{3,2,1,0:T(8,128)S(1)}, f32[1,8,32,256]{3,2,1,0:T(8,128)S(1)}, u32[]{:S(2)}, u32[]{:S(2)}) collective-permute-start(f32[1,8,32,256]{3,2,1,0:T(8,128)S(1)} %bitcast.30), channel_id=1, source_target_pairs={{0,1},{1,0},{2,3},{3,2},{4,5},{5,4},{6,7},{7,6},{8,9},{9,8},{10,11... | collective-permute-start | bytes 786440 | tf_op jit(solution)/shard_map/cond/branch_1_fun/ppermute | solution.py:602
  51.7 2.9 %prompt_attention.2 = (bf16[640,4096]{1,0:T(8,128)(2,1)}, f32[8,128]{1,0:T(8,128)}) custom-call(s32[1]{0:T(128)} %get-tuple-element.72.flag_ref, bf16[640,4096]{1,0:T(8,128)(2,1)} %get-tuple-element.81.q_ref, bf16[640,1024]{1,0:T(8,128)(2,1)S(1)} %copy-done.3, f32[8,128]{1,0:T(8,128)} %copy-done.2), custom_call_target="tpu_custom_call" | custom-call | flops 1 | bytes 1 | tf_op jit(solution)/shard_map/cond/branch_1_fun/prompt_attention/pallas_call | solution.py:92
  54.5 4.9 %collective-permute-done.2 = f32[1,8,32,256]{3,2,1,0:T(8,128)S(1)} collective-permute-done((f32[1,8,32,256]{3,2,1,0:T(8,128)S(1)}, f32[1,8,32,256]{3,2,1,0:T(8,128)S(1)}, u32[]{:S(2)}, u32[]{:S(2)}) %collective-permute-start.2) | collective-permute-done | bytes 262176 | tf_op jit(solution)/shard_map/cond/branch_1_fun/ppermute | solution.py:602
  59.5 0.0 copy-start
  59.5 0.7 copy-done
  60.2 1.5 %combine_parts.1 = (bf16[4,64,128]{2,1,0:T(8,128)(2,1)S(1)}, f32[8,128]{1,0:T(8,128)S(1)}) custom-call(s32[1]{0:T(128)} %get-tuple-element.72.flag_ref, f32[1,8,32,256]{3,2,1,0:T(8,128)S(1)} %get-tuple-element.155.refs_0_, f32[1,8,32,256]{3,2,1,0:T(8,128)S(1)} %get-tuple-element.154.refs_1_, f32[8,128]{1,0:T(8,128)S(1)} %copy-done), custom_call_target="tpu_custom_call" | custom-call | flops 1 | bytes 1 | tf_op jit(solution)/shard_map/cond/branch_1_fun/combine_parts/pallas_call | solution.py:195
  61.6 0.0 all-to-all-done.1.refs_0_
  61.6 1.7 %for_neighbour.1 = (bf16[4,2,2,8,1024]{4,3,2,1,0:T(8,128)(2,1)S(1)}, f32[8,128]{1,0:T(8,128)}) custom-call(s32[11]{0:T(128)S(1)} %get-tuple-element.68.prefetch_ref, bf16[16,3,8,1024]{3,2,1,0:T(8,128)(2,1)} %all-to-all-done.1.refs_0_, f32[8,128]{1,0:T(8,128)S(1)} %get-tuple-element.85.refs_1_), custom_call_target="tpu_custom_call" | custom-call | flops 1 | bytes 1 | tf_op jit(solution)/shard_map/cond/branch_1_fun/for_neighbour/pallas_call | solution.py:327
  63.4 0.7 collective-permute-start.3
  64.1 0.1 copy.24
  64.1 0.0 collective-permute-done.3.refs_1_
  64.1 1.8 %for_receivers.1 = (bf16[2,4,8,1024]{3,2,1,0:T(8,128)(2,1)}, bf16[2,4,8,1024]{3,2,1,0:T(8,128)(2,1)}, bf16[2,4,8,1024]{3,2,1,0:T(8,128)(2,1)}, bf16[2,4,8,1024]{3,2,1,0:T(8,128)(2,1)S(1)}, f32[8,128]{1,0:T(8,128)}) custom-call(s32[11]{0:T(128)S(1)} %get-tuple-element.68.prefetch_ref, bf16[16,3,8,1024]{3,2,1,0:T(8,128)(2,1)} %all-to-all-done.1.refs_0_, ...), custom_call_target="tpu_custom_call" | custom-call | flops 1 | bytes 1 | tf_op jit(solution)/shard_map/cond/branch_1_fun/for_receivers/pallas_call | solution.py:327
  66.0 0.0 copy-start.5
  66.0 6.3 %collective-permute-start.9 = (bf16[2,4,8,1024]{3,2,1,0:T(8,128)(2,1)}, bf16[2,4,8,1024]{3,2,1,0:T(8,128)(2,1)S(1)}, u32[]{:S(2)}, u32[]{:S(2)}) collective-permute-start(bf16[2,4,8,1024]{3,2,1,0:T(8,128)(2,1)} %get-tuple-element.140), channel_id=1, source_target_pairs={{0,16},{2,18},{4,20},{6,22},{8,24},{10,26},{12,28},{14,30},{16,0},... | collective-permute-start | bytes 393224 | tf_op jit(solution)/shard_map/ppermute | solution.py:423
  72.3 0.0 collective-permute-done.5
  72.3 1.0 collective-permute-start.10
  73.3 0.0 collective-permute-done.6
  73.3 2.8 %collective-permute-start.11 = (bf16[2,4,8,1024]{3,2,1,0:T(8,128)(2,1)}, bf16[2,4,8,1024]{3,2,1,0:T(8,128)(2,1)S(1)}, u32[]{:S(2)}, u32[]{:S(2)}) collective-permute-start(bf16[2,4,8,1024]{3,2,1,0:T(8,128)(2,1)} %get-tuple-element.142), channel_id=1, source_target_pairs={{0,24},{2,26},{4,28},{6,30},{8,16},{10,18},{12,20},{14,22},{24,0},... | collective-permute-start | bytes 393224 | tf_op jit(solution)/shard_map/ppermute | solution.py:423
  76.2 0.0 collective-permute-done.7
  76.2 1.0 collective-permute-start.12
  77.1 0.0 collective-permute-done.8
  77.1 0.0 copy-done.5
  77.2 48.7 %conditional.3 = (bf16[640,4096]{1,0:T(8,128)(2,1)}, bf16[16,4,8,1024]{3,2,1,0:T(8,128)(2,1)}, bf16[1,8192]{1,0:T(2,128)(2,1)S(1)}) conditional(s32[]{:T(128)} %bitcast.5, bf16[640,4096]{1,0:T(8,128)(2,1)} %get-tuple-element.132, (s32[]{:T(128)}, pred[]{:T(512)}, s32[8]{0:T(128)S(1)}, s32[]{:T(128)}, bf16[16,3,8,1024]{3,2,1,0:T(8,128)(2,1)}, ...), branch_computations={%region_3.4_spmd, %region_4.5_spmd} | conditional | flops 8208 | bytes 10125610 | solution.py:541
  77.2 0.0 copy-start.4
  77.2 0.6 dynamic_slice.7
  77.8 0.7 pad_add_fusion.info_ref
  78.5 3.7 %fresh_attention.1 = bf16[8,1024]{1,0:T(8,128)(2,1)S(1)} custom-call(s32[3]{0:T(128)S(1)} %pad_add_fusion.info_ref, bf16[16,3,8,1024]{3,2,1,0:T(8,128)(2,1)} %get-tuple-element.106.q_ref, bf16[640,1024]{1,0:T(8,128)(2,1)} %get-tuple-element.95.kv_ref), custom_call_target="tpu_custom_call" | custom-call | flops 1 | bytes 1 | tf_op jit(solution)/shard_map/cond/branch_1_fun/fresh_attention/pallas_call | solution.py:241
  82.2 1.3 %collective-permute-start = (bf16[8,1024]{1,0:T(8,128)(2,1)S(1)}, bf16[8,1024]{1,0:T(8,128)(2,1)S(1)}, u32[]{:S(2)}, u32[]{:S(2)}) collective-permute-start(bf16[8,1024]{1,0:T(8,128)(2,1)S(1)} %fresh_attention.1), channel_id=1, source_target_pairs={{0,16},{2,18},{4,20},{6,22},{8,24},{10,26},{12,28},{14,30},{1,17},... | collective-permute-start | bytes 49160 | tf_op jit(solution)/shard_map/cond/branch_1_fun/ppermute | solution.py:622
  83.5 5.5 %collective-permute-done.refs_4_.fresh_ref = bf16[8,1024]{1,0:T(8,128)(2,1)S(1)} collective-permute-done((bf16[8,1024]{1,0:T(8,128)(2,1)S(1)}, bf16[8,1024]{1,0:T(8,128)(2,1)S(1)}, u32[]{:S(2)}, u32[]{:S(2)}) %collective-permute-start) | collective-permute-done | bytes 16416 | tf_op jit(solution)/shard_map/cond/branch_1_fun/ppermute | solution.py:622
  89.1 1.7 %split_relays.1 = (bf16[4,2,3,8,1024]{4,3,2,1,0:T(8,128)(2,1)S(1)}, bf16[4,2,3,8,1024]{4,3,2,1,0:T(8,128)(2,1)S(1)}, f32[8,128]{1,0:T(8,128)}) custom-call(s32[11]{0:T(128)S(1)} %get-tuple-element.97.prefetch_ref, bf16[2,6,8,1024]{3,2,1,0:T(8,128)(2,1)S(1)} %get-tuple-element.98.refs_0_, bf16[2,6,8,1024]{3,2,1,0:T(8,128)(2,1)S(1)} %get-tuple-element.99.refs_1_, ...), custom_call_target="tpu_custom_call" | custom-call | flops 1 | bytes 1 | tf_op jit(solution)/shard_map/cond/branch_1_fun/split_relays/pallas_call | solution.py:327
  90.8 1.9 %collective-permute-start.1 = (bf16[4,2,3,8,1024]{4,3,2,1,0:T(8,128)(2,1)S(1)}, bf16[4,2,3,8,1024]{4,3,2,1,0:T(8,128)(2,1)S(1)}, u32[]{:S(2)}, u32[]{:S(2)}) collective-permute-start(bf16[4,2,3,8,1024]{4,3,2,1,0:T(8,128)(2,1)S(1)} %get-tuple-element.108), channel_id=1, source_target_pairs={{16,18},{18,16},{20,22},{22,20},{24,26},{26,24},{28,30},{30,28},{1... | collective-permute-start | bytes 1179656 | tf_op jit(solution)/shard_map/cond/branch_1_fun/ppermute | solution.py:426
  92.7 1.7 %collective-permute-done.1.recv_ref = bf16[4,2,3,8,1024]{4,3,2,1,0:T(8,128)(2,1)S(1)} collective-permute-done((bf16[4,2,3,8,1024]{4,3,2,1,0:T(8,128)(2,1)S(1)}, bf16[4,2,3,8,1024]{4,3,2,1,0:T(8,128)(2,1)S(1)}, u32[]{:S(2)}, u32[]{:S(2)}) %collective-permute-start.1) | collective-permute-done | bytes 393248 | tf_op jit(solution)/shard_map/cond/branch_1_fun/ppermute | solution.py:426
  94.4 1.8 %relay_slots.1 = (bf16[16,4,8,1024]{3,2,1,0:T(8,128)(2,1)}, f32[8,128]{1,0:T(8,128)S(1)}) custom-call(s32[11]{0:T(128)S(1)} %get-tuple-element.97.prefetch_ref, bf16[4,2,3,8,1024]{4,3,2,1,0:T(8,128)(2,1)S(1)} %get-tuple-element.107.keep_ref, bf16[4,2,3,8,1024]{4,3,2,1,0:T(8,128)(2,1)S(1)} %collective-permute-done.1.recv_ref, ...), custom_call_target="tpu_custom_call" | custom-call | flops 1 | bytes 1 | tf_op jit(solution)/shard_map/cond/branch_1_fun/relay_slots/pallas_call | solution.py:518
  96.2 0.0 copy-start.1
  96.2 0.6 copy-done.1
  96.8 11.4 %all-to-all-start = ((bf16[16,4,8,1024]{3,2,1,0:T(8,128)(2,1)}), bf16[16,4,8,1024]{3,2,1,0:T(8,128)(2,1)}, u32[]{:S(2)}, u32[]{:S(2)}) async-start(bf16[16,4,8,1024]{3,2,1,0:T(8,128)(2,1)} %get-tuple-element.111), calls=%async_computation | async-start | bytes 2097152 | tf_op jit(solution)/shard_map/cond/branch_1_fun/all_to_all | solution.py:429
  108.2 0.6 dynamic_slice.8
  108.8 0.6 pad_add_fusion.1.info_ref
  109.5 3.7 %prompt_attention.3 = (bf16[640,4096]{1,0:T(8,128)(2,1)}, f32[8,128]{1,0:T(8,128)}) custom-call(s32[1]{0:T(128)} %get-tuple-element.93.flag_ref, bf16[640,4096]{1,0:T(8,128)(2,1)} %get-tuple-element.94.q_ref, bf16[640,1024]{1,0:T(8,128)(2,1)S(1)} %copy-done.4, bf16[640,4096]{1,0:T(8,128)(2,1)} %get-tuple-element.96.rest_0_, ...), custom_call_target="tpu_custom_call", output_to_operand_aliasing={{0}: (3, {})} | custom-call | flops 1 | bytes 1 | tf_op jit(solution)/shard_map/cond/branch_1_fun/prompt_attention/pallas_call | solution.py:92
  113.2 11.3 %all-to-all-done = bf16[16,4,8,1024]{3,2,1,0:T(8,128)(2,1)} async-done(((bf16[16,4,8,1024]{3,2,1,0:T(8,128)(2,1)}), bf16[16,4,8,1024]{3,2,1,0:T(8,128)(2,1)}, u32[]{:S(2)}, u32[]{:S(2)}) %all-to-all-start) | async-done | bytes 1048608 | tf_op jit(solution)/shard_map/cond/branch_1_fun/all_to_all | solution.py:429
  124.5 1.3 %arrival_results.1 = f32[64,128]{1,0:T(8,128)S(1)} custom-call(s32[2]{0:T(128)S(1)} %pad_add_fusion.1.info_ref, bf16[2,8,4,8,1024]{4,3,2,1,0:T(8,128)(2,1)} %bitcast.4.unit_ref), custom_call_target="tpu_custom_call" | custom-call | flops 1 | bytes 1 | tf_op jit(solution)/shard_map/cond/branch_1_fun/arrival_results/pallas_call | solution.py:271
  125.8 0.0 copy-start.6
  125.8 0.0 collective-permute-done.9.refs_0_
  125.8 0.0 collective-permute-done.10.refs_1_
  125.9 0.0 collective-permute-done.11.refs_2_
  125.9 0.0 collective-permute-done.12.refs_3_
  125.9 3.0 %rows.1 = bf16[40,8,2048]{2,1,0:T(8,128)(2,1)} custom-call(s32[11]{0:T(128)S(1)} %pad_add_fusion.2.prefetch_ref, bf16[16,4,8,1024]{3,2,1,0:T(8,128)(2,1)} %get-tuple-element.139.slots_ref, bf16[2,4,8,1024]{3,2,1,0:T(8,128)(2,1)S(1)} %collective-permute-done.9.refs_0_, bf16[2,4,8,1024]{3,2,1,0:T(8,128)(2,1)S(1)} %collective-permute-done.10.refs_1_, ...), custom_call_target="tpu_custom_call" | custom-call | flops 1 | bytes 1 | tf_op jit(solution)/shard_map/rows/pallas_call | solution.py:551
  (11 shorter events, 0.1 us)
Async XLA Ops:
  2.2 70.2 %collective-permute-start.5 = (bf16[2,6,8,1024]{3,2,1,0:T(8,128)(2,1)S(1)}, bf16[2,6,8,1024]{3,2,1,0:T(8,128)(2,1)S(1)}, u32[]{:S(2)}, u32[]{:S(2)}) collective-permute-start(bf16[2,6,8,1024]{3,2,1,0:T(8,128)(2,1)S(1)} %get-tuple-element.134), channel_id=1, source_target_pairs={{0,16},{2,18},{4,20},{6,22},{8,24},{10,26},{12,28},{14,30},{16,0},... | collective-permute-start | bytes 589832 | tf_op jit(solution)/shard_map/ppermute | solution.py:423
  2.3 71.0 %collective-permute-start.6 = (bf16[2,6,8,1024]{3,2,1,0:T(8,128)(2,1)S(1)}, bf16[2,6,8,1024]{3,2,1,0:T(8,128)(2,1)S(1)}, u32[]{:S(2)}, u32[]{:S(2)}) collective-permute-start(bf16[2,6,8,1024]{3,2,1,0:T(8,128)(2,1)S(1)} %get-tuple-element.135), channel_id=1, source_target_pairs={{0,20},{2,22},{4,24},{6,26},{8,28},{10,30},{12,16},{14,18},{20,0},... | collective-permute-start | bytes 589832 | tf_op jit(solution)/shard_map/ppermute | solution.py:423
  6.2 70.0 %collective-permute-start.7 = (bf16[2,6,8,1024]{3,2,1,0:T(8,128)(2,1)S(1)}, bf16[2,6,8,1024]{3,2,1,0:T(8,128)(2,1)S(1)}, u32[]{:S(2)}, u32[]{:S(2)}) collective-permute-start(bf16[2,6,8,1024]{3,2,1,0:T(8,128)(2,1)S(1)} %get-tuple-element.136), channel_id=1, source_target_pairs={{0,24},{2,26},{4,28},{6,30},{8,16},{10,18},{12,20},{14,22},{24,0},... | collective-permute-start | bytes 589832 | tf_op jit(solution)/shard_map/ppermute | solution.py:423
  7.7 26.6 %collective-permute-start.4 = (bf16[1,8192]{1,0:T(2,128)(2,1)}, bf16[1,8192]{1,0:T(2,128)(2,1)S(1)}, u32[]{:S(2)}, u32[]{:S(2)}) collective-permute-start(bf16[1,8192]{1,0:T(2,128)(2,1)} %param.15), channel_id=1, source_target_pairs={{16,0},{18,2},{20,4},{22,6},{24,8},{26,10},{28,12},{30,14},{17,1},... | collective-permute-start | bytes 49160 | tf_op jit(solution)/shard_map/ppermute | solution.py:543
  11.8 65.3 %collective-permute-start.8 = (bf16[2,6,8,1024]{3,2,1,0:T(8,128)(2,1)S(1)}, bf16[2,6,8,1024]{3,2,1,0:T(8,128)(2,1)S(1)}, u32[]{:S(2)}, u32[]{:S(2)}) collective-permute-start(bf16[2,6,8,1024]{3,2,1,0:T(8,128)(2,1)S(1)} %get-tuple-element.137), channel_id=1, source_target_pairs={{0,28},{2,30},{4,16},{6,18},{8,20},{10,22},{12,24},{14,26},{28,0},... | collective-permute-start | bytes 589832 | tf_op jit(solution)/shard_map/ppermute | solution.py:423
  34.3 42.8 %copy-start.7 = (s32[8]{0:T(128)S(1)}, s32[8]{0:T(128)}, u32[]{:S(2)}) copy-start(s32[8]{0:T(128)} %param.19) | copy-start | bytes 100
  34.3 17.4 %copy-start.3 = (bf16[640,1024]{1,0:T(8,128)(2,1)S(1)}, bf16[640,1024]{1,0:T(8,128)(2,1)}, u32[]{:S(2)}) copy-start(bf16[640,1024]{1,0:T(8,128)(2,1)} %get-tuple-element.82.kv_ref) | copy-start | bytes 3932164 | tf_op jit(solution)/shard_map/cond
  36.6 25.1 %all-to-all-start.1 = ((bf16[16,3,8,1024]{3,2,1,0:T(8,128)(2,1)}), bf16[16,3,8,1024]{3,2,1,0:T(8,128)(2,1)}, u32[]{:S(2)}, u32[]{:S(2)}) async-start(bf16[16,3,8,1024]{3,2,1,0:T(8,128)(2,1)} %get-tuple-element.71), calls=%async_computation.1 | async-start | bytes 1572864 | tf_op jit(solution)/shard_map/cond/branch_1_fun/all_to_all | solution.py:429
  49.2 0.6 copy-start.2
  49.8 9.6 %collective-permute-start.2 = (f32[1,8,32,256]{3,2,1,0:T(8,128)S(1)}, f32[1,8,32,256]{3,2,1,0:T(8,128)S(1)}, u32[]{:S(2)}, u32[]{:S(2)}) collective-permute-start(f32[1,8,32,256]{3,2,1,0:T(8,128)S(1)} %bitcast.30), channel_id=1, source_target_pairs={{0,1},{1,0},{2,3},{3,2},{4,5},{5,4},{6,7},{7,6},{8,9},{9,8},{10,11... | collective-permute-start | bytes 786440 | tf_op jit(solution)/shard_map/cond/branch_1_fun/ppermute | solution.py:602
  59.5 0.7 copy-start
  63.4 0.7 collective-permute-start.3
  66.0 11.2 %copy-start.5 = (bf16[4,8192]{1,0:T(4,128)(2,1)}, bf16[4,8192]{1,0:T(4,128)(2,1)S(1)}, u32[]{:S(2)}) copy-start(bf16[4,8192]{1,0:T(4,128)(2,1)S(1)} %get-tuple-element.130) | copy-start | bytes 196612
  66.0 59.8 %collective-permute-start.9 = (bf16[2,4,8,1024]{3,2,1,0:T(8,128)(2,1)}, bf16[2,4,8,1024]{3,2,1,0:T(8,128)(2,1)S(1)}, u32[]{:S(2)}, u32[]{:S(2)}) collective-permute-start(bf16[2,4,8,1024]{3,2,1,0:T(8,128)(2,1)} %get-tuple-element.140), channel_id=1, source_target_pairs={{0,16},{2,18},{4,20},{6,22},{8,24},{10,26},{12,28},{14,30},{16,0},... | collective-permute-start | bytes 393224 | tf_op jit(solution)/shard_map/ppermute | solution.py:423
  72.3 53.5 %collective-permute-start.10 = (bf16[2,4,8,1024]{3,2,1,0:T(8,128)(2,1)}, bf16[2,4,8,1024]{3,2,1,0:T(8,128)(2,1)S(1)}, u32[]{:S(2)}, u32[]{:S(2)}) collective-permute-start(bf16[2,4,8,1024]{3,2,1,0:T(8,128)(2,1)} %get-tuple-element.141), channel_id=1, source_target_pairs={{0,20},{2,22},{4,24},{6,26},{8,28},{10,30},{12,16},{14,18},{20,0},... | collective-permute-start | bytes 393224 | tf_op jit(solution)/shard_map/ppermute | solution.py:423
  73.3 52.5 %collective-permute-start.11 = (bf16[2,4,8,1024]{3,2,1,0:T(8,128)(2,1)}, bf16[2,4,8,1024]{3,2,1,0:T(8,128)(2,1)S(1)}, u32[]{:S(2)}, u32[]{:S(2)}) collective-permute-start(bf16[2,4,8,1024]{3,2,1,0:T(8,128)(2,1)} %get-tuple-element.142), channel_id=1, source_target_pairs={{0,24},{2,26},{4,28},{6,30},{8,16},{10,18},{12,20},{14,22},{24,0},... | collective-permute-start | bytes 393224 | tf_op jit(solution)/shard_map/ppermute | solution.py:423
  76.2 49.7 %collective-permute-start.12 = (bf16[2,4,8,1024]{3,2,1,0:T(8,128)(2,1)S(1)}, bf16[2,4,8,1024]{3,2,1,0:T(8,128)(2,1)S(1)}, u32[]{:S(2)}, u32[]{:S(2)}) collective-permute-start(bf16[2,4,8,1024]{3,2,1,0:T(8,128)(2,1)S(1)} %get-tuple-element.143), channel_id=1, source_target_pairs={{0,28},{2,30},{4,16},{6,18},{8,20},{10,22},{12,24},{14,26},{28,0},... | collective-permute-start | bytes 393224 | tf_op jit(solution)/shard_map/ppermute | solution.py:423
  77.2 32.3 %copy-start.4 = (bf16[640,1024]{1,0:T(8,128)(2,1)S(1)}, bf16[640,1024]{1,0:T(8,128)(2,1)}, u32[]{:S(2)}) copy-start(bf16[640,1024]{1,0:T(8,128)(2,1)} %get-tuple-element.95.kv_ref) | copy-start | bytes 3932164 | tf_op jit(solution)/shard_map/cond
  82.2 6.8 %collective-permute-start = (bf16[8,1024]{1,0:T(8,128)(2,1)S(1)}, bf16[8,1024]{1,0:T(8,128)(2,1)S(1)}, u32[]{:S(2)}, u32[]{:S(2)}) collective-permute-start(bf16[8,1024]{1,0:T(8,128)(2,1)S(1)} %fresh_attention.1), channel_id=1, source_target_pairs={{0,16},{2,18},{4,20},{6,22},{8,24},{10,26},{12,28},{14,30},{1,17},... | collective-permute-start | bytes 49160 | tf_op jit(solution)/shard_map/cond/branch_1_fun/ppermute | solution.py:622
  90.8 3.6 %collective-permute-start.1 = (bf16[4,2,3,8,1024]{4,3,2,1,0:T(8,128)(2,1)S(1)}, bf16[4,2,3,8,1024]{4,3,2,1,0:T(8,128)(2,1)S(1)}, u32[]{:S(2)}, u32[]{:S(2)}) collective-permute-start(bf16[4,2,3,8,1024]{4,3,2,1,0:T(8,128)(2,1)S(1)} %get-tuple-element.108), channel_id=1, source_target_pairs={{16,18},{18,16},{20,22},{22,20},{24,26},{26,24},{28,30},{30,28},{1... | collective-permute-start | bytes 1179656 | tf_op jit(solution)/shard_map/cond/branch_1_fun/ppermute | solution.py:426
  96.2 0.6 copy-start.1
  96.8 27.7 %all-to-all-start = ((bf16[16,4,8,1024]{3,2,1,0:T(8,128)(2,1)}), bf16[16,4,8,1024]{3,2,1,0:T(8,128)(2,1)}, u32[]{:S(2)}, u32[]{:S(2)}) async-start(bf16[16,4,8,1024]{3,2,1,0:T(8,128)(2,1)} %get-tuple-element.111), calls=%async_computation | async-start | bytes 2097152 | tf_op jit(solution)/shard_map/cond/branch_1_fun/all_to_all | solution.py:429
  125.8 3.1 %copy-start.6 = (bf16[1,8192]{1,0:T(2,128)(2,1)}, bf16[1,8192]{1,0:T(2,128)(2,1)S(1)}, u32[]{:S(2)}) copy-start(bf16[1,8192]{1,0:T(2,128)(2,1)S(1)} %get-tuple-element.131) | copy-start | bytes 49156

commit v3 on v2

--- a/solution.py
+++ b/solution.py
@@ -22,6 +22,26 @@
 COST = pl.CostEstimate(flops=1, bytes_accessed=1, transcendentals=0)
 
 
+INST, TP, FIRST = 0, 1, 2
+
+
+def on_prefill(info):
+    return info[INST] < info.shape[0] - FIRST
+
+
+def order(info):
+    half = info.shape[0] - FIRST
+    return info[INST] - jnp.where(on_prefill(info), 0, half)
+
+
+def source_of(info, receiver):
+    half = info.shape[0] - FIRST
+    found = jnp.int32(0)
+    for p in range(half):
+        found = jnp.where(info[FIRST + p] == receiver, p, found)
+    return found
+
+
 def dot_t(a, b):
     return lax.dot_general(a, b, (((1,), (1,)), ((), ())), preferred_element_type=jnp.float32)
 
@@ -30,15 +50,15 @@
     return lax.dot_general(a, b, (((1,), (0,)), ((), ())), preferred_element_type=jnp.float32)
 
 
-def prompt_kernel(heads, flag_ref, q_ref, kv_ref, *rest):
+def prompt_kernel(heads, info_ref, q_ref, kv_ref, *rest):
     out_ref = rest[-2]
     length = q_ref.shape[0]
 
-    @pl.when(flag_ref[0] == 0)
+    @pl.when(jnp.logical_not(on_prefill(info_ref)))
     def _():
         out_ref[...] = jnp.zeros_like(out_ref)
 
-    @pl.when(flag_ref[0] != 0)
+    @pl.when(on_prefill(info_ref))
     def _():
         rows_all = lax.broadcasted_iota(jnp.int32, (TILE, TILE), 0)
         cols_all = lax.broadcasted_iota(jnp.int32, (TILE, TILE), 1)
@@ -69,21 +89,21 @@
 IN_VMEM = pl.BlockSpec(memory_space=pltpu.VMEM)
 
 
-def prompt_attention(flag, queries, pairs, first, steps, heads, earlier, after):
+def prompt_attention(info, queries, pairs, first, steps, heads, earlier, after):
     length, width = queries.shape
     per_kv = GROUP // heads
 
-    def q_map(i, flag_ref):
-        return (0, jnp.where(flag_ref[0] != 0, i + first, 0))
-
-    def kv_map(i, flag_ref):
-        return (0, jnp.where(flag_ref[0] != 0, (i + first) // per_kv, 0))
+    def q_map(i, info_ref):
+        return (0, jnp.where(on_prefill(info_ref), i + first, 0))
+
+    def kv_map(i, info_ref):
+        return (0, jnp.where(on_prefill(info_ref), (i + first) // per_kv, 0))
 
     in_specs = [
         pl.BlockSpec((length, heads * HEADDIM), q_map),
         pl.BlockSpec((length, 2 * HEADDIM), kv_map),
     ]
-    operands = [flag, queries, pairs]
+    operands = [info, queries, pairs]
     aliases = {}
     if earlier is not None:
         in_specs.append(ANYWHERE)
@@ -97,7 +117,7 @@
             grid=(steps,),
             in_specs=in_specs + [IN_HBM] * len(after),
             out_specs=(
-                pl.BlockSpec((length, heads * HEADDIM), lambda i, flag_ref: (0, i + first)),
+                pl.BlockSpec((length, heads * HEADDIM), lambda i, info_ref: (0, i + first)),
                 IN_HBM,
             ),
         ),
@@ -112,23 +132,23 @@
     out_ref, _, count_ref = rest[-3:]
     rows, slots = table_ref.shape
 
-    @pl.when(info_ref[0] != 0)
+    @pl.when(jnp.logical_and(on_prefill(info_ref), pl.program_id(0) == 0))
     def _():
         out_ref[...] = jnp.zeros_like(out_ref)
 
-    @pl.when(jnp.logical_and(info_ref[0] == 0, pl.program_id(0) == 0))
+    @pl.when(jnp.logical_and(jnp.logical_not(on_prefill(info_ref)), pl.program_id(0) == 0))
     def _():
         token = lax.broadcasted_iota(jnp.int32, (GROUP, count_ref.shape[1]), 1)
         page, offset = token // page_len, token % page_len
         for r in range(rows):
             count = jnp.zeros(token.shape, jnp.float32)
             for slot in range(slots):
-                left = lengths_ref[r] - (info_ref[1] * slots + slot) * page_len
+                left = lengths_ref[r] - (info_ref[TP] * slots + slot) * page_len
                 valid = jnp.logical_and(page == table_ref[r, slot], offset < left)
                 count = count + jnp.where(valid, 1.0, 0.0)
             count_ref[r * GROUP : (r + 1) * GROUP] = count
 
-    @pl.when(info_ref[0] == 0)
+    @pl.when(jnp.logical_not(on_prefill(info_ref)))
     def _():
         count = count_ref[...]
         here = count > 0.0
@@ -147,6 +167,10 @@
 def cache_attention(info, table, lengths, queries, pool, page_len, after):
     rows = queries.shape[0]
     tokens = pool.shape[0]
+
+    def head(h, info):
+        return jnp.where(on_prefill(info), 0, h)
+
     return pl.pallas_call(
         functools.partial(cache_kernel, page_len),
         out_shape=(
@@ -157,30 +181,30 @@
             num_scalar_prefetch=3,
             grid=(KVHEADS,),
             in_specs=[
-                pl.BlockSpec((rows, GROUP, HEADDIM), lambda h, *_: (0, h, 0)),
-                pl.BlockSpec((tokens, 2 * HEADDIM), lambda h, info, *_: (0, h * (1 - info[0]))),
+                pl.BlockSpec((rows, GROUP, HEADDIM), lambda h, info, *_: (0, head(h, info), 0)),
+                pl.BlockSpec((tokens, 2 * HEADDIM), lambda h, info, *_: (0, head(h, info))),
             ]
             + [IN_HBM] * len(after),
             out_specs=(
-                pl.BlockSpec((1, rows * GROUP, 2 * HEADDIM), lambda h, *_: (h, 0, 0)),
+                pl.BlockSpec((1, rows * GROUP, 2 * HEADDIM), lambda h, info, *_: (head(h, info), 0, 0)),
                 IN_HBM,
             ),
             scratch_shapes=[pltpu.VMEM((rows * GROUP, tokens), jnp.float32)],
         ),
-        compiler_params=pltpu.CompilerParams(vmem_limit_bytes=VMEM),
+        compiler_params=pltpu.CompilerParams(vmem_limit_bytes=LARGE),
         cost_estimate=COST,
         name="cache_attention",
     )(info, table, lengths, queries, pool, *after)
 
 
-def combine_kernel(count, flag_ref, *refs):
+def combine_kernel(count, info_ref, *refs):
     part_refs, out_ref = refs[:count], refs[-2]
 
-    @pl.when(flag_ref[0] != 0)
+    @pl.when(on_prefill(info_ref))
     def _():
         out_ref[...] = jnp.zeros_like(out_ref)
 
-    @pl.when(flag_ref[0] == 0)
+    @pl.when(jnp.logical_not(on_prefill(info_ref)))
     def _():
         parts = [ref[n] for ref in part_refs for n in range(ref.shape[0])]
         peaks = [part[:, HEADDIM : HEADDIM + 1] for part in parts]
@@ -191,7 +215,7 @@
         out_ref[...] = (mixed / total).reshape(out_ref.shape).astype(jnp.bfloat16)
 
 
-def combine_parts(flag, parts, rows, after):
+def combine_parts(info, parts, rows, after):
     return pl.pallas_call(
         functools.partial(combine_kernel, len(parts)),
         out_shape=(jax.ShapeDtypeStruct((rows, QHEADS, HEADDIM), jnp.bfloat16), MARK),
@@ -201,55 +225,63 @@
             in_specs=[
                 pl.BlockSpec(
                     (part.shape[0], None, rows * GROUP, 2 * HEADDIM),
-                    lambda h, flag_ref: (0, h, 0, 0),
+                    lambda h, info_ref: (0, h, 0, 0),
                 )
                 for part in parts
             ]
             + [IN_HBM] * len(after),
             out_specs=(
-                pl.BlockSpec((rows, GROUP, HEADDIM), lambda h, flag_ref: (0, h, 0)),
+                pl.BlockSpec((rows, GROUP, HEADDIM), lambda h, info_ref: (0, h, 0)),
                 IN_HBM,
             ),
         ),
-        compiler_params=pltpu.CompilerParams(vmem_limit_bytes=VMEM),
+        compiler_params=pltpu.CompilerParams(vmem_limit_bytes=LARGE),
         cost_estimate=COST,
         name="combine_parts",
-    )(flag, *parts, *after)
+    )(info, *parts, *after)
 
 
 def fresh_kernel(info_ref, q_ref, kv_ref, *rest):
     out_ref = rest[-1]
+    heads = kv_ref.shape[1] // (2 * HEADDIM)
     units = q_ref[...].astype(jnp.float32)
     row = lax.broadcasted_iota(jnp.int32, units.shape, 0)
-    mine = jnp.where(row == info_ref[1] + pl.program_id(0), units, 0.0)
-    mine = jnp.sum(mine, axis=0, keepdims=True)
-    queries = jnp.concatenate(
-        [mine[:, g * HEADDIM : (g + 1) * HEADDIM] for g in range(GROUP)], axis=0
-    )
-    scores = dot_t(queries.astype(jnp.bfloat16), kv_ref[:, :HEADDIM]) * SCALE
-    peak = jnp.max(scores, axis=1, keepdims=True)
-    weights = jnp.exp(scores - peak)
-    total = jnp.sum(weights, axis=1, keepdims=True)
-    mixed = dot(weights.astype(jnp.bfloat16), kv_ref[:, HEADDIM:])
-    out_ref[:, :HEADDIM] = (mixed / total).astype(jnp.bfloat16)
-    out_ref[:, HEADDIM:] = jnp.zeros_like(mixed).astype(jnp.bfloat16)
-
-
-def fresh_attention(info, queries, pairs, after=()):
+    for h in range(heads):
+        mine = jnp.where(row == info_ref[TP] * heads + h, units, 0.0)
+        mine = jnp.sum(mine, axis=0, keepdims=True)
+        queries = jnp.concatenate(
+            [mine[:, g * HEADDIM : (g + 1) * HEADDIM] for g in range(GROUP)], axis=0
+        )
+        start = 2 * h * HEADDIM
+        keys = kv_ref[:, start : start + HEADDIM]
+        scores = dot_t(queries.astype(jnp.bfloat16), keys) * SCALE
+        peak = jnp.max(scores, axis=1, keepdims=True)
+        weights = jnp.exp(scores - peak)
+        total = jnp.sum(weights, axis=1, keepdims=True)
+        mixed = dot(
+            weights.astype(jnp.bfloat16), kv_ref[:, start + HEADDIM : start + 2 * HEADDIM]
+        )
+        out_ref[:, start : start + HEADDIM] = (mixed / total).astype(jnp.bfloat16)
+        out_ref[:, start + HEADDIM : start + 2 * HEADDIM] = jnp.zeros(mixed.shape, jnp.bfloat16)
+
+
+def fresh_attention(info, queries, unit, pairs, after):
     length, width = pairs.shape
-    unit = (None, None) + queries.shape[2:]
     return pl.pallas_call(
         fresh_kernel,
         out_shape=jax.ShapeDtypeStruct((GROUP, width), jnp.bfloat16),
         grid_spec=pltpu.PrefetchScalarGridSpec(
             num_scalar_prefetch=1,
-            grid=(width // (2 * HEADDIM),),
+            grid=(1,),
             in_specs=[
-                pl.BlockSpec(unit, lambda h, info_ref: (info_ref[0], info_ref[2], 0, 0)),
-                pl.BlockSpec((length, 2 * HEADDIM), lambda h, info_ref: (0, h)),
+                pl.BlockSpec(
+                    (None, None) + queries.shape[2:],
+                    lambda n, info_ref: (info_ref[FIRST + order(info_ref)], unit, 0, 0),
+                ),
+                pl.BlockSpec((length, width), lambda n, info_ref: (0, 0)),
             ]
             + [IN_HBM] * len(after),
-            out_specs=pl.BlockSpec((GROUP, 2 * HEADDIM), lambda h, info_ref: (0, h)),
+            out_specs=pl.BlockSpec((GROUP, width), lambda n, info_ref: (0, 0)),
         ),
         compiler_params=pltpu.CompilerParams(vmem_limit_bytes=VMEM),
         cost_estimate=COST,
@@ -261,7 +293,7 @@
     heads = out_ref.shape[0] // GROUP
     for h in range(heads):
         result = unit_ref[:, 2 * h * HEADDIM : (2 * h + 1) * HEADDIM].astype(jnp.float32)
-        result = jnp.where(info_ref[1] != 0, 0.0, result)
+        result = jnp.where(on_prefill(info_ref), 0.0, result)
         out_ref[h * GROUP : (h + 1) * GROUP] = result
 
 
@@ -277,7 +309,7 @@
             in_specs=[
                 pl.BlockSpec(
                     (None, None, None, GROUP, width),
-                    lambda t, info_ref: (t, info_ref[0], units - 1, 0, 0),
+                    lambda t, info_ref: (t, source_of(info_ref, order(info_ref)), units - 1, 0, 0),
                 )
             ],
             out_specs=pl.BlockSpec((heads * GROUP, HEADDIM), lambda t, info_ref: (t, 0)),
@@ -288,8 +320,11 @@
     )(info, slots)
 
 
-def relay_handoff(pairs, source, inst_count):
+def relay_handoff(pairs, assignment, inst_count):
     half = inst_count // 2
+    decode_ids = jnp.arange(half, dtype=jnp.int32)
+    matches = assignment[None, :] == decode_ids[:, None]
+    source = jnp.sum(jnp.where(matches, decode_ids[None, :], 0), axis=1).astype(jnp.int32)
     moved = lax.all_to_all(pairs, "tp", split_axis=0, concat_axis=1, tiled=True)
     lanes = 1024 if moved.size % (inst_count * 1024) == 0 else HEADDIM
     pieces = moved.reshape(inst_count, -1, lanes)
@@ -304,17 +339,17 @@
 
 UNIT = 8
 PAIRS = 4
-PREFILL, DECODE = 1, 0
-
-
-def copy_kernel(plan, side, counts, prefetch_ref, *refs):
+PREFILL, DECODE = True, False
+
+
+def copy_kernel(plan, side, counts, info_ref, *refs):
     inputs, marks, outputs = counts
     sources, targets, sems = refs[:inputs], refs[inputs + marks : inputs + marks + outputs], refs[-1]
 
-    @pl.when(prefetch_ref[2] == side)
+    @pl.when(on_prefill(info_ref) == side)
     def _():
         started = []
-        for source, target in plan(prefetch_ref, sources, targets):
+        for source, target in plan(info_ref, sources, targets):
             started.append(pltpu.make_async_copy(source, target, sems.at[len(started)]))
         for copy in started:
             copy.start()
@@ -322,7 +357,7 @@
             copy.wait()
 
 
-def copies(plan, number, prefetch, operands, shapes, name, after=(), inside=True, side=PREFILL):
+def copies(plan, number, info, operands, shapes, name, after=(), inside=True, side=PREFILL):
     place = IN_VMEM if inside else ANYWHERE
     return pl.pallas_call(
         functools.partial(copy_kernel, plan, side, (len(operands), len(after), len(shapes))),
@@ -337,19 +372,20 @@
         compiler_params=pltpu.CompilerParams(vmem_limit_bytes=MEDIUM if inside else SMALL),
         cost_estimate=COST,
         name=name,
-    )(prefetch, *operands, *after)
-
-
-def relay_slots_kernel(far, prefetch_ref, keep_ref, recv_ref, fresh_ref, out_ref, mark_ref, sems, fresh_sems):
+    )(info, *operands, *after)
+
+
+def relay_slots_kernel(far, info_ref, keep_ref, recv_ref, fresh_ref, out_ref, sems, fresh_sems):
     half = 2 * PAIRS
 
-    @pl.when(prefetch_ref[2] == DECODE)
-    def _():
+    @pl.when(jnp.logical_not(on_prefill(info_ref)))
+    def _():
+        here = order(info_ref)
         waits = []
         for d in range(half):
-            pair = lax.div(prefetch_ref[3 + d], 2)
-            same = lax.rem(prefetch_ref[3 + d], 2) == prefetch_ref[1]
-            shift = lax.rem(prefetch_ref[0] + PAIRS - pair, PAIRS)
+            source = source_of(info_ref, d)
+            same = lax.rem(source, 2) == lax.rem(here, 2)
+            shift = lax.rem(lax.div(here, 2) + PAIRS - lax.div(source, 2), PAIRS)
             for tau in range(2):
                 slot = tau * half + d
                 target = out_ref.at[slot, pl.ds(0, far)]
@@ -364,19 +400,19 @@
             copy.wait()
 
 
-def rows_kernel(near, far, prefetch_ref, slots_ref, *refs):
+def rows_kernel(near, far, info_ref, slots_ref, *refs):
     *parts, out_ref, zero_ref, sems = refs
     half = 2 * PAIRS
     width = slots_ref.shape[-1]
     near_all = near * half
 
-    @pl.when(prefetch_ref[2] == 0)
+    @pl.when(jnp.logical_not(on_prefill(info_ref)))
     def _():
         waits = []
         for t in range(2):
             columns = pl.ds(t * width, width)
             for s, part in enumerate(parts):
-                pair = lax.rem(prefetch_ref[0] + PAIRS - s, PAIRS)
+                pair = lax.rem(lax.div(order(info_ref), 2) + PAIRS - s, PAIRS)
                 target = out_ref.at[pl.ds(pair * 2 * near, 2 * near), :, columns]
                 waits.append(pltpu.make_async_copy(part.at[t], target, sems.at[len(waits)]))
             for i in range(half):
@@ -388,7 +424,7 @@
         for copy in waits:
             copy.wait()
 
-    @pl.when(prefetch_ref[2] != 0)
+    @pl.when(on_prefill(info_ref))
     def _():
         zero_ref[...] = jnp.zeros_like(zero_ref)
         size = zero_ref.shape[0]
@@ -402,16 +438,13 @@
             copy.wait()
 
 
-def two_way_handoff(pairs, source, flag, always, arrival_query, fresh_of, results_of, prompt_part, extra):
+def two_way_handoff(pairs, info, always, arrival_query, fresh_of, results_of, prompt_part, extra):
     half = 2 * PAIRS
     rows, width = pairs.shape
     units = rows // (2 * UNIT)
     far_all = -(-units * 3 // (5 * half)) * half
     near_all = units - far_all
     near, far = near_all // half, far_all // half
-    inst = lax.axis_index("inst")
-    pair, side = lax.div(lax.rem(inst, half), 2), lax.rem(inst, 2)
-    prefetch = jnp.concatenate([jnp.stack([pair, side, flag[0]]), source])
     block = (UNIT, width)
     by_unit = pairs.reshape((rows // UNIT,) + block)
     groups = [[base + 2 * i + tau for tau in range(2) for i in range(half)] for base in (0, 2 * half)]
@@ -420,7 +453,7 @@
         hops = [
             (2 * p + k, half + 2 * ((p + s) % PAIRS) + k) for p in range(PAIRS) for k in range(2)
         ]
-        return lax.ppermute(array, "inst", hops + [(there, here) for here, there in hops])
+        return lax.ppermute(array, "inst", hops)
 
     def beside(array, base):
         return lax.ppermute(array, "inst", [(base + i, base + (i ^ 1)) for i in range(half)])
@@ -433,7 +466,7 @@
     def cut(pre, sources, targets):
         plan = []
         for s in range(PAIRS):
-            start = near_all + lax.rem(pre[0] + s, PAIRS) * (2 * far)
+            start = near_all + lax.rem(lax.div(order(pre), 2) + s, PAIRS) * (2 * far)
             for tau in range(2):
                 plan.append((sources[0].at[pl.ds(tau * units + start, 2 * far)], targets[s].at[tau]))
         return plan
@@ -451,20 +484,20 @@
     def for_neighbour(pre, sources, targets):
         plan = []
         for s in range(PAIRS):
-            receiver = lax.rem(pre[0] + s, PAIRS) * 2 + 1 - pre[1]
+            receiver = lax.rem(lax.div(order(pre), 2) + s, PAIRS) * 2 + 1 - lax.rem(order(pre), 2)
             for t in range(2):
-                origin = t * half + pre[3 + receiver]
+                origin = t * half + source_of(pre, receiver)
                 plan.append((sources[0].at[origin, pl.ds(0, near)], targets[0].at[s, t]))
         return plan
 
     def for_receivers(pre, sources, targets):
         plan = []
         for s in range(PAIRS):
-            receiver = lax.rem(pre[0] + s, PAIRS) * 2 + pre[1]
+            receiver = lax.rem(lax.div(order(pre), 2) + s, PAIRS) * 2 + lax.rem(order(pre), 2)
             for t in range(2):
-                origin = t * half + pre[3 + receiver]
-                mine = targets[s].at[t, pl.ds(pre[1] * near, near)]
-                other = targets[s].at[t, pl.ds((1 - pre[1]) * near, near)]
+                origin = t * half + source_of(pre, receiver)
+                mine = targets[s].at[t, pl.ds(lax.rem(order(pre), 2) * near, near)]
+                other = targets[s].at[t, pl.ds((1 - lax.rem(order(pre), 2)) * near, near)]
                 plan.append((sources[0].at[origin, pl.ds(0, near)], mine))
                 plan.append((sources[1].at[s, t], other))
         return plan
@@ -473,8 +506,8 @@
         plan = []
         for s in range(PAIRS):
             for tau in range(2):
-                mine = sources[s].at[tau, pl.ds(pre[1] * far, far)]
-                other = sources[s].at[tau, pl.ds((1 - pre[1]) * far, far)]
+                mine = sources[s].at[tau, pl.ds(lax.rem(order(pre), 2) * far, far)]
+                other = sources[s].at[tau, pl.ds((1 - lax.rem(order(pre), 2)) * far, far)]
                 plan.append((mine, targets[0].at[s, tau]))
                 plan.append((other, targets[1].at[s, tau]))
         return plan
@@ -482,56 +515,56 @@
     near_shape = (2, 2 * near) + block
 
     def first_stage(by_unit, asked):
-        spread, mark = copies(
+        slots, _ = copies(
             near_slots,
             8 * PAIRS,
-            prefetch,
+            info,
             [by_unit, asked.reshape(block)],
             [(2 * half, near + 1) + block],
             "near_slots",
         )
-        spread = spread_out(spread)
-        part, mark = extra[0]([mark])
-        prompt, mark = prompt_part(0, None, [mark])
-        more, mark = extra[1](part, [mark])
-        outgoing, mark = copies(
-            for_neighbour,
-            2 * PAIRS,
-            prefetch,
-            [spread],
-            [(PAIRS, 2, near) + block],
-            "for_neighbour",
-            [mark],
+        prompt, mark = prompt_part(0, None, [slots])
+        spread = spread_out(slots)
+        fresh = fresh_of(spread, near, [mark])
+        outgoing, _ = copies(
+            for_neighbour, 2 * PAIRS, info, [spread], [(PAIRS, 2, near) + block], "for_neighbour", [fresh]
         )
         incoming = beside(outgoing, 0)
-        *near_parts, mark = copies(
-            for_receivers, 4 * PAIRS, prefetch, [spread, incoming], [near_shape] * PAIRS, "for_receivers"
-        )
-        return *near_parts, prompt, spread, more
-
-    def second_stage(prompt, spread, *far_here):
-        fresh = fresh_of(spread, near)
-        keep, give, mark = copies(
-            split, 4 * PAIRS, prefetch, list(far_here), [(PAIRS, 2, far) + block] * 2, "split_relays", [fresh], side=DECODE
+        *near_parts, _ = copies(
+            for_receivers, 4 * PAIRS, info, [spread, incoming], [near_shape] * PAIRS, "for_receivers"
+        )
+        return *near_parts, prompt, fresh
+
+    def second_stage(prompt, fresh, *far_here):
+        keep, give, _ = copies(
+            split,
+            4 * PAIRS,
+            info,
+            list(far_here),
+            [(PAIRS, 2, far) + block] * 2,
+            "split_relays",
+            side=DECODE,
         )
         taken = beside(give, half)
-        slots, mark = pl.pallas_call(
+        slots = pl.pallas_call(
             functools.partial(relay_slots_kernel, far),
-            out_shape=(jax.ShapeDtypeStruct((2 * half, far + 1) + block, jnp.bfloat16), MARK),
+            out_shape=jax.ShapeDtypeStruct((2 * half, far + 1) + block, jnp.bfloat16),
             grid_spec=pltpu.PrefetchScalarGridSpec(
                 num_scalar_prefetch=1,
                 grid=(1,),
                 in_specs=[IN_VMEM] * 3,
-                out_specs=(ANYWHERE, IN_HBM),
+                out_specs=ANYWHERE,
                 scratch_shapes=[pltpu.SemaphoreType.DMA((2 * half,))] * 2,
             ),
             compiler_params=pltpu.CompilerParams(vmem_limit_bytes=MEDIUM),
             cost_estimate=COST,
             name="relay_slots",
-        )(prefetch, keep, taken, fresh)
+        )(info, keep, taken, fresh)
+        parts, mark = extra[0]([slots])
         slots = spread_out(slots)
         prompt, mark = prompt_part(1, prompt, [mark])
-        return prompt, slots, results_of(slots.reshape((2, half, far + 1) + block))
+        more, _ = extra[1](parts, [mark])
+        return prompt, slots, results_of(slots.reshape((2, half, far + 1) + block)), more
 
     def staged(stage, *operands):
         def never(*operands):
@@ -542,12 +575,12 @@
 
     asked = lax.ppermute(arrival_query, "inst", [(i + half, i) for i in range(half)])
     *far_parts, _ = copies(
-        cut, 2 * PAIRS, prefetch, [by_unit], [(2, 2 * far) + block] * PAIRS, "cut_far", inside=False
+        cut, 2 * PAIRS, info, [by_unit], [(2, 2 * far) + block] * PAIRS, "cut_far", inside=False
     )
     far_here = [crossing(part, s) for s, part in enumerate(far_parts)]
-    *near_parts, prompt, spread, more = staged(first_stage, by_unit, asked)
+    *near_parts, prompt, fresh = staged(first_stage, by_unit, asked)
     near_here = [crossing(part, s) for s, part in enumerate(near_parts)]
-    prompt, slots, results = staged(second_stage, prompt, spread, *far_here)
+    prompt, slots, results, more = staged(second_stage, prompt, fresh, *far_here)
     handed = pl.pallas_call(
         functools.partial(rows_kernel, near, far),
         out_shape=jax.ShapeDtypeStruct((units, UNIT, 2 * width), jnp.bfloat16),
@@ -564,7 +597,7 @@
         compiler_params=pltpu.CompilerParams(vmem_limit_bytes=MEDIUM),
         cost_estimate=COST,
         name="rows",
-    )(prefetch, slots, *near_here)
+    )(info, slots, *near_here)
     return handed.reshape(rows // 2, 2 * width), results, prompt, more
 
 
@@ -583,17 +616,13 @@
     half = inst_count // 2
     inst = lax.axis_index("inst")
     tp_index = lax.axis_index("tp")
-    is_prefill = inst < half
-    flag = is_prefill.astype(jnp.int32).reshape(1)
+    info = jnp.concatenate([jnp.stack([inst, tp_index]), assignment])
     groups = [list(range(half)), list(range(half, inst_count))]
-    decode_ids = jnp.arange(half, dtype=jnp.int32)
-    matches = assignment[None, :] == decode_ids[:, None]
-    source = jnp.sum(jnp.where(matches, decode_ids[None, :], 0), axis=1).astype(jnp.int32)
+
     rows = decode_query.shape[0]
     pages, page_len = cache_pool.shape[0], cache_pool.shape[1]
     by_token = cache_pool.reshape(pages * page_len, -1)
     by_head = decode_query.reshape(rows, QHEADS, HEADDIM)
-    info = jnp.stack([flag[0], tp_index])
 
     def cached(after=()):
         part, mark = cache_attention(info, page_table, lengths, by_head, by_token, page_len, after)
@@ -606,28 +635,24 @@
         if tp_count == 2:
             here, there = parts
             parts = jnp.where(tp_index == 0, here, there), jnp.where(tp_index == 0, there, here)
-        out, mark = combine_parts(flag, parts, rows, after)
+        out, mark = combine_parts(info, parts, rows, after)
         return out.reshape(rows, QHEADS * HEADDIM), mark
 
     heads = GROUP // 2
     steps = prompt_query.shape[1] // (heads * HEADDIM)
     kv_here = prompt_pairs.shape[1] // (2 * HEADDIM)
-    width = kv_here * GROUP * HEADDIM
-    from_inst = lax.dynamic_index_in_dim(source, lax.rem(inst, half), 0, False)
-    target = lax.dynamic_index_in_dim(assignment, lax.rem(inst, half), 0, False)
-
-    def fresh_of(queries, unit):
-        info = jnp.stack([target, tp_index * kv_here, jnp.int32(unit)])
-        fresh = fresh_attention(info, queries, prompt_pairs)
+
+    def fresh_of(queries, unit, after=()):
+        fresh = fresh_attention(info, queries, unit, prompt_pairs, after)
         return lax.ppermute(fresh, "inst", [(i, i + half) for i in range(half)])
 
     def results_of(slots):
-        found = arrival_results(jnp.stack([from_inst, flag[0]]), slots)
+        found = arrival_results(info, slots)
         return found.astype(jnp.bfloat16).reshape(1, QHEADS * HEADDIM)
 
     def prompt_part(first, last, earlier, after=()):
         return prompt_attention(
-            flag, prompt_query, prompt_pairs, first, last - first, heads, earlier, after
+            info, prompt_query, prompt_pairs, first, last - first, heads, earlier, after
         )
 
     row_units = prompt_pairs.shape[0] // (2 * UNIT)
@@ -635,8 +660,7 @@
         cuts = (0, 3, 8)
         handed, arrival_out, prefill_out, decode_out = two_way_handoff(
             prompt_pairs,
-            source,
-            flag,
+            info,
             assignment[0] >= 0,
             arrival_query,
             fresh_of,
@@ -645,7 +669,7 @@
             (cached, combined),
         )
     else:
-        handed = relay_handoff(prompt_pairs, source, inst_count)
+        handed = relay_handoff(prompt_pairs, assignment, inst_count)
         sent = lax.ppermute(arrival_query, "inst", [(i + half, i) for i in range(half)])
         every = lax.all_gather(sent, "inst", axis=0, tiled=True, axis_index_groups=groups)
         fresh = fresh_of(every.reshape(half, 1, KVHEADS, GROUP * HEADDIM), 0)

time: 130 us -> 106 us (0.82)
  the two profiles are of different devices: /device:TPU:16 before, /device:TPU:0 now
where the time goes in v3:
time: 106 us; the launch traced here: 104 us
  Pallas kernels  47.8 us (45%)
  starting transfers between devices  38.8 us (37%)
  waiting for transfers between devices  11.3 us (11%)
  local copies, waits for them, and re-layouts  3.14 us (3%)
  other arithmetic  1.66 us (2%)
  between operations  1.47 us (1%)
    pallas_call x2, Pallas kernels, prompt_attention(): pl.pallas_call(functools.partial(prompt_kernel, heads), out_shape=(jax.Sh...  24 us
    ppermute x8, starting transfers between devices, crossing(): return lax.ppermute(array, 'inst', hops)  20.3 us
    pallas_call x5, Pallas kernels, copies(): pl.pallas_call(functools.partial(copy_kernel, plan, side, (len(operands),...  9.34 us
    all_to_all x2, starting transfers between devices, spread_out(): lax.all_to_all(array, ('inst', 'tp'), 0, 0, axis_index_groups=groups, til...  8.6 us
    ppermute x1, waiting for transfers between devices, two_way_handoff(): lax.ppermute(arrival_query, 'inst', [(i + half, i) for i in range(half)])  4.97 us
    pallas_call x1, Pallas kernels, combine_parts(): pl.pallas_call(functools.partial(combine_kernel, len(parts)), out_shape=(...  4.88 us
    ppermute x1, starting transfers between devices, fresh_of(): return lax.ppermute(fresh, 'inst', [(i, i + half) for i in range(half)])  4.23 us
    all_to_all x2, waiting for transfers between devices, spread_out(): lax.all_to_all(array, ('inst', 'tp'), 0, 0, axis_index_groups=groups, til...  3.7 us
  transfers between devices with their start and end apart: 15, of which 5 were waited for; matrix products, arithmetic and copies ran while one was open for 3% of the time, Pallas kernels for 41%

profile of v3, /device:TPU:0, one launch (start us, length us, event | category | flops | bytes accessed | tf_op | source)
XLA Modules:
  0.0 104.4 jit_solution(13406956577138169448)
XLA Ops:
  0.6 0.7 pad_add_fusion.info_ref
  1.4 1.8 %cut_far.1 = (bf16[2,6,8,1024]{3,2,1,0:T(8,128)(2,1)S(1)}, bf16[2,6,8,1024]{3,2,1,0:T(8,128)(2,1)S(1)}, bf16[2,6,8,1024]{3,2,1,0:T(8,128)(2,1)S(1)}, bf16[2,6,8,1024]{3,2,1,0:T(8,128)(2,1)S(1)}, f32[8,128]{1,0:T(8,128)}) custom-call(s32[10]{0:T(128)S(1)} %pad_add_fusion.info_ref, bf16[80,8,1024]{2,1,0:T(8,128)(2,1)} %bitcast.25), custom_call_target="tpu_custom_call" | custom-call | flops 1 | bytes 1 | tf_op jit(solution)/shard_map/cut_far/pallas_call | solution.py:362
  3.2 4.8 %collective-permute-start.5 = (bf16[2,6,8,1024]{3,2,1,0:T(8,128)(2,1)S(1)}, bf16[2,6,8,1024]{3,2,1,0:T(8,128)(2,1)S(1)}, u32[]{:S(2)}, u32[]{:S(2)}) collective-permute-start(bf16[2,6,8,1024]{3,2,1,0:T(8,128)(2,1)S(1)} %get-tuple-element.94), channel_id=1, source_target_pairs={{0,16},{2,18},{4,20},{6,22},{8,24},{10,26},{12,28},{14,30},{1,17},... | collective-permute-start | bytes 589832 | tf_op jit(solution)/shard_map/ppermute | solution.py:456
  8.0 2.9 %collective-permute-start.6 = (bf16[2,6,8,1024]{3,2,1,0:T(8,128)(2,1)S(1)}, bf16[2,6,8,1024]{3,2,1,0:T(8,128)(2,1)}, u32[]{:S(2)}, u32[]{:S(2)}) collective-permute-start(bf16[2,6,8,1024]{3,2,1,0:T(8,128)(2,1)S(1)} %get-tuple-element.95), channel_id=1, source_target_pairs={{0,20},{2,22},{4,24},{6,26},{8,28},{10,30},{12,16},{14,18},{1,21},... | collective-permute-start | bytes 589832 | tf_op jit(solution)/shard_map/ppermute | solution.py:456
  10.9 2.0 %collective-permute-start.7 = (bf16[2,6,8,1024]{3,2,1,0:T(8,128)(2,1)S(1)}, bf16[2,6,8,1024]{3,2,1,0:T(8,128)(2,1)}, u32[]{:S(2)}, u32[]{:S(2)}) collective-permute-start(bf16[2,6,8,1024]{3,2,1,0:T(8,128)(2,1)S(1)} %get-tuple-element.96), channel_id=1, source_target_pairs={{0,24},{2,26},{4,28},{6,30},{8,16},{10,18},{12,20},{14,22},{1,25},... | collective-permute-start | bytes 589832 | tf_op jit(solution)/shard_map/ppermute | solution.py:456
  12.8 1.9 %collective-permute-start.8 = (bf16[2,6,8,1024]{3,2,1,0:T(8,128)(2,1)S(1)}, bf16[2,6,8,1024]{3,2,1,0:T(8,128)(2,1)}, u32[]{:S(2)}, u32[]{:S(2)}) collective-permute-start(bf16[2,6,8,1024]{3,2,1,0:T(8,128)(2,1)S(1)} %get-tuple-element.97), channel_id=1, source_target_pairs={{0,28},{2,30},{4,16},{6,18},{8,20},{10,22},{12,24},{14,26},{1,29},... | collective-permute-start | bytes 589832 | tf_op jit(solution)/shard_map/ppermute | solution.py:456
  14.8 1.3 %collective-permute-start.4 = (bf16[1,8192]{1,0:T(2,128)(2,1)}, bf16[1,8192]{1,0:T(2,128)(2,1)S(1)}, u32[]{:S(2)}, u32[]{:S(2)}) collective-permute-start(bf16[1,8192]{1,0:T(2,128)(2,1)} %param.15), channel_id=1, source_target_pairs={{16,0},{18,2},{20,4},{22,6},{24,8},{26,10},{28,12},{30,14},{17,1},... | collective-permute-start | bytes 49160 | tf_op jit(solution)/shard_map/ppermute | solution.py:576
  16.7 5.0 %collective-permute-done.4 = bf16[1,8192]{1,0:T(2,128)(2,1)S(1)} collective-permute-done((bf16[1,8192]{1,0:T(2,128)(2,1)}, bf16[1,8192]{1,0:T(2,128)(2,1)S(1)}, u32[]{:S(2)}, u32[]{:S(2)}) %collective-permute-start.4) | collective-permute-done | bytes 16416 | tf_op jit(solution)/shard_map/ppermute | solution.py:576
  21.7 0.0 copy-start.7
  21.7 34.2 %conditional.2 = (bf16[2,4,8,1024]{3,2,1,0:T(8,128)(2,1)}, bf16[2,4,8,1024]{3,2,1,0:T(8,128)(2,1)}, bf16[2,4,8,1024]{3,2,1,0:T(8,128)(2,1)}, bf16[2,4,8,1024]{3,...) conditional(s32[]{:T(128)} %bitcast.3, () %tuple.24, (bf16[1,8192]{1,0:T(2,128)(2,1)S(1)}, ...), branch_computations={%region_0.0_spmd, %region_1.0_spmd} | conditional | flops 5 | bytes 8798431 | solution.py:574
  21.7 0.1 reduce
  21.8 3.0 %near_slots.1 = (bf16[16,3,8,1024]{3,2,1,0:T(8,128)(2,1)}, f32[8,128]{1,0:T(8,128)}) custom-call(s32[10]{0:T(128)S(1)} %get-tuple-element.41.info_ref, bf16[80,8,1024]{2,1,0:T(8,128)(2,1)} %bitcast.27, bf16[8,1024]{1,0:T(8,128)(2,1)S(1)} %reshape.30.refs_1_), custom_call_target="tpu_custom_call" | custom-call | flops 1 | bytes 1 | tf_op jit(solution)/shard_map/cond/branch_1_fun/near_slots/pallas_call | solution.py:362
  24.8 4.2 %all-to-all-start = ((bf16[16,3,8,1024]{3,2,1,0:T(8,128)(2,1)}), bf16[16,3,8,1024]{3,2,1,0:T(8,128)(2,1)S(1)}, u32[]{:S(2)}, u32[]{:S(2)}) async-start(bf16[16,3,8,1024]{3,2,1,0:T(8,128)(2,1)} %get-tuple-element.44.rest_0_), calls=%async_computation | async-start | bytes 1572864 | tf_op jit(solution)/shard_map/cond/branch_1_fun/all_to_all | solution.py:462
  29.1 9.7 %prompt_attention.2 = (bf16[640,4096]{1,0:T(8,128)(2,1)}, f32[8,128]{1,0:T(8,128)}) custom-call(s32[10]{0:T(128)S(1)} %get-tuple-element.41.info_ref, bf16[640,4096]{1,0:T(8,128)(2,1)} %get-tuple-element.46.q_ref, bf16[640,1024]{1,0:T(8,128)(2,1)} %get-tuple-element.45.kv_ref, bf16[16,3,8,1024]{3,2,1,0:T(8,128)(2,1)} %get-tuple-element.44.rest_0_), custom_call_target="tpu_custom_call" | custom-call | flops 1 | bytes 1 | tf_op jit(solution)/shard_map/cond/branch_1_fun/prompt_attention/pallas_call | solution.py:112
  38.7 3.7 %all-to-all-done.q_ref.refs_0_ = bf16[16,3,8,1024]{3,2,1,0:T(8,128)(2,1)S(1)} async-done(((bf16[16,3,8,1024]{3,2,1,0:T(8,128)(2,1)}), bf16[16,3,8,1024]{3,2,1,0:T(8,128)(2,1)S(1)}, u32[]{:S(2)}, u32[]{:S(2)}) %all-to-all-start) | async-done | bytes 786464 | tf_op jit(solution)/shard_map/cond/branch_1_fun/all_to_all | solution.py:462
  42.4 0.0 copy-done.1
  42.4 0.7 copy-done
  43.1 1.8 %fresh_attention.1 = bf16[8,1024]{1,0:T(8,128)(2,1)S(1)} custom-call(s32[10]{0:T(128)S(1)} %get-tuple-element.41.info_ref, bf16[16,3,8,1024]{3,2,1,0:T(8,128)(2,1)S(1)} %all-to-all-done.q_ref.refs_0_, bf16[640,1024]{1,0:T(8,128)(2,1)S(1)} %copy-done.1, f32[8,128]{1,0:T(8,128)S(1)} %copy-done), custom_call_target="tpu_custom_call" | custom-call | flops 1 | bytes 1 | tf_op jit(solution)/shard_map/cond/branch_1_fun/fresh_attention/pallas_call | solution.py:270
  44.9 4.2 %collective-permute-start = (bf16[8,1024]{1,0:T(8,128)(2,1)S(1)}, bf16[8,1024]{1,0:T(8,128)(2,1)}, u32[]{:S(2)}, u32[]{:S(2)}) collective-permute-start(bf16[8,1024]{1,0:T(8,128)(2,1)S(1)} %fresh_attention.1), channel_id=1, source_target_pairs={{0,16},{2,18},{4,20},{6,22},{8,24},{10,26},{12,28},{14,30},{1,17},... | collective-permute-start | bytes 49160 | tf_op jit(solution)/shard_map/cond/branch_1_fun/ppermute | solution.py:647
  49.2 0.8 collective-permute-done.refs_1_
  50.0 1.0 for_neighbour.1
  51.0 1.9 %collective-permute-start.1 = (bf16[4,2,2,8,1024]{4,3,2,1,0:T(8,128)(2,1)S(1)}, bf16[4,2,2,8,1024]{4,3,2,1,0:T(8,128)(2,1)S(1)}, u32[]{:S(2)}, u32[]{:S(2)}) collective-permute-start(bf16[4,2,2,8,1024]{4,3,2,1,0:T(8,128)(2,1)S(1)} %get-tuple-element.48), channel_id=1, source_target_pairs={{0,2},{2,0},{4,6},{6,4},{8,10},{10,8},{12,14},{14,12},{1,3},{3,1},... | collective-permute-start | bytes 786440 | tf_op jit(solution)/shard_map/cond/branch_1_fun/ppermute | solution.py:459
  52.9 1.5 %collective-permute-done.1.refs_1_ = bf16[4,2,2,8,1024]{4,3,2,1,0:T(8,128)(2,1)S(1)} collective-permute-done((bf16[4,2,2,8,1024]{4,3,2,1,0:T(8,128)(2,1)S(1)}, bf16[4,2,2,8,1024]{4,3,2,1,0:T(8,128)(2,1)S(1)}, u32[]{:S(2)}, u32[]{:S(2)}) %collective-permute-start.1) | collective-permute-done | bytes 262176 | tf_op jit(solution)/shard_map/cond/branch_1_fun/ppermute | solution.py:459
  54.4 1.5 %for_receivers.1 = (bf16[2,4,8,1024]{3,2,1,0:T(8,128)(2,1)}, bf16[2,4,8,1024]{3,2,1,0:T(8,128)(2,1)}, bf16[2,4,8,1024]{3,2,1,0:T(8,128)(2,1)}, bf16[2,4,8,1024]{3,2,1,0:T(8,128)(2,1)S(1)}, f32[8,128]{1,0:T(8,128)}) custom-call(s32[10]{0:T(128)S(1)} %get-tuple-element.41.info_ref, bf16[16,3,8,1024]{3,2,1,0:T(8,128)(2,1)S(1)} %all-to-all-done.q_ref.refs_0_, ...), custom_call_target="tpu_custom_call" | custom-call | flops 1 | bytes 1 | tf_op jit(solution)/shard_map/cond/branch_1_fun/for_receivers/pallas_call | solution.py:362
  55.9 1.3 %collective-permute-start.9 = (bf16[2,4,8,1024]{3,2,1,0:T(8,128)(2,1)}, bf16[2,4,8,1024]{3,2,1,0:T(8,128)(2,1)S(1)}, u32[]{:S(2)}, u32[]{:S(2)}) collective-permute-start(bf16[2,4,8,1024]{3,2,1,0:T(8,128)(2,1)} %get-tuple-element.101), channel_id=1, source_target_pairs={{0,16},{2,18},{4,20},{6,22},{8,24},{10,26},{12,28},{14,30},{1,17},... | collective-permute-start | bytes 393224 | tf_op jit(solution)/shard_map/ppermute | solution.py:456
  57.2 0.0 collective-permute-done.5
  57.2 1.3 %collective-permute-start.10 = (bf16[2,4,8,1024]{3,2,1,0:T(8,128)(2,1)}, bf16[2,4,8,1024]{3,2,1,0:T(8,128)(2,1)S(1)}, u32[]{:S(2)}, u32[]{:S(2)}) collective-permute-start(bf16[2,4,8,1024]{3,2,1,0:T(8,128)(2,1)} %get-tuple-element.102), channel_id=1, source_target_pairs={{0,20},{2,22},{4,24},{6,26},{8,28},{10,30},{12,16},{14,18},{1,21},... | collective-permute-start | bytes 393224 | tf_op jit(solution)/shard_map/ppermute | solution.py:456
  58.6 0.0 collective-permute-done.6
  58.6 2.9 %collective-permute-start.11 = (bf16[2,4,8,1024]{3,2,1,0:T(8,128)(2,1)}, bf16[2,4,8,1024]{3,2,1,0:T(8,128)(2,1)S(1)}, u32[]{:S(2)}, u32[]{:S(2)}) collective-permute-start(bf16[2,4,8,1024]{3,2,1,0:T(8,128)(2,1)} %get-tuple-element.103), channel_id=1, source_target_pairs={{0,24},{2,26},{4,28},{6,30},{8,16},{10,18},{12,20},{14,22},{1,25},... | collective-permute-start | bytes 393224 | tf_op jit(solution)/shard_map/ppermute | solution.py:456
  61.5 0.0 collective-permute-done.7
  61.5 3.2 %collective-permute-start.12 = (bf16[2,4,8,1024]{3,2,1,0:T(8,128)(2,1)S(1)}, bf16[2,4,8,1024]{3,2,1,0:T(8,128)(2,1)S(1)}, u32[]{:S(2)}, u32[]{:S(2)}) collective-permute-start(bf16[2,4,8,1024]{3,2,1,0:T(8,128)(2,1)S(1)} %get-tuple-element.104), channel_id=1, source_target_pairs={{0,28},{2,30},{4,16},{6,18},{8,20},{10,22},{12,24},{14,26},{1,29},... | collective-permute-start | bytes 393224 | tf_op jit(solution)/shard_map/ppermute | solution.py:456
  64.7 0.0 collective-permute-done.8
  64.8 0.0 copy-done.7
  64.8 0.0 copy-done.8
  64.8 36.5 %conditional.3 = (bf16[640,4096]{1,0:T(8,128)(2,1)}, bf16[16,4,8,1024]{3,2,1,0:T(8,128)(2,1)}, bf16[1,8192]{1,0:T(2,128)(2,1)S(1)}, bf16[4,8192]{1,0:T(4,128)(2,1)S(1)}) conditional(s32[]{:T(128)} %bitcast.3, bf16[640,4096]{1,0:T(8,128)(2,1)} %get-tuple-element.93, (bf16[4,8192]{1,0:T(4,128)(2,1)}, bf16[5,64,2048]{2,1,0:T(8,128)(2,1)}, ...), branch_computations={%region_2.0_spmd, %region_3.4_spmd} | conditional | flops 139271 | bytes 18694388 | solution.py:574
  64.8 0.0 copy-start.3
  64.8 0.0 copy-start.2
  64.8 2.0 %split_relays.1 = (bf16[4,2,3,8,1024]{4,3,2,1,0:T(8,128)(2,1)S(1)}, bf16[4,2,3,8,1024]{4,3,2,1,0:T(8,128)(2,1)S(1)}, f32[8,128]{1,0:T(8,128)}) custom-call(s32[10]{0:T(128)S(1)} %get-tuple-element.54.info_ref, bf16[2,6,8,1024]{3,2,1,0:T(8,128)(2,1)S(1)} %get-tuple-element.62.refs_0_, bf16[2,6,8,1024]{3,2,1,0:T(8,128)(2,1)} %get-tuple-element.63.refs_1_, ...), custom_call_target="tpu_custom_call" | custom-call | flops 1 | bytes 1 | tf_op jit(solution)/shard_map/cond/branch_1_fun/split_relays/pallas_call | solution.py:362
  66.8 0.7 collective-permute-start.2
  67.5 0.0 collective-permute-done.2.recv_ref
  67.6 1.5 %relay_slots.1.rest_0_ = bf16[16,4,8,1024]{3,2,1,0:T(8,128)(2,1)} custom-call(s32[10]{0:T(128)S(1)} %get-tuple-element.54.info_ref, bf16[4,2,3,8,1024]{4,3,2,1,0:T(8,128)(2,1)S(1)} %get-tuple-element.66.keep_ref, bf16[4,2,3,8,1024]{4,3,2,1,0:T(8,128)(2,1)S(1)} %collective-permute-done.2.recv_ref, bf16[8,1024]{1,0:T(8,128)(2,1)} %get-tuple-element.68.fresh_ref), custom_call_target="tpu_custom_call" | custom-call | flops 1 | bytes 1 | tf_op jit(solution)/shard_map/cond/branch_1_fun/relay_slots/pallas_call | solution.py:549
  69.1 4.3 %all-to-all-start.1 = ((bf16[16,4,8,1024]{3,2,1,0:T(8,128)(2,1)}), bf16[16,4,8,1024]{3,2,1,0:T(8,128)(2,1)}, u32[]{:S(2)}, u32[]{:S(2)}) async-start(bf16[16,4,8,1024]{3,2,1,0:T(8,128)(2,1)} %relay_slots.1.rest_0_), calls=%async_computation.1 | async-start | bytes 2097152 | tf_op jit(solution)/shard_map/cond/branch_1_fun/all_to_all | solution.py:462
  73.5 1.5 %copy.24 = bf16[1,4,64,128]{3,2,1,0:T(8,128)(2,1)} copy(bf16[1,4,64,128]{3,1,2,0:T(4,128)(2,1)} %bitcast.32) | data formatting | bytes 131072 | tf_op jit(solution)/shard_map/cond
  74.9 0.0 copy-done.3
  74.9 1.9 %cache_attention.1 = (f32[8,32,256]{2,1,0:T(8,128)}, f32[8,128]{1,0:T(8,128)}) custom-call(s32[10]{0:T(128)S(1)} %get-tuple-element.54.info_ref, s32[4,8]{1,0:T(4,128)S(1)} %get-tuple-element.113.table_ref, s32[4]{0:T(128)S(1)} %get-tuple-element.114.lengths_ref, bf16[4,64,128]{2,1,0:T(8,128)(2,1)} %bitcast.30, bf16[320,2048]{1,0:T(8,128)(2,1)S(1)} %bitcast.28, ...), custom_call_target="tpu_custom_call" | custom-call | flops 1 | bytes 1 | tf_op jit(solution)/shard_map/cond/branch_1_fun/cache_attention/pallas_call | solution.py:174
  76.8 1.8 %collective-permute-start.3 = (f32[1,8,32,256]{3,2,1,0:T(8,128)}, f32[1,8,32,256]{3,2,1,0:T(8,128)S(1)}, u32[]{:S(2)}, u32[]{:S(2)}) collective-permute-start(f32[1,8,32,256]{3,2,1,0:T(8,128)} %bitcast.31), channel_id=1, source_target_pairs={{0,1},{1,0},{2,3},{3,2},{4,5},{5,4},{6,7},{7,6},{8,9},{9,8},{10,11... | collective-permute-start | bytes 786440 | tf_op jit(solution)/shard_map/cond/branch_1_fun/ppermute | solution.py:631
  78.6 0.0 copy-done.2
  78.6 14.4 %prompt_attention.3 = (bf16[640,4096]{1,0:T(8,128)(2,1)}, f32[8,128]{1,0:T(8,128)}) custom-call(s32[10]{0:T(128)S(1)} %get-tuple-element.54.info_ref, bf16[640,4096]{1,0:T(8,128)(2,1)} %get-tuple-element.55.q_ref, bf16[640,1024]{1,0:T(8,128)(2,1)S(1)} %copy-done.2, bf16[640,4096]{1,0:T(8,128)(2,1)} %get-tuple-element.57.rest_0_, ...), custom_call_target="tpu_custom_call", output_to_operand_aliasing={{0}: (3, {})} | custom-call | flops 1 | bytes 1 | tf_op jit(solution)/shard_map/cond/branch_1_fun/prompt_attention/pallas_call | solution.py:112
  93.0 0.3 collective-permute-done.3
  93.3 0.0 copy-done.4
  93.3 0.8 broadcast_select_fusion
  94.1 4.9 %combine_parts.1 = (bf16[4,64,128]{2,1,0:T(8,128)(2,1)}, f32[8,128]{1,0:T(8,128)}) custom-call(s32[10]{0:T(128)S(1)} %get-tuple-element.54.info_ref, f32[1,8,32,256]{3,2,1,0:T(8,128)} %get-tuple-element.116.refs_0_, f32[1,8,32,256]{3,2,1,0:T(8,128)} %get-tuple-element.115.refs_1_, f32[8,128]{1,0:T(8,128)} %get-tuple-element.73.refs_2_), custom_call_target="tpu_custom_call" | custom-call | flops 1 | bytes 1 | tf_op jit(solution)/shard_map/cond/branch_1_fun/combine_parts/pallas_call | solution.py:219
  99.0 0.9 copy.23
  99.9 0.0 all-to-all-done.1
  99.9 1.3 %arrival_results.1 = f32[64,128]{1,0:T(8,128)S(1)} custom-call(s32[10]{0:T(128)S(1)} %get-tuple-element.54.info_ref, bf16[2,8,4,8,1024]{4,3,2,1,0:T(8,128)(2,1)} %bitcast.1.unit_ref), custom_call_target="tpu_custom_call" | custom-call | flops 1 | bytes 1 | tf_op jit(solution)/shard_map/cond/branch_1_fun/arrival_results/pallas_call | solution.py:303
  101.3 0.0 copy-start.5
  101.3 0.0 copy-start.6
  101.3 0.0 collective-permute-done.9.refs_0_
  101.3 0.0 collective-permute-done.10.refs_1_
  101.3 0.0 collective-permute-done.11.refs_2_
  101.3 0.0 collective-permute-done.12.refs_3_
  101.3 3.0 %rows.1 = bf16[40,8,2048]{2,1,0:T(8,128)(2,1)} custom-call(s32[10]{0:T(128)S(1)} %pad_add_fusion.info_ref, bf16[16,4,8,1024]{3,2,1,0:T(8,128)(2,1)} %get-tuple-element.100.slots_ref, bf16[2,4,8,1024]{3,2,1,0:T(8,128)(2,1)S(1)} %collective-permute-done.9.refs_0_, bf16[2,4,8,1024]{3,2,1,0:T(8,128)(2,1)S(1)} %collective-permute-done.10.refs_1_, ...), custom_call_target="tpu_custom_call" | custom-call | flops 1 | bytes 1 | tf_op jit(solution)/shard_map/rows/pallas_call | solution.py:584
  104.4 0.0 copy-done.5
  104.4 0.0 copy-done.6
  (7 shorter events, 0.1 us)
Async XLA Ops:
  3.2 54.0 %collective-permute-start.5 = (bf16[2,6,8,1024]{3,2,1,0:T(8,128)(2,1)S(1)}, bf16[2,6,8,1024]{3,2,1,0:T(8,128)(2,1)S(1)}, u32[]{:S(2)}, u32[]{:S(2)}) collective-permute-start(bf16[2,6,8,1024]{3,2,1,0:T(8,128)(2,1)S(1)} %get-tuple-element.94), channel_id=1, source_target_pairs={{0,16},{2,18},{4,20},{6,22},{8,24},{10,26},{12,28},{14,30},{1,17},... | collective-permute-start | bytes 589832 | tf_op jit(solution)/shard_map/ppermute | solution.py:456
  8.0 50.6 %collective-permute-start.6 = (bf16[2,6,8,1024]{3,2,1,0:T(8,128)(2,1)S(1)}, bf16[2,6,8,1024]{3,2,1,0:T(8,128)(2,1)}, u32[]{:S(2)}, u32[]{:S(2)}) collective-permute-start(bf16[2,6,8,1024]{3,2,1,0:T(8,128)(2,1)S(1)} %get-tuple-element.95), channel_id=1, source_target_pairs={{0,20},{2,22},{4,24},{6,26},{8,28},{10,30},{12,16},{14,18},{1,21},... | collective-permute-start | bytes 589832 | tf_op jit(solution)/shard_map/ppermute | solution.py:456
  10.9 50.6 %collective-permute-start.7 = (bf16[2,6,8,1024]{3,2,1,0:T(8,128)(2,1)S(1)}, bf16[2,6,8,1024]{3,2,1,0:T(8,128)(2,1)}, u32[]{:S(2)}, u32[]{:S(2)}) collective-permute-start(bf16[2,6,8,1024]{3,2,1,0:T(8,128)(2,1)S(1)} %get-tuple-element.96), channel_id=1, source_target_pairs={{0,24},{2,26},{4,28},{6,30},{8,16},{10,18},{12,20},{14,22},{1,25},... | collective-permute-start | bytes 589832 | tf_op jit(solution)/shard_map/ppermute | solution.py:456
  12.8 51.9 %collective-permute-start.8 = (bf16[2,6,8,1024]{3,2,1,0:T(8,128)(2,1)S(1)}, bf16[2,6,8,1024]{3,2,1,0:T(8,128)(2,1)}, u32[]{:S(2)}, u32[]{:S(2)}) collective-permute-start(bf16[2,6,8,1024]{3,2,1,0:T(8,128)(2,1)S(1)} %get-tuple-element.97), channel_id=1, source_target_pairs={{0,28},{2,30},{4,16},{6,18},{8,20},{10,22},{12,24},{14,26},{1,29},... | collective-permute-start | bytes 589832 | tf_op jit(solution)/shard_map/ppermute | solution.py:456
  14.8 6.9 %collective-permute-start.4 = (bf16[1,8192]{1,0:T(2,128)(2,1)}, bf16[1,8192]{1,0:T(2,128)(2,1)S(1)}, u32[]{:S(2)}, u32[]{:S(2)}) collective-permute-start(bf16[1,8192]{1,0:T(2,128)(2,1)} %param.15), channel_id=1, source_target_pairs={{16,0},{18,2},{20,4},{22,6},{24,8},{26,10},{28,12},{30,14},{17,1},... | collective-permute-start | bytes 49160 | tf_op jit(solution)/shard_map/ppermute | solution.py:576
  21.7 43.0 %copy-start.7 = (s32[4,8]{1,0:T(4,128)S(1)}, s32[4,8]{1,0:T(4,128)}, u32[]{:S(2)}) copy-start(s32[4,8]{1,0:T(4,128)} %param.17) | copy-start | bytes 388
  21.7 43.1 %copy-start.8 = (s32[4]{0:T(128)S(1)}, s32[4]{0:T(128)}, u32[]{:S(2)}) copy-start(s32[4]{0:T(128)} %param.18) | copy-start | bytes 52
  21.7 20.7 %copy-start.1 = (bf16[640,1024]{1,0:T(8,128)(2,1)S(1)}, bf16[640,1024]{1,0:T(8,128)(2,1)}, u32[]{:S(2)}) copy-start(bf16[640,1024]{1,0:T(8,128)(2,1)} %get-tuple-element.45.kv_ref) | copy-start | bytes 3932164 | tf_op jit(solution)/shard_map/cond
  24.8 17.6 %all-to-all-start = ((bf16[16,3,8,1024]{3,2,1,0:T(8,128)(2,1)}), bf16[16,3,8,1024]{3,2,1,0:T(8,128)(2,1)S(1)}, u32[]{:S(2)}, u32[]{:S(2)}) async-start(bf16[16,3,8,1024]{3,2,1,0:T(8,128)(2,1)} %get-tuple-element.44.rest_0_), calls=%async_computation | async-start | bytes 1572864 | tf_op jit(solution)/shard_map/cond/branch_1_fun/all_to_all | solution.py:462
  42.4 0.7 copy-start
  44.9 5.1 %collective-permute-start = (bf16[8,1024]{1,0:T(8,128)(2,1)S(1)}, bf16[8,1024]{1,0:T(8,128)(2,1)}, u32[]{:S(2)}, u32[]{:S(2)}) collective-permute-start(bf16[8,1024]{1,0:T(8,128)(2,1)S(1)} %fresh_attention.1), channel_id=1, source_target_pairs={{0,16},{2,18},{4,20},{6,22},{8,24},{10,26},{12,28},{14,30},{1,17},... | collective-permute-start | bytes 49160 | tf_op jit(solution)/shard_map/cond/branch_1_fun/ppermute | solution.py:647
  51.0 3.4 %collective-permute-start.1 = (bf16[4,2,2,8,1024]{4,3,2,1,0:T(8,128)(2,1)S(1)}, bf16[4,2,2,8,1024]{4,3,2,1,0:T(8,128)(2,1)S(1)}, u32[]{:S(2)}, u32[]{:S(2)}) collective-permute-start(bf16[4,2,2,8,1024]{4,3,2,1,0:T(8,128)(2,1)S(1)} %get-tuple-element.48), channel_id=1, source_target_pairs={{0,2},{2,0},{4,6},{6,4},{8,10},{10,8},{12,14},{14,12},{1,3},{3,1},... | collective-permute-start | bytes 786440 | tf_op jit(solution)/shard_map/cond/branch_1_fun/ppermute | solution.py:459
  55.9 45.4 %collective-permute-start.9 = (bf16[2,4,8,1024]{3,2,1,0:T(8,128)(2,1)}, bf16[2,4,8,1024]{3,2,1,0:T(8,128)(2,1)S(1)}, u32[]{:S(2)}, u32[]{:S(2)}) collective-permute-start(bf16[2,4,8,1024]{3,2,1,0:T(8,128)(2,1)} %get-tuple-element.101), channel_id=1, source_target_pairs={{0,16},{2,18},{4,20},{6,22},{8,24},{10,26},{12,28},{14,30},{1,17},... | collective-permute-start | bytes 393224 | tf_op jit(solution)/shard_map/ppermute | solution.py:456
  57.2 44.1 %collective-permute-start.10 = (bf16[2,4,8,1024]{3,2,1,0:T(8,128)(2,1)}, bf16[2,4,8,1024]{3,2,1,0:T(8,128)(2,1)S(1)}, u32[]{:S(2)}, u32[]{:S(2)}) collective-permute-start(bf16[2,4,8,1024]{3,2,1,0:T(8,128)(2,1)} %get-tuple-element.102), channel_id=1, source_target_pairs={{0,20},{2,22},{4,24},{6,26},{8,28},{10,30},{12,16},{14,18},{1,21},... | collective-permute-start | bytes 393224 | tf_op jit(solution)/shard_map/ppermute | solution.py:456
  58.6 42.8 %collective-permute-start.11 = (bf16[2,4,8,1024]{3,2,1,0:T(8,128)(2,1)}, bf16[2,4,8,1024]{3,2,1,0:T(8,128)(2,1)S(1)}, u32[]{:S(2)}, u32[]{:S(2)}) collective-permute-start(bf16[2,4,8,1024]{3,2,1,0:T(8,128)(2,1)} %get-tuple-element.103), channel_id=1, source_target_pairs={{0,24},{2,26},{4,28},{6,30},{8,16},{10,18},{12,20},{14,22},{1,25},... | collective-permute-start | bytes 393224 | tf_op jit(solution)/shard_map/ppermute | solution.py:456
  61.5 39.8 %collective-permute-start.12 = (bf16[2,4,8,1024]{3,2,1,0:T(8,128)(2,1)S(1)}, bf16[2,4,8,1024]{3,2,1,0:T(8,128)(2,1)S(1)}, u32[]{:S(2)}, u32[]{:S(2)}) collective-permute-start(bf16[2,4,8,1024]{3,2,1,0:T(8,128)(2,1)S(1)} %get-tuple-element.104), channel_id=1, source_target_pairs={{0,28},{2,30},{4,16},{6,18},{8,20},{10,22},{12,24},{14,26},{1,29},... | collective-permute-start | bytes 393224 | tf_op jit(solution)/shard_map/ppermute | solution.py:456
  64.8 10.2 %copy-start.3 = (bf16[5,64,2048]{2,1,0:T(8,128)(2,1)S(1)}, bf16[5,64,2048]{2,1,0:T(8,128)(2,1)}, u32[]{:S(2)}) copy-start(bf16[5,64,2048]{2,1,0:T(8,128)(2,1)} %get-tuple-element.112) | copy-start | bytes 3932164 | tf_op jit(solution)/shard_map/cond
  64.8 13.8 %copy-start.2 = (bf16[640,1024]{1,0:T(8,128)(2,1)S(1)}, bf16[640,1024]{1,0:T(8,128)(2,1)}, u32[]{:S(2)}) copy-start(bf16[640,1024]{1,0:T(8,128)(2,1)} %get-tuple-element.56.kv_ref) | copy-start | bytes 3932164 | tf_op jit(solution)/shard_map/cond
  66.8 0.7 collective-permute-start.2
  69.1 30.8 %all-to-all-start.1 = ((bf16[16,4,8,1024]{3,2,1,0:T(8,128)(2,1)}), bf16[16,4,8,1024]{3,2,1,0:T(8,128)(2,1)}, u32[]{:S(2)}, u32[]{:S(2)}) async-start(bf16[16,4,8,1024]{3,2,1,0:T(8,128)(2,1)} %relay_slots.1.rest_0_), calls=%async_computation.1 | async-start | bytes 2097152 | tf_op jit(solution)/shard_map/cond/branch_1_fun/all_to_all | solution.py:462
  76.8 16.5 %collective-permute-start.3 = (f32[1,8,32,256]{3,2,1,0:T(8,128)}, f32[1,8,32,256]{3,2,1,0:T(8,128)S(1)}, u32[]{:S(2)}, u32[]{:S(2)}) collective-permute-start(f32[1,8,32,256]{3,2,1,0:T(8,128)} %bitcast.31), channel_id=1, source_target_pairs={{0,1},{1,0},{2,3},{3,2},{4,5},{5,4},{6,7},{7,6},{8,9},{9,8},{10,11... | collective-permute-start | bytes 786440 | tf_op jit(solution)/shard_map/cond/branch_1_fun/ppermute | solution.py:631
  78.6 14.7 %copy-start.4 = (f32[8,32,256]{2,1,0:T(8,128)S(1)}, f32[8,32,256]{2,1,0:T(8,128)}, u32[]{:S(2)}) copy-start(f32[8,32,256]{2,1,0:T(8,128)} %get-tuple-element.72) | copy-start | bytes 786436 | tf_op jit(solution)/shard_map/cond
  101.3 3.1 %copy-start.5 = (bf16[4,8192]{1,0:T(4,128)(2,1)}, bf16[4,8192]{1,0:T(4,128)(2,1)S(1)}, u32[]{:S(2)}) copy-start(bf16[4,8192]{1,0:T(4,128)(2,1)S(1)} %get-tuple-element.91) | copy-start | bytes 196612
  101.3 3.1 %copy-start.6 = (bf16[1,8192]{1,0:T(2,128)(2,1)}, bf16[1,8192]{1,0:T(2,128)(2,1)S(1)}, u32[]{:S(2)}) copy-start(bf16[1,8192]{1,0:T(2,128)(2,1)S(1)} %get-tuple-element.92) | copy-start | bytes 49156

commit v4 on v3

v4 whole, which is shorter than its diff:
```python
import functools

import jax
import jax.numpy as jnp
from jax import lax
from jax.experimental import pallas as pl
from jax.experimental.pallas import tpu as pltpu
from jax.sharding import PartitionSpec as P

QHEADS = 64
KVHEADS = 8
HEADDIM = 128
GROUP = QHEADS // KVHEADS
SCALE = HEADDIM ** (-0.5)
LOG2E = 1.4426950408889634
NEG_FILL = -1e30
TILE = 128
VMEM = 24 * 1024 * 1024
SMALL = 1024 * 1024
MEDIUM = 8 * 1024 * 1024
LARGE = 57 * 1024 * 1024
COST = pl.CostEstimate(flops=1, bytes_accessed=1, transcendentals=0)


INST, TP, FIRST = 0, 1, 2


def on_prefill(info):
    return info[INST] < info.shape[0] - FIRST


def order(info):
    half = info.shape[0] - FIRST
    return info[INST] - jnp.where(on_prefill(info), 0, half)


def source_of(info, receiver):
    half = info.shape[0] - FIRST
    found = jnp.int32(0)
    for p in range(half):
        found = jnp.where(info[FIRST + p] == receiver, p, found)
    return found


def dot_t(a, b):
    return lax.dot_general(a, b, (((1,), (1,)), ((), ())), preferred_element_type=jnp.float32)


def dot(a, b):
    return lax.dot_general(a, b, (((1,), (0,)), ((), ())), preferred_element_type=jnp.float32)


def prompt_kernel(heads, info_ref, q_ref, kv_ref, *rest):
    out_ref = rest[-2]
    length = q_ref.shape[0]

    @pl.when(jnp.logical_not(on_prefill(info_ref)))
    def _():
        out_ref[...] = jnp.zeros_like(out_ref)

    @pl.when(on_prefill(info_ref))
    def _():
        rows_all = lax.broadcasted_iota(jnp.int32, (TILE, TILE), 0)
        cols_all = lax.broadcasted_iota(jnp.int32, (TILE, TILE), 1)
        below = jnp.concatenate([rows_all >= cols_all] * heads, axis=0)
        ones = jnp.ones((length, HEADDIM), jnp.bfloat16)
        values = jnp.concatenate([kv_ref[:, HEADDIM:], ones], axis=1)
        for start in range(0, length, TILE):
            stop = start + TILE
            queries = jnp.concatenate(
                [q_ref[start:stop, h * HEADDIM : (h + 1) * HEADDIM] for h in range(heads)], axis=0
            )
            scores = dot_t(queries, kv_ref[:stop, :HEADDIM])
            last = jnp.where(below, scores[:, start:], NEG_FILL)
            scores = jnp.concatenate([scores[:, :start], last], axis=1) if start else last
            peak = jnp.max(scores, axis=1, keepdims=True)
            weights = jnp.exp2((scores - peak) * (SCALE * LOG2E)).astype(jnp.bfloat16)
            mixed = dot(weights, values[:stop])
            result = (mixed[:, :HEADDIM] / mixed[:, HEADDIM:]).astype(jnp.bfloat16)
            for h in range(heads):
                out_ref[start:stop, h * HEADDIM : (h + 1) * HEADDIM] = result[
                    h * TILE : (h + 1) * TILE
                ]


MARK = jax.ShapeDtypeStruct((8, 128), jnp.float32)
IN_HBM = pl.BlockSpec(memory_space=pltpu.HBM)
ANYWHERE = pl.BlockSpec(memory_space=pl.ANY)
IN_VMEM = pl.BlockSpec(memory_space=pltpu.VMEM)


def prompt_attention(info, queries, pairs, first, steps, heads, earlier, after):
    length, width = queries.shape
    per_kv = GROUP // heads

    def q_map(i, info_ref):
        return (0, jnp.where(on_prefill(info_ref), i + first, 0))

    def kv_map(i, info_ref):
        return (0, jnp.where(on_prefill(info_ref), (i + first) // per_kv, 0))

    in_specs = [
        pl.BlockSpec((length, heads * HEADDIM), q_map),
        pl.BlockSpec((length, 2 * HEADDIM), kv_map),
    ]
    operands = [info, queries, pairs]
    aliases = {}
    if earlier is not None:
        in_specs.append(ANYWHERE)
        operands.append(earlier)
        aliases = {3: 0}
    return pl.pallas_call(
        functools.partial(prompt_kernel, heads),
        out_shape=(jax.ShapeDtypeStruct((length, width), jnp.bfloat16), MARK),
        grid_spec=pltpu.PrefetchScalarGridSpec(
            num_scalar_prefetch=1,
            grid=(steps,),
            in_specs=in_specs + [IN_HBM] * len(after),
            out_specs=(
                pl.BlockSpec((length, heads * HEADDIM), lambda i, info_ref: (0, i + first)),
                IN_HBM,
            ),
        ),
        input_output_aliases=aliases,
        compiler_params=pltpu.CompilerParams(vmem_limit_bytes=LARGE),
        cost_estimate=COST,
        name="prompt_attention",
    )(*operands, *after)


def head_queries(block, head):
    start = head * GROUP * HEADDIM
    return jnp.concatenate(
        [
            block[r : r + 1, start + g * HEADDIM : start + (g + 1) * HEADDIM]
            for r in range(block.shape[0])
            for g in range(GROUP)
        ],
        axis=0,
    ).astype(jnp.bfloat16)


def store_part(out_ref, head, mixed, peak, total):
    lane = lax.broadcasted_iota(jnp.int32, mixed.shape, 1)
    out_ref[head, :, :HEADDIM] = mixed
    out_ref[head, :, HEADDIM:] = jnp.where(lane < HEADDIM // 2, peak, total)


def merged(parts):
    peaks = [part[:, HEADDIM : HEADDIM + 1] for part in parts]
    peak = functools.reduce(jnp.maximum, peaks)
    factors = [jnp.exp(p - peak) for p in peaks]
    total = sum(part[:, -1:] * f for part, f in zip(parts, factors))
    mixed = sum(part[:, :HEADDIM] * f for part, f in zip(parts, factors))
    return mixed, peak, total


def cache_kernel(page_len, info_ref, table_ref, lengths_ref, q_ref, kv_ref, *rest):
    out_ref, _, count_ref = rest[-3:]
    rows, slots = table_ref.shape

    @pl.when(jnp.logical_and(jnp.logical_not(on_prefill(info_ref)), pl.program_id(0) == 0))
    def _():
        token = lax.broadcasted_iota(jnp.int32, (GROUP, count_ref.shape[1]), 1)
        page, offset = token // page_len, token % page_len
        for r in range(rows):
            count = jnp.zeros(token.shape, jnp.float32)
            for slot in range(slots):
                left = lengths_ref[r] - (info_ref[TP] * slots + slot) * page_len
                valid = jnp.logical_and(page == table_ref[r, slot], offset < left)
                count = count + jnp.where(valid, 1.0, 0.0)
            count_ref[r * GROUP : (r + 1) * GROUP] = count

    @pl.when(on_prefill(info_ref))
    def _():
        out_ref[...] = jnp.zeros_like(out_ref)

    @pl.when(jnp.logical_not(on_prefill(info_ref)))
    def _():
        count = count_ref[...]
        here = count > 0.0
        block = q_ref[...].astype(jnp.float32)
        for head in range(out_ref.shape[0]):
            start = 2 * head * HEADDIM
            keys = kv_ref[:, start : start + HEADDIM]
            values = kv_ref[:, start + HEADDIM : start + 2 * HEADDIM]
            scores = dot_t(head_queries(block, head), keys) * SCALE
            scores = jnp.where(here, scores, NEG_FILL)
            peak = jnp.max(scores, axis=1, keepdims=True)
            weights = jnp.where(here, jnp.exp(scores - peak), 0.0)
            total = jnp.sum(weights * count, axis=1, keepdims=True)
            rounded = weights.astype(jnp.bfloat16).astype(jnp.float32) * count
            store_part(out_ref, head, dot(rounded.astype(jnp.bfloat16), values), peak, total)


def cache_attention(info, table, lengths, queries, pool, page_len, after):
    rows = queries.shape[0]
    tokens = pool.shape[0]
    steps = 2
    heads = KVHEADS // steps

    def step(n, info):
        return jnp.where(on_prefill(info), 0, n)

    return pl.pallas_call(
        functools.partial(cache_kernel, page_len),
        out_shape=(
            jax.ShapeDtypeStruct((KVHEADS, rows * GROUP, 2 * HEADDIM), jnp.float32),
            MARK,
        ),
        grid_spec=pltpu.PrefetchScalarGridSpec(
            num_scalar_prefetch=3,
            grid=(steps,),
            in_specs=[
                pl.BlockSpec((rows, heads * GROUP * HEADDIM), lambda n, info, *_: (0, step(n, info))),
                pl.BlockSpec((tokens, 2 * heads * HEADDIM), lambda n, info, *_: (0, step(n, info))),
            ]
            + [IN_HBM] * len(after),
            out_specs=(
                pl.BlockSpec(
                    (heads, rows * GROUP, 2 * HEADDIM), lambda n, info, *_: (step(n, info), 0, 0)
                ),
                IN_HBM,
            ),
            scratch_shapes=[pltpu.VMEM((rows * GROUP, tokens), jnp.float32)],
        ),
        compiler_params=pltpu.CompilerParams(vmem_limit_bytes=LARGE),
        cost_estimate=COST,
        name="cache_attention",
    )(info, table, lengths, queries, pool, *after)


def rows_part(queries, rows, out_ref, earlier_ref):
    block = queries[...].astype(jnp.float32)
    heads = rows[0].shape[1] // (2 * HEADDIM)
    for head in range(KVHEADS):
        held = rows[head // heads]
        start = 2 * (head % heads) * HEADDIM
        scores = dot_t(head_queries(block, head), held[:, start : start + HEADDIM]) * SCALE
        peak = jnp.max(scores, axis=1, keepdims=True)
        weights = jnp.exp(scores - peak)
        total = jnp.sum(weights, axis=1, keepdims=True)
        values = held[:, start + HEADDIM : start + 2 * HEADDIM]
        mixed = dot(weights.astype(jnp.bfloat16), values)
        store_part(out_ref, head, mixed, peak, total)
        if earlier_ref is not None:
            store_part(out_ref, head, *merged([out_ref[head], earlier_ref[head]]))


def flat_rows(pieces):
    wide = [piece.astype(jnp.float32).reshape(-1, piece.shape[-1]) for piece in pieces]
    return jnp.concatenate(wide, axis=0).astype(jnp.bfloat16)


def whole_rows_kernel(info_ref, q_ref, rows_ref, out_ref):
    rows_part(q_ref, [rows_ref[...]], out_ref, None)


def far_rows_kernel(info_ref, q_ref, slots_ref, out_ref, held_ref, sem):
    @pl.when(jnp.logical_not(on_prefill(info_ref)))
    def _():
        copy = pltpu.make_async_copy(slots_ref, held_ref, sem)
        copy.start()
        copy.wait()
        half = 2 * PAIRS
        rows = [
            flat_rows([held_ref[t * half + i] for i in range(half)]) for t in range(2)
        ]
        rows_part(q_ref, rows, out_ref, None)


def near_rows_kernel(info_ref, q_ref, earlier_ref, *refs):
    *part_refs, out_ref = refs

    @pl.when(jnp.logical_not(on_prefill(info_ref)))
    def _():
        rows = [flat_rows([part[t] for part in part_refs]) for t in range(2)]
        rows_part(q_ref, rows, out_ref, earlier_ref)


def arrival_part(kernel, info, query, operands, places, scratch, name):
    return pl.pallas_call(
        kernel,
        out_shape=jax.ShapeDtypeStruct((KVHEADS, GROUP, 2 * HEADDIM), jnp.float32),
        grid_spec=pltpu.PrefetchScalarGridSpec(
            num_scalar_prefetch=1,
            grid=(1,),
            in_specs=[IN_VMEM] + places,
            out_specs=IN_VMEM,
            scratch_shapes=scratch,
        ),
        compiler_params=pltpu.CompilerParams(vmem_limit_bytes=VMEM),
        cost_estimate=COST,
        name=name,
    )(info, query, *operands)


def combine_kernel(count, info_ref, *refs):
    part_refs, out_ref = refs[:count], refs[-2]

    @pl.when(on_prefill(info_ref))
    def _():
        out_ref[...] = jnp.zeros_like(out_ref)

    @pl.when(jnp.logical_not(on_prefill(info_ref)))
    def _():
        results = []
        for head in range(KVHEADS):
            if count == 2:
                here, there = part_refs[0][head], part_refs[1][head]
                first = info_ref[TP] == 0
                parts = [jnp.where(first, here, there), jnp.where(first, there, here)]
            else:
                parts = [part_refs[0][n, head] for n in range(part_refs[0].shape[0])]
            mixed, _, total = merged(parts)
            results.append(mixed / total)
        for r in range(out_ref.shape[0]):
            row = [
                results[head][r * GROUP + g : r * GROUP + g + 1]
                for head in range(KVHEADS)
                for g in range(GROUP)
            ]
            out_ref[r : r + 1] = jnp.concatenate(row, axis=1).astype(jnp.bfloat16)


def combine_parts(info, parts, after=()):
    rows = parts[0].shape[-2] // GROUP
    return pl.pallas_call(
        functools.partial(combine_kernel, len(parts)),
        out_shape=(jax.ShapeDtypeStruct((rows, QHEADS * HEADDIM), jnp.bfloat16), MARK),
        grid_spec=pltpu.PrefetchScalarGridSpec(
            num_scalar_prefetch=1,
            grid=(1,),
            in_specs=[IN_VMEM] * len(parts) + [IN_HBM] * len(after),
            out_specs=(IN_VMEM, IN_HBM),
        ),
        compiler_params=pltpu.CompilerParams(vmem_limit_bytes=VMEM),
        cost_estimate=COST,
        name="combine_parts",
    )(info, *parts, *after)


def relay_handoff(pairs, assignment, inst_count):
    half = inst_count // 2
    decode_ids = jnp.arange(half, dtype=jnp.int32)
    matches = assignment[None, :] == decode_ids[:, None]
    source = jnp.sum(jnp.where(matches, decode_ids[None, :], 0), axis=1).astype(jnp.int32)
    moved = lax.all_to_all(pairs, "tp", split_axis=0, concat_axis=1, tiled=True)
    lanes = 1024 if moved.size % (inst_count * 1024) == 0 else HEADDIM
    pieces = moved.reshape(inst_count, -1, lanes)
    spread = lax.all_to_all(pieces, "inst", split_axis=0, concat_axis=0, tiled=True)
    chosen = jnp.stack(
        [lax.dynamic_index_in_dim(spread, source[d], 0, False) for d in range(half)], axis=0
    )
    outgoing = jnp.concatenate([jnp.zeros_like(chosen), chosen], axis=0)
    delivered = lax.all_to_all(outgoing, "inst", split_axis=0, concat_axis=0, tiled=True)
    return delivered.reshape(moved.shape)


UNIT = 8
PAIRS = 4
PREFILL, DECODE = True, False


def copy_kernel(plan, side, counts, info_ref, *refs):
    inputs, marks, outputs, stages = counts
    sources, targets = refs[:inputs], refs[inputs + marks : inputs + marks + outputs]
    held, sems = refs[-1 - stages : -1], refs[-1]

    @pl.when(on_prefill(info_ref) == side)
    def _():
        started = []
        for source, target in zip(sources, held):
            started.append(pltpu.make_async_copy(source, target, sems.at[len(started)]))
        for copy in started:
            copy.start()
        for copy in started:
            copy.wait()
        started = []
        for source, target in plan(info_ref, held or sources, targets):
            started.append(pltpu.make_async_copy(source, target, sems.at[len(started)]))
        for copy in started:
            copy.start()
        for copy in started:
            copy.wait()


def copies(plan, number, info, operands, shapes, name, after=(), stage=False, side=PREFILL):
    held = [pltpu.VMEM(x.shape, x.dtype) for x in operands] if stage else []
    return pl.pallas_call(
        functools.partial(copy_kernel, plan, side, (len(operands), len(after), len(shapes), len(held))),
        out_shape=tuple(jax.ShapeDtypeStruct(shape, jnp.bfloat16) for shape in shapes),
        grid_spec=pltpu.PrefetchScalarGridSpec(
            num_scalar_prefetch=1,
            grid=(1,),
            in_specs=[ANYWHERE] * len(operands) + [IN_HBM] * len(after),
            out_specs=tuple([ANYWHERE] * len(shapes)),
            scratch_shapes=held + [pltpu.SemaphoreType.DMA((number,))],
        ),
        compiler_params=pltpu.CompilerParams(vmem_limit_bytes=MEDIUM if stage else SMALL),
        cost_estimate=COST,
        name=name,
    )(info, *operands, *after)


def relay_slots_kernel(far, info_ref, keep_ref, recv_ref, out_ref, sems):
    half = 2 * PAIRS

    @pl.when(jnp.logical_not(on_prefill(info_ref)))
    def _():
        here = order(info_ref)
        waits = []
        for d in range(half):
            source = source_of(info_ref, d)
            same = lax.rem(source, 2) == lax.rem(here, 2)
            shift = lax.rem(lax.div(here, 2) + PAIRS - lax.div(source, 2), PAIRS)
            for tau in range(2):
                slot = tau * half + d
                target = out_ref.at[slot]
                mine = pltpu.make_async_copy(keep_ref.at[shift, tau], target, sems.at[slot])
                other = pltpu.make_async_copy(recv_ref.at[shift, tau], target, sems.at[slot])
                pl.when(same)(mine.start)
                pl.when(jnp.logical_not(same))(other.start)
                waits.append(mine)
        for copy in waits:
            copy.wait()


def rows_kernel(near, far, info_ref, slots_ref, *refs):
    *parts, out_ref, zero_ref, held_ref, sems = refs
    half = 2 * PAIRS
    width = slots_ref.shape[-1]
    near_all = near * half

    @pl.when(jnp.logical_not(on_prefill(info_ref)))
    def _():
        last = sems.shape[0] - 1
        staged = pltpu.make_async_copy(slots_ref, held_ref, sems.at[last])
        staged.start()
        waits = []
        for t in range(2):
            for s, part in enumerate(parts):
                pair = lax.rem(lax.div(order(info_ref), 2) + PAIRS - s, PAIRS)
                target = out_ref.at[pl.ds(pair * 2 * near, 2 * near), :, pl.ds(t * width, width)]
                waits.append(pltpu.make_async_copy(part.at[t], target, sems.at[len(waits)]))
                waits[-1].start()
        staged.wait()
        for t in range(2):
            for i in range(half):
                target = out_ref.at[pl.ds(near_all + i * far, far), :, pl.ds(t * width, width)]
                waits.append(
                    pltpu.make_async_copy(held_ref.at[t * half + i], target, sems.at[len(waits)])
                )
                waits[-1].start()
        for copy in waits:
            copy.wait()

    @pl.when(on_prefill(info_ref))
    def _():
        zero_ref[...] = jnp.zeros_like(zero_ref)
        size = zero_ref.shape[0]
        waits = []
        for n in range(out_ref.shape[0] // size):
            target = out_ref.at[pl.ds(n * size, size)]
            waits.append(pltpu.make_async_copy(zero_ref, target, sems.at[n]))
        for copy in waits:
            copy.start()
        for copy in waits:
            copy.wait()


def two_way_handoff(pairs, info, always, arrival_query, prompt_part, cached, combined):
    half = 2 * PAIRS
    rows, width = pairs.shape
    units = rows // (2 * UNIT)
    far_all = -(-units * 3 // (5 * half)) * half
    near_all = units - far_all
    near, far = near_all // half, far_all // half
    block = (UNIT, width)
    by_unit = pairs.reshape((rows // UNIT,) + block)
    groups = [[base + 2 * i + tau for tau in range(2) for i in range(half)] for base in (0, 2 * half)]

    def crossing(array, s):
        hops = [
            (2 * p + k, half + 2 * ((p + s) % PAIRS) + k) for p in range(PAIRS) for k in range(2)
        ]
        return lax.ppermute(array, "inst", hops)

    def beside(array, base):
        return lax.ppermute(array, "inst", [(base + i, base + (i ^ 1)) for i in range(half)])

    def spread_out(array):
        return lax.all_to_all(
            array, ("inst", "tp"), 0, 0, axis_index_groups=groups, tiled=True
        )

    def cut(pre, sources, targets):
        plan = []
        for s in range(PAIRS):
            start = near_all + lax.rem(lax.div(order(pre), 2) + s, PAIRS) * (2 * far)
            for tau in range(2):
                plan.append((sources[0].at[pl.ds(tau * units + start, 2 * far)], targets[s].at[tau]))
        for tau in range(2):
            plan.append((sources[0].at[pl.ds(tau * units, near_all)], targets[PAIRS].at[tau]))
        return plan

    def for_neighbour(pre, sources, targets):
        plan = []
        for s in range(PAIRS):
            receiver = lax.rem(lax.div(order(pre), 2) + s, PAIRS) * 2 + 1 - lax.rem(order(pre), 2)
            for t in range(2):
                origin = t * half + source_of(pre, receiver)
                plan.append((sources[0].at[origin], targets[0].at[s, t]))
        return plan

    def for_receivers(pre, sources, targets):
        plan = []
        for s in range(PAIRS):
            receiver = lax.rem(lax.div(order(pre), 2) + s, PAIRS) * 2 + lax.rem(order(pre), 2)
            for t in range(2):
                origin = t * half + source_of(pre, receiver)
                mine = targets[s].at[t, pl.ds(lax.rem(order(pre), 2) * near, near)]
                other = targets[s].at[t, pl.ds((1 - lax.rem(order(pre), 2)) * near, near)]
                plan.append((sources[0].at[origin], mine))
                plan.append((sources[1].at[s, t], other))
        return plan

    def split(pre, sources, targets):
        plan = []
        for s in range(PAIRS):
            for tau in range(2):
                mine = sources[s].at[tau, pl.ds(lax.rem(order(pre), 2) * far, far)]
                other = sources[s].at[tau, pl.ds((1 - lax.rem(order(pre), 2)) * far, far)]
                plan.append((mine, targets[0].at[s, tau]))
                plan.append((other, targets[1].at[s, tau]))
        return plan

    near_shape = (2, 2 * near) + block

    def first_stage(slots):
        parts, mark = cached([slots])
        prompt, mark = prompt_part(0, None, [mark])
        spread = spread_out(slots)
        (outgoing,) = copies(
            for_neighbour, 2 * PAIRS, info, [spread], [(PAIRS, 2, near) + block], "for_neighbour", [mark]
        )
        incoming = beside(outgoing, 0)
        near_parts = copies(
            for_receivers, 4 * PAIRS, info, [spread, incoming], [near_shape] * PAIRS, "for_receivers"
        )
        return *near_parts, prompt, parts

    def second_stage(prompt, parts, *far_here):
        keep, give = copies(
            split,
            4 * PAIRS,
            info,
            list(far_here),
            [(PAIRS, 2, far) + block] * 2,
            "split_relays",
            stage=True,
            side=DECODE,
        )
        taken = beside(give, half)
        slots = pl.pallas_call(
            functools.partial(relay_slots_kernel, far),
            out_shape=jax.ShapeDtypeStruct((2 * half, far) + block, jnp.bfloat16),
            grid_spec=pltpu.PrefetchScalarGridSpec(
                num_scalar_prefetch=1,
                grid=(1,),
                in_specs=[ANYWHERE] * 2,
                out_specs=ANYWHERE,
                scratch_shapes=[pltpu.SemaphoreType.DMA((2 * half,))],
            ),
            compiler_params=pltpu.CompilerParams(vmem_limit_bytes=SMALL),
            cost_estimate=COST,
            name="relay_slots",
        )(info, keep, taken)
        prompt, mark = prompt_part(1, prompt, [slots])
        decode_out = combined(parts, [mark])
        slots = spread_out(slots)
        arrival = arrival_part(
            far_rows_kernel,
            info,
            arrival_query,
            [slots],
            [ANYWHERE],
            [pltpu.VMEM(slots.shape, slots.dtype), pltpu.SemaphoreType.DMA],
            "far_rows",
        )
        return prompt, slots, decode_out, arrival

    def staged(stage, *operands):
        def never(*operands):
            outs = [jnp.zeros(out.shape, out.dtype) for out in jax.eval_shape(stage, *operands)]
            return tuple(outs) if stage is first_stage else (operands[0], *outs[1:])

        return lax.cond(always, lambda *operands: tuple(stage(*operands)), never, *operands)

    *far_parts, near_rows = copies(
        cut,
        2 * PAIRS + 2,
        info,
        [by_unit],
        [(2, 2 * far) + block] * PAIRS + [(2, near_all) + block],
        "cut_rows",
        stage=True,
    )
    far_here = [crossing(part, s) for s, part in enumerate(far_parts)]
    near_rows = near_rows.reshape((2 * half, near) + block)
    *near_parts, prompt, parts = staged(first_stage, near_rows)
    near_here = [crossing(part, s) for s, part in enumerate(near_parts)]
    prompt, slots, decode_out, arrival = staged(second_stage, prompt, parts, *far_here)
    arrival = arrival_part(
        near_rows_kernel,
        info,
        arrival_query,
        [arrival, *near_here],
        [IN_VMEM] * (PAIRS + 1),
        [],
        "near_rows",
    )
    handed = pl.pallas_call(
        functools.partial(rows_kernel, near, far),
        out_shape=jax.ShapeDtypeStruct((units, UNIT, 2 * width), jnp.bfloat16),
        grid_spec=pltpu.PrefetchScalarGridSpec(
            num_scalar_prefetch=1,
            grid=(1,),
            in_specs=[ANYWHERE] * (PAIRS + 1),
            out_specs=ANYWHERE,
            scratch_shapes=[
                pltpu.VMEM((half, UNIT, 2 * width), jnp.bfloat16),
                pltpu.VMEM(slots.shape, slots.dtype),
                pltpu.SemaphoreType.DMA((2 * (half + PAIRS) + 1,)),
            ],
        ),
        compiler_params=pltpu.CompilerParams(vmem_limit_bytes=MEDIUM),
        cost_estimate=COST,
        name="rows",
    )(info, slots, *near_here)
    return prompt, handed.reshape(rows // 2, 2 * width), decode_out, combined(arrival)


def shards(
    prompt_query,
    prompt_pairs,
    decode_query,
    arrival_query,
    cache_pool,
    page_table,
    lengths,
    assignment,
):
    inst_count = lax.axis_size("inst")
    tp_count = lax.axis_size("tp")
    half = inst_count // 2
    inst = lax.axis_index("inst")
    tp_index = lax.axis_index("tp")
    info = jnp.concatenate([jnp.stack([inst, tp_index]), assignment])
    pages, page_len = cache_pool.shape[0], cache_pool.shape[1]
    by_token = cache_pool.reshape(pages * page_len, -1)

    def cached(after=()):
        return cache_attention(info, page_table, lengths, decode_query, by_token, page_len, after)

    def combined(part, after=()):
        if tp_count == 2:
            parts = [part, lax.ppermute(part, "tp", [(0, 1), (1, 0)])]
        else:
            parts = [lax.all_gather(part, "tp")]
        return combine_parts(info, parts, after)[0]

    heads = GROUP // 2
    steps = prompt_query.shape[1] // (heads * HEADDIM)

    def prompt_part(first, last, earlier, after=()):
        return prompt_attention(
            info, prompt_query, prompt_pairs, first, last - first, heads, earlier, after
        )

    row_units = prompt_pairs.shape[0] // (2 * UNIT)
    if inst_count == 4 * PAIRS and tp_count == 2 and row_units == 5 * half and steps == 8:
        cuts = (0, 4, 8)
        return two_way_handoff(
            prompt_pairs,
            info,
            assignment[0] >= 0,
            arrival_query,
            lambda n, earlier, after: prompt_part(cuts[n], cuts[n + 1], earlier, after),
            cached,
            combined,
        )
    handed = relay_handoff(prompt_pairs, assignment, inst_count)
    arrival = arrival_part(
        whole_rows_kernel, info, arrival_query, [handed], [IN_VMEM], [], "whole_rows"
    )
    prefill_out, _ = prompt_part(0, steps, None)
    return prefill_out, handed, combined(cached()[0]), combined(arrival)


def solution(mesh):
    return jax.shard_map(
        shards,
        mesh=mesh,
        in_specs=(
            P("inst", "tp"),
            P("inst", "tp"),
            P("inst", None),
            P("inst", None),
            P(("inst", "tp"), None, None),
            P("inst", "tp"),
            P("inst"),
            P(),
        ),
        out_specs=(P("inst", "tp"), P(("inst", "tp"), None), P("inst", None), P("inst", None)),
        check_vma=False,
    )
```

time: 106 us -> 90.3 us (0.85)
  the two profiles are of different devices: /device:TPU:0 before, /device:TPU:24 now
where the time goes in v4:
time: 90.3 us; the launch traced here: 89.4 us
  Pallas kernels  30.4 us (34%)
  waiting for transfers between devices  29.9 us (33%)
  starting transfers between devices  25.5 us (28%)
  between operations  1.46 us (2%)
  local copies, waits for them, and re-layouts  1.38 us (2%)
    all_to_all x2, waiting for transfers between devices, spread_out(): lax.all_to_all(array, ('inst', 'tp'), 0, 0, axis_index_groups=groups, til...  16.2 us
    ppermute x2, waiting for transfers between devices, combined(): parts = [part, lax.ppermute(part, 'tp', [(0, 1), (1, 0)])]  12.3 us
    ppermute x8, starting transfers between devices, crossing(): return lax.ppermute(array, 'inst', hops)  10.3 us
    all_to_all x2, starting transfers between devices, spread_out(): lax.all_to_all(array, ('inst', 'tp'), 0, 0, axis_index_groups=groups, til...  10.1 us
    pallas_call x2, Pallas kernels, prompt_attention(): pl.pallas_call(functools.partial(prompt_kernel, heads), out_shape=(jax.Sh...  7.44 us
    pallas_call x2, Pallas kernels, arrival_part(): pl.pallas_call(kernel, out_shape=jax.ShapeDtypeStruct((KVHEADS, GROUP, 2...  6.63 us
    pallas_call x4, Pallas kernels, copies(): pl.pallas_call(functools.partial(copy_kernel, plan, side, (len(operands),...  4.71 us
    pallas_call x1, Pallas kernels, cache_attention(): pl.pallas_call(functools.partial(cache_kernel, page_len), out_shape=(jax....  4.1 us
  transfers between devices with their start and end apart: 14, of which 4 were waited for; matrix products, arithmetic and copies ran while one was open for 0% of the time, Pallas kernels for 29%

profile of v4, /device:TPU:24, one launch (start us, length us, event | category | flops | bytes accessed | tf_op | source)
XLA Modules:
  0.0 89.4 jit_solution(13403292421355464649)
XLA Ops:
  0.6 0.7 pad_add_fusion.info_ref
  1.4 0.6 cut_rows.1
  2.0 1.3 %collective-permute-start.3 = (bf16[2,6,8,1024]{3,2,1,0:T(8,128)(2,1)S(1)}, bf16[2,6,8,1024]{3,2,1,0:T(8,128)(2,1)S(1)}, u32[]{:S(2)}, u32[]{:S(2)}) collective-permute-start(bf16[2,6,8,1024]{3,2,1,0:T(8,128)(2,1)S(1)} %get-tuple-element.92), channel_id=1, source_target_pairs={{0,16},{2,18},{4,20},{6,22},{8,24},{10,26},{12,28},{14,30},{1,17},... | collective-permute-start | bytes 589832 | tf_op jit(solution)/shard_map/ppermute | solution.py:487
  3.3 1.3 %collective-permute-start.4 = (bf16[2,6,8,1024]{3,2,1,0:T(8,128)(2,1)S(1)}, bf16[2,6,8,1024]{3,2,1,0:T(8,128)(2,1)S(1)}, u32[]{:S(2)}, u32[]{:S(2)}) collective-permute-start(bf16[2,6,8,1024]{3,2,1,0:T(8,128)(2,1)S(1)} %get-tuple-element.93), channel_id=1, source_target_pairs={{0,20},{2,22},{4,24},{6,26},{8,28},{10,30},{12,16},{14,18},{1,21},... | collective-permute-start | bytes 589832 | tf_op jit(solution)/shard_map/ppermute | solution.py:487
  4.6 1.3 %collective-permute-start.5 = (bf16[2,6,8,1024]{3,2,1,0:T(8,128)(2,1)S(1)}, bf16[2,6,8,1024]{3,2,1,0:T(8,128)(2,1)S(1)}, u32[]{:S(2)}, u32[]{:S(2)}) collective-permute-start(bf16[2,6,8,1024]{3,2,1,0:T(8,128)(2,1)S(1)} %get-tuple-element.94), channel_id=1, source_target_pairs={{0,24},{2,26},{4,28},{6,30},{8,16},{10,18},{12,20},{14,22},{1,25},... | collective-permute-start | bytes 589832 | tf_op jit(solution)/shard_map/ppermute | solution.py:487
  5.9 1.3 %collective-permute-start.6 = (bf16[2,6,8,1024]{3,2,1,0:T(8,128)(2,1)S(1)}, bf16[2,6,8,1024]{3,2,1,0:T(8,128)(2,1)S(1)}, u32[]{:S(2)}, u32[]{:S(2)}) collective-permute-start(bf16[2,6,8,1024]{3,2,1,0:T(8,128)(2,1)S(1)} %get-tuple-element.95), channel_id=1, source_target_pairs={{0,28},{2,30},{4,16},{6,18},{8,20},{10,22},{12,24},{14,26},{1,29},... | collective-permute-start | bytes 589832 | tf_op jit(solution)/shard_map/ppermute | solution.py:487
  7.9 0.0 copy-start.2
  7.9 32.0 %conditional.2 = (bf16[2,4,8,1024]{3,2,1,0:T(8,128)(2,1)S(1)}, bf16[2,4,8,1024]{3,2,1,0:T(8,128)(2,1)S(1)}, bf16[2,4,8,1024]{3,2,1,0:T(8,128)(2,1)S(1)}, bf16[2,...) conditional(s32[]{:T(128)} %bitcast.2, () %tuple.24, ...), branch_computations={%region_0.0_spmd, %region_1.0_spmd} | conditional | flops 4 | bytes 6029374 | solution.py:598
  7.9 5.2 %all-to-all-start = ((bf16[16,2,8,1024]{3,2,1,0:T(8,128)(2,1)}), bf16[16,2,8,1024]{3,2,1,0:T(8,128)(2,1)S(1)}, u32[]{:S(2)}, u32[]{:S(2)}) async-start(bf16[16,2,8,1024]{3,2,1,0:T(8,128)(2,1)} %bitcast.rest_0_), calls=%async_computation | async-start | bytes 1048576 | tf_op jit(solution)/shard_map/cond/branch_1_fun/all_to_all | solution.py:493
  13.1 4.1 %cache_attention.1 = (f32[8,32,256]{2,1,0:T(8,128)S(1)}, f32[8,128]{1,0:T(8,128)}) custom-call(s32[10]{0:T(128)S(1)} %get-tuple-element.39.info_ref, s32[4,8]{1,0:T(4,128)} %get-tuple-element.111.table_ref, s32[4]{0:T(128)} %get-tuple-element.112.lengths_ref, bf16[4,8192]{1,0:T(4,128)(2,1)} %get-tuple-element.113.q_ref, bf16[320,2048]{1,0:T(8,128)(2,1)} %bitcast.9, ...), custom_call_target="tpu_custom_call" | custom-call | flops 1 | bytes 1 | tf_op jit(solution)/shard_map/cond/branch_1_fun/cache_attention/pallas_call | solution.py:205
  17.2 3.7 %prompt_attention.2 = (bf16[640,4096]{1,0:T(8,128)(2,1)}, f32[8,128]{1,0:T(8,128)}) custom-call(s32[10]{0:T(128)S(1)} %get-tuple-element.39.info_ref, bf16[640,4096]{1,0:T(8,128)(2,1)} %get-tuple-element.41.q_ref, bf16[640,1024]{1,0:T(8,128)(2,1)} %get-tuple-element.42.kv_ref, f32[8,128]{1,0:T(8,128)} %get-tuple-element.47.rest_0_), custom_call_target="tpu_custom_call" | custom-call | flops 1 | bytes 1 | tf_op jit(solution)/shard_map/cond/branch_1_fun/prompt_attention/pallas_call | solution.py:112
  20.9 16.2 %all-to-all-done.refs_0_ = bf16[16,2,8,1024]{3,2,1,0:T(8,128)(2,1)S(1)} async-done(((bf16[16,2,8,1024]{3,2,1,0:T(8,128)(2,1)}), bf16[16,2,8,1024]{3,2,1,0:T(8,128)(2,1)S(1)}, u32[]{:S(2)}, u32[]{:S(2)}) %all-to-all-start) | async-done | bytes 524320 | tf_op jit(solution)/shard_map/cond/branch_1_fun/all_to_all | solution.py:493
  37.2 0.0 copy-start.1
  37.2 0.7 copy-done.1
  37.8 0.6 for_neighbour.1
  38.5 0.7 collective-permute-start
  39.2 0.0 collective-permute-done.refs_1_
  39.2 0.7 for_receivers.1
  39.9 1.3 %collective-permute-start.7 = (bf16[2,4,8,1024]{3,2,1,0:T(8,128)(2,1)S(1)}, bf16[2,4,8,1024]{3,2,1,0:T(8,128)(2,1)S(1)}, u32[]{:S(2)}, u32[]{:S(2)}) collective-permute-start(bf16[2,4,8,1024]{3,2,1,0:T(8,128)(2,1)S(1)} %get-tuple-element.99), channel_id=1, source_target_pairs={{0,16},{2,18},{4,20},{6,22},{8,24},{10,26},{12,28},{14,30},{1,17},... | collective-permute-start | bytes 393224 | tf_op jit(solution)/shard_map/ppermute | solution.py:487
  41.2 0.0 collective-permute-done.3
  41.2 1.3 %collective-permute-start.8 = (bf16[2,4,8,1024]{3,2,1,0:T(8,128)(2,1)S(1)}, bf16[2,4,8,1024]{3,2,1,0:T(8,128)(2,1)S(1)}, u32[]{:S(2)}, u32[]{:S(2)}) collective-permute-start(bf16[2,4,8,1024]{3,2,1,0:T(8,128)(2,1)S(1)} %get-tuple-element.100), channel_id=1, source_target_pairs={{0,20},{2,22},{4,24},{6,26},{8,28},{10,30},{12,16},{14,18},{1,21},... | collective-permute-start | bytes 393224 | tf_op jit(solution)/shard_map/ppermute | solution.py:487
  42.5 0.0 collective-permute-done.4
  42.5 1.3 %collective-permute-start.9 = (bf16[2,4,8,1024]{3,2,1,0:T(8,128)(2,1)S(1)}, bf16[2,4,8,1024]{3,2,1,0:T(8,128)(2,1)S(1)}, u32[]{:S(2)}, u32[]{:S(2)}) collective-permute-start(bf16[2,4,8,1024]{3,2,1,0:T(8,128)(2,1)S(1)} %get-tuple-element.101), channel_id=1, source_target_pairs={{0,24},{2,26},{4,28},{6,30},{8,16},{10,18},{12,20},{14,22},{1,25},... | collective-permute-start | bytes 393224 | tf_op jit(solution)/shard_map/ppermute | solution.py:487
  43.8 0.0 collective-permute-done.5
  43.8 1.3 %collective-permute-start.10 = (bf16[2,4,8,1024]{3,2,1,0:T(8,128)(2,1)S(1)}, bf16[2,4,8,1024]{3,2,1,0:T(8,128)(2,1)S(1)}, u32[]{:S(2)}, u32[]{:S(2)}) collective-permute-start(bf16[2,4,8,1024]{3,2,1,0:T(8,128)(2,1)S(1)} %get-tuple-element.102), channel_id=1, source_target_pairs={{0,28},{2,30},{4,16},{6,18},{8,20},{10,22},{12,24},{14,26},{1,29},... | collective-permute-start | bytes 393224 | tf_op jit(solution)/shard_map/ppermute | solution.py:487
  45.1 0.0 collective-permute-done.6
  45.1 0.0 copy-done.2
  45.1 35.8 %conditional.3 = (bf16[640,4096]{1,0:T(8,128)(2,1)}, bf16[16,3,8,1024]{3,2,1,0:T(8,128)(2,1)}, bf16[4,8192]{1,0:T(4,128)(2,1)}, f32[8,8,256]{2,1,0:T(8,128)S(1)}) conditional(s32[]{:T(128)} %bitcast.2, bf16[640,4096]{1,0:T(8,128)(2,1)} %get-tuple-element.91, (s32[10]{0:T(128)S(1)}, bf16[2,6,8,1024]{3,2,1,0:T(8,128)(2,1)S(1)}, ...), branch_computations={%region_2.0_spmd, %region_3.0_spmd} | conditional | flops 5 | bytes 4997297 | solution.py:598
  45.1 2.8 %split_relays.1 = (bf16[4,2,3,8,1024]{4,3,2,1,0:T(8,128)(2,1)S(1)}, bf16[4,2,3,8,1024]{4,3,2,1,0:T(8,128)(2,1)S(1)}) custom-call(s32[10]{0:T(128)S(1)} %get-tuple-element.55.info_ref, bf16[2,6,8,1024]{3,2,1,0:T(8,128)(2,1)S(1)} %get-tuple-element.59.refs_0_, bf16[2,6,8,1024]{3,2,1,0:T(8,128)(2,1)S(1)} %get-tuple-element.60.refs_1_, ...), custom_call_target="tpu_custom_call" | custom-call | flops 1 | bytes 1 | tf_op jit(solution)/shard_map/cond/branch_1_fun/split_relays/pallas_call | solution.py:390
  47.9 2.3 %collective-permute-start.1 = (bf16[4,2,3,8,1024]{4,3,2,1,0:T(8,128)(2,1)S(1)}, bf16[4,2,3,8,1024]{4,3,2,1,0:T(8,128)(2,1)S(1)}, u32[]{:S(2)}, u32[]{:S(2)}) collective-permute-start(bf16[4,2,3,8,1024]{4,3,2,1,0:T(8,128)(2,1)S(1)} %get-tuple-element.64), channel_id=1, source_target_pairs={{16,18},{18,16},{20,22},{22,20},{24,26},{26,24},{28,30},{30,28},{1... | collective-permute-start | bytes 1179656 | tf_op jit(solution)/shard_map/cond/branch_1_fun/ppermute | solution.py:490
  50.2 1.3 %collective-permute-done.1.recv_ref = bf16[4,2,3,8,1024]{4,3,2,1,0:T(8,128)(2,1)S(1)} collective-permute-done((bf16[4,2,3,8,1024]{4,3,2,1,0:T(8,128)(2,1)S(1)}, bf16[4,2,3,8,1024]{4,3,2,1,0:T(8,128)(2,1)S(1)}, u32[]{:S(2)}, u32[]{:S(2)}) %collective-permute-start.1) | collective-permute-done | bytes 393248 | tf_op jit(solution)/shard_map/cond/branch_1_fun/ppermute | solution.py:490
  51.5 1.6 %relay_slots.1.rest_1_ = bf16[16,3,8,1024]{3,2,1,0:T(8,128)(2,1)} custom-call(s32[10]{0:T(128)S(1)} %get-tuple-element.55.info_ref, bf16[4,2,3,8,1024]{4,3,2,1,0:T(8,128)(2,1)S(1)} %get-tuple-element.63.keep_ref, bf16[4,2,3,8,1024]{4,3,2,1,0:T(8,128)(2,1)S(1)} %collective-permute-done.1.recv_ref), custom_call_target="tpu_custom_call" | custom-call | flops 1 | bytes 1 | tf_op jit(solution)/shard_map/cond/branch_1_fun/relay_slots/pallas_call | solution.py:565
  53.1 4.9 %all-to-all-start.1 = ((bf16[16,3,8,1024]{3,2,1,0:T(8,128)(2,1)}), bf16[16,3,8,1024]{3,2,1,0:T(8,128)(2,1)}, u32[]{:S(2)}, u32[]{:S(2)}) async-start(bf16[16,3,8,1024]{3,2,1,0:T(8,128)(2,1)} %relay_slots.1.rest_1_), calls=%async_computation.1 | async-start | bytes 1572864 | tf_op jit(solution)/shard_map/cond/branch_1_fun/all_to_all | solution.py:493
  58.0 1.5 %collective-permute-start.2 = (f32[8,32,256]{2,1,0:T(8,128)S(1)}, f32[8,32,256]{2,1,0:T(8,128)S(1)}, u32[]{:S(2)}, u32[]{:S(2)}) collective-permute-start(f32[8,32,256]{2,1,0:T(8,128)S(1)} %get-tuple-element.66.refs_0_), channel_id=1, source_target_pairs={{0,1},{1,0},{2,3},{3,2},{4,5},{5,4},{6,7},{7,6},{8,9},{9,8},{10,11... | collective-permute-start | bytes 786440 | tf_op jit(solution)/shard_map/cond/branch_1_fun/ppermute | solution.py:668
  59.5 3.7 %prompt_attention.3 = (bf16[640,4096]{1,0:T(8,128)(2,1)}, f32[8,128]{1,0:T(8,128)}) custom-call(s32[10]{0:T(128)S(1)} %get-tuple-element.55.info_ref, bf16[640,4096]{1,0:T(8,128)(2,1)} %get-tuple-element.56.q_ref, bf16[640,1024]{1,0:T(8,128)(2,1)} %get-tuple-element.57.kv_ref, ...), custom_call_target="tpu_custom_call", output_to_operand_aliasing={{0}: (3, {})} | custom-call | flops 1 | bytes 1 | tf_op jit(solution)/shard_map/cond/branch_1_fun/prompt_attention/pallas_call | solution.py:112
  63.2 11.5 %collective-permute-done.2.refs_1_ = f32[8,32,256]{2,1,0:T(8,128)S(1)} collective-permute-done((f32[8,32,256]{2,1,0:T(8,128)S(1)}, f32[8,32,256]{2,1,0:T(8,128)S(1)}, u32[]{:S(2)}, u32[]{:S(2)}) %collective-permute-start.2) | collective-permute-done | bytes 262176 | tf_op jit(solution)/shard_map/cond/branch_1_fun/ppermute | solution.py:668
  74.7 0.0 copy-start
  74.7 0.7 copy-done
  75.4 1.7 %combine_parts.2 = (bf16[4,8192]{1,0:T(4,128)(2,1)}, f32[8,128]{1,0:T(8,128)}) custom-call(s32[10]{0:T(128)S(1)} %get-tuple-element.55.info_ref, f32[8,32,256]{2,1,0:T(8,128)S(1)} %get-tuple-element.66.refs_0_, f32[8,32,256]{2,1,0:T(8,128)S(1)} %collective-permute-done.2.refs_1_, f32[8,128]{1,0:T(8,128)S(1)} %copy-done), custom_call_target="tpu_custom_call" | custom-call | flops 1 | bytes 1 | tf_op jit(solution)/shard_map/cond/branch_1_fun/combine_parts/pallas_call | solution.py:328
  77.1 0.0 all-to-all-done.1.slots_ref
  77.1 3.8 %far_rows.1 = f32[8,8,256]{2,1,0:T(8,128)S(1)} custom-call(s32[10]{0:T(128)S(1)} %get-tuple-element.55.info_ref, bf16[1,8192]{1,0:T(2,128)(2,1)S(1)} %get-tuple-element.69.q_ref, bf16[16,3,8,1024]{3,2,1,0:T(8,128)(2,1)} %all-to-all-done.1.slots_ref), custom_call_target="tpu_custom_call" | custom-call | flops 1 | bytes 1 | tf_op jit(solution)/shard_map/cond/branch_1_fun/far_rows/pallas_call | solution.py:282
  80.9 0.0 collective-permute-done.7.refs_0_
  80.9 0.0 collective-permute-done.8.refs_1_
  80.9 0.0 collective-permute-done.9.refs_2_
  81.0 0.0 collective-permute-done.10.refs_3_
  81.0 2.8 %near_rows.1.refs_0_ = f32[8,8,256]{2,1,0:T(8,128)S(1)} custom-call(s32[10]{0:T(128)S(1)} %pad_add_fusion.info_ref, bf16[1,8192]{1,0:T(2,128)(2,1)S(1)} %copy-done.2, f32[8,8,256]{2,1,0:T(8,128)S(1)} %get-tuple-element.104.earlier_ref, bf16[2,4,8,1024]{3,2,1,0:T(8,128)(2,1)S(1)} %collective-permute-done.7.refs_0_, ...), custom_call_target="tpu_custom_call" | custom-call | flops 1 | bytes 1 | tf_op jit(solution)/shard_map/near_rows/pallas_call | solution.py:282
  83.8 0.6 collective-permute-start.11
  84.4 2.9 %rows.1 = bf16[40,8,2048]{2,1,0:T(8,128)(2,1)} custom-call(s32[10]{0:T(128)S(1)} %pad_add_fusion.info_ref, bf16[16,3,8,1024]{3,2,1,0:T(8,128)(2,1)} %get-tuple-element.98.slots_ref, bf16[2,4,8,1024]{3,2,1,0:T(8,128)(2,1)S(1)} %collective-permute-done.7.refs_0_, bf16[2,4,8,1024]{3,2,1,0:T(8,128)(2,1)S(1)} %collective-permute-done.8.refs_1_, ...), custom_call_target="tpu_custom_call" | custom-call | flops 1 | bytes 1 | tf_op jit(solution)/shard_map/rows/pallas_call | solution.py:623
  87.3 0.8 collective-permute-done.11.refs_1_
  88.1 1.4 %combine_parts.3 = (bf16[1,8192]{1,0:T(2,128)(2,1)}, f32[8,128]{1,0:T(8,128)}) custom-call(s32[10]{0:T(128)S(1)} %pad_add_fusion.info_ref, f32[8,8,256]{2,1,0:T(8,128)S(1)} %near_rows.1.refs_0_, f32[8,8,256]{2,1,0:T(8,128)S(1)} %collective-permute-done.11.refs_1_), custom_call_target="tpu_custom_call" | custom-call | flops 1 | bytes 1 | tf_op jit(solution)/shard_map/combine_parts/pallas_call | solution.py:328
Async XLA Ops:
  2.0 39.2 %collective-permute-start.3 = (bf16[2,6,8,1024]{3,2,1,0:T(8,128)(2,1)S(1)}, bf16[2,6,8,1024]{3,2,1,0:T(8,128)(2,1)S(1)}, u32[]{:S(2)}, u32[]{:S(2)}) collective-permute-start(bf16[2,6,8,1024]{3,2,1,0:T(8,128)(2,1)S(1)} %get-tuple-element.92), channel_id=1, source_target_pairs={{0,16},{2,18},{4,20},{6,22},{8,24},{10,26},{12,28},{14,30},{1,17},... | collective-permute-start | bytes 589832 | tf_op jit(solution)/shard_map/ppermute | solution.py:487
  3.3 39.2 %collective-permute-start.4 = (bf16[2,6,8,1024]{3,2,1,0:T(8,128)(2,1)S(1)}, bf16[2,6,8,1024]{3,2,1,0:T(8,128)(2,1)S(1)}, u32[]{:S(2)}, u32[]{:S(2)}) collective-permute-start(bf16[2,6,8,1024]{3,2,1,0:T(8,128)(2,1)S(1)} %get-tuple-element.93), channel_id=1, source_target_pairs={{0,20},{2,22},{4,24},{6,26},{8,28},{10,30},{12,16},{14,18},{1,21},... | collective-permute-start | bytes 589832 | tf_op jit(solution)/shard_map/ppermute | solution.py:487
  4.6 39.2 %collective-permute-start.5 = (bf16[2,6,8,1024]{3,2,1,0:T(8,128)(2,1)S(1)}, bf16[2,6,8,1024]{3,2,1,0:T(8,128)(2,1)S(1)}, u32[]{:S(2)}, u32[]{:S(2)}) collective-permute-start(bf16[2,6,8,1024]{3,2,1,0:T(8,128)(2,1)S(1)} %get-tuple-element.94), channel_id=1, source_target_pairs={{0,24},{2,26},{4,28},{6,30},{8,16},{10,18},{12,20},{14,22},{1,25},... | collective-permute-start | bytes 589832 | tf_op jit(solution)/shard_map/ppermute | solution.py:487
  5.9 39.2 %collective-permute-start.6 = (bf16[2,6,8,1024]{3,2,1,0:T(8,128)(2,1)S(1)}, bf16[2,6,8,1024]{3,2,1,0:T(8,128)(2,1)S(1)}, u32[]{:S(2)}, u32[]{:S(2)}) collective-permute-start(bf16[2,6,8,1024]{3,2,1,0:T(8,128)(2,1)S(1)} %get-tuple-element.95), channel_id=1, source_target_pairs={{0,28},{2,30},{4,16},{6,18},{8,20},{10,22},{12,24},{14,26},{1,29},... | collective-permute-start | bytes 589832 | tf_op jit(solution)/shard_map/ppermute | solution.py:487
  7.9 37.3 %copy-start.2 = (bf16[1,8192]{1,0:T(2,128)(2,1)S(1)}, bf16[1,8192]{1,0:T(2,128)(2,1)}, u32[]{:S(2)}) copy-start(bf16[1,8192]{1,0:T(2,128)(2,1)} %q_ref.1) | copy-start | bytes 49156
  7.9 29.3 %all-to-all-start = ((bf16[16,2,8,1024]{3,2,1,0:T(8,128)(2,1)}), bf16[16,2,8,1024]{3,2,1,0:T(8,128)(2,1)S(1)}, u32[]{:S(2)}, u32[]{:S(2)}) async-start(bf16[16,2,8,1024]{3,2,1,0:T(8,128)(2,1)} %bitcast.rest_0_), calls=%async_computation | async-start | bytes 1048576 | tf_op jit(solution)/shard_map/cond/branch_1_fun/all_to_all | solution.py:493
  37.2 0.7 copy-start.1
  38.5 0.7 collective-permute-start
  39.9 41.1 %collective-permute-start.7 = (bf16[2,4,8,1024]{3,2,1,0:T(8,128)(2,1)S(1)}, bf16[2,4,8,1024]{3,2,1,0:T(8,128)(2,1)S(1)}, u32[]{:S(2)}, u32[]{:S(2)}) collective-permute-start(bf16[2,4,8,1024]{3,2,1,0:T(8,128)(2,1)S(1)} %get-tuple-element.99), channel_id=1, source_target_pairs={{0,16},{2,18},{4,20},{6,22},{8,24},{10,26},{12,28},{14,30},{1,17},... | collective-permute-start | bytes 393224 | tf_op jit(solution)/shard_map/ppermute | solution.py:487
  41.2 39.8 %collective-permute-start.8 = (bf16[2,4,8,1024]{3,2,1,0:T(8,128)(2,1)S(1)}, bf16[2,4,8,1024]{3,2,1,0:T(8,128)(2,1)S(1)}, u32[]{:S(2)}, u32[]{:S(2)}) collective-permute-start(bf16[2,4,8,1024]{3,2,1,0:T(8,128)(2,1)S(1)} %get-tuple-element.100), channel_id=1, source_target_pairs={{0,20},{2,22},{4,24},{6,26},{8,28},{10,30},{12,16},{14,18},{1,21},... | collective-permute-start | bytes 393224 | tf_op jit(solution)/shard_map/ppermute | solution.py:487
  42.5 38.5 %collective-permute-start.9 = (bf16[2,4,8,1024]{3,2,1,0:T(8,128)(2,1)S(1)}, bf16[2,4,8,1024]{3,2,1,0:T(8,128)(2,1)S(1)}, u32[]{:S(2)}, u32[]{:S(2)}) collective-permute-start(bf16[2,4,8,1024]{3,2,1,0:T(8,128)(2,1)S(1)} %get-tuple-element.101), channel_id=1, source_target_pairs={{0,24},{2,26},{4,28},{6,30},{8,16},{10,18},{12,20},{14,22},{1,25},... | collective-permute-start | bytes 393224 | tf_op jit(solution)/shard_map/ppermute | solution.py:487
  43.8 37.2 %collective-permute-start.10 = (bf16[2,4,8,1024]{3,2,1,0:T(8,128)(2,1)S(1)}, bf16[2,4,8,1024]{3,2,1,0:T(8,128)(2,1)S(1)}, u32[]{:S(2)}, u32[]{:S(2)}) collective-permute-start(bf16[2,4,8,1024]{3,2,1,0:T(8,128)(2,1)S(1)} %get-tuple-element.102), channel_id=1, source_target_pairs={{0,28},{2,30},{4,16},{6,18},{8,20},{10,22},{12,24},{14,26},{1,29},... | collective-permute-start | bytes 393224 | tf_op jit(solution)/shard_map/ppermute | solution.py:487
  47.9 3.6 %collective-permute-start.1 = (bf16[4,2,3,8,1024]{4,3,2,1,0:T(8,128)(2,1)S(1)}, bf16[4,2,3,8,1024]{4,3,2,1,0:T(8,128)(2,1)S(1)}, u32[]{:S(2)}, u32[]{:S(2)}) collective-permute-start(bf16[4,2,3,8,1024]{4,3,2,1,0:T(8,128)(2,1)S(1)} %get-tuple-element.64), channel_id=1, source_target_pairs={{16,18},{18,16},{20,22},{22,20},{24,26},{26,24},{28,30},{30,28},{1... | collective-permute-start | bytes 1179656 | tf_op jit(solution)/shard_map/cond/branch_1_fun/ppermute | solution.py:490
  53.1 24.0 %all-to-all-start.1 = ((bf16[16,3,8,1024]{3,2,1,0:T(8,128)(2,1)}), bf16[16,3,8,1024]{3,2,1,0:T(8,128)(2,1)}, u32[]{:S(2)}, u32[]{:S(2)}) async-start(bf16[16,3,8,1024]{3,2,1,0:T(8,128)(2,1)} %relay_slots.1.rest_1_), calls=%async_computation.1 | async-start | bytes 1572864 | tf_op jit(solution)/shard_map/cond/branch_1_fun/all_to_all | solution.py:493
  58.0 16.7 %collective-permute-start.2 = (f32[8,32,256]{2,1,0:T(8,128)S(1)}, f32[8,32,256]{2,1,0:T(8,128)S(1)}, u32[]{:S(2)}, u32[]{:S(2)}) collective-permute-start(f32[8,32,256]{2,1,0:T(8,128)S(1)} %get-tuple-element.66.refs_0_), channel_id=1, source_target_pairs={{0,1},{1,0},{2,3},{3,2},{4,5},{5,4},{6,7},{7,6},{8,9},{9,8},{10,11... | collective-permute-start | bytes 786440 | tf_op jit(solution)/shard_map/cond/branch_1_fun/ppermute | solution.py:668
  74.7 0.7 copy-start
  83.8 4.3 %collective-permute-start.11 = (f32[8,8,256]{2,1,0:T(8,128)S(1)}, f32[8,8,256]{2,1,0:T(8,128)S(1)}, u32[]{:S(2)}, u32[]{:S(2)}) collective-permute-start(f32[8,8,256]{2,1,0:T(8,128)S(1)} %near_rows.1.refs_0_), channel_id=1, source_target_pairs={{0,1},{1,0},{2,3},{3,2},{4,5},{5,4},{6,7},{7,6},{8,9},{9,8},{10,11... | collective-permute-start | bytes 196616 | tf_op jit(solution)/shard_map/ppermute | solution.py:668

commit v5 on v4

--- a/solution.py
+++ b/solution.py
@@ -171,10 +171,6 @@
                 count = count + jnp.where(valid, 1.0, 0.0)
             count_ref[r * GROUP : (r + 1) * GROUP] = count
 
-    @pl.when(on_prefill(info_ref))
-    def _():
-        out_ref[...] = jnp.zeros_like(out_ref)
-
     @pl.when(jnp.logical_not(on_prefill(info_ref)))
     def _():
         count = count_ref[...]
@@ -233,16 +229,20 @@
 def rows_part(queries, rows, out_ref, earlier_ref):
     block = queries[...].astype(jnp.float32)
     heads = rows[0].shape[1] // (2 * HEADDIM)
+    places = [(rows[head // heads], 2 * (head % heads) * HEADDIM) for head in range(KVHEADS)]
+    scores = [
+        dot_t(head_queries(block, head), held[:, start : start + HEADDIM]) * SCALE
+        for head, (held, start) in enumerate(places)
+    ]
+    peaks = [jnp.max(score, axis=1, keepdims=True) for score in scores]
+    weights = [jnp.exp(score - peak) for score, peak in zip(scores, peaks)]
+    totals = [jnp.sum(weight, axis=1, keepdims=True) for weight in weights]
+    mixes = [
+        dot(weight.astype(jnp.bfloat16), held[:, start + HEADDIM : start + 2 * HEADDIM])
+        for weight, (held, start) in zip(weights, places)
+    ]
     for head in range(KVHEADS):
-        held = rows[head // heads]
-        start = 2 * (head % heads) * HEADDIM
-        scores = dot_t(head_queries(block, head), held[:, start : start + HEADDIM]) * SCALE
-        peak = jnp.max(scores, axis=1, keepdims=True)
-        weights = jnp.exp(scores - peak)
-        total = jnp.sum(weights, axis=1, keepdims=True)
-        values = held[:, start + HEADDIM : start + 2 * HEADDIM]
-        mixed = dot(weights.astype(jnp.bfloat16), values)
-        store_part(out_ref, head, mixed, peak, total)
+        store_part(out_ref, head, mixes[head], peaks[head], totals[head])
         if earlier_ref is not None:
             store_part(out_ref, head, *merged([out_ref[head], earlier_ref[head]]))
 
@@ -469,11 +469,11 @@
             copy.wait()
 
 
-def two_way_handoff(pairs, info, always, arrival_query, prompt_part, cached, combined):
+def two_way_handoff(pairs, info, always, arrival_query, prompt_part, cached, exchanged):
     half = 2 * PAIRS
     rows, width = pairs.shape
     units = rows // (2 * UNIT)
-    far_all = -(-units * 3 // (5 * half)) * half
+    far_all = units * 2 // (5 * half) * half
     near_all = units - far_all
     near, far = near_all // half, far_all // half
     block = (UNIT, width)
@@ -494,14 +494,17 @@
             array, ("inst", "tp"), 0, 0, axis_index_groups=groups, tiled=True
         )
 
-    def cut(pre, sources, targets):
+    def cut_near(pre, sources, targets):
+        return [
+            (sources[0].at[pl.ds(tau * units, near_all)], targets[0].at[tau]) for tau in range(2)
+        ]
+
+    def cut_far(pre, sources, targets):
         plan = []
         for s in range(PAIRS):
             start = near_all + lax.rem(lax.div(order(pre), 2) + s, PAIRS) * (2 * far)
             for tau in range(2):
                 plan.append((sources[0].at[pl.ds(tau * units + start, 2 * far)], targets[s].at[tau]))
-        for tau in range(2):
-            plan.append((sources[0].at[pl.ds(tau * units, near_all)], targets[PAIRS].at[tau]))
         return plan
 
     def for_neighbour(pre, sources, targets):
@@ -537,20 +540,16 @@
 
     near_shape = (2, 2 * near) + block
 
-    def first_stage(slots):
-        parts, mark = cached([slots])
-        prompt, mark = prompt_part(0, None, [mark])
-        spread = spread_out(slots)
+    def first_stage(spread, *marks):
         (outgoing,) = copies(
-            for_neighbour, 2 * PAIRS, info, [spread], [(PAIRS, 2, near) + block], "for_neighbour", [mark]
+            for_neighbour, 2 * PAIRS, info, [spread], [(PAIRS, 2, near) + block], "for_neighbour", marks
         )
         incoming = beside(outgoing, 0)
-        near_parts = copies(
+        return copies(
             for_receivers, 4 * PAIRS, info, [spread, incoming], [near_shape] * PAIRS, "for_receivers"
         )
-        return *near_parts, prompt, parts
-
-    def second_stage(prompt, parts, *far_here):
+
+    def second_stage(prompt, part, other, *far_here):
         keep, give = copies(
             split,
             4 * PAIRS,
@@ -577,7 +576,7 @@
             name="relay_slots",
         )(info, keep, taken)
         prompt, mark = prompt_part(1, prompt, [slots])
-        decode_out = combined(parts, [mark])
+        decode_out, _ = combine_parts(info, [part, other], [mark])
         slots = spread_out(slots)
         arrival = arrival_part(
             far_rows_kernel,
@@ -597,20 +596,20 @@
 
         return lax.cond(always, lambda *operands: tuple(stage(*operands)), never, *operands)
 
-    *far_parts, near_rows = copies(
-        cut,
-        2 * PAIRS + 2,
-        info,
-        [by_unit],
-        [(2, 2 * far) + block] * PAIRS + [(2, near_all) + block],
-        "cut_rows",
-        stage=True,
+    (near_rows,) = copies(
+        cut_near, 2, info, [by_unit], [(2, near_all) + block], "cut_near", stage=True
     )
+    far_parts = copies(
+        cut_far, 2 * PAIRS, info, [by_unit], [(2, 2 * far) + block] * PAIRS, "cut_far", [near_rows]
+    )
+    spread = spread_out(near_rows.reshape((2 * half, near) + block))
     far_here = [crossing(part, s) for s, part in enumerate(far_parts)]
-    near_rows = near_rows.reshape((2 * half, near) + block)
-    *near_parts, prompt, parts = staged(first_stage, near_rows)
-    near_here = [crossing(part, s) for s, part in enumerate(near_parts)]
-    prompt, slots, decode_out, arrival = staged(second_stage, prompt, parts, *far_here)
+    part, mark = cached([near_rows])
+    prompt, mark = prompt_part(0, None, [mark])
+    other = exchanged(part)
+    near_parts = staged(first_stage, spread, mark, other)
+    near_here = [crossing(near_part, s) for s, near_part in enumerate(near_parts)]
+    prompt, slots, decode_out, arrival = staged(second_stage, prompt, part, other, *far_here)
     arrival = arrival_part(
         near_rows_kernel,
         info,
@@ -638,7 +637,8 @@
         cost_estimate=COST,
         name="rows",
     )(info, slots, *near_here)
-    return prompt, handed.reshape(rows // 2, 2 * width), decode_out, combined(arrival)
+    arrival_out, _ = combine_parts(info, [arrival, exchanged(arrival)])
+    return prompt, handed.reshape(rows // 2, 2 * width), decode_out, arrival_out
 
 
 def shards(
@@ -663,12 +663,11 @@
     def cached(after=()):
         return cache_attention(info, page_table, lengths, decode_query, by_token, page_len, after)
 
-    def combined(part, after=()):
-        if tp_count == 2:
-            parts = [part, lax.ppermute(part, "tp", [(0, 1), (1, 0)])]
-        else:
-            parts = [lax.all_gather(part, "tp")]
-        return combine_parts(info, parts, after)[0]
+    def exchanged(part):
+        return lax.ppermute(part, "tp", [(0, 1), (1, 0)])
+
+    def combined(part):
+        return combine_parts(info, [lax.all_gather(part, "tp")])[0]
 
     heads = GROUP // 2
     steps = prompt_query.shape[1] // (heads * HEADDIM)
@@ -680,7 +679,7 @@
 
     row_units = prompt_pairs.shape[0] // (2 * UNIT)
     if inst_count == 4 * PAIRS and tp_count == 2 and row_units == 5 * half and steps == 8:
-        cuts = (0, 4, 8)
+        cuts = (0, 2, 8)
         return two_way_handoff(
             prompt_pairs,
             info,
@@ -688,7 +687,7 @@
             arrival_query,
             lambda n, earlier, after: prompt_part(cuts[n], cuts[n + 1], earlier, after),
             cached,
-            combined,
+            exchanged,
         )
     handed = relay_handoff(prompt_pairs, assignment, inst_count)
     arrival = arrival_part(

time: 90.3 us -> 112 us (1.24)
  the two profiles are of different devices: /device:TPU:24 before, /device:TPU:0 now
where the time goes in v5:
time: 112 us; the launch traced here: 111 us
  starting transfers between devices  50.5 us (45%)
  Pallas kernels  40.3 us (36%)
  waiting for transfers between devices  17.5 us (16%)
    all_to_all x2, starting transfers between devices, spread_out(): lax.all_to_all(array, ('inst', 'tp'), 0, 0, axis_index_groups=groups, til...  28.9 us
    pallas_call x2, Pallas kernels, prompt_attention(): pl.pallas_call(functools.partial(prompt_kernel, heads), out_shape=(jax.Sh...  24 us
    ppermute x8, starting transfers between devices, crossing(): return lax.ppermute(array, 'inst', hops)  15.2 us
    ppermute x8, waiting for transfers between devices, crossing(): return lax.ppermute(array, 'inst', hops)  15.2 us
    pallas_call x5, Pallas kernels, copies(): pl.pallas_call(functools.partial(copy_kernel, plan, side, (len(operands),...  7.57 us
    ppermute x2, starting transfers between devices, exchanged(): return lax.ppermute(part, 'tp', [(0, 1), (1, 0)])  3.79 us
    ppermute x2, starting transfers between devices, beside(): lax.ppermute(array, 'inst', [(base + i, base + (i ^ 1)) for i in range(ha...  2.6 us
    pallas_call x2, Pallas kernels, combine_parts(): pl.pallas_call(functools.partial(combine_kernel, len(parts)), out_shape=(...  2.36 us
  transfers between devices with their start and end apart: 14, of which 3 were waited for; matrix products, arithmetic and copies ran while one was open for 0% of the time, Pallas kernels for 32%

profile of v5, /device:TPU:0, one launch (start us, length us, event | category | flops | bytes accessed | tf_op | source)
XLA Modules:
  0.0 110.8 jit_solution(4630554622811690111)
XLA Ops:
  0.6 0.0 copy-start.1
  0.6 0.8 pad_add_fusion.info_ref
  1.5 2.7 %cut_near.1.rest_0_.refs_1_ = bf16[2,24,8,1024]{3,2,1,0:T(8,128)(2,1)} custom-call(s32[10]{0:T(128)S(1)} %pad_add_fusion.info_ref, bf16[80,8,1024]{2,1,0:T(8,128)(2,1)} %bitcast.8), custom_call_target="tpu_custom_call" | custom-call | flops 1 | bytes 1 | tf_op jit(solution)/shard_map/cut_near/pallas_call | solution.py:390
  4.2 6.3 %all-to-all-start.1 = ((bf16[16,3,8,1024]{3,2,1,0:T(8,128)(2,1)}), bf16[16,3,8,1024]{3,2,1,0:T(8,128)(2,1)S(1)}, u32[]{:S(2)}, u32[]{:S(2)}) async-start(bf16[16,3,8,1024]{3,2,1,0:T(8,128)(2,1)} %bitcast.5), calls=%async_computation.1 | async-start | bytes 1572864 | tf_op jit(solution)/shard_map/all_to_all | solution.py:493
  10.5 0.0 copy-start.5
  10.6 2.0 %cache_attention.1 = (f32[8,32,256]{2,1,0:T(8,128)S(1)}, f32[8,128]{1,0:T(8,128)}) custom-call(s32[10]{0:T(128)S(1)} %pad_add_fusion.info_ref, s32[4,8]{1,0:T(4,128)} %table_ref.1, s32[4]{0:T(128)} %lengths_ref.1, bf16[4,8192]{1,0:T(4,128)(2,1)} %q_ref.3, bf16[320,2048]{1,0:T(8,128)(2,1)} %bitcast.10, bf16[2,24,8,1024]{3,2,1,0:T(8,128)(2,1)} %cut_near.1.rest_0_.refs_1_), custom_call_target="tpu_custom_call" | custom-call | flops 1 | bytes 1 | tf_op jit(solution)/shard_map/cache_attention/pallas_call | solution.py:201
  12.5 0.0 copy-start.2
  12.5 1.9 %collective-permute-start.6 = (f32[8,32,256]{2,1,0:T(8,128)S(1)}, f32[8,32,256]{2,1,0:T(8,128)S(1)}, u32[]{:S(2)}, u32[]{:S(2)}) collective-permute-start(f32[8,32,256]{2,1,0:T(8,128)S(1)} %get-tuple-element.78), channel_id=1, source_target_pairs={{0,1},{1,0},{2,3},{3,2},{4,5},{5,4},{6,7},{7,6},{8,9},{9,8},{10,11... | collective-permute-start | bytes 786440 | tf_op jit(solution)/shard_map/ppermute | solution.py:667
  14.5 0.0 copy-done.1
  14.5 1.3 %cut_far.1 = (bf16[2,4,8,1024]{3,2,1,0:T(8,128)(2,1)S(1)}, bf16[2,4,8,1024]{3,2,1,0:T(8,128)(2,1)S(1)}, bf16[2,4,8,1024]{3,2,1,0:T(8,128)(2,1)S(1)}, bf16[2,4,8,1024]{3,2,1,0:T(8,128)(2,1)S(1)}) custom-call(s32[10]{0:T(128)S(1)} %pad_add_fusion.info_ref, bf16[80,8,1024]{2,1,0:T(8,128)(2,1)S(1)} %bitcast.9, bf16[2,24,8,1024]{3,2,1,0:T(8,128)(2,1)} %cut_near.1.rest_0_.refs_1_), custom_call_target="tpu_custom_call" | custom-call | flops 1 | bytes 1 | tf_op jit(solution)/shard_map/cut_far/pallas_call | solution.py:390
  15.8 4.0 %collective-permute-start.2 = (bf16[2,4,8,1024]{3,2,1,0:T(8,128)(2,1)S(1)}, bf16[2,4,8,1024]{3,2,1,0:T(8,128)(2,1)S(1)}, u32[]{:S(2)}, u32[]{:S(2)}) collective-permute-start(bf16[2,4,8,1024]{3,2,1,0:T(8,128)(2,1)S(1)} %get-tuple-element.74), channel_id=1, source_target_pairs={{0,16},{2,18},{4,20},{6,22},{8,24},{10,26},{12,28},{14,30},{1,17},... | collective-permute-start | bytes 393224 | tf_op jit(solution)/shard_map/ppermute | solution.py:487
  19.7 2.9 %collective-permute-start.3 = (bf16[2,4,8,1024]{3,2,1,0:T(8,128)(2,1)S(1)}, bf16[2,4,8,1024]{3,2,1,0:T(8,128)(2,1)}, u32[]{:S(2)}, u32[]{:S(2)}) collective-permute-start(bf16[2,4,8,1024]{3,2,1,0:T(8,128)(2,1)S(1)} %get-tuple-element.75), channel_id=1, source_target_pairs={{0,20},{2,22},{4,24},{6,26},{8,28},{10,30},{12,16},{14,18},{1,21},... | collective-permute-start | bytes 393224 | tf_op jit(solution)/shard_map/ppermute | solution.py:487
  22.6 1.9 %collective-permute-start.4 = (bf16[2,4,8,1024]{3,2,1,0:T(8,128)(2,1)S(1)}, bf16[2,4,8,1024]{3,2,1,0:T(8,128)(2,1)}, u32[]{:S(2)}, u32[]{:S(2)}) collective-permute-start(bf16[2,4,8,1024]{3,2,1,0:T(8,128)(2,1)S(1)} %get-tuple-element.76), channel_id=1, source_target_pairs={{0,24},{2,26},{4,28},{6,30},{8,16},{10,18},{12,20},{14,22},{1,25},... | collective-permute-start | bytes 393224 | tf_op jit(solution)/shard_map/ppermute | solution.py:487
  24.5 7.2 %prompt_attention.3 = (bf16[640,4096]{1,0:T(8,128)(2,1)}, f32[8,128]{1,0:T(8,128)S(1)}) custom-call(s32[10]{0:T(128)S(1)} %pad_add_fusion.info_ref, bf16[640,4096]{1,0:T(8,128)(2,1)} %q_ref.4, bf16[640,1024]{1,0:T(8,128)(2,1)S(1)} %copy-done.1, f32[8,128]{1,0:T(8,128)} %get-tuple-element.72.rest_0_), custom_call_target="tpu_custom_call" | custom-call | flops 1 | bytes 1 | tf_op jit(solution)/shard_map/prompt_attention/pallas_call | solution.py:112
  31.7 0.0 copy-done.5
  31.8 0.0 collective-permute-done.6
  31.8 0.0 all-to-all-done.1
  31.8 0.0 copy-done.2
  31.8 6.5 %conditional.3 = ((bf16[2,6,8,1024]{3,2,1,0:T(8,128)(2,1)}, bf16[2,6,8,1024]{3,2,1,0:T(8,128)(2,1)}, bf16[2,6,8,1024]{3,2,1,0:T(8,128)(2,1)}, bf16[2,6,8,1024]{3,2,1,0:T(8,128)(2,1)})) conditional(s32[]{:T(128)} %bitcast, () %tuple.24, (s32[10]{0:T(128)S(1)}, bf16[16,3,8,1024]{3,2,1,0:T(8,128)(2,1)S(1)}, f32[8,128]{1,0:T(8,128)S(1)}, ...), branch_computations={%region_2.0_spmd, %region_3.0_spmd} | conditional | flops 2 | bytes 1572914 | solution.py:597
  31.8 1.2 %for_neighbour.1 = bf16[4,2,3,8,1024]{4,3,2,1,0:T(8,128)(2,1)S(1)} custom-call(s32[10]{0:T(128)S(1)} %get-tuple-element.47.info_ref, bf16[16,3,8,1024]{3,2,1,0:T(8,128)(2,1)S(1)} %get-tuple-element.48.refs_0_, f32[8,128]{1,0:T(8,128)S(1)} %get-tuple-element.49.refs_1_, f32[8,32,256]{2,1,0:T(8,128)S(1)} %get-tuple-element.50.refs_2_), custom_call_target="tpu_custom_call" | custom-call | flops 1 | bytes 1 | tf_op jit(solution)/shard_map/cond/branch_1_fun/for_neighbour/pallas_call | solution.py:390
  33.0 1.9 %collective-permute-start.1 = (bf16[4,2,3,8,1024]{4,3,2,1,0:T(8,128)(2,1)S(1)}, bf16[4,2,3,8,1024]{4,3,2,1,0:T(8,128)(2,1)S(1)}, u32[]{:S(2)}, u32[]{:S(2)}) collective-permute-start(bf16[4,2,3,8,1024]{4,3,2,1,0:T(8,128)(2,1)S(1)} %for_neighbour.1), channel_id=1, source_target_pairs={{0,2},{2,0},{4,6},{6,4},{8,10},{10,8},{12,14},{14,12},{1,3},{3,1},... | collective-permute-start | bytes 1179656 | tf_op jit(solution)/shard_map/cond/branch_1_fun/ppermute | solution.py:490
  34.9 1.7 %collective-permute-done.1.refs_1_ = bf16[4,2,3,8,1024]{4,3,2,1,0:T(8,128)(2,1)S(1)} collective-permute-done((bf16[4,2,3,8,1024]{4,3,2,1,0:T(8,128)(2,1)S(1)}, bf16[4,2,3,8,1024]{4,3,2,1,0:T(8,128)(2,1)S(1)}, u32[]{:S(2)}, u32[]{:S(2)}) %collective-permute-start.1) | collective-permute-done | bytes 393248 | tf_op jit(solution)/shard_map/cond/branch_1_fun/ppermute | solution.py:490
  36.6 1.6 %for_receivers.1 = (bf16[2,6,8,1024]{3,2,1,0:T(8,128)(2,1)}, bf16[2,6,8,1024]{3,2,1,0:T(8,128)(2,1)}, bf16[2,6,8,1024]{3,2,1,0:T(8,128)(2,1)}, bf16[2,6,8,1024]{3,2,1,0:T(8,128)(2,1)}) custom-call(s32[10]{0:T(128)S(1)} %get-tuple-element.47.info_ref, bf16[16,3,8,1024]{3,2,1,0:T(8,128)(2,1)S(1)} %get-tuple-element.48.refs_0_, ...), custom_call_target="tpu_custom_call" | custom-call | flops 1 | bytes 1 | tf_op jit(solution)/shard_map/cond/branch_1_fun/for_receivers/pallas_call | solution.py:390
  38.3 1.3 %collective-permute-start.7 = (bf16[2,6,8,1024]{3,2,1,0:T(8,128)(2,1)}, bf16[2,6,8,1024]{3,2,1,0:T(8,128)(2,1)S(1)}, u32[]{:S(2)}, u32[]{:S(2)}) collective-permute-start(bf16[2,6,8,1024]{3,2,1,0:T(8,128)(2,1)} %get-tuple-element.82), channel_id=1, source_target_pairs={{0,16},{2,18},{4,20},{6,22},{8,24},{10,26},{12,28},{14,30},{1,17},... | collective-permute-start | bytes 589832 | tf_op jit(solution)/shard_map/ppermute | solution.py:487
  39.6 1.3 %collective-permute-start.8 = (bf16[2,6,8,1024]{3,2,1,0:T(8,128)(2,1)}, bf16[2,6,8,1024]{3,2,1,0:T(8,128)(2,1)S(1)}, u32[]{:S(2)}, u32[]{:S(2)}) collective-permute-start(bf16[2,6,8,1024]{3,2,1,0:T(8,128)(2,1)} %get-tuple-element.83), channel_id=1, source_target_pairs={{0,20},{2,22},{4,24},{6,26},{8,28},{10,30},{12,16},{14,18},{1,21},... | collective-permute-start | bytes 589832 | tf_op jit(solution)/shard_map/ppermute | solution.py:487
  40.9 0.0 collective-permute-done.2
  40.9 1.3 %collective-permute-start.9 = (bf16[2,6,8,1024]{3,2,1,0:T(8,128)(2,1)}, bf16[2,6,8,1024]{3,2,1,0:T(8,128)(2,1)S(1)}, u32[]{:S(2)}, u32[]{:S(2)}) collective-permute-start(bf16[2,6,8,1024]{3,2,1,0:T(8,128)(2,1)} %get-tuple-element.84), channel_id=1, source_target_pairs={{0,24},{2,26},{4,28},{6,30},{8,16},{10,18},{12,20},{14,22},{1,25},... | collective-permute-start | bytes 589832 | tf_op jit(solution)/shard_map/ppermute | solution.py:487
  42.2 0.0 collective-permute-done.3
  42.2 1.3 %collective-permute-start.10 = (bf16[2,6,8,1024]{3,2,1,0:T(8,128)(2,1)}, bf16[2,6,8,1024]{3,2,1,0:T(8,128)(2,1)S(1)}, u32[]{:S(2)}, u32[]{:S(2)}) collective-permute-start(bf16[2,6,8,1024]{3,2,1,0:T(8,128)(2,1)} %get-tuple-element.85), channel_id=1, source_target_pairs={{0,28},{2,30},{4,16},{6,18},{8,20},{10,22},{12,24},{14,26},{1,29},... | collective-permute-start | bytes 589832 | tf_op jit(solution)/shard_map/ppermute | solution.py:487
  43.5 0.0 collective-permute-done.4
  43.5 1.3 %collective-permute-start.5 = (bf16[2,4,8,1024]{3,2,1,0:T(8,128)(2,1)S(1)}, bf16[2,4,8,1024]{3,2,1,0:T(8,128)(2,1)S(1)}, u32[]{:S(2)}, u32[]{:S(2)}) collective-permute-start(bf16[2,4,8,1024]{3,2,1,0:T(8,128)(2,1)S(1)} %get-tuple-element.77), channel_id=1, source_target_pairs={{0,28},{2,30},{4,16},{6,18},{8,20},{10,22},{12,24},{14,26},{1,29},... | collective-permute-start | bytes 393224 | tf_op jit(solution)/shard_map/ppermute | solution.py:487
  44.8 15.2 %collective-permute-done.5 = bf16[2,4,8,1024]{3,2,1,0:T(8,128)(2,1)S(1)} collective-permute-done((bf16[2,4,8,1024]{3,2,1,0:T(8,128)(2,1)S(1)}, bf16[2,4,8,1024]{3,2,1,0:T(8,128)(2,1)S(1)}, u32[]{:S(2)}, u32[]{:S(2)}) %collective-permute-start.5) | collective-permute-done | bytes 131104 | tf_op jit(solution)/shard_map/ppermute | solution.py:487
  60.0 43.9 %conditional.2 = (bf16[640,4096]{1,0:T(8,128)(2,1)}, bf16[16,2,8,1024]{3,2,1,0:T(8,128)(2,1)}, bf16[4,8192]{1,0:T(4,128)(2,1)}, f32[8,8,256]{2,1,0:T(8,128)S(1)}) conditional(s32[]{:T(128)} %bitcast, bf16[640,4096]{1,0:T(8,128)(2,1)} %get-tuple-element.73, (s32[10]{0:T(128)S(1)}, bf16[2,4,8,1024]{3,2,1,0:T(8,128)(2,1)S(1)}, ...), branch_computations={%region_0.0_spmd, %region_1.0_spmd} | conditional | flops 5 | bytes 3752129 | solution.py:597
  60.0 0.7 split_relays.1
  60.7 0.7 collective-permute-start
  61.4 0.0 collective-permute-done.recv_ref
  61.4 0.7 relay_slots.1.rest_1_
  62.1 22.6 %all-to-all-start = ((bf16[16,2,8,1024]{3,2,1,0:T(8,128)(2,1)}), bf16[16,2,8,1024]{3,2,1,0:T(8,128)(2,1)}, u32[]{:S(2)}, u32[]{:S(2)}) async-start(bf16[16,2,8,1024]{3,2,1,0:T(8,128)(2,1)} %relay_slots.1.rest_1_), calls=%async_computation | async-start | bytes 1048576 | tf_op jit(solution)/shard_map/cond/branch_1_fun/all_to_all | solution.py:493
  84.6 0.0 copy-start.3
  84.7 0.0 copy-start.4
  84.7 16.8 %prompt_attention.2 = (bf16[640,4096]{1,0:T(8,128)(2,1)}, f32[8,128]{1,0:T(8,128)}) custom-call(s32[10]{0:T(128)S(1)} %get-tuple-element.31.info_ref, bf16[640,4096]{1,0:T(8,128)(2,1)} %get-tuple-element.32.q_ref, bf16[640,1024]{1,0:T(8,128)(2,1)S(1)} %get-tuple-element.33.kv_ref, ...), custom_call_target="tpu_custom_call", output_to_operand_aliasing={{0}: (3, {})} | custom-call | flops 1 | bytes 1 | tf_op jit(solution)/shard_map/cond/branch_1_fun/prompt_attention/pallas_call | solution.py:112
  101.5 0.0 copy-done.3
  101.5 0.0 copy-start
  101.5 0.7 copy-done
  102.2 1.2 %combine_parts.2 = (bf16[4,8192]{1,0:T(4,128)(2,1)}, f32[8,128]{1,0:T(8,128)}) custom-call(s32[10]{0:T(128)S(1)} %get-tuple-element.31.info_ref, f32[8,32,256]{2,1,0:T(8,128)S(1)} %copy-done.3, f32[8,32,256]{2,1,0:T(8,128)S(1)} %get-tuple-element.43.refs_1_, f32[8,128]{1,0:T(8,128)S(1)} %copy-done), custom_call_target="tpu_custom_call" | custom-call | flops 1 | bytes 1 | tf_op jit(solution)/shard_map/cond/branch_1_fun/combine_parts/pallas_call | solution.py:328
  103.3 0.0 all-to-all-done.slots_ref
  103.3 0.0 copy-done.4
  103.3 0.6 far_rows.1
  103.9 0.0 collective-permute-done.7.refs_0_
  103.9 0.0 collective-permute-done.8.refs_1_
  103.9 0.0 collective-permute-done.9.refs_2_
  103.9 0.0 collective-permute-done.10.refs_3_
  104.0 1.3 %near_rows.1.refs_0_ = f32[8,8,256]{2,1,0:T(8,128)S(1)} custom-call(s32[10]{0:T(128)S(1)} %pad_add_fusion.info_ref, bf16[1,8192]{1,0:T(2,128)(2,1)} %q_ref.5, f32[8,8,256]{2,1,0:T(8,128)S(1)} %get-tuple-element.87.earlier_ref, bf16[2,6,8,1024]{3,2,1,0:T(8,128)(2,1)S(1)} %collective-permute-done.7.refs_0_, ...), custom_call_target="tpu_custom_call" | custom-call | flops 1 | bytes 1 | tf_op jit(solution)/shard_map/near_rows/pallas_call | solution.py:282
  105.3 1.9 %collective-permute-start.11 = (f32[8,8,256]{2,1,0:T(8,128)S(1)}, f32[8,8,256]{2,1,0:T(8,128)S(1)}, u32[]{:S(2)}, u32[]{:S(2)}) collective-permute-start(f32[8,8,256]{2,1,0:T(8,128)S(1)} %near_rows.1.refs_0_), channel_id=1, source_target_pairs={{0,1},{1,0},{2,3},{3,2},{4,5},{5,4},{6,7},{7,6},{8,9},{9,8},{10,11... | collective-permute-start | bytes 196616 | tf_op jit(solution)/shard_map/ppermute | solution.py:667
  107.1 1.8 %rows.1 = bf16[40,8,2048]{2,1,0:T(8,128)(2,1)} custom-call(s32[10]{0:T(128)S(1)} %pad_add_fusion.info_ref, bf16[16,2,8,1024]{3,2,1,0:T(8,128)(2,1)} %get-tuple-element.80.slots_ref, bf16[2,6,8,1024]{3,2,1,0:T(8,128)(2,1)S(1)} %collective-permute-done.7.refs_0_, bf16[2,6,8,1024]{3,2,1,0:T(8,128)(2,1)S(1)} %collective-permute-done.8.refs_1_, ...), custom_call_target="tpu_custom_call" | custom-call | flops 1 | bytes 1 | tf_op jit(solution)/shard_map/rows/pallas_call | solution.py:622
  109.0 0.6 collective-permute-done.11.refs_1_
  109.6 1.2 %combine_parts.3 = (bf16[1,8192]{1,0:T(2,128)(2,1)}, f32[8,128]{1,0:T(8,128)}) custom-call(s32[10]{0:T(128)S(1)} %pad_add_fusion.info_ref, f32[8,8,256]{2,1,0:T(8,128)S(1)} %near_rows.1.refs_0_, f32[8,8,256]{2,1,0:T(8,128)S(1)} %collective-permute-done.11.refs_1_), custom_call_target="tpu_custom_call" | custom-call | flops 1 | bytes 1 | tf_op jit(solution)/shard_map/combine_parts/pallas_call | solution.py:328
Async XLA Ops:
  0.6 13.8 %copy-start.1 = (bf16[640,1024]{1,0:T(8,128)(2,1)S(1)}, bf16[640,1024]{1,0:T(8,128)(2,1)}, u32[]{:S(2)}) copy-start(bf16[640,1024]{1,0:T(8,128)(2,1)} %kv_ref.1) | copy-start | bytes 3932164
  4.2 27.5 %all-to-all-start.1 = ((bf16[16,3,8,1024]{3,2,1,0:T(8,128)(2,1)}), bf16[16,3,8,1024]{3,2,1,0:T(8,128)(2,1)S(1)}, u32[]{:S(2)}, u32[]{:S(2)}) async-start(bf16[16,3,8,1024]{3,2,1,0:T(8,128)(2,1)} %bitcast.5), calls=%async_computation.1 | async-start | bytes 1572864 | tf_op jit(solution)/shard_map/all_to_all | solution.py:493
  10.5 21.2 %copy-start.5 = (s32[8]{0:T(128)S(1)}, s32[8]{0:T(128)}, u32[]{:S(2)}) copy-start(s32[8]{0:T(128)} %param.19) | copy-start | bytes 100
  12.5 19.3 %copy-start.2 = (f32[8,32,256]{2,1,0:T(8,128)}, f32[8,32,256]{2,1,0:T(8,128)S(1)}, u32[]{:S(2)}) copy-start(f32[8,32,256]{2,1,0:T(8,128)S(1)} %get-tuple-element.78) | copy-start | bytes 786436
  12.5 19.2 %collective-permute-start.6 = (f32[8,32,256]{2,1,0:T(8,128)S(1)}, f32[8,32,256]{2,1,0:T(8,128)S(1)}, u32[]{:S(2)}, u32[]{:S(2)}) collective-permute-start(f32[8,32,256]{2,1,0:T(8,128)S(1)} %get-tuple-element.78), channel_id=1, source_target_pairs={{0,1},{1,0},{2,3},{3,2},{4,5},{5,4},{6,7},{7,6},{8,9},{9,8},{10,11... | collective-permute-start | bytes 786440 | tf_op jit(solution)/shard_map/ppermute | solution.py:667
  15.8 25.1 %collective-permute-start.2 = (bf16[2,4,8,1024]{3,2,1,0:T(8,128)(2,1)S(1)}, bf16[2,4,8,1024]{3,2,1,0:T(8,128)(2,1)S(1)}, u32[]{:S(2)}, u32[]{:S(2)}) collective-permute-start(bf16[2,4,8,1024]{3,2,1,0:T(8,128)(2,1)S(1)} %get-tuple-element.74), channel_id=1, source_target_pairs={{0,16},{2,18},{4,20},{6,22},{8,24},{10,26},{12,28},{14,30},{1,17},... | collective-permute-start | bytes 393224 | tf_op jit(solution)/shard_map/ppermute | solution.py:487
  19.7 22.5 %collective-permute-start.3 = (bf16[2,4,8,1024]{3,2,1,0:T(8,128)(2,1)S(1)}, bf16[2,4,8,1024]{3,2,1,0:T(8,128)(2,1)}, u32[]{:S(2)}, u32[]{:S(2)}) collective-permute-start(bf16[2,4,8,1024]{3,2,1,0:T(8,128)(2,1)S(1)} %get-tuple-element.75), channel_id=1, source_target_pairs={{0,20},{2,22},{4,24},{6,26},{8,28},{10,30},{12,16},{14,18},{1,21},... | collective-permute-start | bytes 393224 | tf_op jit(solution)/shard_map/ppermute | solution.py:487
  22.6 20.9 %collective-permute-start.4 = (bf16[2,4,8,1024]{3,2,1,0:T(8,128)(2,1)S(1)}, bf16[2,4,8,1024]{3,2,1,0:T(8,128)(2,1)}, u32[]{:S(2)}, u32[]{:S(2)}) collective-permute-start(bf16[2,4,8,1024]{3,2,1,0:T(8,128)(2,1)S(1)} %get-tuple-element.76), channel_id=1, source_target_pairs={{0,24},{2,26},{4,28},{6,30},{8,16},{10,18},{12,20},{14,22},{1,25},... | collective-permute-start | bytes 393224 | tf_op jit(solution)/shard_map/ppermute | solution.py:487
  33.0 3.6 %collective-permute-start.1 = (bf16[4,2,3,8,1024]{4,3,2,1,0:T(8,128)(2,1)S(1)}, bf16[4,2,3,8,1024]{4,3,2,1,0:T(8,128)(2,1)S(1)}, u32[]{:S(2)}, u32[]{:S(2)}) collective-permute-start(bf16[4,2,3,8,1024]{4,3,2,1,0:T(8,128)(2,1)S(1)} %for_neighbour.1), channel_id=1, source_target_pairs={{0,2},{2,0},{4,6},{6,4},{8,10},{10,8},{12,14},{14,12},{1,3},{3,1},... | collective-permute-start | bytes 1179656 | tf_op jit(solution)/shard_map/cond/branch_1_fun/ppermute | solution.py:490
  38.3 65.7 %collective-permute-start.7 = (bf16[2,6,8,1024]{3,2,1,0:T(8,128)(2,1)}, bf16[2,6,8,1024]{3,2,1,0:T(8,128)(2,1)S(1)}, u32[]{:S(2)}, u32[]{:S(2)}) collective-permute-start(bf16[2,6,8,1024]{3,2,1,0:T(8,128)(2,1)} %get-tuple-element.82), channel_id=1, source_target_pairs={{0,16},{2,18},{4,20},{6,22},{8,24},{10,26},{12,28},{14,30},{1,17},... | collective-permute-start | bytes 589832 | tf_op jit(solution)/shard_map/ppermute | solution.py:487
  39.6 64.4 %collective-permute-start.8 = (bf16[2,6,8,1024]{3,2,1,0:T(8,128)(2,1)}, bf16[2,6,8,1024]{3,2,1,0:T(8,128)(2,1)S(1)}, u32[]{:S(2)}, u32[]{:S(2)}) collective-permute-start(bf16[2,6,8,1024]{3,2,1,0:T(8,128)(2,1)} %get-tuple-element.83), channel_id=1, source_target_pairs={{0,20},{2,22},{4,24},{6,26},{8,28},{10,30},{12,16},{14,18},{1,21},... | collective-permute-start | bytes 589832 | tf_op jit(solution)/shard_map/ppermute | solution.py:487
  40.9 63.0 %collective-permute-start.9 = (bf16[2,6,8,1024]{3,2,1,0:T(8,128)(2,1)}, bf16[2,6,8,1024]{3,2,1,0:T(8,128)(2,1)S(1)}, u32[]{:S(2)}, u32[]{:S(2)}) collective-permute-start(bf16[2,6,8,1024]{3,2,1,0:T(8,128)(2,1)} %get-tuple-element.84), channel_id=1, source_target_pairs={{0,24},{2,26},{4,28},{6,30},{8,16},{10,18},{12,20},{14,22},{1,25},... | collective-permute-start | bytes 589832 | tf_op jit(solution)/shard_map/ppermute | solution.py:487
  42.2 61.7 %collective-permute-start.10 = (bf16[2,6,8,1024]{3,2,1,0:T(8,128)(2,1)}, bf16[2,6,8,1024]{3,2,1,0:T(8,128)(2,1)S(1)}, u32[]{:S(2)}, u32[]{:S(2)}) collective-permute-start(bf16[2,6,8,1024]{3,2,1,0:T(8,128)(2,1)} %get-tuple-element.85), channel_id=1, source_target_pairs={{0,28},{2,30},{4,16},{6,18},{8,20},{10,22},{12,24},{14,26},{1,29},... | collective-permute-start | bytes 589832 | tf_op jit(solution)/shard_map/ppermute | solution.py:487
  43.5 16.5 %collective-permute-start.5 = (bf16[2,4,8,1024]{3,2,1,0:T(8,128)(2,1)S(1)}, bf16[2,4,8,1024]{3,2,1,0:T(8,128)(2,1)S(1)}, u32[]{:S(2)}, u32[]{:S(2)}) collective-permute-start(bf16[2,4,8,1024]{3,2,1,0:T(8,128)(2,1)S(1)} %get-tuple-element.77), channel_id=1, source_target_pairs={{0,28},{2,30},{4,16},{6,18},{8,20},{10,22},{12,24},{14,26},{1,29},... | collective-permute-start | bytes 393224 | tf_op jit(solution)/shard_map/ppermute | solution.py:487
  60.7 0.7 collective-permute-start
  62.1 41.3 %all-to-all-start = ((bf16[16,2,8,1024]{3,2,1,0:T(8,128)(2,1)}), bf16[16,2,8,1024]{3,2,1,0:T(8,128)(2,1)}, u32[]{:S(2)}, u32[]{:S(2)}) async-start(bf16[16,2,8,1024]{3,2,1,0:T(8,128)(2,1)} %relay_slots.1.rest_1_), calls=%async_computation | async-start | bytes 1048576 | tf_op jit(solution)/shard_map/cond/branch_1_fun/all_to_all | solution.py:493
  84.6 16.8 %copy-start.3 = (f32[8,32,256]{2,1,0:T(8,128)S(1)}, f32[8,32,256]{2,1,0:T(8,128)}, u32[]{:S(2)}) copy-start(f32[8,32,256]{2,1,0:T(8,128)} %get-tuple-element.42.refs_0_) | copy-start | bytes 786436 | tf_op jit(solution)/shard_map/cond
  84.7 18.7 %copy-start.4 = (bf16[1,8192]{1,0:T(2,128)(2,1)S(1)}, bf16[1,8192]{1,0:T(2,128)(2,1)}, u32[]{:S(2)}) copy-start(bf16[1,8192]{1,0:T(2,128)(2,1)} %get-tuple-element.46.q_ref) | copy-start | bytes 49156 | tf_op jit(solution)/shard_map/cond
  101.5 0.7 copy-start
  105.3 4.3 %collective-permute-start.11 = (f32[8,8,256]{2,1,0:T(8,128)S(1)}, f32[8,8,256]{2,1,0:T(8,128)S(1)}, u32[]{:S(2)}, u32[]{:S(2)}) collective-permute-start(f32[8,8,256]{2,1,0:T(8,128)S(1)} %near_rows.1.refs_0_), channel_id=1, source_target_pairs={{0,1},{1,0},{2,3},{3,2},{4,5},{5,4},{6,7},{7,6},{8,9},{9,8},{10,11... | collective-permute-start | bytes 196616 | tf_op jit(solution)/shard_map/ppermute | solution.py:667

commit v6 on v5

--- a/solution.py
+++ b/solution.py
@@ -606,9 +606,9 @@
     far_here = [crossing(part, s) for s, part in enumerate(far_parts)]
     part, mark = cached([near_rows])
     prompt, mark = prompt_part(0, None, [mark])
+    near_parts = staged(first_stage, spread, mark)
+    near_here = [crossing(near_part, s) for s, near_part in enumerate(near_parts)]
     other = exchanged(part)
-    near_parts = staged(first_stage, spread, mark, other)
-    near_here = [crossing(near_part, s) for s, near_part in enumerate(near_parts)]
     prompt, slots, decode_out, arrival = staged(second_stage, prompt, part, other, *far_here)
     arrival = arrival_part(
         near_rows_kernel,

time: 112 us -> 80.6 us (0.72)
  the two profiles are of different devices: /device:TPU:0 before, /device:TPU:24 now
where the time goes in v6:
time: 80.6 us; the launch traced here: 79.8 us
  Pallas kernels  27 us (33%)
  waiting for transfers between devices  26.8 us (33%)
  starting transfers between devices  23.6 us (29%)
  between operations  0.86 us (1%)
  other arithmetic  0.83 us (1%)
    all_to_all x2, waiting for transfers between devices, spread_out(): lax.all_to_all(array, ('inst', 'tp'), 0, 0, axis_index_groups=groups, til...  13.6 us
    ppermute x8, waiting for transfers between devices, crossing(): return lax.ppermute(array, 'inst', hops)  10.9 us
    ppermute x8, starting transfers between devices, crossing(): return lax.ppermute(array, 'inst', hops)  10.3 us
    all_to_all x2, starting transfers between devices, spread_out(): lax.all_to_all(array, ('inst', 'tp'), 0, 0, axis_index_groups=groups, til...  9.44 us
    pallas_call x2, Pallas kernels, prompt_attention(): pl.pallas_call(functools.partial(prompt_kernel, heads), out_shape=(jax.Sh...  7.28 us
    pallas_call x5, Pallas kernels, copies(): pl.pallas_call(functools.partial(copy_kernel, plan, side, (len(operands),...  4.98 us
    pallas_call x1, Pallas kernels, cache_attention(): pl.pallas_call(functools.partial(cache_kernel, page_len), out_shape=(jax....  4.1 us
    pallas_call x2, Pallas kernels, arrival_part(): pl.pallas_call(kernel, out_shape=jax.ShapeDtypeStruct((KVHEADS, GROUP, 2...  3.23 us
  transfers between devices with their start and end apart: 14, of which 8 were waited for; matrix products, arithmetic and copies ran while one was open for 0% of the time, Pallas kernels for 30%

profile of v6, /device:TPU:24, one launch (start us, length us, event | category | flops | bytes accessed | tf_op | source)
XLA Modules:
  0.0 79.8 jit_solution(7446192025784084107)
XLA Ops:
  0.6 0.0 copy-start.1
  0.6 0.8 %pad_add_fusion.info_ref = s32[10]{0:T(128)S(1)} fusion(s32[8]{0:T(128)} %param.19, s32[1]{0:T(128)} %bitcast.2, s32[1]{0:T(128)} %bitcast.1), kind=kLoop, calls=%fused_computation | loop fusion | flops 20 | bytes 80 | tf_op jit(solution)/shard_map/concatenate | solution.py:659
  1.5 0.6 cut_near.1.rest_0_.refs_1_
  2.1 5.2 %all-to-all-start.1 = ((bf16[16,3,8,1024]{3,2,1,0:T(8,128)(2,1)}), bf16[16,3,8,1024]{3,2,1,0:T(8,128)(2,1)S(1)}, u32[]{:S(2)}, u32[]{:S(2)}) async-start(bf16[16,3,8,1024]{3,2,1,0:T(8,128)(2,1)} %bitcast.5), calls=%async_computation.1 | async-start | bytes 1572864 | tf_op jit(solution)/shard_map/all_to_all | solution.py:493
  7.3 0.0 copy-start.3
  7.3 0.6 cut_far.1
  7.9 1.3 %collective-permute-start.2 = (bf16[2,4,8,1024]{3,2,1,0:T(8,128)(2,1)S(1)}, bf16[2,4,8,1024]{3,2,1,0:T(8,128)(2,1)}, u32[]{:S(2)}, u32[]{:S(2)}) collective-permute-start(bf16[2,4,8,1024]{3,2,1,0:T(8,128)(2,1)S(1)} %get-tuple-element.71), channel_id=1, source_target_pairs={{0,16},{2,18},{4,20},{6,22},{8,24},{10,26},{12,28},{14,30},{1,17},... | collective-permute-start | bytes 393224 | tf_op jit(solution)/shard_map/ppermute | solution.py:487
  9.2 1.3 %collective-permute-start.3 = (bf16[2,4,8,1024]{3,2,1,0:T(8,128)(2,1)S(1)}, bf16[2,4,8,1024]{3,2,1,0:T(8,128)(2,1)}, u32[]{:S(2)}, u32[]{:S(2)}) collective-permute-start(bf16[2,4,8,1024]{3,2,1,0:T(8,128)(2,1)S(1)} %get-tuple-element.72), channel_id=1, source_target_pairs={{0,20},{2,22},{4,24},{6,26},{8,28},{10,30},{12,16},{14,18},{1,21},... | collective-permute-start | bytes 393224 | tf_op jit(solution)/shard_map/ppermute | solution.py:487
  10.5 1.3 %collective-permute-start.4 = (bf16[2,4,8,1024]{3,2,1,0:T(8,128)(2,1)S(1)}, bf16[2,4,8,1024]{3,2,1,0:T(8,128)(2,1)}, u32[]{:S(2)}, u32[]{:S(2)}) collective-permute-start(bf16[2,4,8,1024]{3,2,1,0:T(8,128)(2,1)S(1)} %get-tuple-element.73), channel_id=1, source_target_pairs={{0,24},{2,26},{4,28},{6,30},{8,16},{10,18},{12,20},{14,22},{1,25},... | collective-permute-start | bytes 393224 | tf_op jit(solution)/shard_map/ppermute | solution.py:487
  11.8 1.3 %collective-permute-start.5 = (bf16[2,4,8,1024]{3,2,1,0:T(8,128)(2,1)S(1)}, bf16[2,4,8,1024]{3,2,1,0:T(8,128)(2,1)}, u32[]{:S(2)}, u32[]{:S(2)}) collective-permute-start(bf16[2,4,8,1024]{3,2,1,0:T(8,128)(2,1)S(1)} %get-tuple-element.74), channel_id=1, source_target_pairs={{0,28},{2,30},{4,16},{6,18},{8,20},{10,22},{12,24},{14,26},{1,29},... | collective-permute-start | bytes 393224 | tf_op jit(solution)/shard_map/ppermute | solution.py:487
  13.1 4.1 %cache_attention.1 = (f32[8,32,256]{2,1,0:T(8,128)S(1)}, f32[8,128]{1,0:T(8,128)}) custom-call(s32[10]{0:T(128)S(1)} %pad_add_fusion.info_ref, s32[4,8]{1,0:T(4,128)} %table_ref.1, s32[4]{0:T(128)} %lengths_ref.1, bf16[4,8192]{1,0:T(4,128)(2,1)} %q_ref.3, bf16[320,2048]{1,0:T(8,128)(2,1)} %bitcast.10, bf16[2,24,8,1024]{3,2,1,0:T(8,128)(2,1)} %cut_near.1.rest_0_.refs_1_), custom_call_target="tpu_custom_call" | custom-call | flops 1 | bytes 1 | tf_op jit(solution)/shard_map/cache_attention/pallas_call | solution.py:201
  17.2 0.0 copy-start.2
  17.2 0.0 copy-done.1
  17.2 2.8 %prompt_attention.3 = (bf16[640,4096]{1,0:T(8,128)(2,1)}, f32[8,128]{1,0:T(8,128)S(1)}) custom-call(s32[10]{0:T(128)S(1)} %pad_add_fusion.info_ref, bf16[640,4096]{1,0:T(8,128)(2,1)} %q_ref.4, bf16[640,1024]{1,0:T(8,128)(2,1)S(1)} %copy-done.1, f32[8,128]{1,0:T(8,128)} %get-tuple-element.69.rest_0_), custom_call_target="tpu_custom_call" | custom-call | flops 1 | bytes 1 | tf_op jit(solution)/shard_map/prompt_attention/pallas_call | solution.py:112
  20.0 0.0 copy-done.3
  20.1 2.2 %all-to-all-done.1 = bf16[16,3,8,1024]{3,2,1,0:T(8,128)(2,1)S(1)} async-done(((bf16[16,3,8,1024]{3,2,1,0:T(8,128)(2,1)}), bf16[16,3,8,1024]{3,2,1,0:T(8,128)(2,1)S(1)}, u32[]{:S(2)}, u32[]{:S(2)}) %all-to-all-start.1) | async-done | bytes 786464 | tf_op jit(solution)/shard_map/all_to_all | solution.py:493
  22.3 2.0 %conditional.3 = ((bf16[2,6,8,1024]{3,2,1,0:T(8,128)(2,1)}, bf16[2,6,8,1024]{3,2,1,0:T(8,128)(2,1)}, bf16[2,6,8,1024]{3,2,1,0:T(8,128)(2,1)S(1)}, bf16[2,6,8,1024]{3,2,1,0:T(8,128)(2,1)S(1)})) conditional(s32[]{:T(128)} %bitcast, () %tuple.24, (s32[10]{0:T(128)S(1)}, bf16[16,3,8,1024]{3,2,1,0:T(8,128)(2,1)S(1)}, f32[8,128]{1,0:T(8,128)S(1)}) %tuple.25), branch_computations={%region_2.0_spmd, %region_3.0_spmd} | conditional | flops 2 | bytes 1572914 | solution.py:597
  22.3 0.6 for_neighbour.1
  22.9 0.7 collective-permute-start.1
  23.6 0.0 collective-permute-done.1.refs_1_
  23.6 0.7 for_receivers.1
  24.3 0.6 collective-permute-start.6
  24.9 0.0 collective-permute-done.2
  24.9 1.3 %collective-permute-start.7 = (bf16[2,6,8,1024]{3,2,1,0:T(8,128)(2,1)}, bf16[2,6,8,1024]{3,2,1,0:T(8,128)(2,1)S(1)}, u32[]{:S(2)}, u32[]{:S(2)}) collective-permute-start(bf16[2,6,8,1024]{3,2,1,0:T(8,128)(2,1)} %get-tuple-element.79), channel_id=1, source_target_pairs={{0,16},{2,18},{4,20},{6,22},{8,24},{10,26},{12,28},{14,30},{1,17},... | collective-permute-start | bytes 589832 | tf_op jit(solution)/shard_map/ppermute | solution.py:487
  26.2 0.4 collective-permute-done.3
  26.6 1.3 %collective-permute-start.8 = (bf16[2,6,8,1024]{3,2,1,0:T(8,128)(2,1)}, bf16[2,6,8,1024]{3,2,1,0:T(8,128)(2,1)S(1)}, u32[]{:S(2)}, u32[]{:S(2)}) collective-permute-start(bf16[2,6,8,1024]{3,2,1,0:T(8,128)(2,1)} %get-tuple-element.80), channel_id=1, source_target_pairs={{0,20},{2,22},{4,24},{6,26},{8,28},{10,30},{12,16},{14,18},{1,21},... | collective-permute-start | bytes 589832 | tf_op jit(solution)/shard_map/ppermute | solution.py:487
  27.9 0.1 collective-permute-done.4
  28.0 1.3 %collective-permute-start.9 = (bf16[2,6,8,1024]{3,2,1,0:T(8,128)(2,1)S(1)}, bf16[2,6,8,1024]{3,2,1,0:T(8,128)(2,1)S(1)}, u32[]{:S(2)}, u32[]{:S(2)}) collective-permute-start(bf16[2,6,8,1024]{3,2,1,0:T(8,128)(2,1)S(1)} %get-tuple-element.81), channel_id=1, source_target_pairs={{0,24},{2,26},{4,28},{6,30},{8,16},{10,18},{12,20},{14,22},{1,25},... | collective-permute-start | bytes 589832 | tf_op jit(solution)/shard_map/ppermute | solution.py:487
  29.3 8.2 %collective-permute-done.5 = bf16[2,4,8,1024]{3,2,1,0:T(8,128)(2,1)} collective-permute-done((bf16[2,4,8,1024]{3,2,1,0:T(8,128)(2,1)S(1)}, bf16[2,4,8,1024]{3,2,1,0:T(8,128)(2,1)}, u32[]{:S(2)}, u32[]{:S(2)}) %collective-permute-start.5) | collective-permute-done | bytes 131104 | tf_op jit(solution)/shard_map/ppermute | solution.py:487
  37.5 1.3 %collective-permute-start.10 = (bf16[2,6,8,1024]{3,2,1,0:T(8,128)(2,1)S(1)}, bf16[2,6,8,1024]{3,2,1,0:T(8,128)(2,1)S(1)}, u32[]{:S(2)}, u32[]{:S(2)}) collective-permute-start(bf16[2,6,8,1024]{3,2,1,0:T(8,128)(2,1)S(1)} %get-tuple-element.82), channel_id=1, source_target_pairs={{0,28},{2,30},{4,16},{6,18},{8,20},{10,22},{12,24},{14,26},{1,29},... | collective-permute-start | bytes 589832 | tf_op jit(solution)/shard_map/ppermute | solution.py:487
  38.8 0.0 collective-permute-done.6
  38.8 0.0 copy-done.2
  38.9 32.0 %conditional.2 = (bf16[640,4096]{1,0:T(8,128)(2,1)}, bf16[16,2,8,1024]{3,2,1,0:T(8,128)(2,1)}, bf16[4,8192]{1,0:T(4,128)(2,1)}, f32[8,8,256]{2,1,0:T(8,128)S(1)}) conditional(s32[]{:T(128)} %bitcast, bf16[640,4096]{1,0:T(8,128)(2,1)} %get-tuple-element.70, (s32[10]{0:T(128)S(1)}, bf16[2,4,8,1024]{3,2,1,0:T(8,128)(2,1)}, ...), branch_computations={%region_0.0_spmd, %region_1.0_spmd} | conditional | flops 5 | bytes 2637961 | solution.py:597
  38.9 2.5 %split_relays.1 = (bf16[4,2,2,8,1024]{4,3,2,1,0:T(8,128)(2,1)S(1)}, bf16[4,2,2,8,1024]{4,3,2,1,0:T(8,128)(2,1)S(1)}) custom-call(s32[10]{0:T(128)S(1)} %get-tuple-element.29.info_ref, bf16[2,4,8,1024]{3,2,1,0:T(8,128)(2,1)} %get-tuple-element.33.refs_0_, bf16[2,4,8,1024]{3,2,1,0:T(8,128)(2,1)} %get-tuple-element.34.refs_1_, ...), custom_call_target="tpu_custom_call" | custom-call | flops 1 | bytes 1 | tf_op jit(solution)/shard_map/cond/branch_1_fun/split_relays/pallas_call | solution.py:390
  41.3 1.9 %collective-permute-start = (bf16[4,2,2,8,1024]{4,3,2,1,0:T(8,128)(2,1)S(1)}, bf16[4,2,2,8,1024]{4,3,2,1,0:T(8,128)(2,1)S(1)}, u32[]{:S(2)}, u32[]{:S(2)}) collective-permute-start(bf16[4,2,2,8,1024]{4,3,2,1,0:T(8,128)(2,1)S(1)} %get-tuple-element.38), channel_id=1, source_target_pairs={{16,18},{18,16},{20,22},{22,20},{24,26},{26,24},{28,30},{30,28},{1... | collective-permute-start | bytes 786440 | tf_op jit(solution)/shard_map/cond/branch_1_fun/ppermute | solution.py:490
  43.3 1.5 %collective-permute-done.recv_ref = bf16[4,2,2,8,1024]{4,3,2,1,0:T(8,128)(2,1)S(1)} collective-permute-done((bf16[4,2,2,8,1024]{4,3,2,1,0:T(8,128)(2,1)S(1)}, bf16[4,2,2,8,1024]{4,3,2,1,0:T(8,128)(2,1)S(1)}, u32[]{:S(2)}, u32[]{:S(2)}) %collective-permute-start) | collective-permute-done | bytes 262176 | tf_op jit(solution)/shard_map/cond/branch_1_fun/ppermute | solution.py:490
  44.8 1.5 %relay_slots.1.rest_1_ = bf16[16,2,8,1024]{3,2,1,0:T(8,128)(2,1)} custom-call(s32[10]{0:T(128)S(1)} %get-tuple-element.29.info_ref, bf16[4,2,2,8,1024]{4,3,2,1,0:T(8,128)(2,1)S(1)} %get-tuple-element.37.keep_ref, bf16[4,2,2,8,1024]{4,3,2,1,0:T(8,128)(2,1)S(1)} %collective-permute-done.recv_ref), custom_call_target="tpu_custom_call" | custom-call | flops 1 | bytes 1 | tf_op jit(solution)/shard_map/cond/branch_1_fun/relay_slots/pallas_call | solution.py:564
  46.2 4.2 %all-to-all-start = ((bf16[16,2,8,1024]{3,2,1,0:T(8,128)(2,1)}), bf16[16,2,8,1024]{3,2,1,0:T(8,128)(2,1)}, u32[]{:S(2)}, u32[]{:S(2)}) async-start(bf16[16,2,8,1024]{3,2,1,0:T(8,128)(2,1)} %relay_slots.1.rest_1_), calls=%async_computation | async-start | bytes 1048576 | tf_op jit(solution)/shard_map/cond/branch_1_fun/all_to_all | solution.py:493
  50.5 4.5 %prompt_attention.2 = (bf16[640,4096]{1,0:T(8,128)(2,1)}, f32[8,128]{1,0:T(8,128)}) custom-call(s32[10]{0:T(128)S(1)} %get-tuple-element.29.info_ref, bf16[640,4096]{1,0:T(8,128)(2,1)} %get-tuple-element.30.q_ref, bf16[640,1024]{1,0:T(8,128)(2,1)S(1)} %get-tuple-element.31.kv_ref, ...), custom_call_target="tpu_custom_call", output_to_operand_aliasing={{0}: (3, {})} | custom-call | flops 1 | bytes 1 | tf_op jit(solution)/shard_map/cond/branch_1_fun/prompt_attention/pallas_call | solution.py:112
  55.0 0.0 copy-start
  55.0 0.7 copy-done
  55.7 1.7 %combine_parts.2 = (bf16[4,8192]{1,0:T(4,128)(2,1)}, f32[8,128]{1,0:T(8,128)}) custom-call(s32[10]{0:T(128)S(1)} %get-tuple-element.29.info_ref, f32[8,32,256]{2,1,0:T(8,128)S(1)} %get-tuple-element.40.refs_0_, f32[8,32,256]{2,1,0:T(8,128)S(1)} %get-tuple-element.41.refs_1_, f32[8,128]{1,0:T(8,128)S(1)} %copy-done), custom_call_target="tpu_custom_call" | custom-call | flops 1 | bytes 1 | tf_op jit(solution)/shard_map/cond/branch_1_fun/combine_parts/pallas_call | solution.py:328
  57.4 11.4 %all-to-all-done.slots_ref = bf16[16,2,8,1024]{3,2,1,0:T(8,128)(2,1)} async-done(((bf16[16,2,8,1024]{3,2,1,0:T(8,128)(2,1)}), bf16[16,2,8,1024]{3,2,1,0:T(8,128)(2,1)}, u32[]{:S(2)}, u32[]{:S(2)}) %all-to-all-start) | async-done | bytes 524320 | tf_op jit(solution)/shard_map/cond/branch_1_fun/all_to_all | solution.py:493
  68.8 2.0 %far_rows.1 = f32[8,8,256]{2,1,0:T(8,128)S(1)} custom-call(s32[10]{0:T(128)S(1)} %get-tuple-element.29.info_ref, bf16[1,8192]{1,0:T(2,128)(2,1)S(1)} %get-tuple-element.44.q_ref, bf16[16,2,8,1024]{3,2,1,0:T(8,128)(2,1)} %all-to-all-done.slots_ref), custom_call_target="tpu_custom_call" | custom-call | flops 1 | bytes 1 | tf_op jit(solution)/shard_map/cond/branch_1_fun/far_rows/pallas_call | solution.py:282
  70.9 0.0 collective-permute-done.7.refs_0_
  70.9 0.0 collective-permute-done.8.refs_1_
  70.9 0.0 collective-permute-done.9.refs_2_
  70.9 2.1 %collective-permute-done.10.refs_3_ = bf16[2,6,8,1024]{3,2,1,0:T(8,128)(2,1)S(1)} collective-permute-done((bf16[2,6,8,1024]{3,2,1,0:T(8,128)(2,1)S(1)}, bf16[2,6,8,1024]{3,2,1,0:T(8,128)(2,1)S(1)}, u32[]{:S(2)}, u32[]{:S(2)}) %collective-permute-start.10) | collective-permute-done | bytes 196640 | tf_op jit(solution)/shard_map/ppermute | solution.py:487
  73.0 1.2 %near_rows.1.refs_0_ = f32[8,8,256]{2,1,0:T(8,128)S(1)} custom-call(s32[10]{0:T(128)S(1)} %pad_add_fusion.info_ref, bf16[1,8192]{1,0:T(2,128)(2,1)S(1)} %copy-done.2, f32[8,8,256]{2,1,0:T(8,128)S(1)} %get-tuple-element.84.earlier_ref, bf16[2,6,8,1024]{3,2,1,0:T(8,128)(2,1)S(1)} %collective-permute-done.7.refs_0_, ...), custom_call_target="tpu_custom_call" | custom-call | flops 1 | bytes 1 | tf_op jit(solution)/shard_map/near_rows/pallas_call | solution.py:282
  74.2 0.7 collective-permute-start.11
  74.8 2.9 %rows.1 = bf16[40,8,2048]{2,1,0:T(8,128)(2,1)} custom-call(s32[10]{0:T(128)S(1)} %pad_add_fusion.info_ref, bf16[16,2,8,1024]{3,2,1,0:T(8,128)(2,1)} %get-tuple-element.77.slots_ref, bf16[2,6,8,1024]{3,2,1,0:T(8,128)(2,1)S(1)} %collective-permute-done.7.refs_0_, bf16[2,6,8,1024]{3,2,1,0:T(8,128)(2,1)S(1)} %collective-permute-done.8.refs_1_, ...), custom_call_target="tpu_custom_call" | custom-call | flops 1 | bytes 1 | tf_op jit(solution)/shard_map/rows/pallas_call | solution.py:622
  77.7 0.8 collective-permute-done.11.refs_1_
  78.5 1.4 %combine_parts.3 = (bf16[1,8192]{1,0:T(2,128)(2,1)}, f32[8,128]{1,0:T(8,128)}) custom-call(s32[10]{0:T(128)S(1)} %pad_add_fusion.info_ref, f32[8,8,256]{2,1,0:T(8,128)S(1)} %near_rows.1.refs_0_, f32[8,8,256]{2,1,0:T(8,128)S(1)} %collective-permute-done.11.refs_1_), custom_call_target="tpu_custom_call" | custom-call | flops 1 | bytes 1 | tf_op jit(solution)/shard_map/combine_parts/pallas_call | solution.py:328
Async XLA Ops:
  0.6 16.6 %copy-start.1 = (bf16[640,1024]{1,0:T(8,128)(2,1)S(1)}, bf16[640,1024]{1,0:T(8,128)(2,1)}, u32[]{:S(2)}) copy-start(bf16[640,1024]{1,0:T(8,128)(2,1)} %kv_ref.1) | copy-start | bytes 3932164
  2.1 20.2 %all-to-all-start.1 = ((bf16[16,3,8,1024]{3,2,1,0:T(8,128)(2,1)}), bf16[16,3,8,1024]{3,2,1,0:T(8,128)(2,1)S(1)}, u32[]{:S(2)}, u32[]{:S(2)}) async-start(bf16[16,3,8,1024]{3,2,1,0:T(8,128)(2,1)} %bitcast.5), calls=%async_computation.1 | async-start | bytes 1572864 | tf_op jit(solution)/shard_map/all_to_all | solution.py:493
  7.3 12.7 %copy-start.3 = (s32[8]{0:T(128)S(1)}, s32[8]{0:T(128)}, u32[]{:S(2)}) copy-start(s32[8]{0:T(128)} %param.19) | copy-start | bytes 100
  7.9 17.0 %collective-permute-start.2 = (bf16[2,4,8,1024]{3,2,1,0:T(8,128)(2,1)S(1)}, bf16[2,4,8,1024]{3,2,1,0:T(8,128)(2,1)}, u32[]{:S(2)}, u32[]{:S(2)}) collective-permute-start(bf16[2,4,8,1024]{3,2,1,0:T(8,128)(2,1)S(1)} %get-tuple-element.71), channel_id=1, source_target_pairs={{0,16},{2,18},{4,20},{6,22},{8,24},{10,26},{12,28},{14,30},{1,17},... | collective-permute-start | bytes 393224 | tf_op jit(solution)/shard_map/ppermute | solution.py:487
  9.2 17.4 %collective-permute-start.3 = (bf16[2,4,8,1024]{3,2,1,0:T(8,128)(2,1)S(1)}, bf16[2,4,8,1024]{3,2,1,0:T(8,128)(2,1)}, u32[]{:S(2)}, u32[]{:S(2)}) collective-permute-start(bf16[2,4,8,1024]{3,2,1,0:T(8,128)(2,1)S(1)} %get-tuple-element.72), channel_id=1, source_target_pairs={{0,20},{2,22},{4,24},{6,26},{8,28},{10,30},{12,16},{14,18},{1,21},... | collective-permute-start | bytes 393224 | tf_op jit(solution)/shard_map/ppermute | solution.py:487
  10.5 17.5 %collective-permute-start.4 = (bf16[2,4,8,1024]{3,2,1,0:T(8,128)(2,1)S(1)}, bf16[2,4,8,1024]{3,2,1,0:T(8,128)(2,1)}, u32[]{:S(2)}, u32[]{:S(2)}) collective-permute-start(bf16[2,4,8,1024]{3,2,1,0:T(8,128)(2,1)S(1)} %get-tuple-element.73), channel_id=1, source_target_pairs={{0,24},{2,26},{4,28},{6,30},{8,16},{10,18},{12,20},{14,22},{1,25},... | collective-permute-start | bytes 393224 | tf_op jit(solution)/shard_map/ppermute | solution.py:487
  11.8 25.7 %collective-permute-start.5 = (bf16[2,4,8,1024]{3,2,1,0:T(8,128)(2,1)S(1)}, bf16[2,4,8,1024]{3,2,1,0:T(8,128)(2,1)}, u32[]{:S(2)}, u32[]{:S(2)}) collective-permute-start(bf16[2,4,8,1024]{3,2,1,0:T(8,128)(2,1)S(1)} %get-tuple-element.74), channel_id=1, source_target_pairs={{0,28},{2,30},{4,16},{6,18},{8,20},{10,22},{12,24},{14,26},{1,29},... | collective-permute-start | bytes 393224 | tf_op jit(solution)/shard_map/ppermute | solution.py:487
  17.2 21.6 %copy-start.2 = (bf16[1,8192]{1,0:T(2,128)(2,1)S(1)}, bf16[1,8192]{1,0:T(2,128)(2,1)}, u32[]{:S(2)}) copy-start(bf16[1,8192]{1,0:T(2,128)(2,1)} %q_ref.5) | copy-start | bytes 49156
  22.9 0.7 collective-permute-start.1
  24.3 14.5 %collective-permute-start.6 = (f32[8,32,256]{2,1,0:T(8,128)S(1)}, f32[8,32,256]{2,1,0:T(8,128)S(1)}, u32[]{:S(2)}, u32[]{:S(2)}) collective-permute-start(f32[8,32,256]{2,1,0:T(8,128)S(1)} %get-tuple-element.75), channel_id=1, source_target_pairs={{0,1},{1,0},{2,3},{3,2},{4,5},{5,4},{6,7},{7,6},{8,9},{9,8},{10,11... | collective-permute-start | bytes 786440 | tf_op jit(solution)/shard_map/ppermute | solution.py:667
  24.9 46.0 %collective-permute-start.7 = (bf16[2,6,8,1024]{3,2,1,0:T(8,128)(2,1)}, bf16[2,6,8,1024]{3,2,1,0:T(8,128)(2,1)S(1)}, u32[]{:S(2)}, u32[]{:S(2)}) collective-permute-start(bf16[2,6,8,1024]{3,2,1,0:T(8,128)(2,1)} %get-tuple-element.79), channel_id=1, source_target_pairs={{0,16},{2,18},{4,20},{6,22},{8,24},{10,26},{12,28},{14,30},{1,17},... | collective-permute-start | bytes 589832 | tf_op jit(solution)/shard_map/ppermute | solution.py:487
  26.6 44.3 %collective-permute-start.8 = (bf16[2,6,8,1024]{3,2,1,0:T(8,128)(2,1)}, bf16[2,6,8,1024]{3,2,1,0:T(8,128)(2,1)S(1)}, u32[]{:S(2)}, u32[]{:S(2)}) collective-permute-start(bf16[2,6,8,1024]{3,2,1,0:T(8,128)(2,1)} %get-tuple-element.80), channel_id=1, source_target_pairs={{0,20},{2,22},{4,24},{6,26},{8,28},{10,30},{12,16},{14,18},{1,21},... | collective-permute-start | bytes 589832 | tf_op jit(solution)/shard_map/ppermute | solution.py:487
  28.0 42.9 %collective-permute-start.9 = (bf16[2,6,8,1024]{3,2,1,0:T(8,128)(2,1)S(1)}, bf16[2,6,8,1024]{3,2,1,0:T(8,128)(2,1)S(1)}, u32[]{:S(2)}, u32[]{:S(2)}) collective-permute-start(bf16[2,6,8,1024]{3,2,1,0:T(8,128)(2,1)S(1)} %get-tuple-element.81), channel_id=1, source_target_pairs={{0,24},{2,26},{4,28},{6,30},{8,16},{10,18},{12,20},{14,22},{1,25},... | collective-permute-start | bytes 589832 | tf_op jit(solution)/shard_map/ppermute | solution.py:487
  37.5 35.5 %collective-permute-start.10 = (bf16[2,6,8,1024]{3,2,1,0:T(8,128)(2,1)S(1)}, bf16[2,6,8,1024]{3,2,1,0:T(8,128)(2,1)S(1)}, u32[]{:S(2)}, u32[]{:S(2)}) collective-permute-start(bf16[2,6,8,1024]{3,2,1,0:T(8,128)(2,1)S(1)} %get-tuple-element.82), channel_id=1, source_target_pairs={{0,28},{2,30},{4,16},{6,18},{8,20},{10,22},{12,24},{14,26},{1,29},... | collective-permute-start | bytes 589832 | tf_op jit(solution)/shard_map/ppermute | solution.py:487
  41.3 3.4 %collective-permute-start = (bf16[4,2,2,8,1024]{4,3,2,1,0:T(8,128)(2,1)S(1)}, bf16[4,2,2,8,1024]{4,3,2,1,0:T(8,128)(2,1)S(1)}, u32[]{:S(2)}, u32[]{:S(2)}) collective-permute-start(bf16[4,2,2,8,1024]{4,3,2,1,0:T(8,128)(2,1)S(1)} %get-tuple-element.38), channel_id=1, source_target_pairs={{16,18},{18,16},{20,22},{22,20},{24,26},{26,24},{28,30},{30,28},{1... | collective-permute-start | bytes 786440 | tf_op jit(solution)/shard_map/cond/branch_1_fun/ppermute | solution.py:490
  46.2 22.6 %all-to-all-start = ((bf16[16,2,8,1024]{3,2,1,0:T(8,128)(2,1)}), bf16[16,2,8,1024]{3,2,1,0:T(8,128)(2,1)}, u32[]{:S(2)}, u32[]{:S(2)}) async-start(bf16[16,2,8,1024]{3,2,1,0:T(8,128)(2,1)} %relay_slots.1.rest_1_), calls=%async_computation | async-start | bytes 1048576 | tf_op jit(solution)/shard_map/cond/branch_1_fun/all_to_all | solution.py:493
  55.0 0.7 copy-start
  74.2 4.3 %collective-permute-start.11 = (f32[8,8,256]{2,1,0:T(8,128)S(1)}, f32[8,8,256]{2,1,0:T(8,128)S(1)}, u32[]{:S(2)}, u32[]{:S(2)}) collective-permute-start(f32[8,8,256]{2,1,0:T(8,128)S(1)} %near_rows.1.refs_0_), channel_id=1, source_target_pairs={{0,1},{1,0},{2,3},{3,2},{4,5},{5,4},{6,7},{7,6},{8,9},{9,8},{10,11... | collective-permute-start | bytes 196616 | tf_op jit(solution)/shard_map/ppermute | solution.py:667

commit v7 on v6

--- a/solution.py
+++ b/solution.py
@@ -65,17 +65,29 @@
         below = jnp.concatenate([rows_all >= cols_all] * heads, axis=0)
         ones = jnp.ones((length, HEADDIM), jnp.bfloat16)
         values = jnp.concatenate([kv_ref[:, HEADDIM:], ones], axis=1)
-        for start in range(0, length, TILE):
+        def scores_of(start):
             stop = start + TILE
             queries = jnp.concatenate(
                 [q_ref[start:stop, h * HEADDIM : (h + 1) * HEADDIM] for h in range(heads)], axis=0
             )
-            scores = dot_t(queries, kv_ref[:stop, :HEADDIM])
-            last = jnp.where(below, scores[:, start:], NEG_FILL)
-            scores = jnp.concatenate([scores[:, :start], last], axis=1) if start else last
-            peak = jnp.max(scores, axis=1, keepdims=True)
-            weights = jnp.exp2((scores - peak) * (SCALE * LOG2E)).astype(jnp.bfloat16)
-            mixed = dot(weights, values[:stop])
+            last = jnp.where(below, dot_t(queries, kv_ref[start:stop, :HEADDIM]), NEG_FILL)
+            return [dot_t(queries, kv_ref[:start, :HEADDIM]), last] if start else [last]
+
+        coming = scores_of(0)
+        for start in range(0, length, TILE):
+            stop = start + TILE
+            scores = coming
+            if stop < length:
+                coming = scores_of(stop)
+            peak = functools.reduce(
+                jnp.maximum, [jnp.max(part, axis=1, keepdims=True) for part in scores]
+            )
+            weights = [
+                jnp.exp2((part - peak) * (SCALE * LOG2E)).astype(jnp.bfloat16) for part in scores
+            ]
+            mixed = dot(weights[-1], values[start:stop])
+            if start:
+                mixed = mixed + dot(weights[0], values[:start])
             result = (mixed[:, :HEADDIM] / mixed[:, HEADDIM:]).astype(jnp.bfloat16)
             for h in range(heads):
                 out_ref[start:stop, h * HEADDIM : (h + 1) * HEADDIM] = result[
@@ -256,17 +268,40 @@
     rows_part(q_ref, [rows_ref[...]], out_ref, None)
 
 
-def far_rows_kernel(info_ref, q_ref, slots_ref, out_ref, held_ref, sem):
+def far_rows_kernel(near, info_ref, q_ref, slots_ref, part_ref, handed_ref, held_ref, zero_ref, load, sems):
+    half = 2 * PAIRS
+    far, width = slots_ref.shape[1], slots_ref.shape[-1]
+
     @pl.when(jnp.logical_not(on_prefill(info_ref)))
     def _():
-        copy = pltpu.make_async_copy(slots_ref, held_ref, sem)
-        copy.start()
-        copy.wait()
-        half = 2 * PAIRS
-        rows = [
-            flat_rows([held_ref[t * half + i] for i in range(half)]) for t in range(2)
-        ]
-        rows_part(q_ref, rows, out_ref, None)
+        staged = pltpu.make_async_copy(slots_ref, held_ref, load)
+        staged.start()
+        staged.wait()
+        waits = []
+        for t in range(2):
+            for i in range(half):
+                slot = t * half + i
+                target = handed_ref.at[pl.ds(near + i * far, far), :, pl.ds(t * width, width)]
+                waits.append(pltpu.make_async_copy(held_ref.at[slot], target, sems.at[slot]))
+        for copy in waits:
+            copy.start()
+        rows = [flat_rows([held_ref[t * half + i] for i in range(half)]) for t in range(2)]
+        rows_part(q_ref, rows, part_ref, None)
+        for copy in waits:
+            copy.wait()
+
+    @pl.when(on_prefill(info_ref))
+    def _():
+        zero_ref[...] = jnp.zeros_like(zero_ref)
+        size = zero_ref.shape[0]
+        waits = []
+        for n in range(handed_ref.shape[0] // size):
+            target = handed_ref.at[pl.ds(n * size, size)]
+            waits.append(pltpu.make_async_copy(zero_ref, target, sems.at[n]))
+        for copy in waits:
+            copy.start()
+        for copy in waits:
+            copy.wait()
 
 
 def near_rows_kernel(info_ref, q_ref, earlier_ref, *refs):
@@ -403,6 +438,35 @@
     )(info, *operands, *after)
 
 
+def cut_kernel(near, far, rows_ref, near_ref, *refs):
+    *far_refs, held_ref, sems = refs
+    inst, half = lax.axis_index("inst"), lax.axis_size("inst") // 2
+    units = rows_ref.shape[0] // 2
+
+    @pl.when(inst < half)
+    def _():
+        loads, stores, others = [], [], []
+        for tau in range(2):
+            first = tau * units
+            held = held_ref.at[tau]
+            loads.append(pltpu.make_async_copy(rows_ref.at[pl.ds(first, near)], held, sems.at[tau]))
+            stores.append(pltpu.make_async_copy(held, near_ref.at[tau], sems.at[2 + tau]))
+            loads[-1].start()
+        for s, far_ref in enumerate(far_refs):
+            relay = lax.rem(lax.div(inst, 2) + s, PAIRS)
+            for tau in range(2):
+                source = rows_ref.at[pl.ds(tau * units + near + relay * far, far)]
+                others.append(
+                    pltpu.make_async_copy(source, far_ref.at[tau], sems.at[4 + len(others)])
+                )
+                others[-1].start()
+        for load, store in zip(loads, stores):
+            load.wait()
+            store.start()
+        for copy in stores + others:
+            copy.wait()
+
+
 def relay_slots_kernel(far, info_ref, keep_ref, recv_ref, out_ref, sems):
     half = 2 * PAIRS
 
@@ -426,43 +490,18 @@
             copy.wait()
 
 
-def rows_kernel(near, far, info_ref, slots_ref, *refs):
-    *parts, out_ref, zero_ref, held_ref, sems = refs
-    half = 2 * PAIRS
-    width = slots_ref.shape[-1]
-    near_all = near * half
+def store_near_kernel(near, info_ref, *refs):
+    *parts, _, handed_ref, sems = refs
+    width = parts[0].shape[-1]
 
     @pl.when(jnp.logical_not(on_prefill(info_ref)))
     def _():
-        last = sems.shape[0] - 1
-        staged = pltpu.make_async_copy(slots_ref, held_ref, sems.at[last])
-        staged.start()
         waits = []
         for t in range(2):
             for s, part in enumerate(parts):
                 pair = lax.rem(lax.div(order(info_ref), 2) + PAIRS - s, PAIRS)
-                target = out_ref.at[pl.ds(pair * 2 * near, 2 * near), :, pl.ds(t * width, width)]
+                target = handed_ref.at[pl.ds(pair * 2 * near, 2 * near), :, pl.ds(t * width, width)]
                 waits.append(pltpu.make_async_copy(part.at[t], target, sems.at[len(waits)]))
-                waits[-1].start()
-        staged.wait()
-        for t in range(2):
-            for i in range(half):
-                target = out_ref.at[pl.ds(near_all + i * far, far), :, pl.ds(t * width, width)]
-                waits.append(
-                    pltpu.make_async_copy(held_ref.at[t * half + i], target, sems.at[len(waits)])
-                )
-                waits[-1].start()
-        for copy in waits:
-            copy.wait()
-
-    @pl.when(on_prefill(info_ref))
-    def _():
-        zero_ref[...] = jnp.zeros_like(zero_ref)
-        size = zero_ref.shape[0]
-        waits = []
-        for n in range(out_ref.shape[0] // size):
-            target = out_ref.at[pl.ds(n * size, size)]
-            waits.append(pltpu.make_async_copy(zero_ref, target, sems.at[n]))
         for copy in waits:
             copy.start()
         for copy in waits:
@@ -493,19 +532,6 @@
         return lax.all_to_all(
             array, ("inst", "tp"), 0, 0, axis_index_groups=groups, tiled=True
         )
-
-    def cut_near(pre, sources, targets):
-        return [
-            (sources[0].at[pl.ds(tau * units, near_all)], targets[0].at[tau]) for tau in range(2)
-        ]
-
-    def cut_far(pre, sources, targets):
-        plan = []
-        for s in range(PAIRS):
-            start = near_all + lax.rem(lax.div(order(pre), 2) + s, PAIRS) * (2 * far)
-            for tau in range(2):
-                plan.append((sources[0].at[pl.ds(tau * units + start, 2 * far)], targets[s].at[tau]))
-        return plan
 
     def for_neighbour(pre, sources, targets):
         plan = []
@@ -578,16 +604,29 @@
         prompt, mark = prompt_part(1, prompt, [slots])
         decode_out, _ = combine_parts(info, [part, other], [mark])
         slots = spread_out(slots)
-        arrival = arrival_part(
-            far_rows_kernel,
-            info,
-            arrival_query,
-            [slots],
-            [ANYWHERE],
-            [pltpu.VMEM(slots.shape, slots.dtype), pltpu.SemaphoreType.DMA],
-            "far_rows",
-        )
-        return prompt, slots, decode_out, arrival
+        arrival, handed = pl.pallas_call(
+            functools.partial(far_rows_kernel, near_all),
+            out_shape=(
+                jax.ShapeDtypeStruct((KVHEADS, GROUP, 2 * HEADDIM), jnp.float32),
+                jax.ShapeDtypeStruct((units, UNIT, 2 * width), jnp.bfloat16),
+            ),
+            grid_spec=pltpu.PrefetchScalarGridSpec(
+                num_scalar_prefetch=1,
+                grid=(1,),
+                in_specs=[IN_VMEM, ANYWHERE],
+                out_specs=(IN_VMEM, ANYWHERE),
+                scratch_shapes=[
+                    pltpu.VMEM(slots.shape, slots.dtype),
+                    pltpu.VMEM((half, UNIT, 2 * width), jnp.bfloat16),
+                    pltpu.SemaphoreType.DMA,
+                    pltpu.SemaphoreType.DMA((2 * half,)),
+                ],
+            ),
+            compiler_params=pltpu.CompilerParams(vmem_limit_bytes=VMEM),
+            cost_estimate=COST,
+            name="far_rows",
+        )(info, arrival_query, slots)
+        return prompt, handed, decode_out, arrival
 
     def staged(stage, *operands):
         def never(*operands):
@@ -596,20 +635,32 @@
 
         return lax.cond(always, lambda *operands: tuple(stage(*operands)), never, *operands)
 
-    (near_rows,) = copies(
-        cut_near, 2, info, [by_unit], [(2, near_all) + block], "cut_near", stage=True
-    )
-    far_parts = copies(
-        cut_far, 2 * PAIRS, info, [by_unit], [(2, 2 * far) + block] * PAIRS, "cut_far", [near_rows]
-    )
+    near_rows, *far_parts = pl.pallas_call(
+        functools.partial(cut_kernel, near_all, 2 * far),
+        out_shape=tuple(
+            jax.ShapeDtypeStruct(shape + block, jnp.bfloat16)
+            for shape in [(2, near_all)] + [(2, 2 * far)] * PAIRS
+        ),
+        grid=(1,),
+        in_specs=[ANYWHERE],
+        out_specs=(ANYWHERE,) * (1 + PAIRS),
+        scratch_shapes=[
+            pltpu.VMEM((2, near_all) + block, jnp.bfloat16),
+            pltpu.SemaphoreType.DMA((4 + 2 * PAIRS,)),
+        ],
+        compiler_params=pltpu.CompilerParams(vmem_limit_bytes=MEDIUM),
+        cost_estimate=COST,
+        name="cut_rows",
+    )(by_unit)
     spread = spread_out(near_rows.reshape((2 * half, near) + block))
     far_here = [crossing(part, s) for s, part in enumerate(far_parts)]
     part, mark = cached([near_rows])
     prompt, mark = prompt_part(0, None, [mark])
     near_parts = staged(first_stage, spread, mark)
+    near_parts, far_here = lax.optimization_barrier((near_parts, far_here))
     near_here = [crossing(near_part, s) for s, near_part in enumerate(near_parts)]
     other = exchanged(part)
-    prompt, slots, decode_out, arrival = staged(second_stage, prompt, part, other, *far_here)
+    prompt, handed, decode_out, arrival = staged(second_stage, prompt, part, other, *far_here)
     arrival = arrival_part(
         near_rows_kernel,
         info,
@@ -620,23 +671,20 @@
         "near_rows",
     )
     handed = pl.pallas_call(
-        functools.partial(rows_kernel, near, far),
-        out_shape=jax.ShapeDtypeStruct((units, UNIT, 2 * width), jnp.bfloat16),
+        functools.partial(store_near_kernel, near),
+        out_shape=jax.ShapeDtypeStruct(handed.shape, handed.dtype),
         grid_spec=pltpu.PrefetchScalarGridSpec(
             num_scalar_prefetch=1,
             grid=(1,),
             in_specs=[ANYWHERE] * (PAIRS + 1),
             out_specs=ANYWHERE,
-            scratch_shapes=[
-                pltpu.VMEM((half, UNIT, 2 * width), jnp.bfloat16),
-                pltpu.VMEM(slots.shape, slots.dtype),
-                pltpu.SemaphoreType.DMA((2 * (half + PAIRS) + 1,)),
-            ],
-        ),
-        compiler_params=pltpu.CompilerParams(vmem_limit_bytes=MEDIUM),
+            scratch_shapes=[pltpu.SemaphoreType.DMA((2 * PAIRS,))],
+        ),
+        input_output_aliases={PAIRS + 1: 0},
+        compiler_params=pltpu.CompilerParams(vmem_limit_bytes=SMALL),
         cost_estimate=COST,
-        name="rows",
-    )(info, slots, *near_here)
+        name="store_near",
+    )(info, *near_here, handed)
     arrival_out, _ = combine_parts(info, [arrival, exchanged(arrival)])
     return prompt, handed.reshape(rows // 2, 2 * width), decode_out, arrival_out
 
@@ -669,7 +717,7 @@
     def combined(part):
         return combine_parts(info, [lax.all_gather(part, "tp")])[0]
 
-    heads = GROUP // 2
+    heads = GROUP
     steps = prompt_query.shape[1] // (heads * HEADDIM)
 
     def prompt_part(first, last, earlier, after=()):
@@ -678,8 +726,8 @@
         )
 
     row_units = prompt_pairs.shape[0] // (2 * UNIT)
-    if inst_count == 4 * PAIRS and tp_count == 2 and row_units == 5 * half and steps == 8:
-        cuts = (0, 2, 8)
+    if inst_count == 4 * PAIRS and tp_count == 2 and row_units == 5 * half and steps == 4:
+        cuts = (0, 1, 4)
         return two_way_handoff(
             prompt_pairs,
             info,

time: 80.6 us -> 79.4 us (0.985)
  Pallas kernels: 27 us -> 25.6 us
  starting transfers between devices: 23.6 us -> 24.6 us
    all_to_all x2, waiting for transfers between devices: 13.6 us -> 11.3 us  [spread_out(): lax.all_to_all(array, ('inst', 'tp'), 0, 0, axis_index_groups=groups, til...]
    ppermute x8, waiting for transfers between devices: 10.9 us -> 12.6 us  [crossing(): return lax.ppermute(array, 'inst', hops)]
    pallas_call x2 -> x1, Pallas kernels: 3.23 us -> 1.94 us  [arrival_part(): pl.pallas_call(kernel, out_shape=jax.ShapeDtypeStruct((KVHEADS, GROUP, 2...]
    pallas_call x1 -> x3, Pallas kernels: 2.86 us -> 3.9 us  [the longest x1 2.26 us: second_stage(): pl.pallas_call(functools.partial(far_rows_kernel, near_all), out_shape=(j...]
    pallas_call x5 -> x3, Pallas kernels: 4.98 us -> 3.97 us  [copies(): pl.pallas_call(functools.partial(copy_kernel, plan, side, (len(operands),...]
    ppermute x2, starting transfers between devices: 1.26 us -> 2.1 us  [exchanged(): return lax.ppermute(part, 'tp', [(0, 1), (1, 0)])]
  transfers between devices with their start and end apart: 14 -> 14, of which waited for: 8 -> 8; matrix products, arithmetic and copies ran while one was open for 0% -> 0% of each run, Pallas kernels for 30% -> 28%
where the time goes in v7:
time: 79.4 us; the launch traced here: 78.6 us
  waiting for transfers between devices  26.7 us (34%)
  Pallas kernels  25.6 us (32%)
  starting transfers between devices  24.6 us (31%)
  between operations  0.84 us (1%)
    ppermute x8, waiting for transfers between devices, crossing(): return lax.ppermute(array, 'inst', hops)  12.6 us
    all_to_all x2, waiting for transfers between devices, spread_out(): lax.all_to_all(array, ('inst', 'tp'), 0, 0, axis_index_groups=groups, til...  11.3 us
    ppermute x8, starting transfers between devices, crossing(): return lax.ppermute(array, 'inst', hops)  10.5 us
    all_to_all x2, starting transfers between devices, spread_out(): lax.all_to_all(array, ('inst', 'tp'), 0, 0, axis_index_groups=groups, til...  9.44 us
    pallas_call x2, Pallas kernels, prompt_attention(): pl.pallas_call(functools.partial(prompt_kernel, heads), out_shape=(jax.Sh...  7.17 us
    pallas_call x1, Pallas kernels, cache_attention(): pl.pallas_call(functools.partial(cache_kernel, page_len), out_shape=(jax....  4.09 us
    pallas_call x3, Pallas kernels, copies(): pl.pallas_call(functools.partial(copy_kernel, plan, side, (len(operands),...  3.97 us
    pallas_call x2, Pallas kernels, combine_parts(): pl.pallas_call(functools.partial(combine_kernel, len(parts)), out_shape=(...  3.03 us
  transfers between devices with their start and end apart: 14, of which 8 were waited for; matrix products, arithmetic and copies ran while one was open for 0% of the time, Pallas kernels for 28%

profile of v7, /device:TPU:24, one launch (start us, length us, event | category | flops | bytes accessed | tf_op | source)
XLA Modules:
  0.0 78.6 jit_solution(4634030965185862260)
XLA Ops:
  0.6 0.0 copy-start.2
  0.6 0.2 cut_rows.1
  0.8 5.2 %all-to-all-start.1 = ((bf16[16,3,8,1024]{3,2,1,0:T(8,128)(2,1)}), bf16[16,3,8,1024]{3,2,1,0:T(8,128)(2,1)S(1)}, u32[]{:S(2)}, u32[]{:S(2)}) async-start(bf16[16,3,8,1024]{3,2,1,0:T(8,128)(2,1)} %bitcast.5), calls=%async_computation.1 | async-start | bytes 1572864 | tf_op jit(solution)/shard_map/all_to_all | solution.py:532
  6.0 0.0 copy-start.1
  6.0 1.4 %collective-permute-start.2 = (bf16[2,4,8,1024]{3,2,1,0:T(8,128)(2,1)S(1)}, bf16[2,4,8,1024]{3,2,1,0:T(8,128)(2,1)S(1)}, u32[]{:S(2)}, u32[]{:S(2)}) collective-permute-start(bf16[2,4,8,1024]{3,2,1,0:T(8,128)(2,1)S(1)} %get-tuple-element.88), channel_id=1, source_target_pairs={{0,16},{2,18},{4,20},{6,22},{8,24},{10,26},{12,28},{14,30},{1,17},... | collective-permute-start | bytes 393224 | tf_op jit(solution)/shard_map/ppermute | solution.py:526
  7.5 1.3 %collective-permute-start.3 = (bf16[2,4,8,1024]{3,2,1,0:T(8,128)(2,1)S(1)}, bf16[2,4,8,1024]{3,2,1,0:T(8,128)(2,1)S(1)}, u32[]{:S(2)}, u32[]{:S(2)}) collective-permute-start(bf16[2,4,8,1024]{3,2,1,0:T(8,128)(2,1)S(1)} %get-tuple-element.89), channel_id=1, source_target_pairs={{0,20},{2,22},{4,24},{6,26},{8,28},{10,30},{12,16},{14,18},{1,21},... | collective-permute-start | bytes 393224 | tf_op jit(solution)/shard_map/ppermute | solution.py:526
  8.8 1.3 %collective-permute-start.4 = (bf16[2,4,8,1024]{3,2,1,0:T(8,128)(2,1)S(1)}, bf16[2,4,8,1024]{3,2,1,0:T(8,128)(2,1)}, u32[]{:S(2)}, u32[]{:S(2)}) collective-permute-start(bf16[2,4,8,1024]{3,2,1,0:T(8,128)(2,1)S(1)} %get-tuple-element.90), channel_id=1, source_target_pairs={{0,24},{2,26},{4,28},{6,30},{8,16},{10,18},{12,20},{14,22},{1,25},... | collective-permute-start | bytes 393224 | tf_op jit(solution)/shard_map/ppermute | solution.py:526
  10.1 1.3 %collective-permute-start.5 = (bf16[2,4,8,1024]{3,2,1,0:T(8,128)(2,1)S(1)}, bf16[2,4,8,1024]{3,2,1,0:T(8,128)(2,1)}, u32[]{:S(2)}, u32[]{:S(2)}) collective-permute-start(bf16[2,4,8,1024]{3,2,1,0:T(8,128)(2,1)S(1)} %get-tuple-element.91), channel_id=1, source_target_pairs={{0,28},{2,30},{4,16},{6,18},{8,20},{10,22},{12,24},{14,26},{1,29},... | collective-permute-start | bytes 393224 | tf_op jit(solution)/shard_map/ppermute | solution.py:526
  11.4 0.0 copy-done.2
  11.4 0.1 pad_add_fusion.info_ref
  11.4 4.1 %cache_attention.1 = (f32[8,32,256]{2,1,0:T(8,128)S(1)}, f32[8,128]{1,0:T(8,128)}) custom-call(s32[10]{0:T(128)S(1)} %pad_add_fusion.info_ref, s32[4,8]{1,0:T(4,128)} %table_ref.1, s32[4]{0:T(128)} %lengths_ref.1, bf16[4,8192]{1,0:T(4,128)(2,1)} %q_ref.3, bf16[320,2048]{1,0:T(8,128)(2,1)} %bitcast.10, bf16[2,24,8,1024]{3,2,1,0:T(8,128)(2,1)} %get-tuple-element.80.rest_0_), custom_call_target="tpu_custom_call" | custom-call | flops 1 | bytes 1 | tf_op jit(solution)/shard_map/cache_attention/pallas_call | solution.py:213
  15.5 0.0 copy-done.1
  15.6 3.0 %prompt_attention.3 = (bf16[640,4096]{1,0:T(8,128)(2,1)}, f32[8,128]{1,0:T(8,128)S(1)}) custom-call(s32[10]{0:T(128)S(1)} %pad_add_fusion.info_ref, bf16[640,4096]{1,0:T(8,128)(2,1)} %q_ref.4, bf16[640,1024]{1,0:T(8,128)(2,1)S(1)} %copy-done.1, f32[8,128]{1,0:T(8,128)} %get-tuple-element.81.rest_0_), custom_call_target="tpu_custom_call" | custom-call | flops 1 | bytes 1 | tf_op jit(solution)/shard_map/prompt_attention/pallas_call | solution.py:124
  18.6 2.6 %all-to-all-done.1 = bf16[16,3,8,1024]{3,2,1,0:T(8,128)(2,1)S(1)} async-done(((bf16[16,3,8,1024]{3,2,1,0:T(8,128)(2,1)}), bf16[16,3,8,1024]{3,2,1,0:T(8,128)(2,1)S(1)}, u32[]{:S(2)}, u32[]{:S(2)}) %all-to-all-start.1) | async-done | bytes 786464 | tf_op jit(solution)/shard_map/all_to_all | solution.py:532
  21.2 2.0 %conditional.2 = ((bf16[2,6,8,1024]{3,2,1,0:T(8,128)(2,1)}, bf16[2,6,8,1024]{3,2,1,0:T(8,128)(2,1)}, bf16[2,6,8,1024]{3,2,1,0:T(8,128)(2,1)S(1)}, bf16[2,6,8,1024]{3,2,1,0:T(8,128)(2,1)S(1)})) conditional(s32[]{:T(128)} %bitcast, () %tuple.24, (s32[10]{0:T(128)S(1)}, bf16[16,3,8,1024]{3,2,1,0:T(8,128)(2,1)S(1)}, f32[8,128]{1,0:T(8,128)S(1)}) %tuple.25), branch_computations={%region_0.0_spmd, %region_1.0_spmd} | conditional | flops 2 | bytes 1572914 | solution.py:636
  21.2 0.6 for_neighbour.1
  21.8 0.7 collective-permute-start
  22.5 0.0 collective-permute-done.refs_1_
  22.5 0.7 for_receivers.1
  23.2 0.6 collective-permute-start.6
  23.8 0.0 collective-permute-done.2
  23.8 1.1 %collective-permute-done.3 = bf16[2,4,8,1024]{3,2,1,0:T(8,128)(2,1)S(1)} collective-permute-done((bf16[2,4,8,1024]{3,2,1,0:T(8,128)(2,1)S(1)}, bf16[2,4,8,1024]{3,2,1,0:T(8,128)(2,1)S(1)}, u32[]{:S(2)}, u32[]{:S(2)}) %collective-permute-start.3) | collective-permute-done | bytes 131104 | tf_op jit(solution)/shard_map/ppermute | solution.py:526
  24.9 1.5 %collective-permute-done.4 = bf16[2,4,8,1024]{3,2,1,0:T(8,128)(2,1)} collective-permute-done((bf16[2,4,8,1024]{3,2,1,0:T(8,128)(2,1)S(1)}, bf16[2,4,8,1024]{3,2,1,0:T(8,128)(2,1)}, u32[]{:S(2)}, u32[]{:S(2)}) %collective-permute-start.4) | collective-permute-done | bytes 131104 | tf_op jit(solution)/shard_map/ppermute | solution.py:526
  26.4 8.9 %collective-permute-done.5 = bf16[2,4,8,1024]{3,2,1,0:T(8,128)(2,1)} collective-permute-done((bf16[2,4,8,1024]{3,2,1,0:T(8,128)(2,1)S(1)}, bf16[2,4,8,1024]{3,2,1,0:T(8,128)(2,1)}, u32[]{:S(2)}, u32[]{:S(2)}) %collective-permute-start.5) | collective-permute-done | bytes 131104 | tf_op jit(solution)/shard_map/ppermute | solution.py:526
  35.3 1.3 %collective-permute-start.7 = (bf16[2,6,8,1024]{3,2,1,0:T(8,128)(2,1)}, bf16[2,6,8,1024]{3,2,1,0:T(8,128)(2,1)S(1)}, u32[]{:S(2)}, u32[]{:S(2)}) collective-permute-start(bf16[2,6,8,1024]{3,2,1,0:T(8,128)(2,1)} %get-tuple-element.98), channel_id=1, source_target_pairs={{0,16},{2,18},{4,20},{6,22},{8,24},{10,26},{12,28},{14,30},{1,17},... | collective-permute-start | bytes 589832 | tf_op jit(solution)/shard_map/ppermute | solution.py:526
  36.6 1.3 %collective-permute-start.8 = (bf16[2,6,8,1024]{3,2,1,0:T(8,128)(2,1)}, bf16[2,6,8,1024]{3,2,1,0:T(8,128)(2,1)S(1)}, u32[]{:S(2)}, u32[]{:S(2)}) collective-permute-start(bf16[2,6,8,1024]{3,2,1,0:T(8,128)(2,1)} %get-tuple-element.99), channel_id=1, source_target_pairs={{0,20},{2,22},{4,24},{6,26},{8,28},{10,30},{12,16},{14,18},{1,21},... | collective-permute-start | bytes 589832 | tf_op jit(solution)/shard_map/ppermute | solution.py:526
  37.9 1.3 %collective-permute-start.9 = (bf16[2,6,8,1024]{3,2,1,0:T(8,128)(2,1)S(1)}, bf16[2,6,8,1024]{3,2,1,0:T(8,128)(2,1)S(1)}, u32[]{:S(2)}, u32[]{:S(2)}) collective-permute-start(bf16[2,6,8,1024]{3,2,1,0:T(8,128)(2,1)S(1)} %get-tuple-element.100), channel_id=1, source_target_pairs={{0,24},{2,26},{4,28},{6,30},{8,16},{10,18},{12,20},{14,22},{1,25},... | collective-permute-start | bytes 589832 | tf_op jit(solution)/shard_map/ppermute | solution.py:526
  39.2 1.3 %collective-permute-start.10 = (bf16[2,6,8,1024]{3,2,1,0:T(8,128)(2,1)S(1)}, bf16[2,6,8,1024]{3,2,1,0:T(8,128)(2,1)S(1)}, u32[]{:S(2)}, u32[]{:S(2)}) collective-permute-start(bf16[2,6,8,1024]{3,2,1,0:T(8,128)(2,1)S(1)} %get-tuple-element.101), channel_id=1, source_target_pairs={{0,28},{2,30},{4,16},{6,18},{8,20},{10,22},{12,24},{14,26},{1,29},... | collective-permute-start | bytes 589832 | tf_op jit(solution)/shard_map/ppermute | solution.py:526
  40.5 0.0 collective-permute-done.6
  40.5 29.4 %conditional.3 = (bf16[640,4096]{1,0:T(8,128)(2,1)}, bf16[40,8,2048]{2,1,0:T(8,128)(2,1)}, bf16[4,8192]{1,0:T(4,128)(2,1)}, f32[8,8,256]{2,1,0:T(8,128)S(1)}) conditional(s32[]{:T(128)} %bitcast, bf16[640,4096]{1,0:T(8,128)(2,1)} %get-tuple-element.82, (s32[10]{0:T(128)S(1)}, bf16[2,4,8,1024]{3,2,1,0:T(8,128)(2,1)S(1)}, ...), branch_computations={%region_2.0_spmd, %region_3.0_spmd} | conditional | flops 5 | bytes 2637961 | solution.py:636
  40.6 2.7 %split_relays.1 = (bf16[4,2,2,8,1024]{4,3,2,1,0:T(8,128)(2,1)S(1)}, bf16[4,2,2,8,1024]{4,3,2,1,0:T(8,128)(2,1)S(1)}) custom-call(s32[10]{0:T(128)S(1)} %get-tuple-element.32.info_ref, bf16[2,4,8,1024]{3,2,1,0:T(8,128)(2,1)S(1)} %get-tuple-element.36.refs_0_, bf16[2,4,8,1024]{3,2,1,0:T(8,128)(2,1)S(1)} %get-tuple-element.37.refs_1_, ...), custom_call_target="tpu_custom_call" | custom-call | flops 1 | bytes 1 | tf_op jit(solution)/shard_map/cond/branch_1_fun/split_relays/pallas_call | solution.py:425
  43.2 1.9 %collective-permute-start.1 = (bf16[4,2,2,8,1024]{4,3,2,1,0:T(8,128)(2,1)S(1)}, bf16[4,2,2,8,1024]{4,3,2,1,0:T(8,128)(2,1)S(1)}, u32[]{:S(2)}, u32[]{:S(2)}) collective-permute-start(bf16[4,2,2,8,1024]{4,3,2,1,0:T(8,128)(2,1)S(1)} %get-tuple-element.41), channel_id=1, source_target_pairs={{16,18},{18,16},{20,22},{22,20},{24,26},{26,24},{28,30},{30,28},{1... | collective-permute-start | bytes 786440 | tf_op jit(solution)/shard_map/cond/branch_1_fun/ppermute | solution.py:529
  45.2 1.5 %collective-permute-done.1.recv_ref = bf16[4,2,2,8,1024]{4,3,2,1,0:T(8,128)(2,1)S(1)} collective-permute-done((bf16[4,2,2,8,1024]{4,3,2,1,0:T(8,128)(2,1)S(1)}, bf16[4,2,2,8,1024]{4,3,2,1,0:T(8,128)(2,1)S(1)}, u32[]{:S(2)}, u32[]{:S(2)}) %collective-permute-start.1) | collective-permute-done | bytes 262176 | tf_op jit(solution)/shard_map/cond/branch_1_fun/ppermute | solution.py:529
  46.7 1.5 %relay_slots.1.rest_1_ = bf16[16,2,8,1024]{3,2,1,0:T(8,128)(2,1)} custom-call(s32[10]{0:T(128)S(1)} %get-tuple-element.32.info_ref, bf16[4,2,2,8,1024]{4,3,2,1,0:T(8,128)(2,1)S(1)} %get-tuple-element.40.keep_ref, bf16[4,2,2,8,1024]{4,3,2,1,0:T(8,128)(2,1)S(1)} %collective-permute-done.1.recv_ref), custom_call_target="tpu_custom_call" | custom-call | flops 1 | bytes 1 | tf_op jit(solution)/shard_map/cond/branch_1_fun/relay_slots/pallas_call | solution.py:590
  48.1 4.2 %all-to-all-start = ((bf16[16,2,8,1024]{3,2,1,0:T(8,128)(2,1)}), bf16[16,2,8,1024]{3,2,1,0:T(8,128)(2,1)S(1)}, u32[]{:S(2)}, u32[]{:S(2)}) async-start(bf16[16,2,8,1024]{3,2,1,0:T(8,128)(2,1)} %relay_slots.1.rest_1_), calls=%async_computation | async-start | bytes 1048576 | tf_op jit(solution)/shard_map/cond/branch_1_fun/all_to_all | solution.py:532
  52.4 4.2 %prompt_attention.2 = (bf16[640,4096]{1,0:T(8,128)(2,1)}, f32[8,128]{1,0:T(8,128)}) custom-call(s32[10]{0:T(128)S(1)} %get-tuple-element.32.info_ref, bf16[640,4096]{1,0:T(8,128)(2,1)} %get-tuple-element.33.q_ref, bf16[640,1024]{1,0:T(8,128)(2,1)S(1)} %get-tuple-element.34.kv_ref, ...), custom_call_target="tpu_custom_call", output_to_operand_aliasing={{0}: (3, {})} | custom-call | flops 1 | bytes 1 | tf_op jit(solution)/shard_map/cond/branch_1_fun/prompt_attention/pallas_call | solution.py:124
  56.5 0.0 copy-start
  56.5 0.7 copy-done
  57.2 1.7 %combine_parts.2 = (bf16[4,8192]{1,0:T(4,128)(2,1)}, f32[8,128]{1,0:T(8,128)}) custom-call(s32[10]{0:T(128)S(1)} %get-tuple-element.32.info_ref, f32[8,32,256]{2,1,0:T(8,128)S(1)} %get-tuple-element.45.refs_0_, f32[8,32,256]{2,1,0:T(8,128)S(1)} %get-tuple-element.46.refs_1_, f32[8,128]{1,0:T(8,128)S(1)} %copy-done), custom_call_target="tpu_custom_call" | custom-call | flops 1 | bytes 1 | tf_op jit(solution)/shard_map/cond/branch_1_fun/combine_parts/pallas_call | solution.py:363
  58.9 8.7 %all-to-all-done.slots_ref = bf16[16,2,8,1024]{3,2,1,0:T(8,128)(2,1)S(1)} async-done(((bf16[16,2,8,1024]{3,2,1,0:T(8,128)(2,1)}), bf16[16,2,8,1024]{3,2,1,0:T(8,128)(2,1)S(1)}, u32[]{:S(2)}, u32[]{:S(2)}) %all-to-all-start) | async-done | bytes 524320 | tf_op jit(solution)/shard_map/cond/branch_1_fun/all_to_all | solution.py:532
  67.6 2.3 %far_rows.1 = (f32[8,8,256]{2,1,0:T(8,128)S(1)}, bf16[40,8,2048]{2,1,0:T(8,128)(2,1)}) custom-call(s32[10]{0:T(128)S(1)} %get-tuple-element.32.info_ref, bf16[1,8192]{1,0:T(2,128)(2,1)} %get-tuple-element.43.q_ref, bf16[16,2,8,1024]{3,2,1,0:T(8,128)(2,1)S(1)} %all-to-all-done.slots_ref), custom_call_target="tpu_custom_call" | custom-call | flops 1 | bytes 1 | tf_op jit(solution)/shard_map/cond/branch_1_fun/far_rows/pallas_call | solution.py:607
  69.9 0.0 collective-permute-done.7.refs_0_
  69.9 0.0 collective-permute-done.8.refs_1_
  69.9 0.0 collective-permute-done.9.refs_2_
  69.9 1.1 %collective-permute-done.10.refs_3_ = bf16[2,6,8,1024]{3,2,1,0:T(8,128)(2,1)S(1)} collective-permute-done((bf16[2,6,8,1024]{3,2,1,0:T(8,128)(2,1)S(1)}, bf16[2,6,8,1024]{3,2,1,0:T(8,128)(2,1)S(1)}, u32[]{:S(2)}, u32[]{:S(2)}) %collective-permute-start.10) | collective-permute-done | bytes 196640 | tf_op jit(solution)/shard_map/ppermute | solution.py:526
  71.0 1.9 %near_rows.1.refs_0_ = f32[8,8,256]{2,1,0:T(8,128)S(1)} custom-call(s32[10]{0:T(128)S(1)} %pad_add_fusion.info_ref, bf16[1,8192]{1,0:T(2,128)(2,1)} %q_ref.5, f32[8,8,256]{2,1,0:T(8,128)S(1)} %get-tuple-element.104.earlier_ref, bf16[2,6,8,1024]{3,2,1,0:T(8,128)(2,1)S(1)} %collective-permute-done.7.refs_0_, ...), custom_call_target="tpu_custom_call" | custom-call | flops 1 | bytes 1 | tf_op jit(solution)/shard_map/near_rows/pallas_call | solution.py:317
  72.9 1.5 %collective-permute-start.11 = (f32[8,8,256]{2,1,0:T(8,128)S(1)}, f32[8,8,256]{2,1,0:T(8,128)S(1)}, u32[]{:S(2)}, u32[]{:S(2)}) collective-permute-start(f32[8,8,256]{2,1,0:T(8,128)S(1)} %near_rows.1.refs_0_), channel_id=1, source_target_pairs={{0,1},{1,0},{2,3},{3,2},{4,5},{5,4},{6,7},{7,6},{8,9},{9,8},{10,11... | collective-permute-start | bytes 196616 | tf_op jit(solution)/shard_map/ppermute | solution.py:715
  74.4 1.5 %store_near.1 = bf16[40,8,2048]{2,1,0:T(8,128)(2,1)} custom-call(s32[10]{0:T(128)S(1)} %pad_add_fusion.info_ref, bf16[2,6,8,1024]{3,2,1,0:T(8,128)(2,1)S(1)} %collective-permute-done.7.refs_0_, bf16[2,6,8,1024]{3,2,1,0:T(8,128)(2,1)S(1)} %collective-permute-done.8.refs_1_, ...), custom_call_target="tpu_custom_call", output_to_operand_aliasing={{}: (5, {})} | custom-call | flops 1 | bytes 1 | tf_op jit(solution)/shard_map/store_near/pallas_call | solution.py:673
  75.9 1.3 %collective-permute-done.11.refs_1_ = f32[8,8,256]{2,1,0:T(8,128)S(1)} collective-permute-done((f32[8,8,256]{2,1,0:T(8,128)S(1)}, f32[8,8,256]{2,1,0:T(8,128)S(1)}, u32[]{:S(2)}, u32[]{:S(2)}) %collective-permute-start.11) | collective-permute-done | bytes 65568 | tf_op jit(solution)/shard_map/ppermute | solution.py:715
  77.2 1.4 %combine_parts.3 = (bf16[1,8192]{1,0:T(2,128)(2,1)}, f32[8,128]{1,0:T(8,128)}) custom-call(s32[10]{0:T(128)S(1)} %pad_add_fusion.info_ref, f32[8,8,256]{2,1,0:T(8,128)S(1)} %near_rows.1.refs_0_, f32[8,8,256]{2,1,0:T(8,128)S(1)} %collective-permute-done.11.refs_1_), custom_call_target="tpu_custom_call" | custom-call | flops 1 | bytes 1 | tf_op jit(solution)/shard_map/combine_parts/pallas_call | solution.py:363
Async XLA Ops:
  0.6 10.7 %copy-start.2 = (s32[8]{0:T(128)S(1)}, s32[8]{0:T(128)}, u32[]{:S(2)}) copy-start(s32[8]{0:T(128)} %param.19) | copy-start | bytes 100
  0.8 20.4 %all-to-all-start.1 = ((bf16[16,3,8,1024]{3,2,1,0:T(8,128)(2,1)}), bf16[16,3,8,1024]{3,2,1,0:T(8,128)(2,1)S(1)}, u32[]{:S(2)}, u32[]{:S(2)}) async-start(bf16[16,3,8,1024]{3,2,1,0:T(8,128)(2,1)} %bitcast.5), calls=%async_computation.1 | async-start | bytes 1572864 | tf_op jit(solution)/shard_map/all_to_all | solution.py:532
  6.0 9.5 %copy-start.1 = (bf16[640,1024]{1,0:T(8,128)(2,1)S(1)}, bf16[640,1024]{1,0:T(8,128)(2,1)}, u32[]{:S(2)}) copy-start(bf16[640,1024]{1,0:T(8,128)(2,1)} %kv_ref.1) | copy-start | bytes 3932164
  6.0 17.8 %collective-permute-start.2 = (bf16[2,4,8,1024]{3,2,1,0:T(8,128)(2,1)S(1)}, bf16[2,4,8,1024]{3,2,1,0:T(8,128)(2,1)S(1)}, u32[]{:S(2)}, u32[]{:S(2)}) collective-permute-start(bf16[2,4,8,1024]{3,2,1,0:T(8,128)(2,1)S(1)} %get-tuple-element.88), channel_id=1, source_target_pairs={{0,16},{2,18},{4,20},{6,22},{8,24},{10,26},{12,28},{14,30},{1,17},... | collective-permute-start | bytes 393224 | tf_op jit(solution)/shard_map/ppermute | solution.py:526
  7.5 17.5 %collective-permute-start.3 = (bf16[2,4,8,1024]{3,2,1,0:T(8,128)(2,1)S(1)}, bf16[2,4,8,1024]{3,2,1,0:T(8,128)(2,1)S(1)}, u32[]{:S(2)}, u32[]{:S(2)}) collective-permute-start(bf16[2,4,8,1024]{3,2,1,0:T(8,128)(2,1)S(1)} %get-tuple-element.89), channel_id=1, source_target_pairs={{0,20},{2,22},{4,24},{6,26},{8,28},{10,30},{12,16},{14,18},{1,21},... | collective-permute-start | bytes 393224 | tf_op jit(solution)/shard_map/ppermute | solution.py:526
  8.8 17.7 %collective-permute-start.4 = (bf16[2,4,8,1024]{3,2,1,0:T(8,128)(2,1)S(1)}, bf16[2,4,8,1024]{3,2,1,0:T(8,128)(2,1)}, u32[]{:S(2)}, u32[]{:S(2)}) collective-permute-start(bf16[2,4,8,1024]{3,2,1,0:T(8,128)(2,1)S(1)} %get-tuple-element.90), channel_id=1, source_target_pairs={{0,24},{2,26},{4,28},{6,30},{8,16},{10,18},{12,20},{14,22},{1,25},... | collective-permute-start | bytes 393224 | tf_op jit(solution)/shard_map/ppermute | solution.py:526
  10.1 25.3 %collective-permute-start.5 = (bf16[2,4,8,1024]{3,2,1,0:T(8,128)(2,1)S(1)}, bf16[2,4,8,1024]{3,2,1,0:T(8,128)(2,1)}, u32[]{:S(2)}, u32[]{:S(2)}) collective-permute-start(bf16[2,4,8,1024]{3,2,1,0:T(8,128)(2,1)S(1)} %get-tuple-element.91), channel_id=1, source_target_pairs={{0,28},{2,30},{4,16},{6,18},{8,20},{10,22},{12,24},{14,26},{1,29},... | collective-permute-start | bytes 393224 | tf_op jit(solution)/shard_map/ppermute | solution.py:526
  21.8 0.7 collective-permute-start
  23.2 17.3 %collective-permute-start.6 = (f32[8,32,256]{2,1,0:T(8,128)S(1)}, f32[8,32,256]{2,1,0:T(8,128)S(1)}, u32[]{:S(2)}, u32[]{:S(2)}) collective-permute-start(f32[8,32,256]{2,1,0:T(8,128)S(1)} %get-tuple-element.96), channel_id=1, source_target_pairs={{0,1},{1,0},{2,3},{3,2},{4,5},{5,4},{6,7},{7,6},{8,9},{9,8},{10,11... | collective-permute-start | bytes 786440 | tf_op jit(solution)/shard_map/ppermute | solution.py:715
  35.3 34.6 %collective-permute-start.7 = (bf16[2,6,8,1024]{3,2,1,0:T(8,128)(2,1)}, bf16[2,6,8,1024]{3,2,1,0:T(8,128)(2,1)S(1)}, u32[]{:S(2)}, u32[]{:S(2)}) collective-permute-start(bf16[2,6,8,1024]{3,2,1,0:T(8,128)(2,1)} %get-tuple-element.98), channel_id=1, source_target_pairs={{0,16},{2,18},{4,20},{6,22},{8,24},{10,26},{12,28},{14,30},{1,17},... | collective-permute-start | bytes 589832 | tf_op jit(solution)/shard_map/ppermute | solution.py:526
  36.6 33.3 %collective-permute-start.8 = (bf16[2,6,8,1024]{3,2,1,0:T(8,128)(2,1)}, bf16[2,6,8,1024]{3,2,1,0:T(8,128)(2,1)S(1)}, u32[]{:S(2)}, u32[]{:S(2)}) collective-permute-start(bf16[2,6,8,1024]{3,2,1,0:T(8,128)(2,1)} %get-tuple-element.99), channel_id=1, source_target_pairs={{0,20},{2,22},{4,24},{6,26},{8,28},{10,30},{12,16},{14,18},{1,21},... | collective-permute-start | bytes 589832 | tf_op jit(solution)/shard_map/ppermute | solution.py:526
  37.9 32.0 %collective-permute-start.9 = (bf16[2,6,8,1024]{3,2,1,0:T(8,128)(2,1)S(1)}, bf16[2,6,8,1024]{3,2,1,0:T(8,128)(2,1)S(1)}, u32[]{:S(2)}, u32[]{:S(2)}) collective-permute-start(bf16[2,6,8,1024]{3,2,1,0:T(8,128)(2,1)S(1)} %get-tuple-element.100), channel_id=1, source_target_pairs={{0,24},{2,26},{4,28},{6,30},{8,16},{10,18},{12,20},{14,22},{1,25},... | collective-permute-start | bytes 589832 | tf_op jit(solution)/shard_map/ppermute | solution.py:526
  39.2 31.8 %collective-permute-start.10 = (bf16[2,6,8,1024]{3,2,1,0:T(8,128)(2,1)S(1)}, bf16[2,6,8,1024]{3,2,1,0:T(8,128)(2,1)S(1)}, u32[]{:S(2)}, u32[]{:S(2)}) collective-permute-start(bf16[2,6,8,1024]{3,2,1,0:T(8,128)(2,1)S(1)} %get-tuple-element.101), channel_id=1, source_target_pairs={{0,28},{2,30},{4,16},{6,18},{8,20},{10,22},{12,24},{14,26},{1,29},... | collective-permute-start | bytes 589832 | tf_op jit(solution)/shard_map/ppermute | solution.py:526
  43.2 3.4 %collective-permute-start.1 = (bf16[4,2,2,8,1024]{4,3,2,1,0:T(8,128)(2,1)S(1)}, bf16[4,2,2,8,1024]{4,3,2,1,0:T(8,128)(2,1)S(1)}, u32[]{:S(2)}, u32[]{:S(2)}) collective-permute-start(bf16[4,2,2,8,1024]{4,3,2,1,0:T(8,128)(2,1)S(1)} %get-tuple-element.41), channel_id=1, source_target_pairs={{16,18},{18,16},{20,22},{22,20},{24,26},{26,24},{28,30},{30,28},{1... | collective-permute-start | bytes 786440 | tf_op jit(solution)/shard_map/cond/branch_1_fun/ppermute | solution.py:529
  48.1 19.5 %all-to-all-start = ((bf16[16,2,8,1024]{3,2,1,0:T(8,128)(2,1)}), bf16[16,2,8,1024]{3,2,1,0:T(8,128)(2,1)S(1)}, u32[]{:S(2)}, u32[]{:S(2)}) async-start(bf16[16,2,8,1024]{3,2,1,0:T(8,128)(2,1)} %relay_slots.1.rest_1_), calls=%async_computation | async-start | bytes 1048576 | tf_op jit(solution)/shard_map/cond/branch_1_fun/all_to_all | solution.py:532
  56.5 0.7 copy-start
  72.9 4.3 %collective-permute-start.11 = (f32[8,8,256]{2,1,0:T(8,128)S(1)}, f32[8,8,256]{2,1,0:T(8,128)S(1)}, u32[]{:S(2)}, u32[]{:S(2)}) collective-permute-start(f32[8,8,256]{2,1,0:T(8,128)S(1)} %near_rows.1.refs_0_), channel_id=1, source_target_pairs={{0,1},{1,0},{2,3},{3,2},{4,5},{5,4},{6,7},{7,6},{8,9},{9,8},{10,11... | collective-permute-start | bytes 196616 | tf_op jit(solution)/shard_map/ppermute | solution.py:715

commit v8 on v7

--- a/solution.py
+++ b/solution.py
@@ -349,13 +349,18 @@
                 parts = [part_refs[0][n, head] for n in range(part_refs[0].shape[0])]
             mixed, _, total = merged(parts)
             results.append(mixed / total)
-        for r in range(out_ref.shape[0]):
-            row = [
-                results[head][r * GROUP + g : r * GROUP + g + 1]
-                for head in range(KVHEADS)
-                for g in range(GROUP)
-            ]
-            out_ref[r : r + 1] = jnp.concatenate(row, axis=1).astype(jnp.bfloat16)
+        rows = [
+            jnp.concatenate(
+                [
+                    results[head][r * GROUP + g : r * GROUP + g + 1]
+                    for head in range(KVHEADS)
+                    for g in range(GROUP)
+                ],
+                axis=1,
+            )
+            for r in range(out_ref.shape[0])
+        ]
+        out_ref[...] = jnp.concatenate(rows, axis=0).astype(jnp.bfloat16)
 
 
 def combine_parts(info, parts, after=()):
@@ -566,7 +571,7 @@
 
     near_shape = (2, 2 * near) + block
 
-    def first_stage(spread, *marks):
+    def gather_stage(spread, *marks):
         (outgoing,) = copies(
             for_neighbour, 2 * PAIRS, info, [spread], [(PAIRS, 2, near) + block], "for_neighbour", marks
         )
@@ -574,6 +579,13 @@
         return copies(
             for_receivers, 4 * PAIRS, info, [spread, incoming], [near_shape] * PAIRS, "for_receivers"
         )
+
+    def first_stage(near_rows, *far_parts):
+        spread = spread_out(near_rows.reshape((2 * half, near) + block))
+        far_here = [crossing(part, s) for s, part in enumerate(far_parts, 1)]
+        part, mark = cached([near_rows])
+        prompt, mark = prompt_part(0, None, [mark])
+        return *staged(gather_stage, spread, mark), prompt, part, *far_here
 
     def second_stage(prompt, part, other, *far_here):
         keep, give = copies(
@@ -631,7 +643,7 @@
     def staged(stage, *operands):
         def never(*operands):
             outs = [jnp.zeros(out.shape, out.dtype) for out in jax.eval_shape(stage, *operands)]
-            return tuple(outs) if stage is first_stage else (operands[0], *outs[1:])
+            return (operands[0], *outs[1:]) if stage is second_stage else tuple(outs)
 
         return lax.cond(always, lambda *operands: tuple(stage(*operands)), never, *operands)
 
@@ -652,14 +664,13 @@
         cost_estimate=COST,
         name="cut_rows",
     )(by_unit)
-    spread = spread_out(near_rows.reshape((2 * half, near) + block))
-    far_here = [crossing(part, s) for s, part in enumerate(far_parts)]
-    part, mark = cached([near_rows])
-    prompt, mark = prompt_part(0, None, [mark])
-    near_parts = staged(first_stage, spread, mark)
-    near_parts, far_here = lax.optimization_barrier((near_parts, far_here))
+    first = crossing(far_parts[0], 0)
+    outs = staged(first_stage, near_rows, *far_parts[1:])
+    near_parts, (prompt, part), far_here = outs[:PAIRS], outs[PAIRS : PAIRS + 2], outs[PAIRS + 2 :]
+    other = exchanged(part)
+    near_parts, first = lax.optimization_barrier((near_parts, first))
+    far_here = [first, *far_here]
     near_here = [crossing(near_part, s) for s, near_part in enumerate(near_parts)]
-    other = exchanged(part)
     prompt, handed, decode_out, arrival = staged(second_stage, prompt, part, other, *far_here)
     arrival = arrival_part(
         near_rows_kernel,

time: 79.4 us -> 79.3 us (level)
  Pallas kernels: 25.6 us -> 23.4 us
    ppermute x2, waiting for transfers between devices: 1.31 us -> 3.65 us  [exchanged(): return lax.ppermute(part, 'tp', [(0, 1), (1, 0)])]
    ppermute x8, waiting for transfers between devices: 12.6 us -> 10.5 us  [crossing(): return lax.ppermute(array, 'inst', hops)]
  transfers between devices with their start and end apart: 14 -> 14, of which waited for: 8 -> 9; matrix products, arithmetic and copies ran while one was open for 0% -> 1% of each run, Pallas kernels for 28% -> 26%
where the time goes in v8:
time: 79.3 us; the launch traced here: 78.4 us
  waiting for transfers between devices  27.1 us (34%)
  starting transfers between devices  25 us (32%)
  Pallas kernels  23.4 us (30%)
  between operations  1.39 us (2%)
    all_to_all x2, waiting for transfers between devices, spread_out(): lax.all_to_all(array, ('inst', 'tp'), 0, 0, axis_index_groups=groups, til...  11.5 us
    ppermute x8, waiting for transfers between devices, crossing(): return lax.ppermute(array, 'inst', hops)  10.5 us
    ppermute x8, starting transfers between devices, crossing(): return lax.ppermute(array, 'inst', hops)  10.3 us
    all_to_all x2, starting transfers between devices, spread_out(): lax.all_to_all(array, ('inst', 'tp'), 0, 0, axis_index_groups=groups, til...  9.56 us
    pallas_call x2, Pallas kernels, prompt_attention(): pl.pallas_call(functools.partial(prompt_kernel, heads), out_shape=(jax.Sh...  7.28 us
    pallas_call x1, Pallas kernels, cache_attention(): pl.pallas_call(functools.partial(cache_kernel, page_len), out_shape=(jax....  4.1 us
    pallas_call x3, Pallas kernels, copies(): pl.pallas_call(functools.partial(copy_kernel, plan, side, (len(operands),...  3.87 us
    ppermute x2, waiting for transfers between devices, exchanged(): return lax.ppermute(part, 'tp', [(0, 1), (1, 0)])  3.65 us
  transfers between devices with their start and end apart: 14, of which 9 were waited for; matrix products, arithmetic and copies ran while one was open for 1% of the time, Pallas kernels for 26%

profile of v8, /device:TPU:24, one launch (start us, length us, event | category | flops | bytes accessed | tf_op | source)
XLA Modules:
  0.0 78.4 jit_solution(16923953845013003521)
XLA Ops:
  0.6 0.2 cut_rows.1
  0.8 1.3 %collective-permute-start.5 = (bf16[2,4,8,1024]{3,2,1,0:T(8,128)(2,1)S(1)}, bf16[2,4,8,1024]{3,2,1,0:T(8,128)(2,1)S(1)}, u32[]{:S(2)}, u32[]{:S(2)}) collective-permute-start(bf16[2,4,8,1024]{3,2,1,0:T(8,128)(2,1)S(1)} %get-tuple-element.132), channel_id=1, source_target_pairs={{0,16},{2,18},{4,20},{6,22},{8,24},{10,26},{12,28},{14,30},{1,17},... | collective-permute-start | bytes 393224 | tf_op jit(solution)/shard_map/ppermute | solution.py:531
  2.7 0.7 pad_add_fusion.info_ref
  3.5 0.0 copy-start.2
  3.5 29.8 %conditional.3 = (bf16[2,6,8,1024]{3,2,1,0:T(8,128)(2,1)}, bf16[2,6,8,1024]{3,2,1,0:T(8,128)(2,1)}, bf16[2,6,8,1024]{3,2,1,0:T(8,128)(2,1)}, bf16[2,6,8,1024]{3,...) conditional(s32[]{:T(128)} %convert_element_type.7, () %tuple.32, ...), branch_computations={%region_0.0_spmd, %region_1.0_spmd} | conditional | flops 5 | bytes 6684764 | solution.py:648
  3.5 5.3 %all-to-all-start = ((bf16[16,3,8,1024]{3,2,1,0:T(8,128)(2,1)}), bf16[16,3,8,1024]{3,2,1,0:T(8,128)(2,1)S(1)}, u32[]{:S(2)}, u32[]{:S(2)}) async-start(bf16[16,3,8,1024]{3,2,1,0:T(8,128)(2,1)} %bitcast), calls=%async_computation | async-start | bytes 1572864 | tf_op jit(solution)/shard_map/cond/branch_1_fun/all_to_all | solution.py:537
  8.8 1.3 %collective-permute-start.1 = (bf16[2,4,8,1024]{3,2,1,0:T(8,128)(2,1)S(1)}, bf16[2,4,8,1024]{3,2,1,0:T(8,128)(2,1)}, u32[]{:S(2)}, u32[]{:S(2)}) collective-permute-start(bf16[2,4,8,1024]{3,2,1,0:T(8,128)(2,1)S(1)} %get-tuple-element.74), channel_id=1, source_target_pairs={{0,20},{2,22},{4,24},{6,26},{8,28},{10,30},{12,16},{14,18},{1,21},... | collective-permute-start | bytes 393224 | tf_op jit(solution)/shard_map/cond/branch_1_fun/ppermute | solution.py:531
  10.1 1.3 %collective-permute-start.2 = (bf16[2,4,8,1024]{3,2,1,0:T(8,128)(2,1)S(1)}, bf16[2,4,8,1024]{3,2,1,0:T(8,128)(2,1)}, u32[]{:S(2)}, u32[]{:S(2)}) collective-permute-start(bf16[2,4,8,1024]{3,2,1,0:T(8,128)(2,1)S(1)} %get-tuple-element.75), channel_id=1, source_target_pairs={{0,24},{2,26},{4,28},{6,30},{8,16},{10,18},{12,20},{14,22},{1,25},... | collective-permute-start | bytes 393224 | tf_op jit(solution)/shard_map/cond/branch_1_fun/ppermute | solution.py:531
  11.4 1.3 %collective-permute-start.3 = (bf16[2,4,8,1024]{3,2,1,0:T(8,128)(2,1)S(1)}, bf16[2,4,8,1024]{3,2,1,0:T(8,128)(2,1)}, u32[]{:S(2)}, u32[]{:S(2)}) collective-permute-start(bf16[2,4,8,1024]{3,2,1,0:T(8,128)(2,1)S(1)} %get-tuple-element.76), channel_id=1, source_target_pairs={{0,28},{2,30},{4,16},{6,18},{8,20},{10,22},{12,24},{14,26},{1,29},... | collective-permute-start | bytes 393224 | tf_op jit(solution)/shard_map/cond/branch_1_fun/ppermute | solution.py:531
  12.7 4.1 %cache_attention.1 = (f32[8,32,256]{2,1,0:T(8,128)S(1)}, f32[8,128]{1,0:T(8,128)}) custom-call(s32[10]{0:T(128)S(1)} %get-tuple-element.58.info_ref, s32[4,8]{1,0:T(4,128)} %get-tuple-element.152.table_ref, s32[4]{0:T(128)} %get-tuple-element.153.lengths_ref, bf16[4,8192]{1,0:T(4,128)(2,1)} %get-tuple-element.154.q_ref, bf16[320,2048]{1,0:T(8,128)(2,1)} %bitcast.10, ...), custom_call_target="tpu_custom_call" | custom-call | flops 1 | bytes 1 | tf_op jit(solution)/shard_map/cond/branch_1_fun/cache_attention/pallas_call | solution.py:213
  16.8 3.1 %prompt_attention.2 = (bf16[640,4096]{1,0:T(8,128)(2,1)}, f32[8,128]{1,0:T(8,128)S(1)}) custom-call(s32[10]{0:T(128)S(1)} %get-tuple-element.58.info_ref, bf16[640,4096]{1,0:T(8,128)(2,1)} %get-tuple-element.60.q_ref, bf16[640,1024]{1,0:T(8,128)(2,1)} %get-tuple-element.61.kv_ref, f32[8,128]{1,0:T(8,128)} %get-tuple-element.66.rest_0_), custom_call_target="tpu_custom_call" | custom-call | flops 1 | bytes 1 | tf_op jit(solution)/shard_map/cond/branch_1_fun/prompt_attention/pallas_call | solution.py:124
  19.9 2.9 %all-to-all-done = bf16[16,3,8,1024]{3,2,1,0:T(8,128)(2,1)S(1)} async-done(((bf16[16,3,8,1024]{3,2,1,0:T(8,128)(2,1)}), bf16[16,3,8,1024]{3,2,1,0:T(8,128)(2,1)S(1)}, u32[]{:S(2)}, u32[]{:S(2)}) %all-to-all-start) | async-done | bytes 786464 | tf_op jit(solution)/shard_map/cond/branch_1_fun/all_to_all | solution.py:537
  22.7 2.0 %conditional = ((bf16[2,6,8,1024]{3,2,1,0:T(8,128)(2,1)}, bf16[2,6,8,1024]{3,2,1,0:T(8,128)(2,1)}, bf16[2,6,8,1024]{3,2,1,0:T(8,128)(2,1)}, bf16[2,6,8,1024]{3,2,1,0:T(8,128)(2,1)})) conditional(s32[]{:T(128)} %convert_element_type.1, () %tuple.21, (s32[10]{0:T(128)S(1)}, bf16[16,3,8,1024]{3,2,1,0:T(8,128)(2,1)S(1)}, f32[8,128]{1,0:T(8,128)S(1)}) %tuple.22), branch_computations={%region_2.0_spmd, %region_3.0_spmd} | conditional | flops 2 | bytes 1572914 | solution.py:648
  22.7 0.6 for_neighbour.1
  23.4 0.7 collective-permute-start
  24.0 0.0 collective-permute-done.refs_1_
  24.1 0.7 for_receivers.1
  24.8 1.6 %collective-permute-done.1 = bf16[2,4,8,1024]{3,2,1,0:T(8,128)(2,1)} collective-permute-done((bf16[2,4,8,1024]{3,2,1,0:T(8,128)(2,1)S(1)}, bf16[2,4,8,1024]{3,2,1,0:T(8,128)(2,1)}, u32[]{:S(2)}, u32[]{:S(2)}) %collective-permute-start.1) | collective-permute-done | bytes 131104 | tf_op jit(solution)/shard_map/cond/branch_1_fun/ppermute | solution.py:531
  26.4 1.4 %collective-permute-done.2 = bf16[2,4,8,1024]{3,2,1,0:T(8,128)(2,1)} collective-permute-done((bf16[2,4,8,1024]{3,2,1,0:T(8,128)(2,1)S(1)}, bf16[2,4,8,1024]{3,2,1,0:T(8,128)(2,1)}, u32[]{:S(2)}, u32[]{:S(2)}) %collective-permute-start.2) | collective-permute-done | bytes 131104 | tf_op jit(solution)/shard_map/cond/branch_1_fun/ppermute | solution.py:531
  27.8 5.5 %collective-permute-done.3 = bf16[2,4,8,1024]{3,2,1,0:T(8,128)(2,1)} collective-permute-done((bf16[2,4,8,1024]{3,2,1,0:T(8,128)(2,1)S(1)}, bf16[2,4,8,1024]{3,2,1,0:T(8,128)(2,1)}, u32[]{:S(2)}, u32[]{:S(2)}) %collective-permute-start.3) | collective-permute-done | bytes 131104 | tf_op jit(solution)/shard_map/cond/branch_1_fun/ppermute | solution.py:531
  33.3 1.5 %collective-permute-start.6 = (f32[8,32,256]{2,1,0:T(8,128)S(1)}, f32[8,32,256]{2,1,0:T(8,128)S(1)}, u32[]{:S(2)}, u32[]{:S(2)}) collective-permute-start(f32[8,32,256]{2,1,0:T(8,128)S(1)} %get-tuple-element.137), channel_id=1, source_target_pairs={{0,1},{1,0},{2,3},{3,2},{4,5},{5,4},{6,7},{7,6},{8,9},{9,8},{10,11... | collective-permute-start | bytes 786440 | tf_op jit(solution)/shard_map/ppermute | solution.py:726
  34.7 0.0 collective-permute-done.5
  34.7 1.3 %collective-permute-start.7 = (bf16[2,6,8,1024]{3,2,1,0:T(8,128)(2,1)}, bf16[2,6,8,1024]{3,2,1,0:T(8,128)(2,1)S(1)}, u32[]{:S(2)}, u32[]{:S(2)}) collective-permute-start(bf16[2,6,8,1024]{3,2,1,0:T(8,128)(2,1)} %get-tuple-element.139), channel_id=1, source_target_pairs={{0,16},{2,18},{4,20},{6,22},{8,24},{10,26},{12,28},{14,30},{1,17},... | collective-permute-start | bytes 589832 | tf_op jit(solution)/shard_map/ppermute | solution.py:531
  36.0 1.3 %collective-permute-start.8 = (bf16[2,6,8,1024]{3,2,1,0:T(8,128)(2,1)}, bf16[2,6,8,1024]{3,2,1,0:T(8,128)(2,1)S(1)}, u32[]{:S(2)}, u32[]{:S(2)}) collective-permute-start(bf16[2,6,8,1024]{3,2,1,0:T(8,128)(2,1)} %get-tuple-element.140), channel_id=1, source_target_pairs={{0,20},{2,22},{4,24},{6,26},{8,28},{10,30},{12,16},{14,18},{1,21},... | collective-permute-start | bytes 589832 | tf_op jit(solution)/shard_map/ppermute | solution.py:531
  37.3 1.3 %collective-permute-start.9 = (bf16[2,6,8,1024]{3,2,1,0:T(8,128)(2,1)}, bf16[2,6,8,1024]{3,2,1,0:T(8,128)(2,1)S(1)}, u32[]{:S(2)}, u32[]{:S(2)}) collective-permute-start(bf16[2,6,8,1024]{3,2,1,0:T(8,128)(2,1)} %get-tuple-element.141), channel_id=1, source_target_pairs={{0,24},{2,26},{4,28},{6,30},{8,16},{10,18},{12,20},{14,22},{1,25},... | collective-permute-start | bytes 589832 | tf_op jit(solution)/shard_map/ppermute | solution.py:531
  38.6 1.3 %collective-permute-start.10 = (bf16[2,6,8,1024]{3,2,1,0:T(8,128)(2,1)}, bf16[2,6,8,1024]{3,2,1,0:T(8,128)(2,1)S(1)}, u32[]{:S(2)}, u32[]{:S(2)}) collective-permute-start(bf16[2,6,8,1024]{3,2,1,0:T(8,128)(2,1)} %get-tuple-element.142), channel_id=1, source_target_pairs={{0,28},{2,30},{4,16},{6,18},{8,20},{10,22},{12,24},{14,26},{1,29},... | collective-permute-start | bytes 589832 | tf_op jit(solution)/shard_map/ppermute | solution.py:531
  39.9 1.2 %collective-permute-done.6 = f32[8,32,256]{2,1,0:T(8,128)S(1)} collective-permute-done((f32[8,32,256]{2,1,0:T(8,128)S(1)}, f32[8,32,256]{2,1,0:T(8,128)S(1)}, u32[]{:S(2)}, u32[]{:S(2)}) %collective-permute-start.6) | collective-permute-done | bytes 262176 | tf_op jit(solution)/shard_map/ppermute | solution.py:726
  41.1 0.0 copy-done.2
  41.1 28.5 %conditional.4 = (bf16[640,4096]{1,0:T(8,128)(2,1)}, bf16[40,8,2048]{2,1,0:T(8,128)(2,1)S(1)}, bf16[4,8192]{1,0:T(4,128)(2,1)}, f32[8,8,256]{2,1,0:T(8,128)S(1)}) conditional(s32[]{:T(128)} %convert_element_type.7, bf16[640,4096]{1,0:T(8,128)(2,1)} %get-tuple-element.127, (s32[10]{0:T(128)S(1)}, bf16[2,4,8,1024]{3,2,1,0:T(8,128)(2,1)S(1)}, ...), branch_computations={%region_4.0_spmd, %region_5.0_spmd} | conditional | flops 5 | bytes 2637961 | solution.py:648
  41.1 2.6 %split_relays.1 = (bf16[4,2,2,8,1024]{4,3,2,1,0:T(8,128)(2,1)S(1)}, bf16[4,2,2,8,1024]{4,3,2,1,0:T(8,128)(2,1)S(1)}) custom-call(s32[10]{0:T(128)S(1)} %get-tuple-element.77.info_ref, bf16[2,4,8,1024]{3,2,1,0:T(8,128)(2,1)S(1)} %get-tuple-element.81.refs_0_, bf16[2,4,8,1024]{3,2,1,0:T(8,128)(2,1)} %get-tuple-element.82.refs_1_, ...), custom_call_target="tpu_custom_call" | custom-call | flops 1 | bytes 1 | tf_op jit(solution)/shard_map/cond/branch_1_fun/split_relays/pallas_call | solution.py:430
  43.7 1.9 %collective-permute-start.4 = (bf16[4,2,2,8,1024]{4,3,2,1,0:T(8,128)(2,1)S(1)}, bf16[4,2,2,8,1024]{4,3,2,1,0:T(8,128)(2,1)S(1)}, u32[]{:S(2)}, u32[]{:S(2)}) collective-permute-start(bf16[4,2,2,8,1024]{4,3,2,1,0:T(8,128)(2,1)S(1)} %get-tuple-element.86), channel_id=1, source_target_pairs={{16,18},{18,16},{20,22},{22,20},{24,26},{26,24},{28,30},{30,28},{1... | collective-permute-start | bytes 786440 | tf_op jit(solution)/shard_map/cond/branch_1_fun/ppermute | solution.py:534
  45.6 1.5 %collective-permute-done.4.recv_ref = bf16[4,2,2,8,1024]{4,3,2,1,0:T(8,128)(2,1)S(1)} collective-permute-done((bf16[4,2,2,8,1024]{4,3,2,1,0:T(8,128)(2,1)S(1)}, bf16[4,2,2,8,1024]{4,3,2,1,0:T(8,128)(2,1)S(1)}, u32[]{:S(2)}, u32[]{:S(2)}) %collective-permute-start.4) | collective-permute-done | bytes 262176 | tf_op jit(solution)/shard_map/cond/branch_1_fun/ppermute | solution.py:534
  47.1 1.5 %relay_slots.1.rest_1_ = bf16[16,2,8,1024]{3,2,1,0:T(8,128)(2,1)} custom-call(s32[10]{0:T(128)S(1)} %get-tuple-element.77.info_ref, bf16[4,2,2,8,1024]{4,3,2,1,0:T(8,128)(2,1)S(1)} %get-tuple-element.85.keep_ref, bf16[4,2,2,8,1024]{4,3,2,1,0:T(8,128)(2,1)S(1)} %collective-permute-done.4.recv_ref), custom_call_target="tpu_custom_call" | custom-call | flops 1 | bytes 1 | tf_op jit(solution)/shard_map/cond/branch_1_fun/relay_slots/pallas_call | solution.py:602
  48.6 4.2 %all-to-all-start.1 = ((bf16[16,2,8,1024]{3,2,1,0:T(8,128)(2,1)}), bf16[16,2,8,1024]{3,2,1,0:T(8,128)(2,1)S(1)}, u32[]{:S(2)}, u32[]{:S(2)}) async-start(bf16[16,2,8,1024]{3,2,1,0:T(8,128)(2,1)} %relay_slots.1.rest_1_), calls=%async_computation.1 | async-start | bytes 1048576 | tf_op jit(solution)/shard_map/cond/branch_1_fun/all_to_all | solution.py:537
  52.8 4.2 %prompt_attention.3 = (bf16[640,4096]{1,0:T(8,128)(2,1)}, f32[8,128]{1,0:T(8,128)}) custom-call(s32[10]{0:T(128)S(1)} %get-tuple-element.77.info_ref, bf16[640,4096]{1,0:T(8,128)(2,1)} %get-tuple-element.78.q_ref, bf16[640,1024]{1,0:T(8,128)(2,1)} %get-tuple-element.79.kv_ref, ...), custom_call_target="tpu_custom_call", output_to_operand_aliasing={{0}: (3, {})} | custom-call | flops 1 | bytes 1 | tf_op jit(solution)/shard_map/cond/branch_1_fun/prompt_attention/pallas_call | solution.py:124
  57.0 0.0 copy-start
  57.0 0.7 copy-done
  57.7 1.7 %combine_parts.2 = (bf16[4,8192]{1,0:T(4,128)(2,1)}, f32[8,128]{1,0:T(8,128)}) custom-call(s32[10]{0:T(128)S(1)} %get-tuple-element.77.info_ref, f32[8,32,256]{2,1,0:T(8,128)S(1)} %get-tuple-element.90.refs_0_, f32[8,32,256]{2,1,0:T(8,128)S(1)} %get-tuple-element.91.refs_1_, f32[8,128]{1,0:T(8,128)S(1)} %copy-done), custom_call_target="tpu_custom_call" | custom-call | flops 1 | bytes 1 | tf_op jit(solution)/shard_map/cond/branch_1_fun/combine_parts/pallas_call | solution.py:368
  59.4 8.6 %all-to-all-done.1.slots_ref = bf16[16,2,8,1024]{3,2,1,0:T(8,128)(2,1)S(1)} async-done(((bf16[16,2,8,1024]{3,2,1,0:T(8,128)(2,1)}), bf16[16,2,8,1024]{3,2,1,0:T(8,128)(2,1)S(1)}, u32[]{:S(2)}, u32[]{:S(2)}) %all-to-all-start.1) | async-done | bytes 524320 | tf_op jit(solution)/shard_map/cond/branch_1_fun/all_to_all | solution.py:537
  68.0 1.6 %far_rows.1 = (f32[8,8,256]{2,1,0:T(8,128)S(1)}, bf16[40,8,2048]{2,1,0:T(8,128)(2,1)S(1)}) custom-call(s32[10]{0:T(128)S(1)} %get-tuple-element.77.info_ref, bf16[1,8192]{1,0:T(2,128)(2,1)S(1)} %get-tuple-element.88.q_ref, bf16[16,2,8,1024]{3,2,1,0:T(8,128)(2,1)S(1)} %all-to-all-done.1.slots_ref), custom_call_target="tpu_custom_call" | custom-call | flops 1 | bytes 1 | tf_op jit(solution)/shard_map/cond/branch_1_fun/far_rows/pallas_call | solution.py:619
  69.6 0.0 collective-permute-done.7.refs_0_
  69.6 0.0 collective-permute-done.8.refs_1_
  69.6 0.0 collective-permute-done.9.refs_2_
  69.6 2.0 %collective-permute-done.10.refs_3_ = bf16[2,6,8,1024]{3,2,1,0:T(8,128)(2,1)S(1)} collective-permute-done((bf16[2,6,8,1024]{3,2,1,0:T(8,128)(2,1)}, bf16[2,6,8,1024]{3,2,1,0:T(8,128)(2,1)S(1)}, u32[]{:S(2)}, u32[]{:S(2)}) %collective-permute-start.10) | collective-permute-done | bytes 196640 | tf_op jit(solution)/shard_map/ppermute | solution.py:531
  71.6 1.2 %near_rows.1.refs_0_ = f32[8,8,256]{2,1,0:T(8,128)S(1)} custom-call(s32[10]{0:T(128)S(1)} %pad_add_fusion.info_ref, bf16[1,8192]{1,0:T(2,128)(2,1)S(1)} %copy-done.2, f32[8,8,256]{2,1,0:T(8,128)S(1)} %get-tuple-element.145.earlier_ref, bf16[2,6,8,1024]{3,2,1,0:T(8,128)(2,1)S(1)} %collective-permute-done.7.refs_0_, ...), custom_call_target="tpu_custom_call" | custom-call | flops 1 | bytes 1 | tf_op jit(solution)/shard_map/near_rows/pallas_call | solution.py:317
  72.8 1.0 %collective-permute-start.11 = (f32[8,8,256]{2,1,0:T(8,128)S(1)}, f32[8,8,256]{2,1,0:T(8,128)S(1)}, u32[]{:S(2)}, u32[]{:S(2)}) collective-permute-start(f32[8,8,256]{2,1,0:T(8,128)S(1)} %near_rows.1.refs_0_), channel_id=1, source_target_pairs={{0,1},{1,0},{2,3},{3,2},{4,5},{5,4},{6,7},{7,6},{8,9},{9,8},{10,11... | collective-permute-start | bytes 196616 | tf_op jit(solution)/shard_map/ppermute | solution.py:726
  73.8 0.8 %store_near.1 = bf16[40,8,2048]{2,1,0:T(8,128)(2,1)S(1)} custom-call(s32[10]{0:T(128)S(1)} %pad_add_fusion.info_ref, bf16[2,6,8,1024]{3,2,1,0:T(8,128)(2,1)S(1)} %collective-permute-done.7.refs_0_, bf16[2,6,8,1024]{3,2,1,0:T(8,128)(2,1)S(1)} %collective-permute-done.8.refs_1_, ...), custom_call_target="tpu_custom_call", output_to_operand_aliasing={{}: (5, {})} | custom-call | flops 1 | bytes 1 | tf_op jit(solution)/shard_map/store_near/pallas_call | solution.py:684
  74.6 0.0 copy-start.1
  74.6 2.5 %collective-permute-done.11.refs_1_ = f32[8,8,256]{2,1,0:T(8,128)S(1)} collective-permute-done((f32[8,8,256]{2,1,0:T(8,128)S(1)}, f32[8,8,256]{2,1,0:T(8,128)S(1)}, u32[]{:S(2)}, u32[]{:S(2)}) %collective-permute-start.11) | collective-permute-done | bytes 65568 | tf_op jit(solution)/shard_map/ppermute | solution.py:726
  77.1 1.4 %combine_parts.3 = (bf16[1,8192]{1,0:T(2,128)(2,1)}, f32[8,128]{1,0:T(8,128)}) custom-call(s32[10]{0:T(128)S(1)} %pad_add_fusion.info_ref, f32[8,8,256]{2,1,0:T(8,128)S(1)} %near_rows.1.refs_0_, f32[8,8,256]{2,1,0:T(8,128)S(1)} %collective-permute-done.11.refs_1_), custom_call_target="tpu_custom_call" | custom-call | flops 1 | bytes 1 | tf_op jit(solution)/shard_map/combine_parts/pallas_call | solution.py:368
  78.4 0.0 copy-done.1
Async XLA Ops:
  0.8 33.9 %collective-permute-start.5 = (bf16[2,4,8,1024]{3,2,1,0:T(8,128)(2,1)S(1)}, bf16[2,4,8,1024]{3,2,1,0:T(8,128)(2,1)S(1)}, u32[]{:S(2)}, u32[]{:S(2)}) collective-permute-start(bf16[2,4,8,1024]{3,2,1,0:T(8,128)(2,1)S(1)} %get-tuple-element.132), channel_id=1, source_target_pairs={{0,16},{2,18},{4,20},{6,22},{8,24},{10,26},{12,28},{14,30},{1,17},... | collective-permute-start | bytes 393224 | tf_op jit(solution)/shard_map/ppermute | solution.py:531
  3.5 37.6 %copy-start.2 = (bf16[1,8192]{1,0:T(2,128)(2,1)S(1)}, bf16[1,8192]{1,0:T(2,128)(2,1)}, u32[]{:S(2)}) copy-start(bf16[1,8192]{1,0:T(2,128)(2,1)} %q_ref.1) | copy-start | bytes 49156
  3.5 19.2 %all-to-all-start = ((bf16[16,3,8,1024]{3,2,1,0:T(8,128)(2,1)}), bf16[16,3,8,1024]{3,2,1,0:T(8,128)(2,1)S(1)}, u32[]{:S(2)}, u32[]{:S(2)}) async-start(bf16[16,3,8,1024]{3,2,1,0:T(8,128)(2,1)} %bitcast), calls=%async_computation | async-start | bytes 1572864 | tf_op jit(solution)/shard_map/cond/branch_1_fun/all_to_all | solution.py:537
  8.8 17.6 %collective-permute-start.1 = (bf16[2,4,8,1024]{3,2,1,0:T(8,128)(2,1)S(1)}, bf16[2,4,8,1024]{3,2,1,0:T(8,128)(2,1)}, u32[]{:S(2)}, u32[]{:S(2)}) collective-permute-start(bf16[2,4,8,1024]{3,2,1,0:T(8,128)(2,1)S(1)} %get-tuple-element.74), channel_id=1, source_target_pairs={{0,20},{2,22},{4,24},{6,26},{8,28},{10,30},{12,16},{14,18},{1,21},... | collective-permute-start | bytes 393224 | tf_op jit(solution)/shard_map/cond/branch_1_fun/ppermute | solution.py:531
  10.1 17.7 %collective-permute-start.2 = (bf16[2,4,8,1024]{3,2,1,0:T(8,128)(2,1)S(1)}, bf16[2,4,8,1024]{3,2,1,0:T(8,128)(2,1)}, u32[]{:S(2)}, u32[]{:S(2)}) collective-permute-start(bf16[2,4,8,1024]{3,2,1,0:T(8,128)(2,1)S(1)} %get-tuple-element.75), channel_id=1, source_target_pairs={{0,24},{2,26},{4,28},{6,30},{8,16},{10,18},{12,20},{14,22},{1,25},... | collective-permute-start | bytes 393224 | tf_op jit(solution)/shard_map/cond/branch_1_fun/ppermute | solution.py:531
  11.4 21.8 %collective-permute-start.3 = (bf16[2,4,8,1024]{3,2,1,0:T(8,128)(2,1)S(1)}, bf16[2,4,8,1024]{3,2,1,0:T(8,128)(2,1)}, u32[]{:S(2)}, u32[]{:S(2)}) collective-permute-start(bf16[2,4,8,1024]{3,2,1,0:T(8,128)(2,1)S(1)} %get-tuple-element.76), channel_id=1, source_target_pairs={{0,28},{2,30},{4,16},{6,18},{8,20},{10,22},{12,24},{14,26},{1,29},... | collective-permute-start | bytes 393224 | tf_op jit(solution)/shard_map/cond/branch_1_fun/ppermute | solution.py:531
  23.4 0.7 collective-permute-start
  33.3 7.8 %collective-permute-start.6 = (f32[8,32,256]{2,1,0:T(8,128)S(1)}, f32[8,32,256]{2,1,0:T(8,128)S(1)}, u32[]{:S(2)}, u32[]{:S(2)}) collective-permute-start(f32[8,32,256]{2,1,0:T(8,128)S(1)} %get-tuple-element.137), channel_id=1, source_target_pairs={{0,1},{1,0},{2,3},{3,2},{4,5},{5,4},{6,7},{7,6},{8,9},{9,8},{10,11... | collective-permute-start | bytes 786440 | tf_op jit(solution)/shard_map/ppermute | solution.py:726
  34.7 34.9 %collective-permute-start.7 = (bf16[2,6,8,1024]{3,2,1,0:T(8,128)(2,1)}, bf16[2,6,8,1024]{3,2,1,0:T(8,128)(2,1)S(1)}, u32[]{:S(2)}, u32[]{:S(2)}) collective-permute-start(bf16[2,6,8,1024]{3,2,1,0:T(8,128)(2,1)} %get-tuple-element.139), channel_id=1, source_target_pairs={{0,16},{2,18},{4,20},{6,22},{8,24},{10,26},{12,28},{14,30},{1,17},... | collective-permute-start | bytes 589832 | tf_op jit(solution)/shard_map/ppermute | solution.py:531
  36.0 33.6 %collective-permute-start.8 = (bf16[2,6,8,1024]{3,2,1,0:T(8,128)(2,1)}, bf16[2,6,8,1024]{3,2,1,0:T(8,128)(2,1)S(1)}, u32[]{:S(2)}, u32[]{:S(2)}) collective-permute-start(bf16[2,6,8,1024]{3,2,1,0:T(8,128)(2,1)} %get-tuple-element.140), channel_id=1, source_target_pairs={{0,20},{2,22},{4,24},{6,26},{8,28},{10,30},{12,16},{14,18},{1,21},... | collective-permute-start | bytes 589832 | tf_op jit(solution)/shard_map/ppermute | solution.py:531
  37.3 32.3 %collective-permute-start.9 = (bf16[2,6,8,1024]{3,2,1,0:T(8,128)(2,1)}, bf16[2,6,8,1024]{3,2,1,0:T(8,128)(2,1)S(1)}, u32[]{:S(2)}, u32[]{:S(2)}) collective-permute-start(bf16[2,6,8,1024]{3,2,1,0:T(8,128)(2,1)} %get-tuple-element.141), channel_id=1, source_target_pairs={{0,24},{2,26},{4,28},{6,30},{8,16},{10,18},{12,20},{14,22},{1,25},... | collective-permute-start | bytes 589832 | tf_op jit(solution)/shard_map/ppermute | solution.py:531
  38.6 33.0 %collective-permute-start.10 = (bf16[2,6,8,1024]{3,2,1,0:T(8,128)(2,1)}, bf16[2,6,8,1024]{3,2,1,0:T(8,128)(2,1)S(1)}, u32[]{:S(2)}, u32[]{:S(2)}) collective-permute-start(bf16[2,6,8,1024]{3,2,1,0:T(8,128)(2,1)} %get-tuple-element.142), channel_id=1, source_target_pairs={{0,28},{2,30},{4,16},{6,18},{8,20},{10,22},{12,24},{14,26},{1,29},... | collective-permute-start | bytes 589832 | tf_op jit(solution)/shard_map/ppermute | solution.py:531
  43.7 3.4 %collective-permute-start.4 = (bf16[4,2,2,8,1024]{4,3,2,1,0:T(8,128)(2,1)S(1)}, bf16[4,2,2,8,1024]{4,3,2,1,0:T(8,128)(2,1)S(1)}, u32[]{:S(2)}, u32[]{:S(2)}) collective-permute-start(bf16[4,2,2,8,1024]{4,3,2,1,0:T(8,128)(2,1)S(1)} %get-tuple-element.86), channel_id=1, source_target_pairs={{16,18},{18,16},{20,22},{22,20},{24,26},{26,24},{28,30},{30,28},{1... | collective-permute-start | bytes 786440 | tf_op jit(solution)/shard_map/cond/branch_1_fun/ppermute | solution.py:534
  48.6 19.4 %all-to-all-start.1 = ((bf16[16,2,8,1024]{3,2,1,0:T(8,128)(2,1)}), bf16[16,2,8,1024]{3,2,1,0:T(8,128)(2,1)S(1)}, u32[]{:S(2)}, u32[]{:S(2)}) async-start(bf16[16,2,8,1024]{3,2,1,0:T(8,128)(2,1)} %relay_slots.1.rest_1_), calls=%async_computation.1 | async-start | bytes 1048576 | tf_op jit(solution)/shard_map/cond/branch_1_fun/all_to_all | solution.py:537
  57.0 0.7 copy-start
  72.8 4.3 %collective-permute-start.11 = (f32[8,8,256]{2,1,0:T(8,128)S(1)}, f32[8,8,256]{2,1,0:T(8,128)S(1)}, u32[]{:S(2)}, u32[]{:S(2)}) collective-permute-start(f32[8,8,256]{2,1,0:T(8,128)S(1)} %near_rows.1.refs_0_), channel_id=1, source_target_pairs={{0,1},{1,0},{2,3},{3,2},{4,5},{5,4},{6,7},{7,6},{8,9},{9,8},{10,11... | collective-permute-start | bytes 196616 | tf_op jit(solution)/shard_map/ppermute | solution.py:726
  74.6 3.8 %copy-start.1 = (bf16[40,8,2048]{2,1,0:T(8,128)(2,1)}, bf16[40,8,2048]{2,1,0:T(8,128)(2,1)S(1)}, u32[]{:S(2)}) copy-start(bf16[40,8,2048]{2,1,0:T(8,128)(2,1)S(1)} %store_near.1) | copy-start | bytes 3932164

commit v9 on v8

--- a/solution.py
+++ b/solution.py
@@ -158,12 +158,29 @@
     out_ref[head, :, HEADDIM:] = jnp.where(lane < HEADDIM // 2, peak, total)
 
 
+def store_short(out_ref, found):
+    lane = lax.broadcasted_iota(jnp.int32, out_ref.shape[1:], 1)
+    stats = jnp.zeros(out_ref.shape[1:], jnp.float32)
+    for head, (mixed, peak, total) in enumerate(found):
+        out_ref[head] = mixed
+        stats = jnp.where(lane == head, peak, stats)
+        stats = jnp.where(lane == KVHEADS + head, total, stats)
+    out_ref[KVHEADS] = stats
+
+
+def load_part(ref, head):
+    if ref.shape[-1] == HEADDIM:
+        stats = ref[KVHEADS]
+        return ref[head], stats[:, head : head + 1], stats[:, KVHEADS + head : KVHEADS + head + 1]
+    part = ref[head]
+    return part[:, :HEADDIM], part[:, HEADDIM : HEADDIM + 1], part[:, -1:]
+
+
 def merged(parts):
-    peaks = [part[:, HEADDIM : HEADDIM + 1] for part in parts]
-    peak = functools.reduce(jnp.maximum, peaks)
-    factors = [jnp.exp(p - peak) for p in peaks]
-    total = sum(part[:, -1:] * f for part, f in zip(parts, factors))
-    mixed = sum(part[:, :HEADDIM] * f for part, f in zip(parts, factors))
+    peak = functools.reduce(jnp.maximum, [part[1] for part in parts])
+    factors = [jnp.exp(part[1] - peak) for part in parts]
+    total = sum(part[2] * f for part, f in zip(parts, factors))
+    mixed = sum(part[0] * f for part, f in zip(parts, factors))
     return mixed, peak, total
 
 
@@ -253,10 +270,10 @@
         dot(weight.astype(jnp.bfloat16), held[:, start + HEADDIM : start + 2 * HEADDIM])
         for weight, (held, start) in zip(weights, places)
     ]
-    for head in range(KVHEADS):
-        store_part(out_ref, head, mixes[head], peaks[head], totals[head])
-        if earlier_ref is not None:
-            store_part(out_ref, head, *merged([out_ref[head], earlier_ref[head]]))
+    found = list(zip(mixes, peaks, totals))
+    if earlier_ref is not None:
+        found = [merged([part, load_part(earlier_ref, head)]) for head, part in enumerate(found)]
+    store_short(out_ref, found)
 
 
 def flat_rows(pieces):
@@ -316,7 +333,7 @@
 def arrival_part(kernel, info, query, operands, places, scratch, name):
     return pl.pallas_call(
         kernel,
-        out_shape=jax.ShapeDtypeStruct((KVHEADS, GROUP, 2 * HEADDIM), jnp.float32),
+        out_shape=jax.ShapeDtypeStruct((KVHEADS + 1, GROUP, HEADDIM), jnp.float32),
         grid_spec=pltpu.PrefetchScalarGridSpec(
             num_scalar_prefetch=1,
             grid=(1,),
@@ -342,11 +359,15 @@
         results = []
         for head in range(KVHEADS):
             if count == 2:
-                here, there = part_refs[0][head], part_refs[1][head]
+                here, there = [load_part(ref, head) for ref in part_refs]
                 first = info_ref[TP] == 0
-                parts = [jnp.where(first, here, there), jnp.where(first, there, here)]
+                parts = [
+                    [jnp.where(first, x, y) for x, y in zip(here, there)],
+                    [jnp.where(first, y, x) for x, y in zip(here, there)],
+                ]
             else:
-                parts = [part_refs[0][n, head] for n in range(part_refs[0].shape[0])]
+                every = part_refs[0]
+                parts = [load_part(every.at[n], head) for n in range(every.shape[0])]
             mixed, _, total = merged(parts)
             results.append(mixed / total)
         rows = [
@@ -458,7 +479,7 @@
             stores.append(pltpu.make_async_copy(held, near_ref.at[tau], sems.at[2 + tau]))
             loads[-1].start()
         for s, far_ref in enumerate(far_refs):
-            relay = lax.rem(lax.div(inst, 2) + s, PAIRS)
+            relay = jnp.bitwise_xor(lax.div(inst, 2), s ^ 2)
             for tau in range(2):
                 source = rows_ref.at[pl.ds(tau * units + near + relay * far, far)]
                 others.append(
@@ -482,7 +503,7 @@
         for d in range(half):
             source = source_of(info_ref, d)
             same = lax.rem(source, 2) == lax.rem(here, 2)
-            shift = lax.rem(lax.div(here, 2) + PAIRS - lax.div(source, 2), PAIRS)
+            shift = jnp.bitwise_xor(jnp.bitwise_xor(lax.div(here, 2), lax.div(source, 2)), 2)
             for tau in range(2):
                 slot = tau * half + d
                 target = out_ref.at[slot]
@@ -504,7 +525,7 @@
         waits = []
         for t in range(2):
             for s, part in enumerate(parts):
-                pair = lax.rem(lax.div(order(info_ref), 2) + PAIRS - s, PAIRS)
+                pair = jnp.bitwise_xor(lax.div(order(info_ref), 2), s ^ 2)
                 target = handed_ref.at[pl.ds(pair * 2 * near, 2 * near), :, pl.ds(t * width, width)]
                 waits.append(pltpu.make_async_copy(part.at[t], target, sems.at[len(waits)]))
         for copy in waits:
@@ -526,7 +547,7 @@
 
     def crossing(array, s):
         hops = [
-            (2 * p + k, half + 2 * ((p + s) % PAIRS) + k) for p in range(PAIRS) for k in range(2)
+            (2 * p + k, half + 2 * (p ^ s ^ 2) + k) for p in range(PAIRS) for k in range(2)
         ]
         return lax.ppermute(array, "inst", hops)
 
@@ -541,7 +562,7 @@
     def for_neighbour(pre, sources, targets):
         plan = []
         for s in range(PAIRS):
-            receiver = lax.rem(lax.div(order(pre), 2) + s, PAIRS) * 2 + 1 - lax.rem(order(pre), 2)
+            receiver = jnp.bitwise_xor(lax.div(order(pre), 2), s ^ 2) * 2 + 1 - lax.rem(order(pre), 2)
             for t in range(2):
                 origin = t * half + source_of(pre, receiver)
                 plan.append((sources[0].at[origin], targets[0].at[s, t]))
@@ -550,7 +571,7 @@
     def for_receivers(pre, sources, targets):
         plan = []
         for s in range(PAIRS):
-            receiver = lax.rem(lax.div(order(pre), 2) + s, PAIRS) * 2 + lax.rem(order(pre), 2)
+            receiver = jnp.bitwise_xor(lax.div(order(pre), 2), s ^ 2) * 2 + lax.rem(order(pre), 2)
             for t in range(2):
                 origin = t * half + source_of(pre, receiver)
                 mine = targets[s].at[t, pl.ds(lax.rem(order(pre), 2) * near, near)]
@@ -619,7 +640,7 @@
         arrival, handed = pl.pallas_call(
             functools.partial(far_rows_kernel, near_all),
             out_shape=(
-                jax.ShapeDtypeStruct((KVHEADS, GROUP, 2 * HEADDIM), jnp.float32),
+                jax.ShapeDtypeStruct((KVHEADS + 1, GROUP, HEADDIM), jnp.float32),
                 jax.ShapeDtypeStruct((units, UNIT, 2 * width), jnp.bfloat16),
             ),
             grid_spec=pltpu.PrefetchScalarGridSpec(

time: 79.3 us -> 78.8 us (level)
    all_to_all x2, waiting for transfers between devices: 11.5 us -> 8.4 us  [spread_out(): lax.all_to_all(array, ('inst', 'tp'), 0, 0, axis_index_groups=groups, til...]
    ppermute x8, waiting for transfers between devices: 10.5 us -> 13.5 us  [crossing(): return lax.ppermute(array, 'inst', hops)]
  transfers between devices with their start and end apart: 14 -> 14, of which waited for: 9 -> 8; matrix products, arithmetic and copies ran while one was open for 1% -> 1% of each run, Pallas kernels for 26% -> 27%
where the time goes in v9:
time: 78.8 us; the launch traced here: 78.1 us
  waiting for transfers between devices  27.1 us (34%)
  starting transfers between devices  24.6 us (31%)
  Pallas kernels  23.4 us (30%)
  between operations  1.38 us (2%)
    ppermute x8, waiting for transfers between devices, crossing(): return lax.ppermute(array, 'inst', hops)  13.5 us
    ppermute x8, starting transfers between devices, crossing(): return lax.ppermute(array, 'inst', hops)  10.3 us
    all_to_all x2, starting transfers between devices, spread_out(): lax.all_to_all(array, ('inst', 'tp'), 0, 0, axis_index_groups=groups, til...  9.57 us
    all_to_all x2, waiting for transfers between devices, spread_out(): lax.all_to_all(array, ('inst', 'tp'), 0, 0, axis_index_groups=groups, til...  8.4 us
    pallas_call x2, Pallas kernels, prompt_attention(): pl.pallas_call(functools.partial(prompt_kernel, heads), out_shape=(jax.Sh...  7.28 us
    pallas_call x1, Pallas kernels, cache_attention(): pl.pallas_call(functools.partial(cache_kernel, page_len), out_shape=(jax....  4.1 us
    pallas_call x3, Pallas kernels, copies(): pl.pallas_call(functools.partial(copy_kernel, plan, side, (len(operands),...  3.87 us
    ppermute x2, waiting for transfers between devices, exchanged(): return lax.ppermute(part, 'tp', [(0, 1), (1, 0)])  3.74 us
  transfers between devices with their start and end apart: 14, of which 8 were waited for; matrix products, arithmetic and copies ran while one was open for 1% of the time, Pallas kernels for 27%

profile of v9, /device:TPU:24, one launch (start us, length us, event | category | flops | bytes accessed | tf_op | source)
XLA Modules:
  0.0 78.1 jit_solution(299094570045383557)
XLA Ops:
  0.6 0.1 cut_rows.1
  0.8 1.3 %collective-permute-start.5 = (bf16[2,4,8,1024]{3,2,1,0:T(8,128)(2,1)S(1)}, bf16[2,4,8,1024]{3,2,1,0:T(8,128)(2,1)S(1)}, u32[]{:S(2)}, u32[]{:S(2)}) collective-permute-start(bf16[2,4,8,1024]{3,2,1,0:T(8,128)(2,1)S(1)} %get-tuple-element.132), channel_id=1, source_target_pairs={{0,24},{2,26},{4,28},{6,30},{8,16},{10,18},{12,20},{14,22},{1,25},... | collective-permute-start | bytes 393224 | tf_op jit(solution)/shard_map/ppermute | solution.py:552
  2.7 0.7 pad_add_fusion.info_ref
  3.5 0.0 copy-start.2
  3.5 29.8 %conditional.3 = (bf16[2,6,8,1024]{3,2,1,0:T(8,128)(2,1)}, bf16[2,6,8,1024]{3,2,1,0:T(8,128)(2,1)}, bf16[2,6,8,1024]{3,2,1,0:T(8,128)(2,1)}, bf16[2,6,8,1024]{3,...) conditional(s32[]{:T(128)} %convert_element_type.7, () %tuple.32, ...), branch_computations={%region_0.0_spmd, %region_1.0_spmd} | conditional | flops 5 | bytes 6684764 | solution.py:669
  3.5 5.3 %all-to-all-start = ((bf16[16,3,8,1024]{3,2,1,0:T(8,128)(2,1)}), bf16[16,3,8,1024]{3,2,1,0:T(8,128)(2,1)S(1)}, u32[]{:S(2)}, u32[]{:S(2)}) async-start(bf16[16,3,8,1024]{3,2,1,0:T(8,128)(2,1)} %bitcast), calls=%async_computation | async-start | bytes 1572864 | tf_op jit(solution)/shard_map/cond/branch_1_fun/all_to_all | solution.py:558
  8.8 1.3 %collective-permute-start.1 = (bf16[2,4,8,1024]{3,2,1,0:T(8,128)(2,1)S(1)}, bf16[2,4,8,1024]{3,2,1,0:T(8,128)(2,1)}, u32[]{:S(2)}, u32[]{:S(2)}) collective-permute-start(bf16[2,4,8,1024]{3,2,1,0:T(8,128)(2,1)S(1)} %get-tuple-element.74), channel_id=1, source_target_pairs={{0,28},{2,30},{4,24},{6,26},{8,20},{10,22},{12,16},{14,18},{1,29},... | collective-permute-start | bytes 393224 | tf_op jit(solution)/shard_map/cond/branch_1_fun/ppermute | solution.py:552
  10.1 1.3 %collective-permute-start.2 = (bf16[2,4,8,1024]{3,2,1,0:T(8,128)(2,1)S(1)}, bf16[2,4,8,1024]{3,2,1,0:T(8,128)(2,1)}, u32[]{:S(2)}, u32[]{:S(2)}) collective-permute-start(bf16[2,4,8,1024]{3,2,1,0:T(8,128)(2,1)S(1)} %get-tuple-element.75), channel_id=1, source_target_pairs={{0,16},{2,18},{4,20},{6,22},{8,24},{10,26},{12,28},{14,30},{1,17},... | collective-permute-start | bytes 393224 | tf_op jit(solution)/shard_map/cond/branch_1_fun/ppermute | solution.py:552
  11.4 1.3 %collective-permute-start.3 = (bf16[2,4,8,1024]{3,2,1,0:T(8,128)(2,1)S(1)}, bf16[2,4,8,1024]{3,2,1,0:T(8,128)(2,1)}, u32[]{:S(2)}, u32[]{:S(2)}) collective-permute-start(bf16[2,4,8,1024]{3,2,1,0:T(8,128)(2,1)S(1)} %get-tuple-element.76), channel_id=1, source_target_pairs={{0,20},{2,22},{4,16},{6,18},{8,28},{10,30},{12,24},{14,26},{1,21},... | collective-permute-start | bytes 393224 | tf_op jit(solution)/shard_map/cond/branch_1_fun/ppermute | solution.py:552
  12.7 4.1 %cache_attention.1 = (f32[8,32,256]{2,1,0:T(8,128)S(1)}, f32[8,128]{1,0:T(8,128)}) custom-call(s32[10]{0:T(128)S(1)} %get-tuple-element.58.info_ref, s32[4,8]{1,0:T(4,128)} %get-tuple-element.152.table_ref, s32[4]{0:T(128)} %get-tuple-element.153.lengths_ref, bf16[4,8192]{1,0:T(4,128)(2,1)} %get-tuple-element.154.q_ref, bf16[320,2048]{1,0:T(8,128)(2,1)} %bitcast.10, ...), custom_call_target="tpu_custom_call" | custom-call | flops 1 | bytes 1 | tf_op jit(solution)/shard_map/cond/branch_1_fun/cache_attention/pallas_call | solution.py:230
  16.8 3.1 %prompt_attention.2 = (bf16[640,4096]{1,0:T(8,128)(2,1)}, f32[8,128]{1,0:T(8,128)S(1)}) custom-call(s32[10]{0:T(128)S(1)} %get-tuple-element.58.info_ref, bf16[640,4096]{1,0:T(8,128)(2,1)} %get-tuple-element.60.q_ref, bf16[640,1024]{1,0:T(8,128)(2,1)} %get-tuple-element.61.kv_ref, f32[8,128]{1,0:T(8,128)} %get-tuple-element.66.rest_0_), custom_call_target="tpu_custom_call" | custom-call | flops 1 | bytes 1 | tf_op jit(solution)/shard_map/cond/branch_1_fun/prompt_attention/pallas_call | solution.py:124
  19.9 6.7 %all-to-all-done = bf16[16,3,8,1024]{3,2,1,0:T(8,128)(2,1)S(1)} async-done(((bf16[16,3,8,1024]{3,2,1,0:T(8,128)(2,1)}), bf16[16,3,8,1024]{3,2,1,0:T(8,128)(2,1)S(1)}, u32[]{:S(2)}, u32[]{:S(2)}) %all-to-all-start) | async-done | bytes 786464 | tf_op jit(solution)/shard_map/cond/branch_1_fun/all_to_all | solution.py:558
  26.5 2.0 %conditional = ((bf16[2,6,8,1024]{3,2,1,0:T(8,128)(2,1)}, bf16[2,6,8,1024]{3,2,1,0:T(8,128)(2,1)}, bf16[2,6,8,1024]{3,2,1,0:T(8,128)(2,1)}, bf16[2,6,8,1024]{3,2,1,0:T(8,128)(2,1)})) conditional(s32[]{:T(128)} %convert_element_type.1, () %tuple.21, (s32[10]{0:T(128)S(1)}, bf16[16,3,8,1024]{3,2,1,0:T(8,128)(2,1)S(1)}, f32[8,128]{1,0:T(8,128)S(1)}) %tuple.22), branch_computations={%region_2.0_spmd, %region_3.0_spmd} | conditional | flops 2 | bytes 1572914 | solution.py:669
  26.5 0.6 for_neighbour.1
  27.2 0.7 collective-permute-start
  27.9 0.0 collective-permute-done.refs_1_
  27.9 0.7 for_receivers.1
  28.6 0.0 collective-permute-done.1
  28.6 0.0 collective-permute-done.2
  28.6 4.7 %collective-permute-done.3 = bf16[2,4,8,1024]{3,2,1,0:T(8,128)(2,1)} collective-permute-done((bf16[2,4,8,1024]{3,2,1,0:T(8,128)(2,1)S(1)}, bf16[2,4,8,1024]{3,2,1,0:T(8,128)(2,1)}, u32[]{:S(2)}, u32[]{:S(2)}) %collective-permute-start.3) | collective-permute-done | bytes 131104 | tf_op jit(solution)/shard_map/cond/branch_1_fun/ppermute | solution.py:552
  33.3 1.5 %collective-permute-start.6 = (f32[8,32,256]{2,1,0:T(8,128)S(1)}, f32[8,32,256]{2,1,0:T(8,128)S(1)}, u32[]{:S(2)}, u32[]{:S(2)}) collective-permute-start(f32[8,32,256]{2,1,0:T(8,128)S(1)} %get-tuple-element.137), channel_id=1, source_target_pairs={{0,1},{1,0},{2,3},{3,2},{4,5},{5,4},{6,7},{7,6},{8,9},{9,8},{10,11... | collective-permute-start | bytes 786440 | tf_op jit(solution)/shard_map/ppermute | solution.py:747
  34.8 0.0 collective-permute-done.5
  34.8 1.3 %collective-permute-start.7 = (bf16[2,6,8,1024]{3,2,1,0:T(8,128)(2,1)}, bf16[2,6,8,1024]{3,2,1,0:T(8,128)(2,1)S(1)}, u32[]{:S(2)}, u32[]{:S(2)}) collective-permute-start(bf16[2,6,8,1024]{3,2,1,0:T(8,128)(2,1)} %get-tuple-element.139), channel_id=1, source_target_pairs={{0,24},{2,26},{4,28},{6,30},{8,16},{10,18},{12,20},{14,22},{1,25},... | collective-permute-start | bytes 589832 | tf_op jit(solution)/shard_map/ppermute | solution.py:552
  36.0 1.3 %collective-permute-start.8 = (bf16[2,6,8,1024]{3,2,1,0:T(8,128)(2,1)}, bf16[2,6,8,1024]{3,2,1,0:T(8,128)(2,1)S(1)}, u32[]{:S(2)}, u32[]{:S(2)}) collective-permute-start(bf16[2,6,8,1024]{3,2,1,0:T(8,128)(2,1)} %get-tuple-element.140), channel_id=1, source_target_pairs={{0,28},{2,30},{4,24},{6,26},{8,20},{10,22},{12,16},{14,18},{1,29},... | collective-permute-start | bytes 589832 | tf_op jit(solution)/shard_map/ppermute | solution.py:552
  37.3 1.3 %collective-permute-start.9 = (bf16[2,6,8,1024]{3,2,1,0:T(8,128)(2,1)}, bf16[2,6,8,1024]{3,2,1,0:T(8,128)(2,1)S(1)}, u32[]{:S(2)}, u32[]{:S(2)}) collective-permute-start(bf16[2,6,8,1024]{3,2,1,0:T(8,128)(2,1)} %get-tuple-element.141), channel_id=1, source_target_pairs={{0,16},{2,18},{4,20},{6,22},{8,24},{10,26},{12,28},{14,30},{1,17},... | collective-permute-start | bytes 589832 | tf_op jit(solution)/shard_map/ppermute | solution.py:552
  38.6 1.3 %collective-permute-start.10 = (bf16[2,6,8,1024]{3,2,1,0:T(8,128)(2,1)}, bf16[2,6,8,1024]{3,2,1,0:T(8,128)(2,1)S(1)}, u32[]{:S(2)}, u32[]{:S(2)}) collective-permute-start(bf16[2,6,8,1024]{3,2,1,0:T(8,128)(2,1)} %get-tuple-element.142), channel_id=1, source_target_pairs={{0,20},{2,22},{4,16},{6,18},{8,28},{10,30},{12,24},{14,26},{1,21},... | collective-permute-start | bytes 589832 | tf_op jit(solution)/shard_map/ppermute | solution.py:552
  39.9 1.2 %collective-permute-done.6 = f32[8,32,256]{2,1,0:T(8,128)S(1)} collective-permute-done((f32[8,32,256]{2,1,0:T(8,128)S(1)}, f32[8,32,256]{2,1,0:T(8,128)S(1)}, u32[]{:S(2)}, u32[]{:S(2)}) %collective-permute-start.6) | collective-permute-done | bytes 262176 | tf_op jit(solution)/shard_map/ppermute | solution.py:747
  41.1 0.0 copy-done.2
  41.1 21.5 %conditional.4 = (bf16[640,4096]{1,0:T(8,128)(2,1)}, bf16[40,8,2048]{2,1,0:T(8,128)(2,1)S(1)}, bf16[4,8192]{1,0:T(4,128)(2,1)}, f32[9,8,128]{2,1,0:T(8,128)S(1)}) conditional(s32[]{:T(128)} %convert_element_type.7, bf16[640,4096]{1,0:T(8,128)(2,1)} %get-tuple-element.127, (s32[10]{0:T(128)S(1)}, bf16[2,4,8,1024]{3,2,1,0:T(8,128)(2,1)S(1)}, ...), branch_computations={%region_4.0_spmd, %region_5.0_spmd} | conditional | flops 5 | bytes 2637961 | solution.py:669
  41.1 2.6 %split_relays.1 = (bf16[4,2,2,8,1024]{4,3,2,1,0:T(8,128)(2,1)S(1)}, bf16[4,2,2,8,1024]{4,3,2,1,0:T(8,128)(2,1)S(1)}) custom-call(s32[10]{0:T(128)S(1)} %get-tuple-element.77.info_ref, bf16[2,4,8,1024]{3,2,1,0:T(8,128)(2,1)S(1)} %get-tuple-element.81.refs_0_, bf16[2,4,8,1024]{3,2,1,0:T(8,128)(2,1)} %get-tuple-element.82.refs_1_, ...), custom_call_target="tpu_custom_call" | custom-call | flops 1 | bytes 1 | tf_op jit(solution)/shard_map/cond/branch_1_fun/split_relays/pallas_call | solution.py:451
  43.7 1.9 %collective-permute-start.4 = (bf16[4,2,2,8,1024]{4,3,2,1,0:T(8,128)(2,1)S(1)}, bf16[4,2,2,8,1024]{4,3,2,1,0:T(8,128)(2,1)S(1)}, u32[]{:S(2)}, u32[]{:S(2)}) collective-permute-start(bf16[4,2,2,8,1024]{4,3,2,1,0:T(8,128)(2,1)S(1)} %get-tuple-element.86), channel_id=1, source_target_pairs={{16,18},{18,16},{20,22},{22,20},{24,26},{26,24},{28,30},{30,28},{1... | collective-permute-start | bytes 786440 | tf_op jit(solution)/shard_map/cond/branch_1_fun/ppermute | solution.py:555
  45.6 1.5 %collective-permute-done.4.recv_ref = bf16[4,2,2,8,1024]{4,3,2,1,0:T(8,128)(2,1)S(1)} collective-permute-done((bf16[4,2,2,8,1024]{4,3,2,1,0:T(8,128)(2,1)S(1)}, bf16[4,2,2,8,1024]{4,3,2,1,0:T(8,128)(2,1)S(1)}, u32[]{:S(2)}, u32[]{:S(2)}) %collective-permute-start.4) | collective-permute-done | bytes 262176 | tf_op jit(solution)/shard_map/cond/branch_1_fun/ppermute | solution.py:555
  47.1 1.5 %relay_slots.1.rest_1_ = bf16[16,2,8,1024]{3,2,1,0:T(8,128)(2,1)} custom-call(s32[10]{0:T(128)S(1)} %get-tuple-element.77.info_ref, bf16[4,2,2,8,1024]{4,3,2,1,0:T(8,128)(2,1)S(1)} %get-tuple-element.85.keep_ref, bf16[4,2,2,8,1024]{4,3,2,1,0:T(8,128)(2,1)S(1)} %collective-permute-done.4.recv_ref), custom_call_target="tpu_custom_call" | custom-call | flops 1 | bytes 1 | tf_op jit(solution)/shard_map/cond/branch_1_fun/relay_slots/pallas_call | solution.py:623
  48.6 4.2 %all-to-all-start.1 = ((bf16[16,2,8,1024]{3,2,1,0:T(8,128)(2,1)}), bf16[16,2,8,1024]{3,2,1,0:T(8,128)(2,1)S(1)}, u32[]{:S(2)}, u32[]{:S(2)}) async-start(bf16[16,2,8,1024]{3,2,1,0:T(8,128)(2,1)} %relay_slots.1.rest_1_), calls=%async_computation.1 | async-start | bytes 1048576 | tf_op jit(solution)/shard_map/cond/branch_1_fun/all_to_all | solution.py:558
  52.8 4.2 %prompt_attention.3 = (bf16[640,4096]{1,0:T(8,128)(2,1)}, f32[8,128]{1,0:T(8,128)}) custom-call(s32[10]{0:T(128)S(1)} %get-tuple-element.77.info_ref, bf16[640,4096]{1,0:T(8,128)(2,1)} %get-tuple-element.78.q_ref, bf16[640,1024]{1,0:T(8,128)(2,1)} %get-tuple-element.79.kv_ref, ...), custom_call_target="tpu_custom_call", output_to_operand_aliasing={{0}: (3, {})} | custom-call | flops 1 | bytes 1 | tf_op jit(solution)/shard_map/cond/branch_1_fun/prompt_attention/pallas_call | solution.py:124
  57.1 0.0 copy-start
  57.1 0.7 copy-done
  57.8 1.7 %combine_parts.2 = (bf16[4,8192]{1,0:T(4,128)(2,1)}, f32[8,128]{1,0:T(8,128)}) custom-call(s32[10]{0:T(128)S(1)} %get-tuple-element.77.info_ref, f32[8,32,256]{2,1,0:T(8,128)S(1)} %get-tuple-element.90.refs_0_, f32[8,32,256]{2,1,0:T(8,128)S(1)} %get-tuple-element.91.refs_1_, f32[8,128]{1,0:T(8,128)S(1)} %copy-done), custom_call_target="tpu_custom_call" | custom-call | flops 1 | bytes 1 | tf_op jit(solution)/shard_map/cond/branch_1_fun/combine_parts/pallas_call | solution.py:389
  59.4 1.7 %all-to-all-done.1.slots_ref = bf16[16,2,8,1024]{3,2,1,0:T(8,128)(2,1)S(1)} async-done(((bf16[16,2,8,1024]{3,2,1,0:T(8,128)(2,1)}), bf16[16,2,8,1024]{3,2,1,0:T(8,128)(2,1)S(1)}, u32[]{:S(2)}, u32[]{:S(2)}) %all-to-all-start.1) | async-done | bytes 524320 | tf_op jit(solution)/shard_map/cond/branch_1_fun/all_to_all | solution.py:558
  61.1 1.6 %far_rows.1 = (f32[9,8,128]{2,1,0:T(8,128)S(1)}, bf16[40,8,2048]{2,1,0:T(8,128)(2,1)S(1)}) custom-call(s32[10]{0:T(128)S(1)} %get-tuple-element.77.info_ref, bf16[1,8192]{1,0:T(2,128)(2,1)S(1)} %get-tuple-element.88.q_ref, bf16[16,2,8,1024]{3,2,1,0:T(8,128)(2,1)S(1)} %all-to-all-done.1.slots_ref), custom_call_target="tpu_custom_call" | custom-call | flops 1 | bytes 1 | tf_op jit(solution)/shard_map/cond/branch_1_fun/far_rows/pallas_call | solution.py:640
  62.7 0.0 collective-permute-done.7.refs_0_
  62.7 0.0 collective-permute-done.8.refs_1_
  62.7 6.4 %collective-permute-done.9.refs_2_ = bf16[2,6,8,1024]{3,2,1,0:T(8,128)(2,1)S(1)} collective-permute-done((bf16[2,6,8,1024]{3,2,1,0:T(8,128)(2,1)}, bf16[2,6,8,1024]{3,2,1,0:T(8,128)(2,1)S(1)}, u32[]{:S(2)}, u32[]{:S(2)}) %collective-permute-start.9) | collective-permute-done | bytes 196640 | tf_op jit(solution)/shard_map/ppermute | solution.py:552
  69.1 2.4 %collective-permute-done.10.refs_3_ = bf16[2,6,8,1024]{3,2,1,0:T(8,128)(2,1)S(1)} collective-permute-done((bf16[2,6,8,1024]{3,2,1,0:T(8,128)(2,1)}, bf16[2,6,8,1024]{3,2,1,0:T(8,128)(2,1)S(1)}, u32[]{:S(2)}, u32[]{:S(2)}) %collective-permute-start.10) | collective-permute-done | bytes 196640 | tf_op jit(solution)/shard_map/ppermute | solution.py:552
  71.5 1.2 %near_rows.1.refs_0_ = f32[9,8,128]{2,1,0:T(8,128)S(1)} custom-call(s32[10]{0:T(128)S(1)} %pad_add_fusion.info_ref, bf16[1,8192]{1,0:T(2,128)(2,1)S(1)} %copy-done.2, f32[9,8,128]{2,1,0:T(8,128)S(1)} %get-tuple-element.145.earlier_ref, bf16[2,6,8,1024]{3,2,1,0:T(8,128)(2,1)S(1)} %collective-permute-done.7.refs_0_, ...), custom_call_target="tpu_custom_call" | custom-call | flops 1 | bytes 1 | tf_op jit(solution)/shard_map/near_rows/pallas_call | solution.py:334
  72.7 0.6 collective-permute-start.11
  73.3 0.8 %store_near.1 = bf16[40,8,2048]{2,1,0:T(8,128)(2,1)S(1)} custom-call(s32[10]{0:T(128)S(1)} %pad_add_fusion.info_ref, bf16[2,6,8,1024]{3,2,1,0:T(8,128)(2,1)S(1)} %collective-permute-done.7.refs_0_, bf16[2,6,8,1024]{3,2,1,0:T(8,128)(2,1)S(1)} %collective-permute-done.8.refs_1_, ...), custom_call_target="tpu_custom_call", output_to_operand_aliasing={{}: (5, {})} | custom-call | flops 1 | bytes 1 | tf_op jit(solution)/shard_map/store_near/pallas_call | solution.py:705
  74.1 0.0 copy-start.1
  74.1 2.6 %collective-permute-done.11.refs_1_ = f32[9,8,128]{2,1,0:T(8,128)S(1)} collective-permute-done((f32[9,8,128]{2,1,0:T(8,128)S(1)}, f32[9,8,128]{2,1,0:T(8,128)S(1)}, u32[]{:S(2)}, u32[]{:S(2)}) %collective-permute-start.11) | collective-permute-done | bytes 36896 | tf_op jit(solution)/shard_map/ppermute | solution.py:747
  76.7 1.4 %combine_parts.3 = (bf16[1,8192]{1,0:T(2,128)(2,1)}, f32[8,128]{1,0:T(8,128)}) custom-call(s32[10]{0:T(128)S(1)} %pad_add_fusion.info_ref, f32[9,8,128]{2,1,0:T(8,128)S(1)} %near_rows.1.refs_0_, f32[9,8,128]{2,1,0:T(8,128)S(1)} %collective-permute-done.11.refs_1_), custom_call_target="tpu_custom_call" | custom-call | flops 1 | bytes 1 | tf_op jit(solution)/shard_map/combine_parts/pallas_call | solution.py:389
  78.1 0.0 copy-done.1
Async XLA Ops:
  0.8 34.0 %collective-permute-start.5 = (bf16[2,4,8,1024]{3,2,1,0:T(8,128)(2,1)S(1)}, bf16[2,4,8,1024]{3,2,1,0:T(8,128)(2,1)S(1)}, u32[]{:S(2)}, u32[]{:S(2)}) collective-permute-start(bf16[2,4,8,1024]{3,2,1,0:T(8,128)(2,1)S(1)} %get-tuple-element.132), channel_id=1, source_target_pairs={{0,24},{2,26},{4,28},{6,30},{8,16},{10,18},{12,20},{14,22},{1,25},... | collective-permute-start | bytes 393224 | tf_op jit(solution)/shard_map/ppermute | solution.py:552
  3.5 37.7 %copy-start.2 = (bf16[1,8192]{1,0:T(2,128)(2,1)S(1)}, bf16[1,8192]{1,0:T(2,128)(2,1)}, u32[]{:S(2)}) copy-start(bf16[1,8192]{1,0:T(2,128)(2,1)} %q_ref.1) | copy-start | bytes 49156
  3.5 23.1 %all-to-all-start = ((bf16[16,3,8,1024]{3,2,1,0:T(8,128)(2,1)}), bf16[16,3,8,1024]{3,2,1,0:T(8,128)(2,1)S(1)}, u32[]{:S(2)}, u32[]{:S(2)}) async-start(bf16[16,3,8,1024]{3,2,1,0:T(8,128)(2,1)} %bitcast), calls=%async_computation | async-start | bytes 1572864 | tf_op jit(solution)/shard_map/cond/branch_1_fun/all_to_all | solution.py:558
  8.8 19.8 %collective-permute-start.1 = (bf16[2,4,8,1024]{3,2,1,0:T(8,128)(2,1)S(1)}, bf16[2,4,8,1024]{3,2,1,0:T(8,128)(2,1)}, u32[]{:S(2)}, u32[]{:S(2)}) collective-permute-start(bf16[2,4,8,1024]{3,2,1,0:T(8,128)(2,1)S(1)} %get-tuple-element.74), channel_id=1, source_target_pairs={{0,28},{2,30},{4,24},{6,26},{8,20},{10,22},{12,16},{14,18},{1,29},... | collective-permute-start | bytes 393224 | tf_op jit(solution)/shard_map/cond/branch_1_fun/ppermute | solution.py:552
  10.1 18.5 %collective-permute-start.2 = (bf16[2,4,8,1024]{3,2,1,0:T(8,128)(2,1)S(1)}, bf16[2,4,8,1024]{3,2,1,0:T(8,128)(2,1)}, u32[]{:S(2)}, u32[]{:S(2)}) collective-permute-start(bf16[2,4,8,1024]{3,2,1,0:T(8,128)(2,1)S(1)} %get-tuple-element.75), channel_id=1, source_target_pairs={{0,16},{2,18},{4,20},{6,22},{8,24},{10,26},{12,28},{14,30},{1,17},... | collective-permute-start | bytes 393224 | tf_op jit(solution)/shard_map/cond/branch_1_fun/ppermute | solution.py:552
  11.4 21.9 %collective-permute-start.3 = (bf16[2,4,8,1024]{3,2,1,0:T(8,128)(2,1)S(1)}, bf16[2,4,8,1024]{3,2,1,0:T(8,128)(2,1)}, u32[]{:S(2)}, u32[]{:S(2)}) collective-permute-start(bf16[2,4,8,1024]{3,2,1,0:T(8,128)(2,1)S(1)} %get-tuple-element.76), channel_id=1, source_target_pairs={{0,20},{2,22},{4,16},{6,18},{8,28},{10,30},{12,24},{14,26},{1,21},... | collective-permute-start | bytes 393224 | tf_op jit(solution)/shard_map/cond/branch_1_fun/ppermute | solution.py:552
  27.2 0.7 collective-permute-start
  33.3 7.8 %collective-permute-start.6 = (f32[8,32,256]{2,1,0:T(8,128)S(1)}, f32[8,32,256]{2,1,0:T(8,128)S(1)}, u32[]{:S(2)}, u32[]{:S(2)}) collective-permute-start(f32[8,32,256]{2,1,0:T(8,128)S(1)} %get-tuple-element.137), channel_id=1, source_target_pairs={{0,1},{1,0},{2,3},{3,2},{4,5},{5,4},{6,7},{7,6},{8,9},{9,8},{10,11... | collective-permute-start | bytes 786440 | tf_op jit(solution)/shard_map/ppermute | solution.py:747
  34.8 27.9 %collective-permute-start.7 = (bf16[2,6,8,1024]{3,2,1,0:T(8,128)(2,1)}, bf16[2,6,8,1024]{3,2,1,0:T(8,128)(2,1)S(1)}, u32[]{:S(2)}, u32[]{:S(2)}) collective-permute-start(bf16[2,6,8,1024]{3,2,1,0:T(8,128)(2,1)} %get-tuple-element.139), channel_id=1, source_target_pairs={{0,24},{2,26},{4,28},{6,30},{8,16},{10,18},{12,20},{14,22},{1,25},... | collective-permute-start | bytes 589832 | tf_op jit(solution)/shard_map/ppermute | solution.py:552
  36.0 26.7 %collective-permute-start.8 = (bf16[2,6,8,1024]{3,2,1,0:T(8,128)(2,1)}, bf16[2,6,8,1024]{3,2,1,0:T(8,128)(2,1)S(1)}, u32[]{:S(2)}, u32[]{:S(2)}) collective-permute-start(bf16[2,6,8,1024]{3,2,1,0:T(8,128)(2,1)} %get-tuple-element.140), channel_id=1, source_target_pairs={{0,28},{2,30},{4,24},{6,26},{8,20},{10,22},{12,16},{14,18},{1,29},... | collective-permute-start | bytes 589832 | tf_op jit(solution)/shard_map/ppermute | solution.py:552
  37.3 31.8 %collective-permute-start.9 = (bf16[2,6,8,1024]{3,2,1,0:T(8,128)(2,1)}, bf16[2,6,8,1024]{3,2,1,0:T(8,128)(2,1)S(1)}, u32[]{:S(2)}, u32[]{:S(2)}) collective-permute-start(bf16[2,6,8,1024]{3,2,1,0:T(8,128)(2,1)} %get-tuple-element.141), channel_id=1, source_target_pairs={{0,16},{2,18},{4,20},{6,22},{8,24},{10,26},{12,28},{14,30},{1,17},... | collective-permute-start | bytes 589832 | tf_op jit(solution)/shard_map/ppermute | solution.py:552
  38.6 32.9 %collective-permute-start.10 = (bf16[2,6,8,1024]{3,2,1,0:T(8,128)(2,1)}, bf16[2,6,8,1024]{3,2,1,0:T(8,128)(2,1)S(1)}, u32[]{:S(2)}, u32[]{:S(2)}) collective-permute-start(bf16[2,6,8,1024]{3,2,1,0:T(8,128)(2,1)} %get-tuple-element.142), channel_id=1, source_target_pairs={{0,20},{2,22},{4,16},{6,18},{8,28},{10,30},{12,24},{14,26},{1,21},... | collective-permute-start | bytes 589832 | tf_op jit(solution)/shard_map/ppermute | solution.py:552
  43.7 3.4 %collective-permute-start.4 = (bf16[4,2,2,8,1024]{4,3,2,1,0:T(8,128)(2,1)S(1)}, bf16[4,2,2,8,1024]{4,3,2,1,0:T(8,128)(2,1)S(1)}, u32[]{:S(2)}, u32[]{:S(2)}) collective-permute-start(bf16[4,2,2,8,1024]{4,3,2,1,0:T(8,128)(2,1)S(1)} %get-tuple-element.86), channel_id=1, source_target_pairs={{16,18},{18,16},{20,22},{22,20},{24,26},{26,24},{28,30},{30,28},{1... | collective-permute-start | bytes 786440 | tf_op jit(solution)/shard_map/cond/branch_1_fun/ppermute | solution.py:555
  48.6 12.5 %all-to-all-start.1 = ((bf16[16,2,8,1024]{3,2,1,0:T(8,128)(2,1)}), bf16[16,2,8,1024]{3,2,1,0:T(8,128)(2,1)S(1)}, u32[]{:S(2)}, u32[]{:S(2)}) async-start(bf16[16,2,8,1024]{3,2,1,0:T(8,128)(2,1)} %relay_slots.1.rest_1_), calls=%async_computation.1 | async-start | bytes 1048576 | tf_op jit(solution)/shard_map/cond/branch_1_fun/all_to_all | solution.py:558
  57.1 0.7 copy-start
  72.7 4.0 %collective-permute-start.11 = (f32[9,8,128]{2,1,0:T(8,128)S(1)}, f32[9,8,128]{2,1,0:T(8,128)S(1)}, u32[]{:S(2)}, u32[]{:S(2)}) collective-permute-start(f32[9,8,128]{2,1,0:T(8,128)S(1)} %near_rows.1.refs_0_), channel_id=1, source_target_pairs={{0,1},{1,0},{2,3},{3,2},{4,5},{5,4},{6,7},{7,6},{8,9},{9,8},{10,11... | collective-permute-start | bytes 110600 | tf_op jit(solution)/shard_map/ppermute | solution.py:747
  74.1 3.9 %copy-start.1 = (bf16[40,8,2048]{2,1,0:T(8,128)(2,1)}, bf16[40,8,2048]{2,1,0:T(8,128)(2,1)S(1)}, u32[]{:S(2)}) copy-start(bf16[40,8,2048]{2,1,0:T(8,128)(2,1)S(1)} %store_near.1) | copy-start | bytes 3932164
